TPU v7x, 32 devices: a whole 2x2x4 slice. The times are simulated.
32 devices in a mesh: section: 4 (over x, core), seq: 2 (over y), dp: 4 (over z).
Axes of the slice: x: 2, y: 2, z: 4, core: 2. Of those that a mesh axis runs over, the one named last changes fastest.
Arguments:
- main_hidden: bfloat16 [4, 4, 256, 7168], P('section', 'dp', 'seq'), may hold values from -6 to 6
- embedded: bfloat16 [4, 4, 256, 7168], P('section', 'dp', 'seq'), may hold values from -6 to 6
- cotangent: bfloat16 [4, 4, 256, 7168], P('section', 'dp', 'seq'), may hold values from -6 to 6
- slot_token: int32 [4, 4, 2, 12], P('section', 'dp', None, 'seq'), may hold values from 0 to 127, as said below
- slot_count: int32 [4, 4, 2, 2], P('section', 'dp', None, 'seq'), may hold values from 1 to 6, as said below
- route_gate: float32 [4, 4, 2, 12], P('section', 'dp', None, 'seq'), may hold values from 0.2 to 2
- norm_gain: float32 [2, 2, 7168], replicated, may hold values from 0.5 to 1.5
- expert_weight: bfloat16 [2, 3, 7168, 2048], P(None, None, 'seq', 'dp'), may hold values from -0.0625 to 0.0625
Outputs:
- hidden_grad: bfloat16 [4, 4, 256, 7168], P('section', 'dp', 'seq')
- expert_grad: bfloat16 [4, 2, 3, 7168, 2048], P('section', None, None, 'seq', 'dp')
- gain_grad: float32 [4, 2, 2, 7168], P('section', None, None, ('seq', 'dp'))
Inputs may be any that keep to these rules, and one draw needn't show every extreme that they name: `slot_token`: the slots of one device and depth name distinct positions of that device's block. `slot_count`: in every micro-batch, sequence and depth some device has all 6 slots live.
All inputs are finite; a program needn't handle non-finite values.
Results may differ from a plain program's by a relative error of at most 0.0077.
Values may be sent and summed in bfloat16 or wider, within the bound.
No kernel may reach another device: no remote copies, remote signals or barrier semaphores. Data moves between devices by JAX's collectives and lax.ppermute only.
A program may use at most 128 MiB of HBM per device.

v0:
```python
import jax
import jax.numpy as jnp
from jax import lax
from jax.experimental import pallas as pl
from jax.experimental.pallas import tpu as pltpu
from jax.sharding import PartitionSpec as P

eps_norm = 1e-06
lanes = 128
f32 = jnp.float32
bf16 = jnp.bfloat16
vmem = pl.BlockSpec(memory_space=pltpu.VMEM)
smem = pl.BlockSpec(memory_space=pltpu.SMEM)
anywhere = pl.BlockSpec(memory_space=pl.ANY)


def ring(value, axis, steps):
    count = lax.axis_size(axis)
    return lax.ppermute(value, axis, [(i, (i + steps) % count) for i in range(count)])


def hop(value, section_step, seq_step):
    sections, seqs = lax.axis_size("section"), lax.axis_size("seq")
    pairs = [
        (c * seqs + s, (c + section_step) % sections * seqs + (s + seq_step) % seqs)
        for c in range(sections)
        for s in range(seqs)
    ]
    return lax.ppermute(value, ("section", "seq"), pairs)


def trade_seq(pieces, section_step=0):
    if section_step == 0:
        return [pieces[0]] + [ring(pieces[o], "seq", o) for o in range(1, len(pieces))]
    return [hop(piece, section_step, o) for o, piece in enumerate(pieces)]


def partner(place, step, count):
    return place ^ step if count & (count - 1) == 0 else (place - step) % count


def gather_dp(block):
    count = lax.axis_size("dp")
    return [block] + [
        lax.ppermute(block, "dp", [(partner(z, i, count), z) for z in range(count)])
        for i in range(1, count)
    ]


def return_dp(blocks):
    count = lax.axis_size("dp")
    return [blocks[0]] + [
        lax.ppermute(blocks[i], "dp", [(z, partner(z, i, count)) for z in range(count)])
        for i in range(1, count)
    ]


def pair_seq(own, send):
    if lax.axis_size("seq") == 2:
        return own, ring(send, "seq", 1)
    return lax.psum(own, "seq"), jnp.zeros_like(send)


def inv_rms(value):
    return lax.rsqrt(jnp.mean(value * value, axis=-1, keepdims=True) + eps_norm)


def iota(shape, dim):
    return lax.broadcasted_iota(jnp.int32, shape, dim)


def token_column(token, depth):
    capacity = token.shape[3]
    out = jnp.full((capacity, 1), token[0, 0, depth, 0], jnp.int32)
    for c in range(1, capacity):
        out = jnp.where(iota((capacity, 1), 0) == c, token[0, 0, depth, c], out)
    return out


def gate_column(gate, depth):
    capacity = gate.shape[3]
    out = jnp.full((capacity, 1), gate[0, 0, depth, 0], f32)
    for c in range(1, capacity):
        out = jnp.where(iota((capacity, 1), 0) == c, gate[0, 0, depth, c], out)
    return out


def live_column(count, depth, capacity):
    return (iota((capacity, 1), 0) < count[0, 0, depth, 0]).astype(f32)


def met_column(token, count):
    capacity = token.shape[3]
    second = token_column(token, 1)
    out = jnp.zeros((capacity, 1), f32)
    for c in range(capacity):
        out += ((second == token[0, 0, 0, c]) & (c < count[0, 0, 0, 0])).astype(f32)
    return jnp.minimum(out, 1.0)


def pick(column, table):
    hot = (column == iota((column.shape[0], table.shape[0]), 1)).astype(bf16)
    return jnp.dot(hot, table, preferred_element_type=f32)


def pick_ahead(column, table, after):
    return pick(column, table) + pick(column - table.shape[0], after)


def thirds(column):
    high = column.astype(bf16).astype(f32)
    mid = (column - high).astype(bf16).astype(f32)
    return [high, mid, column - high - mid]


def in_lanes(columns):
    lane = iota((columns[0].shape[0], lanes), 1)
    out = jnp.zeros(lane.shape, f32)
    for k, column in enumerate(columns):
        out = jnp.where(lane == k, column, out)
    return out


def coded(column):
    return in_lanes(thirds(column))


def decoded(block, first=0):
    lane = iota(block.shape, 1)
    inside = (lane >= first) & (lane < first + 3)
    return jnp.sum(jnp.where(inside, block.astype(f32), 0.0), axis=1, keepdims=True)


def piece_of(value, place, count, step):
    width = value.shape[-1] // count
    want = lax.rem(place + step, count)
    out = value[:, :width]
    for p in range(1, count):
        out = jnp.where(want == p, value[:, p * width : (p + 1) * width], out)
    return out


def pieces_of(value, place, count):
    return [piece_of(value, place, count, o) for o in range(count)]


def blocks_of(value, place, count):
    size = value.shape[0] // count
    out = []
    for o in range(count):
        block = value[:size]
        for j in range(1, count):
            want = lax.rem(place + o, count) == j
            block = jnp.where(want, value[j * size : (j + 1) * size], block)
        out.append(block)
    return out


def in_order(got, place, axis):
    count = len(got)
    out = []
    for j in range(count):
        block = got[0]
        for o in range(1, count):
            block = jnp.where(lax.rem(place - o + count, count) == j, got[o], block)
        out.append(block)
    return jnp.concatenate(out, axis)


def as_row(column):
    size = column.shape[0]
    here = iota((size, size), 0) == iota((size, size), 1)
    return jnp.sum(jnp.where(here, column, 0.0), axis=0, keepdims=True)


def folds(rows, width):
    for count in (1, 2, 4, 8):
        if rows * count % 16 == 0 and width % (count * lanes) == 0:
            return count
    return 1


def folded(value, count):
    step = value.shape[1] // count
    return jnp.concatenate([value[:, g * step : (g + 1) * step] for g in range(count)], 0)


def unfolded(value, count):
    rows = value.shape[0] // count
    return jnp.concatenate([value[g * rows : (g + 1) * rows] for g in range(count)], 1)


def column_part(blocks, rows, g):
    return jnp.concatenate(
        [block[g * rows : (g + 1) * rows].astype(f32) for block in blocks], 0
    ).astype(bf16)


def summed(got, parts):
    return unfolded(sum(g.astype(f32) for g in got), parts)


def chunk_of(width):
    for step in (1024, 896, 512, 256, 128):
        if width % step == 0:
            return step
    return width


def call(name, fn, outs, small, *args, after=(), flops=0, limit=12):
    shapes = [jax.ShapeDtypeStruct(shape, kind) for shape, kind in outs]
    n_small, n_args, n_after = len(small), len(args), len(after)

    def body(*refs):
        values = list(refs[:n_small]) + [r[...] for r in refs[n_small : n_small + n_args]]
        for ref, value in zip(refs[n_small + n_args + n_after :], fn(*values)):
            ref[...] = value.astype(ref.dtype)

    size = sum(a.size * a.dtype.itemsize for a in list(args) + shapes)
    return pl.pallas_call(
        body,
        name=name,
        out_shape=shapes,
        in_specs=[smem] * n_small + [vmem] * n_args + [anywhere] * n_after,
        out_specs=[vmem] * len(shapes),
        compiler_params=pltpu.CompilerParams(vmem_limit_bytes=limit << 20),
        cost_estimate=pl.CostEstimate(flops=flops, bytes_accessed=size, transcendentals=0),
    )(*small, *args, *after)


def fetch(weight_ref, depth, kinds, buffer, sems, parts):
    step = weight_ref.shape[2] // parts
    copies = []
    for g in range(parts):
        row = []
        for k, kind in enumerate(kinds):
            copy = pltpu.make_async_copy(
                weight_ref.at[depth, kind, pl.ds(g * step, step)],
                buffer.at[g, k],
                sems.at[g, k],
            )
            copy.start()
            row.append(copy)
        copies.append(row)
    return copies


def fetched(weight, kinds, parts):
    hidden = weight.shape[3]
    return [
        pltpu.VMEM((parts, len(kinds), weight.shape[2] // parts, hidden), bf16),
        pltpu.SemaphoreType.DMA((parts, len(kinds))),
    ]


def project(name, blocks, weight, depth, kinds, parts, others=None, select=None, gain=None, mates=None, after=()):
    groups = len(blocks)
    rows = blocks[0].shape[0] // parts // (1 if others is None else 2)
    width, hidden = weight.shape[2:]
    step = width // parts
    other_kinds = others if others is not None else ()
    first_kinds, kinds = kinds, kinds + other_kinds
    total, many = rows * groups, len(kinds) * hidden
    marked = select is not None or mates is not None
    extra = lanes if marked else 0

    def body(*refs):
        refs = list(refs)
        where_ref = refs.pop(0) if select is not None else None
        x_refs, w_ref, refs = refs[:groups], refs[groups], refs[groups + 1 :]
        if select is not None:
            select_ref, gain_ref = refs.pop(0), refs.pop(0)
        if mates is not None:
            mate_refs, refs = refs[:groups], refs[groups:]
        refs = refs[len(after) :]
        own_ref, send_ref = refs.pop(0), refs.pop(0)
        kept_ref = refs.pop(0) if select is not None else None
        buffer, sems = refs
        copies = fetch(w_ref, depth, kinds, buffer, sems, parts)
        x_all = [r[...] for r in x_refs]
        mate_all = [r[...] for r in mate_refs] if mates is not None else x_all
        if select is not None:
            gain_all = piece_of(gain_ref[1, 0:1, :], where_ref[0], gain.shape[2] // width, 0)
        sums = [jnp.zeros((total, hidden), f32) for _ in kinds]
        mark = jnp.zeros((total, 1), f32)
        for g in range(parts):
            x = column_part(x_all, rows, g)[:, :step]
            if marked:
                mate = x if mates is None else column_part(mate_all, rows, g)
                mark += jnp.sum(x.astype(f32) * mate.astype(f32), axis=1, keepdims=True)
            if select is not None:
                chosen = jnp.dot(select_ref[...], x, preferred_element_type=f32)
                x = (chosen * gain_all[:, g * step : (g + 1) * step]).astype(bf16)
                kept_ref[:, g * step : (g + 1) * step] = x
            for k in range(len(kinds)):
                if k == len(first_kinds):
                    x = column_part(x_all, rows, parts + g)[:, :step]
                copies[g][k].wait()
                sums[k] += jnp.dot(x, buffer[g, k], preferred_element_type=f32)
        for k in range(len(kinds)):
            own_ref[:, k * hidden : (k + 1) * hidden] = sums[k]
            send_ref[:, k * hidden : (k + 1) * hidden] = sums[k].astype(bf16)
        if marked:
            own_ref[:, many:] = in_lanes([mark])
            send_ref[:, many:] = coded(mark).astype(bf16)

    args = list(blocks) + [pltpu.with_memory_space_constraint(weight, pltpu.HBM)]
    specs = [vmem] * groups + [anywhere]
    outs = [
        jax.ShapeDtypeStruct((total, many + extra), f32),
        jax.ShapeDtypeStruct((total, many + extra), bf16),
    ]
    if select is not None:
        where, table = select
        args, specs = [where] + args + [table, gain], [smem] + specs + [vmem, vmem]
        outs.append(jax.ShapeDtypeStruct((total, width), bf16))
    if mates is not None:
        args, specs = args + list(mates), specs + [vmem] * groups
    return pl.pallas_call(
        body,
        name=name,
        in_specs=specs + [anywhere] * len(after),
        out_specs=[vmem] * len(outs),
        out_shape=outs,
        scratch_shapes=fetched(weight, kinds, parts),
        compiler_params=pltpu.CompilerParams(vmem_limit_bytes=16 << 20),
        cost_estimate=pl.CostEstimate(
            flops=2 * total * width * many, bytes_accessed=2 * width * many, transcendentals=0
        ),
    )(*args, *after)


def expand(name, prepare, args, saved, weight, depth, kinds, groups, parts, after=()):
    width, hidden = weight.shape[2:]
    total = saved[0][0][0]
    rows, step = total // groups, width // parts
    count, kept = len(args), len(saved)

    def body(*refs):
        in_refs, w_ref = refs[:count], refs[count]
        refs = refs[count + 1 + len(after) :]
        saved_refs, out_refs, (buffer, sems) = refs[:kept], refs[kept:-2], refs[-2:]
        copies = fetch(w_ref, depth, kinds, buffer, sems, parts)
        for ref, value in zip(saved_refs, prepare(*[r[...] for r in in_refs])):
            ref[...] = value.astype(ref.dtype)
        out = []
        for g in range(parts):
            part = jnp.zeros((total, step), f32)
            for k in range(len(kinds)):
                copies[g][k].wait()
                part += lax.dot_general(
                    saved_refs[k][...], buffer[g, k], (((1,), (1,)), ((), ())),
                    preferred_element_type=f32,
                )
            out.append(part)
        for z in range(groups):
            block = jnp.concatenate([part[z * rows : (z + 1) * rows] for part in out], 0)
            out_refs[z][...] = block.astype(bf16)

    results = pl.pallas_call(
        body,
        name=name,
        in_specs=[vmem] * count + [anywhere] * (1 + len(after)),
        out_specs=[vmem] * (kept + groups),
        out_shape=[jax.ShapeDtypeStruct(shape, kind) for shape, kind in saved]
        + [jax.ShapeDtypeStruct((rows * parts, step), bf16)] * groups,
        scratch_shapes=fetched(weight, kinds, parts),
        compiler_params=pltpu.CompilerParams(vmem_limit_bytes=16 << 20),
        cost_estimate=pl.CostEstimate(
            flops=2 * total * width * hidden * len(kinds),
            bytes_accessed=2 * width * hidden * len(kinds),
            transcendentals=0,
        ),
    )(*args, pltpu.with_memory_space_constraint(weight, pltpu.HBM), *after)
    return results[:kept], results[kept:]


def outer(name, depth, depths, build, args, d_gate, d_up, act, width, parts, before, after=()):
    total, hidden = act.shape
    step = width // parts
    count = len(args)
    earlier = [] if before is None else [pltpu.with_memory_space_constraint(before, pltpu.HBM)]

    def contract(left, right):
        return lax.dot_general(left, right, (((0,), (0,)), ((), ())), preferred_element_type=f32)

    def body(*refs):
        values = [r[...] for r in refs[:count]]
        gate_ref, up_ref, act_ref = refs[count : count + 3]
        out_ref, tick_ref, buffer, sems = refs[-4:]
        tick_ref[...] = jnp.zeros_like(tick_ref)
        copies = []
        for g in range(parts):
            rows, dout = build(values, g)
            pairs = ((rows, gate_ref), (rows, up_ref), (dout, act_ref))
            for k, (left, right_ref) in enumerate(pairs):
                buffer[g, k] = contract(left, right_ref[...]).astype(bf16)
                copy = pltpu.make_async_copy(
                    buffer.at[g, k],
                    out_ref.at[0, depth, k, pl.ds(g * step, step)],
                    sems.at[g, k],
                )
                copy.start()
                copies.append(copy)
        for copy in copies:
            copy.wait()

    return pl.pallas_call(
        body,
        name=name,
        in_specs=[vmem] * (count + 3) + [anywhere] * (len(earlier) + len(after)),
        out_specs=[anywhere, vmem],
        out_shape=[
            jax.ShapeDtypeStruct((1, depths, 3, width, hidden), bf16),
            jax.ShapeDtypeStruct((8, lanes), f32),
        ],
        input_output_aliases={} if before is None else {count + 3: 0},
        scratch_shapes=[
            pltpu.VMEM((parts, 3, step, hidden), bf16),
            pltpu.SemaphoreType.DMA((parts, 3)),
        ],
        compiler_params=pltpu.CompilerParams(vmem_limit_bytes=24 << 20),
        cost_estimate=pl.CostEstimate(
            flops=6 * total * width * hidden, bytes_accessed=6 * width * hidden, transcendentals=0
        ),
    )(*args, d_gate, d_up, act, *earlier, *after)


def backward_rows(hidden, ahead_1, ahead_2, d_mixed_2, keep, gain):
    scale_1 = inv_rms(hidden)
    unit_1 = hidden * scale_1
    unit_e1 = ahead_1 * inv_rms(ahead_1)
    unit_e2 = ahead_2 * inv_rms(ahead_2)
    mixed = (unit_1 * gain[0, 0:1] + unit_e1 * gain[0, 1:2]).astype(bf16).astype(f32)
    scale_2 = inv_rms(mixed)
    unit_2 = mixed * scale_2
    u = d_mixed_2 * gain[1, 0:1]
    grad_1 = (u - unit_2 * jnp.mean(u * unit_2, axis=-1, keepdims=True)) * scale_2
    v = grad_1 * gain[0, 0:1]
    grad_0 = (v - unit_1 * jnp.mean(v * unit_1, axis=-1, keepdims=True)) * scale_1
    kept_1, kept_2 = grad_1 * keep, d_mixed_2 * keep
    terms = [
        jnp.sum(a * b, axis=0, keepdims=True)
        for a, b in ((kept_1, unit_1), (kept_1, unit_e1), (kept_2, unit_2), (kept_2, unit_e2))
    ]
    return grad_0.astype(bf16), jnp.concatenate(terms, 0)


def dense_rows(name, token, count, hidden, embed, next_rows, cotangent, gain, before, half, halves, after=()):
    tokens, width = hidden.shape
    step = next_rows.shape[0]
    blocks = tokens // step // halves
    low, last = half * blocks, tokens // step - 1
    size = 2 * lanes
    capacity = token.shape[3]
    earlier = [] if before is None else list(before)

    def body(token_ref, count_ref, hidden_ref, embed_ref, next_ref, cot_ref, gain_ref, *refs):
        out_ref, terms_ref, mixed_ref, sums_ref = refs[-4:]
        sums_ref[...] = jnp.zeros_like(sums_ref)
        row, column = (iota((2 * step, 2 * step), dim) for dim in range(2))
        shift = (column == jnp.where(row < step, row + 1, row + 2 - step)).astype(bf16)
        places = [pl.ds(at, size) for at in range(0, width, size)]

        def folded_lanes(value):
            return sum(value[:, at : at + lanes] for at in range(0, size, lanes))

        def mean(value):
            return jnp.sum(value, axis=1, keepdims=True) / width

        def one(i, carry):
            block = low + i
            first = pl.multiple_of(block * step, step)
            rows = pl.ds(first, step)
            follow = pl.ds(pl.multiple_of(jnp.minimum(block + 1, last) * step, step), step)
            here = iota((step, 1), 0) + first
            keep = jnp.ones((step, 1), f32)
            for k in range(2):
                for c in range(capacity):
                    out = (here == token_ref[0, 0, k, c]) & (c < count_ref[0, 0, k, 0])
                    keep = jnp.where(out, 0.0, keep)

            def ahead(at, hot):
                after = embed_ref[follow, at]
                if half == halves - 1:
                    after = jnp.where(block == last, next_ref[:, at], after)
                both = jnp.concatenate([embed_ref[rows, at], after], 0)
                return jnp.dot(hot, both, preferred_element_type=f32)

            square_h, square_e = jnp.zeros((step, lanes), f32), jnp.zeros((2 * step, lanes), f32)
            for at in places:
                h, e = hidden_ref[rows, at].astype(f32), ahead(at, shift)
                square_h += folded_lanes(h * h)
                square_e += folded_lanes(e * e)
            scale_1 = lax.rsqrt(mean(square_h) + eps_norm)
            scale_e = lax.rsqrt(mean(square_e) + eps_norm)
            scale_e1, scale_e2 = scale_e[:step], scale_e[step:]

            sums = [jnp.zeros((step, lanes), f32) for _ in range(4)]
            for at in places:
                through = hidden_ref[rows, at].astype(f32) * scale_1 * gain_ref[0, 0:1, at]
                mixed = through + ahead(at, shift[:step]) * scale_e1 * gain_ref[0, 1:2, at]
                kept = mixed.astype(bf16)
                mixed_ref[:, at] = kept
                mixed = kept.astype(f32)
                u = cot_ref[rows, at].astype(f32) * gain_ref[1, 0:1, at]
                pairs = ((mixed, mixed), (u, mixed), (u, through), (mixed, through))
                sums = [c + folded_lanes(a * b) for c, (a, b) in zip(sums, pairs)]
            square, along, u_back, mixed_back = (mean(value) for value in sums)
            scale_2 = lax.rsqrt(square + eps_norm)
            share_2 = scale_2 * scale_2 * along
            share_1 = scale_2 * (u_back - share_2 * mixed_back) * scale_1
            keep_2, keep_h = keep * scale_2, keep * scale_1
            keep_e1, keep_e2 = keep * scale_e1, keep * scale_e2

            for at in places:
                e = ahead(at, shift)
                h = hidden_ref[rows, at].astype(f32)
                mixed = mixed_ref[:, at].astype(f32)
                cot = cot_ref[rows, at].astype(f32)
                grad_1 = (cot * gain_ref[1, 0:1, at] - mixed * share_2) * scale_2
                grad_0 = (grad_1 * gain_ref[0, 0:1, at] - h * share_1) * scale_1
                out_ref[rows, at] = grad_0.astype(bf16)
                terms = (
                    grad_1 * (h * keep_h),
                    grad_1 * (e[:step] * keep_e1),
                    cot * (mixed * keep_2),
                    cot * (e[step:] * keep_e2),
                )
                for k, term in enumerate(terms):
                    sums_ref[k, :, at] += sum(term[r : r + 8] for r in range(0, step, 8))
            return carry

        lax.fori_loop(0, blocks, one, 0)
        for k in range(4):
            term = jnp.sum(sums_ref[k], axis=0, keepdims=True)
            terms_ref[k : k + 1] = term + refs[1][k : k + 1] if earlier else term

    return pl.pallas_call(
        body,
        name=name,
        in_specs=[smem] * 2 + [vmem] * (5 + len(earlier)) + [anywhere] * len(after),
        out_specs=[vmem] * 2,
        out_shape=[
            jax.ShapeDtypeStruct((tokens, width), bf16),
            jax.ShapeDtypeStruct((4, width), f32),
        ],
        input_output_aliases={7: 0} if earlier else {},
        scratch_shapes=[pltpu.VMEM((step, width), bf16), pltpu.VMEM((4, 8, width), f32)],
        compiler_params=pltpu.CompilerParams(vmem_limit_bytes=8 << 20),
        cost_estimate=pl.CostEstimate(
            flops=60 * tokens * width // halves,
            bytes_accessed=10 * tokens * width // halves,
            transcendentals=0,
        ),
    )(token, count, hidden, embed, next_rows, cotangent, gain, *earlier, *after)


def local(
    main_hidden, embedded, cotangent, slot_token, slot_count, route_gate, norm_gain, expert_weight
):
    depths, _, features = norm_gain.shape
    tokens = main_hidden.shape[2]
    slots = slot_token.shape[3]
    seqs, groups = lax.axis_size("seq"), lax.axis_size("dp")
    rows = seqs * slots
    total = groups * rows
    width = features // seqs
    share = width // groups
    hidden_units = expert_weight.shape[3]
    parts = folds(rows, width)
    where = jnp.stack([lax.axis_index("seq"), lax.axis_index("dp")]).astype(jnp.int32)
    source, embed, cot = main_hidden[0, 0], embedded[0, 0], cotangent[0, 0]
    facts = (slot_token, slot_count)
    packed = ((rows * parts, width // parts), bf16)
    part_rows = ((rows, width), f32)

    def payload(value):
        return folded(value, parts)

    asked_token = ring(slot_token, "section", -1)

    def own_rows(where, token, count, gate, embed, cot):
        first, second = token_column(token, 0), token_column(token, 1)
        live_1, live_2 = (live_column(count, k, slots) for k in range(2))
        weight_1, weight_2 = gate_column(gate, 0) * live_1, gate_column(gate, 1) * live_2
        facts = in_lanes(
            [first.astype(f32), second.astype(f32), live_1, live_2]
            + thirds(weight_1)
            + thirds(weight_2)
        )
        ahead_1, ahead_2 = pick(first + 1, embed), pick(first + 2, embed)
        block = jnp.concatenate([ahead_1, ahead_2, pick(first, cot), pick(second, cot) * weight_2], 0)
        notes = jnp.concatenate([coded(inv_rms(ahead_1)), coded(inv_rms(ahead_2)), facts, facts], 0)
        head = embed[:depths].astype(f32)
        scale = coded(inv_rms(head))
        heads = [
            jnp.concatenate([head[:, p * width : (p + 1) * width], scale], 1) for p in range(seqs)
        ]
        return [
            jnp.concatenate([jnp.concatenate([piece, notes], 1)] + heads, 0)
            for piece in pieces_of(block, where[0], seqs)
        ]

    own_sent = call(
        "own_rows", own_rows, [((4 * slots + depths * seqs, width + lanes), bf16)] * seqs,
        (where, slot_token, slot_count, route_gate), embed, cot, after=(asked_token,),
    )
    own_got = trade_seq(own_sent)

    def source_rows(where, asked, source):
        first = pick(token_column(asked, 0), source)
        second = pick(token_column(asked, 1), source)
        scale = coded(inv_rms(first))
        sent = [jnp.concatenate([p, scale], 1) for p in pieces_of(first, where[0], seqs)]
        sent[0] = jnp.concatenate([sent[0], second], 1)
        return sent + [first]

    *sent, asked_rows = call(
        "source_rows", source_rows,
        [((slots, width + lanes + features), bf16)]
        + [((slots, width + lanes), bf16)] * (seqs - 1)
        + [((slots, features), bf16)],
        (where, asked_token), source, after=(own_sent[0],),
    )
    start_got = trade_seq(sent, 1)

    def own_parts(where, *got):
        got = [g.astype(f32) for g in got]
        first = 4 * slots
        block_1, block_2, block_3, block_4 = (
            in_order([g[k * slots : (k + 1) * slots] for g in got], where[0], 0) for k in range(4)
        )
        facts = block_3[:, width:]
        heads = in_order([g[first:] for g in got], where[0], 0)
        heads = [heads[j * depths * seqs : (j + 1) * depths * seqs] for j in range(seqs)]
        units = []
        for k, block in ((1, block_1), (2, block_2)):
            unit = block[:, :width] * decoded(block[:, width:])
            after = []
            for j in range(seqs):
                token = facts[j * slots : (j + 1) * slots, 0:1]
                add = jnp.zeros((slots, width), f32)
                for i in range(k if j + 1 < seqs else 0):
                    row = heads[j + 1][i : i + 1]
                    for p in range(1, seqs):
                        at = p * depths + i
                        row = jnp.where(where[0] == p, heads[j + 1][at : at + 1], row)
                    row = row[:, :width] * decoded(row[:, width:])
                    add += jnp.where(token == float(tokens + i - k), row, 0.0)
                after.append(add)
            units.append(unit + jnp.concatenate(after, 0))
        out = folded(block_4[:, :width], parts)
        none = jnp.zeros(((parts - 1) * rows, lanes), f32)
        tail = facts if parts == 1 else jnp.concatenate([facts, none], 0)
        follow = got[-1][first:, :width]
        follow = jnp.concatenate([follow[p * depths : (p + 1) * depths] for p in range(seqs)], 1)
        follow = jnp.where(where[0] == seqs - 1, 0.0, follow)
        follow = jnp.concatenate([follow, jnp.zeros((16 - depths, features), f32)], 0)
        return block_3[:, :width], jnp.concatenate([out, tail], 1), facts, *units, follow

    cot_1, dout_2, own_facts, unit_e1, unit_e2, next_rows = call(
        "own_parts", own_parts,
        [part_rows, ((rows * parts, width // parts + lanes), bf16), ((rows, lanes), f32)]
        + [part_rows] * 2
        + [((16, features), bf16)],
        (where,), *own_got,
    )

    def first_mixed(where, own_facts, unit_e1, gain, *got):
        start = in_order([g[:, : width + lanes].astype(f32) for g in got], where[0], 0)
        unit = start[:, :width] * decoded(start[:, width:])
        gain_h, gain_e = (piece_of(gain[0, k : k + 1], where[0], seqs, 0) for k in range(2))
        mixed = (unit * gain_h + unit_e1 * gain_e).astype(bf16).astype(f32)
        return payload(mixed * own_facts[:, 2:3]), unit

    rows_1, unit_1 = call(
        "first_mixed", first_mixed, [packed, part_rows],
        (where,), own_facts, unit_e1, norm_gain, *start_got,
    )
    rows_1_all = gather_dp(rows_1)

    def second_base(where, token, count, start, table, after, gain):
        second = token_column(token, 1)
        start = start[:, width + lanes :].astype(f32)
        ahead_1 = pick_ahead(second + 1, table, after)
        ahead_2 = pick_ahead(second + 2, table, after)
        unit = start * inv_rms(start)
        mixed = unit * gain[0, 0:1] + ahead_1 * inv_rms(ahead_1) * gain[0, 1:2]
        mixed = mixed.astype(bf16).astype(f32)
        own = mixed * inv_rms(mixed) * gain[1, 0:1] * (1.0 - met_column(token, count))
        out = (own + ahead_2 * inv_rms(ahead_2) * gain[1, 1:2]) * live_column(count, 1, slots)
        return pieces_of(out, where[0], seqs) + [ahead_1, ahead_2]

    *base_parts, ahead_21, ahead_22 = call(
        "second_base", second_base,
        [((slots, width), bf16)] * seqs + [((slots, features), bf16)] * 2,
        (where, *facts), start_got[0], embed, next_rows, norm_gain, after=(rows_1,),
    )
    base_got = trade_seq(base_parts)

    first_own, first_send = project(
        "gate_up_1", rows_1_all, expert_weight, 0, (0, 1), parts, after=(ahead_21, base_got[-1])
    )
    first = pair_seq(first_own, first_send)

    def fixed_order(where, dout, *got):
        base = payload(in_order([g.astype(f32) for g in got], where[0], 0))
        none = jnp.zeros((base.shape[0], lanes), f32)
        return [jnp.concatenate([jnp.concatenate([base, none], 1), dout.astype(f32)], 0)]

    (fixed_rows,) = call(
        "fixed_order", fixed_order, [((2 * rows * parts, width // parts + lanes), bf16)],
        (where,), dout_2, *base_got, after=(first_send,),
    )
    fixed_all = gather_dp(fixed_rows)

    def forward_1(own, other):
        both = own + other.astype(f32)
        gate, up = both[:, :hidden_units], both[:, hidden_units:]
        return gate * jax.nn.sigmoid(gate) * up, both

    (act_1, both_1), out_blocks = expand(
        "down_1", forward_1, first,
        [((total, hidden_units), bf16), ((total, 2 * hidden_units), f32)],
        expert_weight, 0, (2,), groups, parts, after=(fixed_rows,),
    )
    out_got = return_dp(out_blocks)

    hidden, _ = lax.optimization_barrier((source, rows_1))
    hidden = ring(hidden, "section", 1)
    dense = dense_rows(
        "dense_a", *facts, hidden, embed, next_rows, cot, norm_gain, None, 0, 2,
        after=(out_blocks[0],),
    )

    def second_prev(own_facts, rows_1, *got):
        value = unfolded(rows_1.astype(f32), parts) + summed(got, parts) * decoded(own_facts, 4)
        return payload(value), value.astype(bf16)

    prev, prev_own = call(
        "second_prev", second_prev, [packed, ((rows, width), bf16)],
        (), own_facts, rows_1, *out_got, after=(dense[1],),
    )
    prev_all = gather_dp(prev)

    def slot_facts(*blocks):
        facts = jnp.concatenate(
            [block[rows * parts : rows * (parts + 1)].astype(f32)[:, width // parts :] for block in blocks], 0
        )
        base = (iota((total, 1), 0) // slots * tokens).astype(f32)
        first, second = facts[:, 0:1] + base, facts[:, 1:2] + base
        live = (facts[:, 3:4] > 0) & (as_row(facts[:, 2:3]) > 0)
        same = ((second == as_row(first)) & live).astype(f32)
        return same, same, same[:rows, :rows], decoded(facts, 4)

    same, same_16, same_own, weight_1 = call(
        "slot_facts", slot_facts,
        [((total, total), f32), ((total, total), bf16), ((rows, rows), f32), ((total, 1), f32)],
        (), *fixed_all, after=(prev,),
    )
    fixed_own, fixed_send = project(
        "fixed_2", fixed_all, expert_weight, 1, (0, 1), parts,
        others=(2,), after=(same_own,),
    )
    fixed_pair = pair_seq(fixed_own, fixed_send)

    mixed_own, mixed_send, chosen = project(
        "gate_up_2", prev_all, expert_weight, 1, (0, 1), parts,
        select=(where, same_16), gain=norm_gain, after=(fixed_own,),
    )
    second = pair_seq(mixed_own, mixed_send)
    prev_w_own, prev_w_send = project(
        "prev_down", prev_all, expert_weight, 0, (2,), parts, after=(mixed_send,)
    )
    prev_pair = pair_seq(prev_w_own, prev_w_send)

    def gates_back(gate, up, d_act):
        sig = jax.nn.sigmoid(gate)
        d_gate = d_act * up * sig * (1.0 + gate * (1.0 - sig))
        return d_gate, d_act * gate * sig

    def backward_2(own, other, fixed_own, fixed_other, same):
        many = 2 * hidden_units
        square = own[:, many : many + 1] + decoded(other[:, many:])
        scale = lax.rsqrt(square / features + eps_norm)
        row = jnp.sum(same * as_row(scale), axis=1, keepdims=True)
        both = (own[:, :many] + other[:, :many].astype(f32)) * row
        fixed = fixed_own + fixed_other.astype(f32)
        both = both + fixed[:, :many]
        gate, up = both[:, :hidden_units], both[:, hidden_units:]
        d_gate, d_up = gates_back(gate, up, fixed[:, many:])
        return d_gate, d_up, gate * jax.nn.sigmoid(gate) * up, scale, row

    units = ((total, hidden_units), bf16)
    (d_gate_2, d_up_2, act_2, scale_2, row_2), d_rows_blocks = expand(
        "back_rows_2", backward_2,
        second + fixed_pair + (same,),
        [units, units, units, ((total, 1), f32), ((total, 1), f32)],
        expert_weight, 1, (0, 1), groups, parts, after=(prev_w_own,),
    )
    d_rows_got = return_dp(d_rows_blocks)
    dense, dense_terms = dense_rows(
        "dense_b", *facts, hidden, embed, next_rows, cot, norm_gain, dense, 1, 2,
        after=(d_rows_blocks[0],),
    )
    def first_grad(where, cot, same, gain, *got):
        d_rows = summed(got, parts)
        added = lax.dot_general(
            same, d_rows, (((0,), (0,)), ((), ())),
            precision=lax.Precision.HIGHEST, preferred_element_type=f32,
        )
        d_mixed = cot + added
        u = d_mixed * piece_of(gain[1, 0:1], where[0], seqs, 0)
        return [payload(u), d_mixed] + blocks_of(d_rows, where[0], seqs)

    u, d_mixed_2, *d_rows_back = call(
        "first_grad", first_grad, [packed, part_rows] + [((slots, width), bf16)] * seqs,
        (where,), cot_1, same_own, norm_gain, *d_rows_got, after=(dense_terms, prev_pair[1]),
    )
    u_all = gather_dp(u)
    dense, _ = lax.optimization_barrier((dense, u))
    dense = ring(dense, "section", -1)
    back_got = trade_seq(d_rows_back)

    def build_2(values, g):
        chosen, row, *fixed = values
        step = width // parts
        first = chosen[:, g * step : (g + 1) * step].astype(f32) * row
        first = first + column_part(fixed, rows, g)[:, :step].astype(f32)
        return first.astype(bf16), column_part(fixed, rows, parts + g)[:, :step]

    weight_grad, tick_2 = outer(
        "weight_grad_2", 1, depths, build_2, [chosen, row_2] + fixed_all,
        d_gate_2, d_up_2, act_2, width, parts, None, after=(u, back_got[-1]),
    )

    back_1_own, back_1_send = project(
        "back_1", u_all, expert_weight, 0, (2,), parts, mates=prev_all, after=(tick_2,)
    )
    back_1 = pair_seq(back_1_own, back_1_send)

    def second_grad(where, token, count, start, ahead_1, ahead_2, cot, gain, terms, *got):
        d_rows = in_order([g.astype(f32) for g in got], where[0], 1)
        keep = live_column(count, 1, slots) * (1.0 - met_column(token, count))
        grad, more = backward_rows(
            start[:, width + lanes :].astype(f32), ahead_1.astype(f32), ahead_2.astype(f32),
            pick(token_column(token, 1), cot) + d_rows, keep, gain,
        )
        notes = in_lanes([live_column(count, 0, slots), keep])
        grad = jnp.concatenate([grad.astype(f32), notes], 1)
        return [grad] + pieces_of(terms + more, where[0], seqs)

    grad_2, *terms_parts = call(
        "second_grad", second_grad,
        [((slots, features + lanes), bf16)] + [((2 * depths, width), f32)] * seqs,
        (where, *facts), start_got[0], ahead_21, ahead_22, cot, norm_gain, dense_terms, *back_got,
        after=(back_1_send,),
    )
    grad_2 = ring(grad_2, "section", -1)
    terms_got = trade_seq(terms_parts)

    def backward_1(own, other, prev_own, prev_other, both, scale, weight_1):
        inner = own[:, hidden_units : hidden_units + 1] + decoded(other[:, hidden_units:])
        d_act = own[:, :hidden_units] + other[:, :hidden_units].astype(f32)
        through = scale * scale * inner / features
        d_act = d_act - through * (prev_own + prev_other.astype(f32))
        d_act = d_act * (weight_1 * scale)
        d_gate, d_up = gates_back(both[:, :hidden_units], both[:, hidden_units:], d_act)
        return d_gate, d_up, through

    (d_gate_1, d_up_1, through_1), d_rows_blocks = expand(
        "back_rows_1", backward_1,
        back_1 + prev_pair + (both_1, scale_2, weight_1),
        [units, units, ((total, 1), f32)],
        expert_weight, 0, (0, 1), groups, parts, after=(terms_parts[0],),
    )
    d_rows_got = return_dp(d_rows_blocks)

    def build_1(values, g):
        through, scale, weight = values[:3]
        first, u, prev = (values[3 + k * groups : 3 + (k + 1) * groups] for k in range(3))
        dout = column_part(u, rows, g).astype(f32) - through * column_part(prev, rows, g).astype(f32)
        return column_part(first, rows, g), (dout * (weight * scale)).astype(bf16)

    weight_grad, tick_1 = outer(
        "weight_grad_1", 0, depths, build_1,
        [through_1, scale_2, weight_1] + rows_1_all + u_all + prev_all,
        d_gate_1, d_up_1, act_1, width, parts, weight_grad, after=(d_rows_blocks[0],),
    )

    def last_grad(where, d_mixed_2, prev, scale, through, unit_1, unit_e1, unit_e2, own_facts, gain, *got):
        got, terms = got[:groups], got[groups:]
        d_rows = summed(got, parts)
        gain_1, gain_2 = (piece_of(gain[k, 0:1], where[0], seqs, 0) for k in range(2))
        scale, through = scale[:rows], through[:rows]
        live = own_facts[:, 2:3]
        prev = prev.astype(f32)
        grad_1 = (d_mixed_2 * gain_2 - through * prev) * scale
        d_mixed_1 = grad_1 + d_rows
        kept_1, kept_2 = d_mixed_1 * live, d_mixed_2 * live
        sums = [
            jnp.sum(a * b, axis=0, keepdims=True)
            for a, b in ((kept_1, unit_1), (kept_1, unit_e1), (kept_2, prev * scale), (kept_2, unit_e2))
        ]
        sums = jnp.concatenate(sums, 0) + sum(terms)
        cut = []
        for i in range(groups):
            block = sums[:, :share]
            for z in range(groups):
                at = partner(z, i, groups) * share
                block = jnp.where(where[1] == z, sums[:, at : at + share], block)
            cut.append(block)
        return cut + blocks_of(d_mixed_1 * gain_1, where[0], seqs)

    last = call(
        "last_grad", last_grad,
        [((2 * depths, share), f32)] * groups + [((slots, width), bf16)] * seqs,
        (where,), d_mixed_2, prev_own, scale_2, through_1, unit_1, unit_e1, unit_e2,
        own_facts, norm_gain, *d_rows_got, *terms_got, after=(tick_1,),
    )
    last_got = trade_seq(last[groups:], -1)
    sums_got = return_dp(last[:groups])

    def finish(where, token, dense, asked_rows, grad_2, *got):
        part = in_order([g.astype(f32) for g in got], where[0], 1)
        asked_rows = asked_rows.astype(f32)
        scale = inv_rms(asked_rows)
        unit = asked_rows * scale
        grad_1 = (part - unit * jnp.mean(part * unit, axis=-1, keepdims=True)) * scale
        notes = grad_2[:, features:].astype(f32)
        grads = jnp.concatenate([grad_1, grad_2[:, :features].astype(f32)], 0).astype(bf16)
        lane = iota((slots, tokens), 1)
        chosen = jnp.concatenate(
            [
                jnp.where(lane == token_column(token, k), notes[:, k : k + 1], 0.0)
                for k in range(2)
            ],
            0,
        ).astype(bf16)
        taken = lax.dot_general(
            chosen, jnp.ones((2 * slots, lanes), bf16), (((0,), (0,)), ((), ())),
            preferred_element_type=f32,
        )[:, 0:1]
        out = []
        step = chunk_of(features)
        for at in range(0, features, step):
            placed = lax.dot_general(
                chosen, grads[:, at : at + step], (((0,), (0,)), ((), ())),
                preferred_element_type=f32,
            )
            out.append(jnp.where(taken > 0, placed, dense[:, at : at + step].astype(f32)).astype(bf16))
        return [jnp.concatenate(out, 1), jnp.zeros((8, lanes), f32)]

    hidden_grad, tick = call(
        "finish", finish, [((tokens, features), bf16), ((8, lanes), f32)],
        (where, asked_token), dense, asked_rows, grad_2, *last_got, limit=20,
    )

    def gain_sum(*got):
        sums = sum(got)
        return [jnp.stack([sums[2 * k : 2 * k + 2] for k in range(depths)])[None]]

    (gain_grad,) = call(
        "gain_sum", gain_sum, [((1, depths, 2, share), f32)], (), *sums_got, after=(tick,)
    )
    return (
        hidden_grad[None, None],
        weight_grad,
        gain_grad,
    )


def solution(mesh):
    return jax.shard_map(
        local,
        mesh=mesh,
        in_specs=(
            P("section", "dp", "seq", None),
            P("section", "dp", "seq", None),
            P("section", "dp", "seq", None),
            P("section", "dp", None, "seq"),
            P("section", "dp", None, "seq"),
            P("section", "dp", None, "seq"),
            P(),
            P(None, None, "seq", "dp"),
        ),
        out_specs=(
            P("section", "dp", "seq", None),
            P("section", None, None, "seq", "dp"),
            P("section", None, None, ("seq", "dp")),
        ),
        check_vma=False,
    )
```

profile of v0, /device:TPU:0, one launch (start us, length us, event | category | flops | bytes accessed | tf_op | source)
XLA Modules:
  0.0 152.5 jit_solution(2916788578296110811)
XLA Ops:
  0.6 2.4 %collective-permute-start = (s32[1,1,2,6]{3,2,1,0:T(2,128)}, s32[1,1,2,6]{3,2,1,0:T(2,128)S(1)}, u32[]{:S(2)}, u32[]{:S(2)}) collective-permute-start(s32[1,1,2,6]{3,2,1,0:T(2,128)} %refs_1_.5), channel_id=1, source_target_pairs={{0,24},{8,0},{16,8},{24,16},{1,25},{9,1},{17,9},{25,17},{2,26},{10... | collective-permute-start | bytes 152 | tf_op jit(solution)/shard_map/ppermute | solution.py:19
  3.1 0.7 copy.16.refs_2_.count_ref
  4.6 1.5 copy-done
  6.1 1.5 copy-done.2
  8.9 1.7 %own_rows.1 = (bf16[28,3712]{1,0:T(8,128)(2,1)S(1)}, bf16[28,3712]{1,0:T(8,128)(2,1)S(1)}) custom-call(s32[2]{0:T(128)S(1)} %pad_add_fusion.refs_0_, s32[1,1,2,6]{3,2,1,0:T(2,128)S(1)} %copy-done.6, s32[1,1,2,1]{3,2,1,0:T(2,128)S(1)} %copy.16.refs_2_.count_ref, f32[1,1,2,6]{3,2,1,0:T(2,128)S(1)} %copy-done.8, bf16[128,7168]{1,0:T(8,128)(2,1)S(1)} %bitcast.6, ...), custom_call_target="tpu_custom_call" | custom-call | bytes 4085760 | tf_op jit(solution)/shard_map/own_rows/pallas_call | solution.py:220
  10.6 1.6 %collective-permute-start.1 = (bf16[28,3712]{1,0:T(8,128)(2,1)S(1)}, bf16[28,3712]{1,0:T(8,128)(2,1)S(1)}, u32[]{:S(2)}, u32[]{:S(2)}) collective-permute-start(bf16[28,3712]{1,0:T(8,128)(2,1)S(1)} %get-tuple-element.85), channel_id=1, source_target_pairs={{0,4},{4,0},{1,5},{5,1},{2,6},{6,2},{3,7},{7,3},{8,12},{12,8},{9,1... | collective-permute-start | bytes 623624 | tf_op jit(solution)/shard_map/ppermute | solution.py:19
  12.2 1.1 source_rows.1
  14.2 5.5 %collective-permute-done.1.refs_2_ = bf16[28,3712]{1,0:T(8,128)(2,1)S(1)} collective-permute-done((bf16[28,3712]{1,0:T(8,128)(2,1)S(1)}, bf16[28,3712]{1,0:T(8,128)(2,1)S(1)}, u32[]{:S(2)}, u32[]{:S(2)}) %collective-permute-start.1) | collective-permute-done | bytes 207904 | tf_op jit(solution)/shard_map/ppermute | solution.py:19
  19.6 0.9 own_parts.1
  21.3 1.6 %collective-permute-start.5 = (bf16[48,896]{1,0:T(8,128)(2,1)S(1)}, bf16[48,896]{1,0:T(8,128)(2,1)S(1)}, u32[]{:S(2)}, u32[]{:S(2)}) collective-permute-start(bf16[48,896]{1,0:T(8,128)(2,1)S(1)} %get-tuple-element.90.refs_7_.refs_0_.refs_1_.refs_3_), channel_id=1, source_target_pairs={{1,0},{0,1},{3,2},{2,3},{5,4},{4,5},{7,6},{6,7},{9,8},{8,9},{11,10... | collective-permute-start | bytes 258056 | tf_op jit(solution)/shard_map/ppermute | solution.py:45
  23.0 2.6 %collective-permute-start.6 = (bf16[48,896]{1,0:T(8,128)(2,1)S(1)}, bf16[48,896]{1,0:T(8,128)(2,1)S(1)}, u32[]{:S(2)}, u32[]{:S(2)}) collective-permute-start(bf16[48,896]{1,0:T(8,128)(2,1)S(1)} %get-tuple-element.90.refs_7_.refs_0_.refs_1_.refs_3_), channel_id=1, source_target_pairs={{2,0},{3,1},{0,2},{1,3},{6,4},{7,5},{4,6},{5,7},{10,8},{11,9},{8,1... | collective-permute-start | bytes 258056 | tf_op jit(solution)/shard_map/ppermute | solution.py:45
  25.8 1.5 second_base.1
  27.3 1.6 %collective-permute-start.8 = (bf16[6,3584]{1,0:T(8,128)(2,1)S(1)}, bf16[6,3584]{1,0:T(8,128)(2,1)S(1)}, u32[]{:S(2)}, u32[]{:S(2)}) collective-permute-start(bf16[6,3584]{1,0:T(8,128)(2,1)S(1)} %get-tuple-element.94), channel_id=1, source_target_pairs={{0,4},{4,0},{1,5},{5,1},{2,6},{6,2},{3,7},{7,3},{8,12},{12,8},{9,1... | collective-permute-start | bytes 129032 | tf_op jit(solution)/shard_map/ppermute | solution.py:19
  28.9 2.7 %collective-permute-done.8.refs_6_.refs_3_ = bf16[6,3584]{1,0:T(8,128)(2,1)S(1)} collective-permute-done((bf16[6,3584]{1,0:T(8,128)(2,1)S(1)}, bf16[6,3584]{1,0:T(8,128)(2,1)S(1)}, u32[]{:S(2)}, u32[]{:S(2)}) %collective-permute-start.8) | collective-permute-done | bytes 43040 | tf_op jit(solution)/shard_map/ppermute | solution.py:19
  31.6 1.2 collective-permute-done.6.refs_2_.refs_5_
  32.8 3.5 %gate_up_1.1 = (f32[48,1024]{1,0:T(8,128)S(1)}, bf16[48,1024]{1,0:T(8,128)(2,1)S(1)}) custom-call(bf16[48,896]{1,0:T(8,128)(2,1)S(1)} %get-tuple-element.90.refs_7_.refs_0_.refs_1_.refs_3_, bf16[48,896]{1,0:T(8,128)(2,1)S(1)} %collective-permute-done.5.refs_1_.refs_4_, bf16[48,896]{1,0:T(8,128)(2,1)S(1)} %collective-permute-done.6.refs_2_.refs_5_, ...), custom_call_target="tpu_custom_call" | custom-call | flops 352321536 | bytes 7340032 | tf_op jit(solution)/shard_map/gate_up_1/pallas_call | solution.py:319
  36.2 1.6 %collective-permute-start.9 = (bf16[48,1024]{1,0:T(8,128)(2,1)S(1)}, bf16[48,1024]{1,0:T(8,128)(2,1)S(1)}, u32[]{:S(2)}, u32[]{:S(2)}) collective-permute-start(bf16[48,1024]{1,0:T(8,128)(2,1)S(1)} %get-tuple-element.96.refs_4_), channel_id=1, source_target_pairs={{0,4},{4,0},{1,5},{5,1},{2,6},{6,2},{3,7},{7,3},{8,12},{12,8},{9,1... | collective-permute-start | bytes 294920 | tf_op jit(solution)/shard_map/ppermute | solution.py:19
  38.4 1.9 %collective-permute-start.16 = (bf16[96,1024]{1,0:T(8,128)(2,1)S(1)}, bf16[96,1024]{1,0:T(8,128)(2,1)S(1)}, u32[]{:S(2)}, u32[]{:S(2)}) collective-permute-start(bf16[96,1024]{1,0:T(8,128)(2,1)S(1)} %fixed_order.1.refs_3_.refs_0_.refs_2_), channel_id=1, source_target_pairs={{1,0},{0,1},{3,2},{2,3},{5,4},{4,5},{7,6},{6,7},{9,8},{8,9},{11,10... | collective-permute-start | bytes 589832 | tf_op jit(solution)/shard_map/ppermute | solution.py:45
  40.9 3.0 %down_1.1 = (bf16[48,512]{1,0:T(8,128)(2,1)S(1)}, f32[48,1024]{1,0:T(8,128)S(1)}, bf16[48,896]{1,0:T(8,128)(2,1)S(1)}, bf16[48,896]{1,0:T(8,128)(2,1)S(1)}, bf16...) custom-call(f32[48,1024]{1,0:T(8,128)S(1)} %get-tuple-element.95.refs_0_, ...), custom_call_target="tpu_custom_call" | custom-call | flops 176160768 | bytes 3670016 | tf_op jit(solution)/shard_map/down_1/pallas_call | solution.py:360
  44.0 1.9 %collective-permute-start.10 = (bf16[48,896]{1,0:T(8,128)(2,1)S(1)}, bf16[48,896]{1,0:T(8,128)(2,1)S(1)}, u32[]{:S(2)}, u32[]{:S(2)}) collective-permute-start(bf16[48,896]{1,0:T(8,128)(2,1)S(1)} %get-tuple-element.102), channel_id=1, source_target_pairs={{0,1},{1,0},{2,3},{3,2},{4,5},{5,4},{6,7},{7,6},{8,9},{9,8},{10,11... | collective-permute-start | bytes 258056 | tf_op jit(solution)/shard_map/ppermute | solution.py:53
  45.9 1.4 collective-permute-start.17
  47.3 1.1 collective-permute-start.18
  48.4 0.8 collective-permute-done.10.refs_3_
  49.2 3.2 %collective-permute-start.11 = (bf16[48,896]{1,0:T(8,128)(2,1)S(1)}, bf16[48,896]{1,0:T(8,128)(2,1)S(1)}, u32[]{:S(2)}, u32[]{:S(2)}) collective-permute-start(bf16[48,896]{1,0:T(8,128)(2,1)S(1)} %get-tuple-element.103), channel_id=1, source_target_pairs={{0,2},{1,3},{2,0},{3,1},{4,6},{5,7},{6,4},{7,5},{8,10},{9,11},{10,... | collective-permute-start | bytes 258056 | tf_op jit(solution)/shard_map/ppermute | solution.py:53
  52.4 1.3 collective-permute-start.12
  53.7 5.7 %dense_a.1 = (bf16[128,7168]{1,0:T(8,128)(2,1)S(1)}, f32[4,7168]{1,0:T(4,128)S(1)}) custom-call(s32[1,1,2,6]{3,2,1,0:T(2,128)S(1)} %copy-done.7, s32[1,1,2,1]{3,2,1,0:T(2,128)S(1)} %copy.16.refs_2_.count_ref, bf16[128,7168]{1,0:T(8,128)(2,1)S(1)} %collective-permute-done.4.hidden_ref, bf16[128,7168]{1,0:T(8,128)(2,1)S(1)} %bitcast.8, ...), custom_call_target="tpu_custom_call" | custom-call | flops 27525120 | bytes 4587520 | tf_op jit(solution)/shard_map/dense_a/pallas_call | solution.py:539
  59.3 11.7 %collective-permute-done.11.refs_4_ = bf16[48,896]{1,0:T(8,128)(2,1)S(1)} collective-permute-done((bf16[48,896]{1,0:T(8,128)(2,1)S(1)}, bf16[48,896]{1,0:T(8,128)(2,1)S(1)}, u32[]{:S(2)}, u32[]{:S(2)}) %collective-permute-start.11) | collective-permute-done | bytes 86048 | tf_op jit(solution)/shard_map/ppermute | solution.py:53
  71.1 1.6 %collective-permute-start.13 = (bf16[48,896]{1,0:T(8,128)(2,1)S(1)}, bf16[48,896]{1,0:T(8,128)(2,1)S(1)}, u32[]{:S(2)}, u32[]{:S(2)}) collective-permute-start(bf16[48,896]{1,0:T(8,128)(2,1)S(1)} %get-tuple-element.105.refs_4_.refs_1_.refs_0_.refs_5_.refs_11_), channel_id=1, source_target_pairs={{1,0},{0,1},{3,2},{2,3},{5,4},{4,5},{7,6},{6,7},{9,8},{8,9},{11,10... | collective-permute-start | bytes 258056 | tf_op jit(solution)/shard_map/ppermute | solution.py:45
  72.7 1.2 collective-permute-start.14
  73.9 1.7 %collective-permute-start.15 = (bf16[48,896]{1,0:T(8,128)(2,1)S(1)}, bf16[48,896]{1,0:T(8,128)(2,1)S(1)}, u32[]{:S(2)}, u32[]{:S(2)}) collective-permute-start(bf16[48,896]{1,0:T(8,128)(2,1)S(1)} %get-tuple-element.105.refs_4_.refs_1_.refs_0_.refs_5_.refs_11_), channel_id=1, source_target_pairs={{3,0},{2,1},{1,2},{0,3},{7,4},{6,5},{5,6},{4,7},{11,8},{10,9},{9,1... | collective-permute-start | bytes 258056 | tf_op jit(solution)/shard_map/ppermute | solution.py:45
  75.8 4.6 %fixed_2.1 = (f32[48,1536]{1,0:T(8,128)S(1)}, bf16[48,1536]{1,0:T(8,128)(2,1)S(1)}) custom-call(bf16[96,1024]{1,0:T(8,128)(2,1)S(1)} %fixed_order.1.refs_3_.refs_0_.refs_2_, bf16[96,1024]{1,0:T(8,128)(2,1)S(1)} %collective-permute-done.16.refs_1_.refs_3_, bf16[96,1024]{1,0:T(8,128)(2,1)S(1)} %collective-permute-done.17.refs_2_.refs_4_, ...), custom_call_target="tpu_custom_call" | custom-call | flops 528482304 | bytes 11010048 | tf_op jit(solution)/shard_map/fixed_2/pallas_call | solution.py:319
  80.3 1.6 %collective-permute-start.20 = (bf16[48,1536]{1,0:T(8,128)(2,1)S(1)}, bf16[48,1536]{1,0:T(8,128)(2,1)S(1)}, u32[]{:S(2)}, u32[]{:S(2)}) collective-permute-start(bf16[48,1536]{1,0:T(8,128)(2,1)S(1)} %get-tuple-element.111), channel_id=1, source_target_pairs={{0,4},{4,0},{1,5},{5,1},{2,6},{6,2},{3,7},{7,3},{8,12},{12,8},{9,1... | collective-permute-start | bytes 442376 | tf_op jit(solution)/shard_map/ppermute | solution.py:19
  81.9 4.2 %gate_up_2.1 = (f32[48,1152]{1,0:T(8,128)S(1)}, bf16[48,1152]{1,0:T(8,128)(2,1)S(1)}, bf16[48,3584]{1,0:T(8,128)(2,1)S(1)}) custom-call(s32[2]{0:T(128)S(1)} %pad_add_fusion.refs_0_, bf16[48,896]{1,0:T(8,128)(2,1)S(1)} %get-tuple-element.105.refs_4_.refs_1_.refs_0_.refs_5_.refs_11_, ...), custom_call_target="tpu_custom_call" | custom-call | flops 352321536 | bytes 7340032 | tf_op jit(solution)/shard_map/gate_up_2/pallas_call | solution.py:319
  86.1 1.3 collective-permute-start.19
  87.4 2.3 %prev_down.1 = (f32[48,512]{1,0:T(8,128)S(1)}, bf16[48,512]{1,0:T(8,128)(2,1)S(1)}) custom-call(bf16[48,896]{1,0:T(8,128)(2,1)S(1)} %get-tuple-element.105.refs_4_.refs_1_.refs_0_.refs_5_.refs_11_, bf16[48,896]{1,0:T(8,128)(2,1)S(1)} %collective-permute-done.13.refs_2_.refs_1_.refs_6_.refs_12_, ...), custom_call_target="tpu_custom_call" | custom-call | flops 176160768 | bytes 3670016 | tf_op jit(solution)/shard_map/prev_down/pallas_call | solution.py:319
  89.7 1.2 collective-permute-done.19.refs_1_
  90.9 4.6 %back_rows_2.1 = (bf16[48,512]{1,0:T(8,128)(2,1)S(1)}, bf16[48,512]{1,0:T(8,128)(2,1)S(1)}, bf16[48,512]{1,0:T(8,128)(2,1)S(1)}, f32[48,1]{1,0:T(8,128)S(1)}, f3...) custom-call(f32[48,1152]{1,0:T(8,128)S(1)} %get-tuple-element.109.re, ...), custom_call_target="tpu_custom_call" | custom-call | flops 352321536 | bytes 7340032 | tf_op jit(solution)/shard_map/back_rows_2/pallas_call | solution.py:360
  95.5 1.2 collective-permute-start.21
  96.8 1.5 collective-permute-start.22
  98.3 1.7 %collective-permute-start.23 = (bf16[48,896]{1,0:T(8,128)(2,1)S(1)}, bf16[48,896]{1,0:T(8,128)(2,1)S(1)}, u32[]{:S(2)}, u32[]{:S(2)}) collective-permute-start(bf16[48,896]{1,0:T(8,128)(2,1)S(1)} %get-tuple-element.119), channel_id=1, source_target_pairs={{0,3},{1,2},{2,1},{3,0},{4,7},{5,6},{6,5},{7,4},{8,11},{9,10},{10,... | collective-permute-start | bytes 258056 | tf_op jit(solution)/shard_map/ppermute | solution.py:53
  100.0 1.2 collective-permute-start.24
  101.2 5.5 %dense_b.1 = (bf16[128,7168]{1,0:T(8,128)(2,1)S(1)}, f32[4,7168]{1,0:T(4,128)S(1)}) custom-call(s32[1,1,2,6]{3,2,1,0:T(2,128)S(1)} %copy-done.7, s32[1,1,2,1]{3,2,1,0:T(2,128)S(1)} %copy.16.refs_2_.count_ref, bf16[128,7168]{1,0:T(8,128)(2,1)S(1)} %collective-permute-done.4.hidden_ref, ...), custom_call_target="tpu_custom_call", output_to_operand_aliasing={{0}: (7, {})} | custom-call | flops 27525120 | bytes 4587520 | tf_op jit(solution)/shard_map/dense_b/pallas_call | solution.py:539
  106.8 1.0 first_grad.1
  108.1 0.9 collective-permute-start.26
  109.2 2.4 %collective-permute-start.28 = (bf16[48,896]{1,0:T(8,128)(2,1)S(1)}, bf16[48,896]{1,0:T(8,128)(2,1)S(1)}, u32[]{:S(2)}, u32[]{:S(2)}) collective-permute-start(bf16[48,896]{1,0:T(8,128)(2,1)S(1)} %get-tuple-element.122.refs_9_.refs_0_.refs_7_), channel_id=1, source_target_pairs={{2,0},{3,1},{0,2},{1,3},{6,4},{7,5},{4,6},{5,7},{10,8},{11,9},{8,1... | collective-permute-start | bytes 258056 | tf_op jit(solution)/shard_map/ppermute | solution.py:45
  111.6 1.7 %collective-permute-start.29 = (bf16[48,896]{1,0:T(8,128)(2,1)S(1)}, bf16[48,896]{1,0:T(8,128)(2,1)S(1)}, u32[]{:S(2)}, u32[]{:S(2)}) collective-permute-start(bf16[48,896]{1,0:T(8,128)(2,1)S(1)} %get-tuple-element.122.refs_9_.refs_0_.refs_7_), channel_id=1, source_target_pairs={{3,0},{2,1},{1,2},{0,3},{7,4},{6,5},{5,6},{4,7},{11,8},{10,9},{9,1... | collective-permute-start | bytes 258056 | tf_op jit(solution)/shard_map/ppermute | solution.py:45
  113.4 4.7 %weight_grad_2.1 = (bf16[1,2,3,3584,512]{4,3,2,1,0:T(8,128)(2,1)}, f32[8,128]{1,0:T(8,128)S(1)}) custom-call(bf16[48,3584]{1,0:T(8,128)(2,1)S(1)} %get-tuple-element.128.refs_0_, f32[48,1]{1,0:T(8,128)S(1)} %get-tuple-element.129.refs_1_, bf16[96,1024]{1,0:T(8,128)(2,1)S(1)} %fixed_order.1.refs_3_.refs_0_.refs_2_, ...), custom_call_target="tpu_custom_call" | custom-call | flops 528482304 | bytes 11010048 | tf_op jit(solution)/shard_map/weight_grad_2/pallas_call | solution.py:408
  118.1 1.0 collective-permute-done.28.refs_2_.refs_9_
  119.1 2.4 %back_1.1 = (f32[48,640]{1,0:T(8,128)S(1)}, bf16[48,640]{1,0:T(8,128)(2,1)S(1)}) custom-call(bf16[48,896]{1,0:T(8,128)(2,1)S(1)} %get-tuple-element.122.refs_9_.refs_0_.refs_7_, bf16[48,896]{1,0:T(8,128)(2,1)S(1)} %collective-permute-done.27.refs_1_.refs_8_, bf16[48,896]{1,0:T(8,128)(2,1)S(1)} %collective-permute-done.28.refs_2_.refs_9_, ...), custom_call_target="tpu_custom_call" | custom-call | flops 176160768 | bytes 3670016 | tf_op jit(solution)/shard_map/back_1/pallas_call | solution.py:319
  121.5 1.6 %collective-permute-start.31 = (bf16[48,640]{1,0:T(8,128)(2,1)S(1)}, bf16[48,640]{1,0:T(8,128)(2,1)S(1)}, u32[]{:S(2)}, u32[]{:S(2)}) collective-permute-start(bf16[48,640]{1,0:T(8,128)(2,1)S(1)} %get-tuple-element.134.refs_11_), channel_id=1, source_target_pairs={{0,4},{4,0},{1,5},{5,1},{2,6},{6,2},{3,7},{7,3},{8,12},{12,8},{9,1... | collective-permute-start | bytes 184328 | tf_op jit(solution)/shard_map/ppermute | solution.py:19
  123.1 1.5 second_grad.1
  125.2 1.1 collective-permute-done.31.refs_1_
  126.3 4.6 %back_rows_1.1 = (bf16[48,512]{1,0:T(8,128)(2,1)S(1)}, bf16[48,512]{1,0:T(8,128)(2,1)S(1)}, f32[48,1]{1,0:T(8,128)S(1)}, bf16[48,896]{1,0:T(8,128)(2,1)S(1)}, bf...) custom-call(f32[48,640]{1,0:T(8,128)S(1)} %get-tuple-element.139.refs_0_, ...), custom_call_target="tpu_custom_call" | custom-call | flops 352321536 | bytes 7340032 | tf_op jit(solution)/shard_map/back_rows_1/pallas_call | solution.py:360
  130.9 1.1 collective-permute-start.32
  132.0 1.5 collective-permute-start.33
  133.5 1.8 %collective-permute-start.34 = (bf16[48,896]{1,0:T(8,128)(2,1)S(1)}, bf16[48,896]{1,0:T(8,128)(2,1)S(1)}, u32[]{:S(2)}, u32[]{:S(2)}) collective-permute-start(bf16[48,896]{1,0:T(8,128)(2,1)S(1)} %get-tuple-element.149), channel_id=1, source_target_pairs={{0,3},{1,2},{2,1},{3,0},{4,7},{5,6},{6,5},{7,4},{8,11},{9,10},{10,... | collective-permute-start | bytes 258056 | tf_op jit(solution)/shard_map/ppermute | solution.py:53
  135.4 4.7 %weight_grad_1.1 = (bf16[1,2,3,3584,512]{4,3,2,1,0:T(8,128)(2,1)}, f32[8,128]{1,0:T(8,128)S(1)}) custom-call(f32[48,1]{1,0:T(8,128)S(1)} %get-tuple-element.143.refs_0_.refs_4_, f32[48,1]{1,0:T(8,128)S(1)} %get-tuple-element.138.refs_5_.refs_1_.refs_3_, f32[48,1]{1,0:T(8,128)S(1)} %get-tuple-element.141.refs_6_.refs_2_, ...), custom_call_target="tpu_custom_call", output_to_operand_aliasing={{0}: (18, {})} | custom-call | flops 528482304 | bytes 11010048 | tf_op jit(solution)/shard_map/weight_grad_1/pallas_call | solution.py:408
  140.1 1.1 last_grad.1
  141.1 1.8 %collective-permute-start.36 = (bf16[6,3584]{1,0:T(8,128)(2,1)S(1)}, bf16[6,3584]{1,0:T(8,128)(2,1)S(1)}, u32[]{:S(2)}, u32[]{:S(2)}) collective-permute-start(bf16[6,3584]{1,0:T(8,128)(2,1)S(1)} %get-tuple-element.156), channel_id=1, source_target_pairs={{0,24},{4,28},{8,0},{12,4},{16,8},{20,12},{24,16},{28,20},{1,25},{... | collective-permute-start | bytes 129032 | tf_op jit(solution)/shard_map/ppermute | solution.py:29
  143.6 1.4 collective-permute-start.38
  145.0 1.4 collective-permute-start.39
  146.4 1.6 %collective-permute-start.40 = (f32[4,896]{1,0:T(4,128)S(1)}, f32[4,896]{1,0:T(4,128)S(1)}, u32[]{:S(2)}, u32[]{:S(2)}) collective-permute-start(f32[4,896]{1,0:T(4,128)S(1)} %get-tuple-element.163), channel_id=1, source_target_pairs={{0,3},{1,2},{2,1},{3,0},{4,7},{5,6},{6,5},{7,4},{8,11},{9,10},{10,... | collective-permute-start | bytes 43016 | tf_op jit(solution)/shard_map/ppermute | solution.py:53
  148.0 2.7 %finish.1 = (bf16[128,7168]{1,0:T(8,128)(2,1)}, f32[8,128]{1,0:T(8,128)S(1)}) custom-call(s32[2]{0:T(128)S(1)} %pad_add_fusion.refs_0_, s32[1,1,2,6]{3,2,1,0:T(2,128)S(1)} %collective-permute-done.refs_6_.refs_1_, bf16[128,7168]{1,0:T(8,128)(2,1)S(1)} %collective-permute-done.25.refs_2_, bf16[6,7168]{1,0:T(8,128)(2,1)S(1)} %get-tuple-element.124.refs_3_, ...), custom_call_target="tpu_custom_call" | custom-call | bytes 3933696 | tf_op jit(solution)/shard_map/finish/pallas_call | solution.py:220
  150.7 1.2 collective-permute-done.40.refs_3_
  (63 shorter events, 7.9 us)
Async XLA Ops:
  0.6 3.9 %collective-permute-start = (s32[1,1,2,6]{3,2,1,0:T(2,128)}, s32[1,1,2,6]{3,2,1,0:T(2,128)S(1)}, u32[]{:S(2)}, u32[]{:S(2)}) collective-permute-start(s32[1,1,2,6]{3,2,1,0:T(2,128)} %refs_1_.5), channel_id=1, source_target_pairs={{0,24},{8,0},{16,8},{24,16},{1,25},{9,1},{17,9},{25,17},{2,26},{10... | collective-permute-start | bytes 152 | tf_op jit(solution)/shard_map/ppermute | solution.py:19
  4.6 1.5 copy-start
  6.1 1.5 copy-start.2
  7.6 0.7 copy-start.6
  8.2 0.7 copy-start.8
  8.9 3.3 %copy-start.5 = (bf16[1,1,128,7168]{3,2,1,0:T(8,128)(2,1)S(1)}, bf16[1,1,128,7168]{3,2,1,0:T(8,128)(2,1)}, u32[]{:S(2)}) copy-start(bf16[1,1,128,7168]{3,2,1,0:T(8,128)(2,1)} %param.8) | copy-start | bytes 5505028
  10.6 10.0 %copy-start.4 = (f32[2,2,7168]{2,1,0:T(2,128)S(1)}, f32[2,2,7168]{2,1,0:T(2,128)}, u32[]{:S(2)}) copy-start(f32[2,2,7168]{2,1,0:T(2,128)} %refs_9_.1) | copy-start | bytes 344068
  10.6 15.2 %copy-start.1 = (bf16[1,1,128,7168]{3,2,1,0:T(8,128)(2,1)S(1)}, bf16[1,1,128,7168]{3,2,1,0:T(8,128)(2,1)}, u32[]{:S(2)}) copy-start(bf16[1,1,128,7168]{3,2,1,0:T(8,128)(2,1)} %param.9) | copy-start | bytes 5505028
  10.6 9.0 %collective-permute-start.1 = (bf16[28,3712]{1,0:T(8,128)(2,1)S(1)}, bf16[28,3712]{1,0:T(8,128)(2,1)S(1)}, u32[]{:S(2)}, u32[]{:S(2)}) collective-permute-start(bf16[28,3712]{1,0:T(8,128)(2,1)S(1)} %get-tuple-element.85), channel_id=1, source_target_pairs={{0,4},{4,0},{1,5},{5,1},{2,6},{6,2},{3,7},{7,3},{8,12},{12,8},{9,1... | collective-permute-start | bytes 623624 | tf_op jit(solution)/shard_map/ppermute | solution.py:19
  13.3 7.2 %collective-permute-start.2 = (bf16[6,10880]{1,0:T(8,128)(2,1)S(1)}, bf16[6,10880]{1,0:T(8,128)(2,1)S(1)}, u32[]{:S(2)}, u32[]{:S(2)}) collective-permute-start(bf16[6,10880]{1,0:T(8,128)(2,1)S(1)} %get-tuple-element.88), channel_id=1, source_target_pairs={{0,8},{4,12},{8,16},{12,20},{16,24},{20,28},{24,0},{28,4},{1,9},{5... | collective-permute-start | bytes 391688 | tf_op jit(solution)/shard_map/ppermute | solution.py:29
  13.7 6.8 %collective-permute-start.3 = (bf16[6,3712]{1,0:T(8,128)(2,1)S(1)}, bf16[6,3712]{1,0:T(8,128)(2,1)S(1)}, u32[]{:S(2)}, u32[]{:S(2)}) collective-permute-start(bf16[6,3712]{1,0:T(8,128)(2,1)S(1)} %get-tuple-element.89), channel_id=1, source_target_pairs={{0,12},{4,8},{8,20},{12,16},{16,28},{20,24},{24,4},{28,0},{1,13},{... | collective-permute-start | bytes 133640 | tf_op jit(solution)/shard_map/ppermute | solution.py:29
  21.3 31.1 %collective-permute-start.4 = (bf16[128,7168]{1,0:T(8,128)(2,1)S(1)}, bf16[128,7168]{1,0:T(8,128)(2,1)S(1)}, u32[]{:S(2)}, u32[]{:S(2)}) collective-permute-start(bf16[128,7168]{1,0:T(8,128)(2,1)S(1)} %bitcast.15), channel_id=1, source_target_pairs={{0,8},{8,16},{16,24},{24,0},{1,9},{9,17},{17,25},{25,1},{2,10},{10... | collective-permute-start | bytes 5505032 | tf_op jit(solution)/shard_map/ppermute | solution.py:19
  21.3 10.2 %collective-permute-start.5 = (bf16[48,896]{1,0:T(8,128)(2,1)S(1)}, bf16[48,896]{1,0:T(8,128)(2,1)S(1)}, u32[]{:S(2)}, u32[]{:S(2)}) collective-permute-start(bf16[48,896]{1,0:T(8,128)(2,1)S(1)} %get-tuple-element.90.refs_7_.refs_0_.refs_1_.refs_3_), channel_id=1, source_target_pairs={{1,0},{0,1},{3,2},{2,3},{5,4},{4,5},{7,6},{6,7},{9,8},{8,9},{11,10... | collective-permute-start | bytes 258056 | tf_op jit(solution)/shard_map/ppermute | solution.py:45
  23.0 9.8 %collective-permute-start.6 = (bf16[48,896]{1,0:T(8,128)(2,1)S(1)}, bf16[48,896]{1,0:T(8,128)(2,1)S(1)}, u32[]{:S(2)}, u32[]{:S(2)}) collective-permute-start(bf16[48,896]{1,0:T(8,128)(2,1)S(1)} %get-tuple-element.90.refs_7_.refs_0_.refs_1_.refs_3_), channel_id=1, source_target_pairs={{2,0},{3,1},{0,2},{1,3},{6,4},{7,5},{4,6},{5,7},{10,8},{11,9},{8,1... | collective-permute-start | bytes 258056 | tf_op jit(solution)/shard_map/ppermute | solution.py:45
  25.6 7.2 %collective-permute-start.7 = (bf16[48,896]{1,0:T(8,128)(2,1)S(1)}, bf16[48,896]{1,0:T(8,128)(2,1)S(1)}, u32[]{:S(2)}, u32[]{:S(2)}) collective-permute-start(bf16[48,896]{1,0:T(8,128)(2,1)S(1)} %get-tuple-element.90.refs_7_.refs_0_.refs_1_.refs_3_), channel_id=1, source_target_pairs={{3,0},{2,1},{1,2},{0,3},{7,4},{6,5},{5,6},{4,7},{11,8},{10,9},{9,1... | collective-permute-start | bytes 258056 | tf_op jit(solution)/shard_map/ppermute | solution.py:45
  27.3 4.2 %collective-permute-start.8 = (bf16[6,3584]{1,0:T(8,128)(2,1)S(1)}, bf16[6,3584]{1,0:T(8,128)(2,1)S(1)}, u32[]{:S(2)}, u32[]{:S(2)}) collective-permute-start(bf16[6,3584]{1,0:T(8,128)(2,1)S(1)} %get-tuple-element.94), channel_id=1, source_target_pairs={{0,4},{4,0},{1,5},{5,1},{2,6},{6,2},{3,7},{7,3},{8,12},{12,8},{9,1... | collective-permute-start | bytes 129032 | tf_op jit(solution)/shard_map/ppermute | solution.py:19
  36.2 4.7 %collective-permute-start.9 = (bf16[48,1024]{1,0:T(8,128)(2,1)S(1)}, bf16[48,1024]{1,0:T(8,128)(2,1)S(1)}, u32[]{:S(2)}, u32[]{:S(2)}) collective-permute-start(bf16[48,1024]{1,0:T(8,128)(2,1)S(1)} %get-tuple-element.96.refs_4_), channel_id=1, source_target_pairs={{0,4},{4,0},{1,5},{5,1},{2,6},{6,2},{3,7},{7,3},{8,12},{12,8},{9,1... | collective-permute-start | bytes 294920 | tf_op jit(solution)/shard_map/ppermute | solution.py:19
  38.4 35.5 %collective-permute-start.16 = (bf16[96,1024]{1,0:T(8,128)(2,1)S(1)}, bf16[96,1024]{1,0:T(8,128)(2,1)S(1)}, u32[]{:S(2)}, u32[]{:S(2)}) collective-permute-start(bf16[96,1024]{1,0:T(8,128)(2,1)S(1)} %fixed_order.1.refs_3_.refs_0_.refs_2_), channel_id=1, source_target_pairs={{1,0},{0,1},{3,2},{2,3},{5,4},{4,5},{7,6},{6,7},{9,8},{8,9},{11,10... | collective-permute-start | bytes 589832 | tf_op jit(solution)/shard_map/ppermute | solution.py:45
  40.9 12.8 %copy-start.3 = (bf16[1,1,128,7168]{3,2,1,0:T(8,128)(2,1)S(1)}, bf16[1,1,128,7168]{3,2,1,0:T(8,128)(2,1)}, u32[]{:S(2)}) copy-start(bf16[1,1,128,7168]{3,2,1,0:T(8,128)(2,1)} %param.10) | copy-start | bytes 5505028
  40.9 12.8 %copy-start.7 = (s32[1,1,2,6]{3,2,1,0:T(2,128)S(1)}, s32[1,1,2,6]{3,2,1,0:T(2,128)}, u32[]{:S(2)}) copy-start(s32[1,1,2,6]{3,2,1,0:T(2,128)} %refs_1_.5) | copy-start | bytes 148
  44.0 5.3 %collective-permute-start.10 = (bf16[48,896]{1,0:T(8,128)(2,1)S(1)}, bf16[48,896]{1,0:T(8,128)(2,1)S(1)}, u32[]{:S(2)}, u32[]{:S(2)}) collective-permute-start(bf16[48,896]{1,0:T(8,128)(2,1)S(1)} %get-tuple-element.102), channel_id=1, source_target_pairs={{0,1},{1,0},{2,3},{3,2},{4,5},{5,4},{6,7},{7,6},{8,9},{9,8},{10,11... | collective-permute-start | bytes 258056 | tf_op jit(solution)/shard_map/ppermute | solution.py:53
  45.9 29.8 %collective-permute-start.17 = (bf16[96,1024]{1,0:T(8,128)(2,1)S(1)}, bf16[96,1024]{1,0:T(8,128)(2,1)S(1)}, u32[]{:S(2)}, u32[]{:S(2)}) collective-permute-start(bf16[96,1024]{1,0:T(8,128)(2,1)S(1)} %fixed_order.1.refs_3_.refs_0_.refs_2_), channel_id=1, source_target_pairs={{2,0},{3,1},{0,2},{1,3},{6,4},{7,5},{4,6},{5,7},{10,8},{11,9},{8,1... | collective-permute-start | bytes 589832 | tf_op jit(solution)/shard_map/ppermute | solution.py:45
  47.3 28.3 %collective-permute-start.18 = (bf16[96,1024]{1,0:T(8,128)(2,1)S(1)}, bf16[96,1024]{1,0:T(8,128)(2,1)S(1)}, u32[]{:S(2)}, u32[]{:S(2)}) collective-permute-start(bf16[96,1024]{1,0:T(8,128)(2,1)S(1)} %fixed_order.1.refs_3_.refs_0_.refs_2_), channel_id=1, source_target_pairs={{3,0},{2,1},{1,2},{0,3},{7,4},{6,5},{5,6},{4,7},{11,8},{10,9},{9,1... | collective-permute-start | bytes 589832 | tf_op jit(solution)/shard_map/ppermute | solution.py:45
  49.2 21.8 %collective-permute-start.11 = (bf16[48,896]{1,0:T(8,128)(2,1)S(1)}, bf16[48,896]{1,0:T(8,128)(2,1)S(1)}, u32[]{:S(2)}, u32[]{:S(2)}) collective-permute-start(bf16[48,896]{1,0:T(8,128)(2,1)S(1)} %get-tuple-element.103), channel_id=1, source_target_pairs={{0,2},{1,3},{2,0},{3,1},{4,6},{5,7},{6,4},{7,5},{8,10},{9,11},{10,... | collective-permute-start | bytes 258056 | tf_op jit(solution)/shard_map/ppermute | solution.py:53
  52.4 18.6 %collective-permute-start.12 = (bf16[48,896]{1,0:T(8,128)(2,1)S(1)}, bf16[48,896]{1,0:T(8,128)(2,1)S(1)}, u32[]{:S(2)}, u32[]{:S(2)}) collective-permute-start(bf16[48,896]{1,0:T(8,128)(2,1)S(1)} %get-tuple-element.104), channel_id=1, source_target_pairs={{0,3},{1,2},{2,1},{3,0},{4,7},{5,6},{6,5},{7,4},{8,11},{9,10},{10,... | collective-permute-start | bytes 258056 | tf_op jit(solution)/shard_map/ppermute | solution.py:53
  71.1 10.8 %collective-permute-start.13 = (bf16[48,896]{1,0:T(8,128)(2,1)S(1)}, bf16[48,896]{1,0:T(8,128)(2,1)S(1)}, u32[]{:S(2)}, u32[]{:S(2)}) collective-permute-start(bf16[48,896]{1,0:T(8,128)(2,1)S(1)} %get-tuple-element.105.refs_4_.refs_1_.refs_0_.refs_5_.refs_11_), channel_id=1, source_target_pairs={{1,0},{0,1},{3,2},{2,3},{5,4},{4,5},{7,6},{6,7},{9,8},{8,9},{11,10... | collective-permute-start | bytes 258056 | tf_op jit(solution)/shard_map/ppermute | solution.py:45
  72.7 9.2 %collective-permute-start.14 = (bf16[48,896]{1,0:T(8,128)(2,1)S(1)}, bf16[48,896]{1,0:T(8,128)(2,1)S(1)}, u32[]{:S(2)}, u32[]{:S(2)}) collective-permute-start(bf16[48,896]{1,0:T(8,128)(2,1)S(1)} %get-tuple-element.105.refs_4_.refs_1_.refs_0_.refs_5_.refs_11_), channel_id=1, source_target_pairs={{2,0},{3,1},{0,2},{1,3},{6,4},{7,5},{4,6},{5,7},{10,8},{11,9},{8,1... | collective-permute-start | bytes 258056 | tf_op jit(solution)/shard_map/ppermute | solution.py:45
  73.9 8.0 %collective-permute-start.15 = (bf16[48,896]{1,0:T(8,128)(2,1)S(1)}, bf16[48,896]{1,0:T(8,128)(2,1)S(1)}, u32[]{:S(2)}, u32[]{:S(2)}) collective-permute-start(bf16[48,896]{1,0:T(8,128)(2,1)S(1)} %get-tuple-element.105.refs_4_.refs_1_.refs_0_.refs_5_.refs_11_), channel_id=1, source_target_pairs={{3,0},{2,1},{1,2},{0,3},{7,4},{6,5},{5,6},{4,7},{11,8},{10,9},{9,1... | collective-permute-start | bytes 258056 | tf_op jit(solution)/shard_map/ppermute | solution.py:45
  80.3 9.4 %collective-permute-start.20 = (bf16[48,1536]{1,0:T(8,128)(2,1)S(1)}, bf16[48,1536]{1,0:T(8,128)(2,1)S(1)}, u32[]{:S(2)}, u32[]{:S(2)}) collective-permute-start(bf16[48,1536]{1,0:T(8,128)(2,1)S(1)} %get-tuple-element.111), channel_id=1, source_target_pairs={{0,4},{4,0},{1,5},{5,1},{2,6},{6,2},{3,7},{7,3},{8,12},{12,8},{9,1... | collective-permute-start | bytes 442376 | tf_op jit(solution)/shard_map/ppermute | solution.py:19
  86.1 4.8 %collective-permute-start.19 = (bf16[48,1152]{1,0:T(8,128)(2,1)S(1)}, bf16[48,1152]{1,0:T(8,128)(2,1)S(1)}, u32[]{:S(2)}, u32[]{:S(2)}) collective-permute-start(bf16[48,1152]{1,0:T(8,128)(2,1)S(1)} %get-tuple-element.110.refs_5_), channel_id=1, source_target_pairs={{0,4},{4,0},{1,5},{5,1},{2,6},{6,2},{3,7},{7,3},{8,12},{12,8},{9,1... | collective-permute-start | bytes 331784 | tf_op jit(solution)/shard_map/ppermute | solution.py:19
  95.5 11.2 %collective-permute-start.21 = (bf16[48,896]{1,0:T(8,128)(2,1)S(1)}, bf16[48,896]{1,0:T(8,128)(2,1)S(1)}, u32[]{:S(2)}, u32[]{:S(2)}) collective-permute-start(bf16[48,896]{1,0:T(8,128)(2,1)S(1)} %get-tuple-element.117), channel_id=1, source_target_pairs={{0,1},{1,0},{2,3},{3,2},{4,5},{5,4},{6,7},{7,6},{8,9},{9,8},{10,11... | collective-permute-start | bytes 258056 | tf_op jit(solution)/shard_map/ppermute | solution.py:53
  96.8 10.0 %collective-permute-start.22 = (bf16[48,896]{1,0:T(8,128)(2,1)S(1)}, bf16[48,896]{1,0:T(8,128)(2,1)S(1)}, u32[]{:S(2)}, u32[]{:S(2)}) collective-permute-start(bf16[48,896]{1,0:T(8,128)(2,1)S(1)} %get-tuple-element.118), channel_id=1, source_target_pairs={{0,2},{1,3},{2,0},{3,1},{4,6},{5,7},{6,4},{7,5},{8,10},{9,11},{10,... | collective-permute-start | bytes 258056 | tf_op jit(solution)/shard_map/ppermute | solution.py:53
  98.3 8.5 %collective-permute-start.23 = (bf16[48,896]{1,0:T(8,128)(2,1)S(1)}, bf16[48,896]{1,0:T(8,128)(2,1)S(1)}, u32[]{:S(2)}, u32[]{:S(2)}) collective-permute-start(bf16[48,896]{1,0:T(8,128)(2,1)S(1)} %get-tuple-element.119), channel_id=1, source_target_pairs={{0,3},{1,2},{2,1},{3,0},{4,7},{5,6},{6,5},{7,4},{8,11},{9,10},{10,... | collective-permute-start | bytes 258056 | tf_op jit(solution)/shard_map/ppermute | solution.py:53
  100.0 6.7 %collective-permute-start.24 = (bf16[48,512]{1,0:T(8,128)(2,1)S(1)}, bf16[48,512]{1,0:T(8,128)(2,1)S(1)}, u32[]{:S(2)}, u32[]{:S(2)}) collective-permute-start(bf16[48,512]{1,0:T(8,128)(2,1)S(1)} %get-tuple-element.121), channel_id=1, source_target_pairs={{0,4},{4,0},{1,5},{5,1},{2,6},{6,2},{3,7},{7,3},{8,12},{12,8},{9,1... | collective-permute-start | bytes 147464 | tf_op jit(solution)/shard_map/ppermute | solution.py:19
  107.8 40.2 %collective-permute-start.25 = (bf16[128,7168]{1,0:T(8,128)(2,1)S(1)}, bf16[128,7168]{1,0:T(8,128)(2,1)S(1)}, u32[]{:S(2)}, u32[]{:S(2)}) collective-permute-start(bf16[128,7168]{1,0:T(8,128)(2,1)S(1)} %get-tuple-element.123), channel_id=1, source_target_pairs={{0,24},{8,0},{16,8},{24,16},{1,25},{9,1},{17,9},{25,17},{2,26},{10... | collective-permute-start | bytes 5505032 | tf_op jit(solution)/shard_map/ppermute | solution.py:19
  108.1 5.3 %collective-permute-start.26 = (bf16[6,3584]{1,0:T(8,128)(2,1)S(1)}, bf16[6,3584]{1,0:T(8,128)(2,1)S(1)}, u32[]{:S(2)}, u32[]{:S(2)}) collective-permute-start(bf16[6,3584]{1,0:T(8,128)(2,1)S(1)} %get-tuple-element.127), channel_id=1, source_target_pairs={{0,4},{4,0},{1,5},{5,1},{2,6},{6,2},{3,7},{7,3},{8,12},{12,8},{9,1... | collective-permute-start | bytes 129032 | tf_op jit(solution)/shard_map/ppermute | solution.py:19
  109.0 9.1 %collective-permute-start.27 = (bf16[48,896]{1,0:T(8,128)(2,1)S(1)}, bf16[48,896]{1,0:T(8,128)(2,1)S(1)}, u32[]{:S(2)}, u32[]{:S(2)}) collective-permute-start(bf16[48,896]{1,0:T(8,128)(2,1)S(1)} %get-tuple-element.122.refs_9_.refs_0_.refs_7_), channel_id=1, source_target_pairs={{1,0},{0,1},{3,2},{2,3},{5,4},{4,5},{7,6},{6,7},{9,8},{8,9},{11,10... | collective-permute-start | bytes 258056 | tf_op jit(solution)/shard_map/ppermute | solution.py:45
  109.2 9.8 %collective-permute-start.28 = (bf16[48,896]{1,0:T(8,128)(2,1)S(1)}, bf16[48,896]{1,0:T(8,128)(2,1)S(1)}, u32[]{:S(2)}, u32[]{:S(2)}) collective-permute-start(bf16[48,896]{1,0:T(8,128)(2,1)S(1)} %get-tuple-element.122.refs_9_.refs_0_.refs_7_), channel_id=1, source_target_pairs={{2,0},{3,1},{0,2},{1,3},{6,4},{7,5},{4,6},{5,7},{10,8},{11,9},{8,1... | collective-permute-start | bytes 258056 | tf_op jit(solution)/shard_map/ppermute | solution.py:45
  111.6 7.5 %collective-permute-start.29 = (bf16[48,896]{1,0:T(8,128)(2,1)S(1)}, bf16[48,896]{1,0:T(8,128)(2,1)S(1)}, u32[]{:S(2)}, u32[]{:S(2)}) collective-permute-start(bf16[48,896]{1,0:T(8,128)(2,1)S(1)} %get-tuple-element.122.refs_9_.refs_0_.refs_7_), channel_id=1, source_target_pairs={{3,0},{2,1},{1,2},{0,3},{7,4},{6,5},{5,6},{4,7},{11,8},{10,9},{9,1... | collective-permute-start | bytes 258056 | tf_op jit(solution)/shard_map/ppermute | solution.py:45
  121.5 4.8 %collective-permute-start.31 = (bf16[48,640]{1,0:T(8,128)(2,1)S(1)}, bf16[48,640]{1,0:T(8,128)(2,1)S(1)}, u32[]{:S(2)}, u32[]{:S(2)}) collective-permute-start(bf16[48,640]{1,0:T(8,128)(2,1)S(1)} %get-tuple-element.134.refs_11_), channel_id=1, source_target_pairs={{0,4},{4,0},{1,5},{5,1},{2,6},{6,2},{3,7},{7,3},{8,12},{12,8},{9,1... | collective-permute-start | bytes 184328 | tf_op jit(solution)/shard_map/ppermute | solution.py:19
  124.6 10.8 %collective-permute-start.35 = (f32[4,3584]{1,0:T(4,128)S(1)}, f32[4,3584]{1,0:T(4,128)S(1)}, u32[]{:S(2)}, u32[]{:S(2)}) collective-permute-start(f32[4,3584]{1,0:T(4,128)S(1)} %get-tuple-element.150), channel_id=1, source_target_pairs={{0,4},{4,0},{1,5},{5,1},{2,6},{6,2},{3,7},{7,3},{8,12},{12,8},{9,1... | collective-permute-start | bytes 172040 | tf_op jit(solution)/shard_map/ppermute | solution.py:19
  130.9 9.1 %collective-permute-start.32 = (bf16[48,896]{1,0:T(8,128)(2,1)S(1)}, bf16[48,896]{1,0:T(8,128)(2,1)S(1)}, u32[]{:S(2)}, u32[]{:S(2)}) collective-permute-start(bf16[48,896]{1,0:T(8,128)(2,1)S(1)} %get-tuple-element.147), channel_id=1, source_target_pairs={{0,1},{1,0},{2,3},{3,2},{4,5},{5,4},{6,7},{7,6},{8,9},{9,8},{10,11... | collective-permute-start | bytes 258056 | tf_op jit(solution)/shard_map/ppermute | solution.py:53
  132.0 8.0 %collective-permute-start.33 = (bf16[48,896]{1,0:T(8,128)(2,1)S(1)}, bf16[48,896]{1,0:T(8,128)(2,1)S(1)}, u32[]{:S(2)}, u32[]{:S(2)}) collective-permute-start(bf16[48,896]{1,0:T(8,128)(2,1)S(1)} %get-tuple-element.148), channel_id=1, source_target_pairs={{0,2},{1,3},{2,0},{3,1},{4,6},{5,7},{6,4},{7,5},{8,10},{9,11},{10,... | collective-permute-start | bytes 258056 | tf_op jit(solution)/shard_map/ppermute | solution.py:53
  133.5 6.5 %collective-permute-start.34 = (bf16[48,896]{1,0:T(8,128)(2,1)S(1)}, bf16[48,896]{1,0:T(8,128)(2,1)S(1)}, u32[]{:S(2)}, u32[]{:S(2)}) collective-permute-start(bf16[48,896]{1,0:T(8,128)(2,1)S(1)} %get-tuple-element.149), channel_id=1, source_target_pairs={{0,3},{1,2},{2,1},{3,0},{4,7},{5,6},{6,5},{7,4},{8,11},{9,10},{10,... | collective-permute-start | bytes 258056 | tf_op jit(solution)/shard_map/ppermute | solution.py:53
  135.4 9.6 %collective-permute-start.30 = (bf16[6,7296]{1,0:T(8,128)(2,1)S(1)}, bf16[6,7296]{1,0:T(8,128)(2,1)S(1)}, u32[]{:S(2)}, u32[]{:S(2)}) collective-permute-start(bf16[6,7296]{1,0:T(8,128)(2,1)S(1)} %get-tuple-element.135), channel_id=1, source_target_pairs={{0,24},{8,0},{16,8},{24,16},{1,25},{9,1},{17,9},{25,17},{2,26},{10... | collective-permute-start | bytes 262664 | tf_op jit(solution)/shard_map/ppermute | solution.py:19
  141.1 5.3 %collective-permute-start.36 = (bf16[6,3584]{1,0:T(8,128)(2,1)S(1)}, bf16[6,3584]{1,0:T(8,128)(2,1)S(1)}, u32[]{:S(2)}, u32[]{:S(2)}) collective-permute-start(bf16[6,3584]{1,0:T(8,128)(2,1)S(1)} %get-tuple-element.156), channel_id=1, source_target_pairs={{0,24},{4,28},{8,0},{12,4},{16,8},{20,12},{24,16},{28,20},{1,25},{... | collective-permute-start | bytes 129032 | tf_op jit(solution)/shard_map/ppermute | solution.py:29
  143.0 5.0 %collective-permute-start.37 = (bf16[6,3584]{1,0:T(8,128)(2,1)S(1)}, bf16[6,3584]{1,0:T(8,128)(2,1)S(1)}, u32[]{:S(2)}, u32[]{:S(2)}) collective-permute-start(bf16[6,3584]{1,0:T(8,128)(2,1)S(1)} %get-tuple-element.157), channel_id=1, source_target_pairs={{0,28},{4,24},{8,4},{12,0},{16,12},{20,8},{24,20},{28,16},{1,29},{... | collective-permute-start | bytes 129032 | tf_op jit(solution)/shard_map/ppermute | solution.py:29
  143.6 7.1 %collective-permute-start.38 = (f32[4,896]{1,0:T(4,128)S(1)}, f32[4,896]{1,0:T(4,128)S(1)}, u32[]{:S(2)}, u32[]{:S(2)}) collective-permute-start(f32[4,896]{1,0:T(4,128)S(1)} %get-tuple-element.161), channel_id=1, source_target_pairs={{0,1},{1,0},{2,3},{3,2},{4,5},{5,4},{6,7},{7,6},{8,9},{9,8},{10,11... | collective-permute-start | bytes 43016 | tf_op jit(solution)/shard_map/ppermute | solution.py:53
  145.0 5.7 %collective-permute-start.39 = (f32[4,896]{1,0:T(4,128)S(1)}, f32[4,896]{1,0:T(4,128)S(1)}, u32[]{:S(2)}, u32[]{:S(2)}) collective-permute-start(f32[4,896]{1,0:T(4,128)S(1)} %get-tuple-element.162), channel_id=1, source_target_pairs={{0,2},{1,3},{2,0},{3,1},{4,6},{5,7},{6,4},{7,5},{8,10},{9,11},{10,... | collective-permute-start | bytes 43016 | tf_op jit(solution)/shard_map/ppermute | solution.py:53
  146.4 5.5 %collective-permute-start.40 = (f32[4,896]{1,0:T(4,128)S(1)}, f32[4,896]{1,0:T(4,128)S(1)}, u32[]{:S(2)}, u32[]{:S(2)}) collective-permute-start(f32[4,896]{1,0:T(4,128)S(1)} %get-tuple-element.163), channel_id=1, source_target_pairs={{0,3},{1,2},{2,1},{3,0},{4,7},{5,6},{6,5},{7,4},{8,11},{9,10},{10,... | collective-permute-start | bytes 43016 | tf_op jit(solution)/shard_map/ppermute | solution.py:53
where the time goes:
time: 153 us
  Pallas kernels  63.4 us (41%)
  starting transfers between devices  55.3 us (36%)
  waiting for transfers between devices  27.7 us (18%)
  local copies, waits for them, and re-layouts  5.12 us (3%)
    ppermute x12, starting transfers between devices, return_dp(): lax.ppermute(blocks[i], 'dp', [(z, partner(z, i, count)) for z in range(c...  19.6 us
    ppermute x12, starting transfers between devices, gather_dp(): lax.ppermute(block, 'dp', [(partner(z, i, count), z) for z in range(count)])  17.7 us
    pallas_call x5, Pallas kernels, project(): pl.pallas_call(body, name=name, in_specs=specs + [anywhere] * len(after),...  16.9 us
    ppermute x13, starting transfers between devices, ring(): lax.ppermute(value, axis, [(i, (i + steps) % count) for i in range(count)])  14.6 us
    ppermute x12, waiting for transfers between devices, return_dp(): lax.ppermute(blocks[i], 'dp', [(z, partner(z, i, count)) for z in range(c...  13.7 us
    pallas_call x13, Pallas kernels, call(): pl.pallas_call(body, name=name, out_shape=shapes, in_specs=[smem] * n_sma...  13.6 us
    pallas_call x3, Pallas kernels, expand(): pl.pallas_call(body, name=name, in_specs=[vmem] * count + [anywhere] * (1...  12.2 us
    ppermute x13, waiting for transfers between devices, ring(): lax.ppermute(value, axis, [(i, (i + steps) % count) for i in range(count)])  11.8 us
  transfers between devices with their start and end apart: 41, of which 11 were waited for; matrix products, arithmetic and copies ran while one was open for 1% of the time, Pallas kernels for 36%

commit v1 on v0

--- a/solution.py
+++ b/solution.py
@@ -156,15 +156,16 @@
     return out
 
 
+def from_block(got, place, block):
+    count = len(got)
+    out = got[0]
+    for o in range(1, count):
+        out = jnp.where(lax.rem(place - o + count, count) == block, got[o], out)
+    return out
+
+
 def in_order(got, place, axis):
-    count = len(got)
-    out = []
-    for j in range(count):
-        block = got[0]
-        for o in range(1, count):
-            block = jnp.where(lax.rem(place - o + count, count) == j, got[o], block)
-        out.append(block)
-    return jnp.concatenate(out, axis)
+    return jnp.concatenate([from_block(got, place, j) for j in range(len(got))], axis)
 
 
 def as_row(column):
@@ -207,42 +208,65 @@
     return width
 
 
-def call(name, fn, outs, small, *args, after=(), flops=0, limit=12):
+def in_hbm(value):
+    return pltpu.with_memory_space_constraint(value, pltpu.HBM)
+
+
+def call(name, fn, outs, small, *args, far=(), after=(), flops=0, limit=12):
     shapes = [jax.ShapeDtypeStruct(shape, kind) for shape, kind in outs]
-    n_small, n_args, n_after = len(small), len(args), len(after)
+    n_small, n_args, n_far, n_outs = len(small), len(args), len(far), len(shapes)
 
     def body(*refs):
-        values = list(refs[:n_small]) + [r[...] for r in refs[n_small : n_small + n_args]]
-        for ref, value in zip(refs[n_small + n_args + n_after :], fn(*values)):
+        refs = list(refs)
+
+        def take(count):
+            taken, refs[:] = refs[:count], refs[count:]
+            return taken
+
+        small_refs, arg_refs, far_refs = take(n_small), take(n_args), take(n_far)
+        take(len(after))
+        out_refs, buffers, sems = take(n_outs), take(n_far), take(n_far)
+        copies = [pltpu.make_async_copy(*trio) for trio in zip(far_refs, buffers, sems)]
+        for copy in copies:
+            copy.start()
+        for copy in copies:
+            copy.wait()
+        values = small_refs + [r[...] for r in arg_refs + buffers]
+        for ref, value in zip(out_refs, fn(*values)):
             ref[...] = value.astype(ref.dtype)
 
-    size = sum(a.size * a.dtype.itemsize for a in list(args) + shapes)
+    size = sum(a.size * a.dtype.itemsize for a in list(args) + list(far) + shapes)
     return pl.pallas_call(
         body,
         name=name,
         out_shape=shapes,
-        in_specs=[smem] * n_small + [vmem] * n_args + [anywhere] * n_after,
-        out_specs=[vmem] * len(shapes),
+        in_specs=[smem] * n_small + [vmem] * n_args + [anywhere] * (n_far + len(after)),
+        out_specs=[vmem] * n_outs,
+        scratch_shapes=[pltpu.VMEM(a.shape, a.dtype) for a in far] + [pltpu.SemaphoreType.DMA] * n_far,
         compiler_params=pltpu.CompilerParams(vmem_limit_bytes=limit << 20),
         cost_estimate=pl.CostEstimate(flops=flops, bytes_accessed=size, transcendentals=0),
-    )(*small, *args, *after)
-
-
-def fetch(weight_ref, depth, kinds, buffer, sems, parts):
+    )(*[in_hbm(a) for a in small], *args, *[in_hbm(a) for a in far], *after)
+
+
+def fetch(weight_ref, depth, kinds, buffer, sems, parts, ahead=4):
     step = weight_ref.shape[2] // parts
-    copies = []
-    for g in range(parts):
-        row = []
-        for k, kind in enumerate(kinds):
-            copy = pltpu.make_async_copy(
-                weight_ref.at[depth, kind, pl.ds(g * step, step)],
-                buffer.at[g, k],
-                sems.at[g, k],
-            )
-            copy.start()
-            row.append(copy)
-        copies.append(row)
-    return copies
+    copies = [
+        pltpu.make_async_copy(
+            weight_ref.at[depth, kind, pl.ds(g * step, step)], buffer.at[g, k], sems.at[g, k]
+        )
+        for g in range(parts)
+        for k, kind in enumerate(kinds)
+    ]
+    for copy in copies[:ahead]:
+        copy.start()
+
+    def wait(g, k):
+        at = g * len(kinds) + k
+        copies[at].wait()
+        if at + ahead < len(copies):
+            copies[at + ahead].start()
+
+    return wait
 
 
 def fetched(weight, kinds, parts):
@@ -255,10 +279,10 @@
 
 def project(name, blocks, weight, depth, kinds, parts, others=None, select=None, gain=None, mates=None, after=()):
     groups = len(blocks)
-    rows = blocks[0].shape[0] // parts // (1 if others is None else 2)
+    rows = blocks[0].shape[0] // parts
     width, hidden = weight.shape[2:]
     step = width // parts
-    other_kinds = others if others is not None else ()
+    other_blocks, other_kinds = others if others is not None else ([], ())
     first_kinds, kinds = kinds, kinds + other_kinds
     total, many = rows * groups, len(kinds) * hidden
     marked = select is not None or mates is not None
@@ -268,6 +292,7 @@
         refs = list(refs)
         where_ref = refs.pop(0) if select is not None else None
         x_refs, w_ref, refs = refs[:groups], refs[groups], refs[groups + 1 :]
+        other_refs, refs = refs[: len(other_blocks)], refs[len(other_blocks) :]
         if select is not None:
             select_ref, gain_ref = refs.pop(0), refs.pop(0)
         if mates is not None:
@@ -276,7 +301,7 @@
         own_ref, send_ref = refs.pop(0), refs.pop(0)
         kept_ref = refs.pop(0) if select is not None else None
         buffer, sems = refs
-        copies = fetch(w_ref, depth, kinds, buffer, sems, parts)
+        wait = fetch(w_ref, depth, kinds, buffer, sems, parts)
         x_all = [r[...] for r in x_refs]
         mate_all = [r[...] for r in mate_refs] if mates is not None else x_all
         if select is not None:
@@ -284,7 +309,7 @@
         sums = [jnp.zeros((total, hidden), f32) for _ in kinds]
         mark = jnp.zeros((total, 1), f32)
         for g in range(parts):
-            x = column_part(x_all, rows, g)[:, :step]
+            x = column_part(x_all, rows, g)
             if marked:
                 mate = x if mates is None else column_part(mate_all, rows, g)
                 mark += jnp.sum(x.astype(f32) * mate.astype(f32), axis=1, keepdims=True)
@@ -294,8 +319,8 @@
                 kept_ref[:, g * step : (g + 1) * step] = x
             for k in range(len(kinds)):
                 if k == len(first_kinds):
-                    x = column_part(x_all, rows, parts + g)[:, :step]
-                copies[g][k].wait()
+                    x = column_part([r[...] for r in other_refs], rows, g)[:, :step]
+                wait(g, k)
                 sums[k] += jnp.dot(x, buffer[g, k], preferred_element_type=f32)
         for k in range(len(kinds)):
             own_ref[:, k * hidden : (k + 1) * hidden] = sums[k]
@@ -304,8 +329,8 @@
             own_ref[:, many:] = in_lanes([mark])
             send_ref[:, many:] = coded(mark).astype(bf16)
 
-    args = list(blocks) + [pltpu.with_memory_space_constraint(weight, pltpu.HBM)]
-    specs = [vmem] * groups + [anywhere]
+    args = list(blocks) + [in_hbm(weight)]
+    args, specs = args + list(other_blocks), [vmem] * groups + [anywhere] + [vmem] * len(other_blocks)
     outs = [
         jax.ShapeDtypeStruct((total, many + extra), f32),
         jax.ShapeDtypeStruct((total, many + extra), bf16),
@@ -340,14 +365,14 @@
         in_refs, w_ref = refs[:count], refs[count]
         refs = refs[count + 1 + len(after) :]
         saved_refs, out_refs, (buffer, sems) = refs[:kept], refs[kept:-2], refs[-2:]
-        copies = fetch(w_ref, depth, kinds, buffer, sems, parts)
+        wait = fetch(w_ref, depth, kinds, buffer, sems, parts)
         for ref, value in zip(saved_refs, prepare(*[r[...] for r in in_refs])):
             ref[...] = value.astype(ref.dtype)
         out = []
         for g in range(parts):
             part = jnp.zeros((total, step), f32)
             for k in range(len(kinds)):
-                copies[g][k].wait()
+                wait(g, k)
                 part += lax.dot_general(
                     saved_refs[k][...], buffer[g, k], (((1,), (1,)), ((), ())),
                     preferred_element_type=f32,
@@ -371,7 +396,7 @@
             bytes_accessed=2 * width * hidden * len(kinds),
             transcendentals=0,
         ),
-    )(*args, pltpu.with_memory_space_constraint(weight, pltpu.HBM), *after)
+    )(*args, in_hbm(weight), *after)
     return results[:kept], results[kept:]
 
 
@@ -379,7 +404,7 @@
     total, hidden = act.shape
     step = width // parts
     count = len(args)
-    earlier = [] if before is None else [pltpu.with_memory_space_constraint(before, pltpu.HBM)]
+    earlier = [] if before is None else [in_hbm(before)]
 
     def contract(left, right):
         return lax.dot_general(left, right, (((0,), (0,)), ((), ())), preferred_element_type=f32)
@@ -553,7 +578,7 @@
             bytes_accessed=10 * tokens * width // halves,
             transcendentals=0,
         ),
-    )(token, count, hidden, embed, next_rows, cotangent, gain, *earlier, *after)
+    )(in_hbm(token), in_hbm(count), hidden, embed, next_rows, cotangent, gain, *earlier, *after)
 
 
 def local(
@@ -590,8 +615,12 @@
             + thirds(weight_2)
         )
         ahead_1, ahead_2 = pick(first + 1, embed), pick(first + 2, embed)
-        block = jnp.concatenate([ahead_1, ahead_2, pick(first, cot), pick(second, cot) * weight_2], 0)
-        notes = jnp.concatenate([coded(inv_rms(ahead_1)), coded(inv_rms(ahead_2)), facts, facts], 0)
+        block = jnp.concatenate([ahead_1, ahead_2, pick(first, cot)], 0)
+        notes = jnp.concatenate([coded(inv_rms(ahead_1)), coded(inv_rms(ahead_2)), facts], 0)
+        dout = folded(pick(second, cot) * weight_2, seqs * parts)
+        none = jnp.zeros(((parts - 1) * slots, lanes), f32)
+        tail = facts if parts == 1 else jnp.concatenate([facts, none], 0)
+        dout = jnp.concatenate([dout, jnp.concatenate([tail] * seqs, 0)], 1)
         head = embed[:depths].astype(f32)
         scale = coded(inv_rms(head))
         heads = [
@@ -600,11 +629,14 @@
         return [
             jnp.concatenate([jnp.concatenate([piece, notes], 1)] + heads, 0)
             for piece in pieces_of(block, where[0], seqs)
-        ]
-
-    own_sent = call(
-        "own_rows", own_rows, [((4 * slots + depths * seqs, width + lanes), bf16)] * seqs,
-        (where, slot_token, slot_count, route_gate), embed, cot, after=(asked_token,),
+        ] + [dout]
+
+    fine = width // parts + lanes
+    *own_sent, dout_2 = call(
+        "own_rows", own_rows,
+        [((3 * slots + depths * seqs, width + lanes), bf16)] * seqs
+        + [((slots * parts * seqs, fine), bf16)],
+        (where, slot_token, slot_count, route_gate), far=(embed, cot), after=(asked_token,),
     )
     own_got = trade_seq(own_sent)
 
@@ -624,12 +656,13 @@
         (where, asked_token), source, after=(own_sent[0],),
     )
     start_got = trade_seq(sent, 1)
-
-    def own_parts(where, *got):
-        got = [g.astype(f32) for g in got]
-        first = 4 * slots
-        block_1, block_2, block_3, block_4 = (
-            in_order([g[k * slots : (k + 1) * slots] for g in got], where[0], 0) for k in range(4)
+    dout_2_sent = gather_dp(dout_2)
+
+    def first_mixed(where, gain, *got):
+        start_got, got = got[:seqs], [g.astype(f32) for g in got[seqs:]]
+        first = 3 * slots
+        block_1, block_2, block_3 = (
+            in_order([g[k * slots : (k + 1) * slots] for g in got], where[0], 0) for k in range(3)
         )
         facts = block_3[:, width:]
         heads = in_order([g[first:] for g in got], where[0], 0)
@@ -650,37 +683,24 @@
                     add += jnp.where(token == float(tokens + i - k), row, 0.0)
                 after.append(add)
             units.append(unit + jnp.concatenate(after, 0))
-        out = folded(block_4[:, :width], parts)
-        none = jnp.zeros(((parts - 1) * rows, lanes), f32)
-        tail = facts if parts == 1 else jnp.concatenate([facts, none], 0)
         follow = got[-1][first:, :width]
         follow = jnp.concatenate([follow[p * depths : (p + 1) * depths] for p in range(seqs)], 1)
         follow = jnp.where(where[0] == seqs - 1, 0.0, follow)
         follow = jnp.concatenate([follow, jnp.zeros((16 - depths, features), f32)], 0)
-        return block_3[:, :width], jnp.concatenate([out, tail], 1), facts, *units, follow
-
-    cot_1, dout_2, own_facts, unit_e1, unit_e2, next_rows = call(
-        "own_parts", own_parts,
-        [part_rows, ((rows * parts, width // parts + lanes), bf16), ((rows, lanes), f32)]
-        + [part_rows] * 2
-        + [((16, features), bf16)],
-        (where,), *own_got,
-    )
-
-    def first_mixed(where, own_facts, unit_e1, gain, *got):
-        start = in_order([g[:, : width + lanes].astype(f32) for g in got], where[0], 0)
+        start = in_order([g[:, : width + lanes].astype(f32) for g in start_got], where[0], 0)
         unit = start[:, :width] * decoded(start[:, width:])
         gain_h, gain_e = (piece_of(gain[0, k : k + 1], where[0], seqs, 0) for k in range(2))
-        mixed = (unit * gain_h + unit_e1 * gain_e).astype(bf16).astype(f32)
-        return payload(mixed * own_facts[:, 2:3]), unit
-
-    rows_1, unit_1 = call(
-        "first_mixed", first_mixed, [packed, part_rows],
-        (where,), own_facts, unit_e1, norm_gain, *start_got,
+        mixed = (unit * gain_h + units[0] * gain_e).astype(bf16).astype(f32)
+        return payload(mixed * facts[:, 2:3]), unit, *units, block_3[:, :width], facts, follow
+
+    rows_1, unit_1, unit_e1, unit_e2, cot_1, own_facts, next_rows = call(
+        "first_mixed", first_mixed,
+        [packed] + [part_rows] * 4 + [((rows, lanes), f32), ((16, features), bf16)],
+        (where,), norm_gain, *start_got, *own_got,
     )
     rows_1_all = gather_dp(rows_1)
 
-    def second_base(where, token, count, start, table, after, gain):
+    def second_base(where, token, count, start, table, after, gain, *dout):
         second = token_column(token, 1)
         start = start[:, width + lanes :].astype(f32)
         ahead_1 = pick_ahead(second + 1, table, after)
@@ -690,30 +710,42 @@
         mixed = mixed.astype(bf16).astype(f32)
         own = mixed * inv_rms(mixed) * gain[1, 0:1] * (1.0 - met_column(token, count))
         out = (own + ahead_2 * inv_rms(ahead_2) * gain[1, 1:2]) * live_column(count, 1, slots)
-        return pieces_of(out, where[0], seqs) + [ahead_1, ahead_2]
-
-    *base_parts, ahead_21, ahead_22 = call(
+        none = jnp.zeros((slots * parts, lanes), f32)
+        bases = [
+            jnp.concatenate([folded(piece, parts), none], 1)
+            for piece in pieces_of(out, where[0], seqs)
+        ]
+        douts = zip(*(blocks_of(block.astype(f32), where[0], seqs) for block in dout))
+        return [jnp.concatenate([base, *more], 0) for base, more in zip(bases, douts)] + [ahead_1, ahead_2]
+
+    *fixed_sent, ahead_21, ahead_22 = call(
         "second_base", second_base,
-        [((slots, width), bf16)] * seqs + [((slots, features), bf16)] * 2,
-        (where, *facts), start_got[0], embed, next_rows, norm_gain, after=(rows_1,),
-    )
-    base_got = trade_seq(base_parts)
+        [((slots * parts * (1 + groups), fine), bf16)] * seqs + [((slots, features), bf16)] * 2,
+        (where, *facts), start_got[0], embed, next_rows, norm_gain, *dout_2_sent, after=(rows_1,),
+    )
+    fixed_got = trade_seq(fixed_sent)
 
     first_own, first_send = project(
-        "gate_up_1", rows_1_all, expert_weight, 0, (0, 1), parts, after=(ahead_21, base_got[-1])
+        "gate_up_1", rows_1_all, expert_weight, 0, (0, 1), parts, after=(ahead_21,)
     )
     first = pair_seq(first_own, first_send)
 
-    def fixed_order(where, dout, *got):
-        base = payload(in_order([g.astype(f32) for g in got], where[0], 0))
-        none = jnp.zeros((base.shape[0], lanes), f32)
-        return [jnp.concatenate([jnp.concatenate([base, none], 1), dout.astype(f32)], 0)]
-
-    (fixed_rows,) = call(
-        "fixed_order", fixed_order, [((2 * rows * parts, width // parts + lanes), bf16)],
-        (where,), dout_2, *base_got, after=(first_send,),
-    )
-    fixed_all = gather_dp(fixed_rows)
+    def fixed_order(where, *got):
+        got = [g.astype(f32) for g in got]
+        size = slots * parts
+        out = []
+        for z in range(1 + groups):
+            blocks = [g[z * size : (z + 1) * size] for g in got]
+            blocks = [from_block(blocks, where[0], j) for j in range(seqs)]
+            pairs = [b[g * slots : (g + 1) * slots] for g in range(parts) for b in blocks]
+            out.append(jnp.concatenate(pairs, 0))
+        return [out[0][:, : width // parts]] + out[1:]
+
+    base_2, *dout_2_all = call(
+        "fixed_order", fixed_order, [packed] + [((rows * parts, fine), bf16)] * groups,
+        (where,), *fixed_got, after=(first_send,),
+    )
+    base_2_all = gather_dp(base_2)
 
     def forward_1(own, other):
         both = own + other.astype(f32)
@@ -723,7 +755,7 @@
     (act_1, both_1), out_blocks = expand(
         "down_1", forward_1, first,
         [((total, hidden_units), bf16), ((total, 2 * hidden_units), f32)],
-        expert_weight, 0, (2,), groups, parts, after=(fixed_rows,),
+        expert_weight, 0, (2,), groups, parts, after=(base_2,),
     )
     out_got = return_dp(out_blocks)
 
@@ -746,7 +778,7 @@
 
     def slot_facts(*blocks):
         facts = jnp.concatenate(
-            [block[rows * parts : rows * (parts + 1)].astype(f32)[:, width // parts :] for block in blocks], 0
+            [block[:rows].astype(f32)[:, width // parts :] for block in blocks], 0
         )
         base = (iota((total, 1), 0) // slots * tokens).astype(f32)
         first, second = facts[:, 0:1] + base, facts[:, 1:2] + base
@@ -757,11 +789,11 @@
     same, same_16, same_own, weight_1 = call(
         "slot_facts", slot_facts,
         [((total, total), f32), ((total, total), bf16), ((rows, rows), f32), ((total, 1), f32)],
-        (), *fixed_all, after=(prev,),
+        (), *dout_2_all, after=(prev,),
     )
     fixed_own, fixed_send = project(
-        "fixed_2", fixed_all, expert_weight, 1, (0, 1), parts,
-        others=(2,), after=(same_own,),
+        "fixed_2", base_2_all, expert_weight, 1, (0, 1), parts,
+        others=(dout_2_all, (2,)), after=(same_own,),
     )
     fixed_pair = pair_seq(fixed_own, fixed_send)
 
@@ -824,14 +856,14 @@
     back_got = trade_seq(d_rows_back)
 
     def build_2(values, g):
-        chosen, row, *fixed = values
+        chosen, row, base, dout = values[0], values[1], values[2 : 2 + groups], values[2 + groups :]
         step = width // parts
         first = chosen[:, g * step : (g + 1) * step].astype(f32) * row
-        first = first + column_part(fixed, rows, g)[:, :step].astype(f32)
-        return first.astype(bf16), column_part(fixed, rows, parts + g)[:, :step]
+        first = first + column_part(base, rows, g).astype(f32)
+        return first.astype(bf16), column_part(dout, rows, g)[:, :step]
 
     weight_grad, tick_2 = outer(
-        "weight_grad_2", 1, depths, build_2, [chosen, row_2] + fixed_all,
+        "weight_grad_2", 1, depths, build_2, [chosen, row_2] + base_2_all + dout_2_all,
         d_gate_2, d_up_2, act_2, width, parts, None, after=(u, back_got[-1]),
     )
 

time: 153 us -> 155 us (1.013)
  Pallas kernels: 63.4 us -> 67.8 us
  local copies, waits for them, and re-layouts: 5.12 us -> 1.32 us
    ppermute x12 -> x15, waiting for transfers between devices: 2.2 us -> 15.7 us  [gather_dp(): lax.ppermute(block, 'dp', [(partner(z, i, count), z) for z in range(count)])]
    ppermute x12, waiting for transfers between devices: 13.7 us -> 2.62 us  [return_dp(): lax.ppermute(blocks[i], 'dp', [(z, partner(z, i, count)) for z in range(c...]
    ppermute x13, waiting for transfers between devices: 11.8 us -> 4.97 us  [ring(): lax.ppermute(value, axis, [(i, (i + steps) % count) for i in range(count)])]
    ppermute x4, waiting for transfers between devices: 0.01 us -> 4.63 us  [hop(): return lax.ppermute(value, ('section', 'seq'), pairs)]
    ppermute x12 -> x15, starting transfers between devices: 17.7 us -> 21.7 us  [gather_dp(): lax.ppermute(block, 'dp', [(partner(z, i, count), z) for z in range(count)])]
    unnamed x19 -> x13, local copies, waits for them, and re-layouts: 5.12 us -> 1.32 us
    pallas_call x13 -> x12, Pallas kernels: 13.6 us -> 16.6 us  [call(): pl.pallas_call(body, name=name, out_shape=shapes, in_specs=[smem] * n_sma...]
    ppermute x12, starting transfers between devices: 19.6 us -> 17.7 us  [return_dp(): lax.ppermute(blocks[i], 'dp', [(z, partner(z, i, count)) for z in range(c...]
  transfers between devices with their start and end apart: 41 -> 44, of which waited for: 11 -> 12; matrix products, arithmetic and copies ran while one was open for 1% -> 1% of each run, Pallas kernels for 36% -> 36%
where the time goes in v1:
time: 155 us; the launch traced here: 154 us
  Pallas kernels  67.8 us (44%)
  starting transfers between devices  55.8 us (36%)
  waiting for transfers between devices  27.9 us (18%)
    ppermute x15, starting transfers between devices, gather_dp(): lax.ppermute(block, 'dp', [(partner(z, i, count), z) for z in range(count)])  21.7 us
    pallas_call x5, Pallas kernels, project(): pl.pallas_call(body, name=name, in_specs=specs + [anywhere] * len(after),...  18 us
    ppermute x12, starting transfers between devices, return_dp(): lax.ppermute(blocks[i], 'dp', [(z, partner(z, i, count)) for z in range(c...  17.7 us
    pallas_call x12, Pallas kernels, call(): pl.pallas_call(body, name=name, out_shape=shapes, in_specs=[smem] * n_sma...  16.6 us
    ppermute x15, waiting for transfers between devices, gather_dp(): lax.ppermute(block, 'dp', [(partner(z, i, count), z) for z in range(count)])  15.7 us
    ppermute x13, starting transfers between devices, ring(): lax.ppermute(value, axis, [(i, (i + steps) % count) for i in range(count)])  12.9 us
    pallas_call x3, Pallas kernels, expand(): pl.pallas_call(body, name=name, in_specs=[vmem] * count + [anywhere] * (1...  12.3 us
    pallas_call x2, Pallas kernels, dense_rows(): pl.pallas_call(body, name=name, in_specs=[smem] * 2 + [vmem] * (5 + len(e...  11.4 us
  transfers between devices with their start and end apart: 44, of which 12 were waited for; matrix products, arithmetic and copies ran while one was open for 1% of the time, Pallas kernels for 36%

profile of v1, /device:TPU:0, one launch (start us, length us, event | category | flops | bytes accessed | tf_op | source)
XLA Modules:
  0.0 154.4 jit_solution(191430513121396755)
XLA Ops:
  0.6 2.4 %collective-permute-start = (s32[1,1,2,6]{3,2,1,0:T(2,128)}, s32[1,1,2,6]{3,2,1,0:T(2,128)S(1)}, u32[]{:S(2)}, u32[]{:S(2)}) collective-permute-start(s32[1,1,2,6]{3,2,1,0:T(2,128)} %refs_1_.7), channel_id=1, source_target_pairs={{0,24},{8,0},{16,8},{24,16},{1,25},{9,1},{17,9},{25,17},{2,26},{10... | collective-permute-start | bytes 152 | tf_op jit(solution)/shard_map/ppermute | solution.py:19
  3.1 1.3 copy.16.refs_2_.count_ref
  5.0 4.0 %own_rows.1 = (bf16[22,3712]{1,0:T(8,128)(2,1)S(1)}, bf16[22,3712]{1,0:T(8,128)(2,1)S(1)}, bf16[48,1024]{1,0:T(8,128)(2,1)S(1)}) custom-call(s32[2]{0:T(128)} %pad_add_fusion.refs_0_, s32[1,1,2,6]{3,2,1,0:T(2,128)} %refs_1_.7, s32[1,1,2,1]{3,2,1,0:T(2,128)} %copy.16.refs_2_.count_ref, f32[1,1,2,6]{3,2,1,0:T(2,128)} %refs_3_.2, bf16[128,7168]{1,0:T(8,128)(2,1)} %bitcast.6, ...), custom_call_target="tpu_custom_call" | custom-call | bytes 4094976 | tf_op jit(solution)/shard_map/own_rows/pallas_call | solution.py:239
  9.0 1.6 %collective-permute-start.3 = (bf16[22,3712]{1,0:T(8,128)(2,1)S(1)}, bf16[22,3712]{1,0:T(8,128)(2,1)S(1)}, u32[]{:S(2)}, u32[]{:S(2)}) collective-permute-start(bf16[22,3712]{1,0:T(8,128)(2,1)S(1)} %get-tuple-element.92), channel_id=1, source_target_pairs={{0,4},{4,0},{1,5},{5,1},{2,6},{6,2},{3,7},{7,3},{8,12},{12,8},{9,1... | collective-permute-start | bytes 489992 | tf_op jit(solution)/shard_map/ppermute | solution.py:19
  10.6 1.3 source_rows.1
  11.9 0.9 collective-permute-start.2
  12.8 4.6 %collective-permute-done.2.refs_3_ = bf16[6,3712]{1,0:T(8,128)(2,1)S(1)} collective-permute-done((bf16[6,3712]{1,0:T(8,128)(2,1)S(1)}, bf16[6,3712]{1,0:T(8,128)(2,1)S(1)}, u32[]{:S(2)}, u32[]{:S(2)}) %collective-permute-start.2) | collective-permute-done | bytes 44576 | tf_op jit(solution)/shard_map/ppermute | solution.py:29
  17.5 1.1 first_mixed.1
  18.7 1.6 %collective-permute-start.8 = (bf16[48,1024]{1,0:T(8,128)(2,1)S(1)}, bf16[48,1024]{1,0:T(8,128)(2,1)S(1)}, u32[]{:S(2)}, u32[]{:S(2)}) collective-permute-start(bf16[48,1024]{1,0:T(8,128)(2,1)S(1)} %get-tuple-element.96.refs_7_), channel_id=1, source_target_pairs={{1,0},{0,1},{3,2},{2,3},{5,4},{4,5},{7,6},{6,7},{9,8},{8,9},{11,10... | collective-permute-start | bytes 294920 | tf_op jit(solution)/shard_map/ppermute | solution.py:45
  20.3 2.6 %collective-permute-start.9 = (bf16[48,1024]{1,0:T(8,128)(2,1)S(1)}, bf16[48,1024]{1,0:T(8,128)(2,1)S(1)}, u32[]{:S(2)}, u32[]{:S(2)}) collective-permute-start(bf16[48,1024]{1,0:T(8,128)(2,1)S(1)} %get-tuple-element.96.refs_7_), channel_id=1, source_target_pairs={{2,0},{3,1},{0,2},{1,3},{6,4},{7,5},{4,6},{5,7},{10,8},{11,9},{8,1... | collective-permute-start | bytes 294920 | tf_op jit(solution)/shard_map/ppermute | solution.py:45
  23.1 1.0 collective-permute-done.8.refs_8_
  24.2 6.9 %collective-permute-done.9.refs_9_ = bf16[48,1024]{1,0:T(8,128)(2,1)S(1)} collective-permute-done((bf16[48,1024]{1,0:T(8,128)(2,1)S(1)}, bf16[48,1024]{1,0:T(8,128)(2,1)S(1)}, u32[]{:S(2)}, u32[]{:S(2)}) %collective-permute-start.9) | collective-permute-done | bytes 98336 | tf_op jit(solution)/shard_map/ppermute | solution.py:45
  31.0 1.7 %second_base.1 = (bf16[120,1024]{1,0:T(8,128)(2,1)S(1)}, bf16[120,1024]{1,0:T(8,128)(2,1)S(1)}, bf16[6,7168]{1,0:T(8,128)(2,1)S(1)}, bf16[6,7168]{1,0:T(8,128)(2,1)S(1)}) custom-call(s32[2]{0:T(128)} %pad_add_fusion.refs_0_, s32[1,1,2,6]{3,2,1,0:T(2,128)} %refs_1_.7, s32[1,1,2,1]{3,2,1,0:T(2,128)} %copy.16.refs_2_.count_ref, ...), custom_call_target="tpu_custom_call" | custom-call | bytes 3366400 | tf_op jit(solution)/shard_map/second_base/pallas_call | solution.py:239
  32.8 1.5 collective-permute-start.12
  34.2 2.2 %collective-permute-start.5 = (bf16[48,896]{1,0:T(8,128)(2,1)S(1)}, bf16[48,896]{1,0:T(8,128)(2,1)S(1)}, u32[]{:S(2)}, u32[]{:S(2)}) collective-permute-start(bf16[48,896]{1,0:T(8,128)(2,1)S(1)} %get-tuple-element.93.refs_11_.refs_0_.refs_1_.refs_3_), channel_id=1, source_target_pairs={{1,0},{0,1},{3,2},{2,3},{5,4},{4,5},{7,6},{6,7},{9,8},{8,9},{11,10... | collective-permute-start | bytes 258056 | tf_op jit(solution)/shard_map/ppermute | solution.py:45
  36.4 1.1 collective-permute-start.6
  37.5 1.5 collective-permute-start.7
  39.3 6.2 %collective-permute-done.6.refs_2_.refs_5_ = bf16[48,896]{1,0:T(8,128)(2,1)S(1)} collective-permute-done((bf16[48,896]{1,0:T(8,128)(2,1)S(1)}, bf16[48,896]{1,0:T(8,128)(2,1)S(1)}, u32[]{:S(2)}, u32[]{:S(2)}) %collective-permute-start.6) | collective-permute-done | bytes 86048 | tf_op jit(solution)/shard_map/ppermute | solution.py:45
  45.5 3.8 %gate_up_1.1 = (f32[48,1024]{1,0:T(8,128)S(1)}, bf16[48,1024]{1,0:T(8,128)(2,1)S(1)}) custom-call(bf16[48,896]{1,0:T(8,128)(2,1)S(1)} %get-tuple-element.93.refs_11_.refs_0_.refs_1_.refs_3_, bf16[48,896]{1,0:T(8,128)(2,1)S(1)} %collective-permute-done.5.refs_1_.refs_4_, bf16[48,896]{1,0:T(8,128)(2,1)S(1)} %collective-permute-done.6.refs_2_.refs_5_, ...), custom_call_target="tpu_custom_call" | custom-call | flops 352321536 | bytes 7340032 | tf_op jit(solution)/shard_map/gate_up_1/pallas_call | solution.py:344
  49.9 0.9 fixed_order.1
  50.8 3.1 %collective-permute-done.11.refs_1_ = bf16[48,1024]{1,0:T(8,128)(2,1)S(1)} collective-permute-done((bf16[48,1024]{1,0:T(8,128)(2,1)S(1)}, bf16[48,1024]{1,0:T(8,128)(2,1)S(1)}, u32[]{:S(2)}, u32[]{:S(2)}) %collective-permute-start.11) | collective-permute-done | bytes 98336 | tf_op jit(solution)/shard_map/ppermute | solution.py:19
  53.9 3.0 %down_1.1 = (bf16[48,512]{1,0:T(8,128)(2,1)S(1)}, f32[48,1024]{1,0:T(8,128)S(1)}, bf16[48,896]{1,0:T(8,128)(2,1)S(1)}, bf16[48,896]{1,0:T(8,128)(2,1)S(1)}, bf16...) custom-call(f32[48,1024]{1,0:T(8,128)S(1)} %get-tuple-element.98.refs_0_, ...), custom_call_target="tpu_custom_call" | custom-call | flops 176160768 | bytes 3670016 | tf_op jit(solution)/shard_map/down_1/pallas_call | solution.py:385
  57.0 1.6 %collective-permute-start.13 = (bf16[48,896]{1,0:T(8,128)(2,1)S(1)}, bf16[48,896]{1,0:T(8,128)(2,1)S(1)}, u32[]{:S(2)}, u32[]{:S(2)}) collective-permute-start(bf16[48,896]{1,0:T(8,128)(2,1)S(1)} %get-tuple-element.107), channel_id=1, source_target_pairs={{0,1},{1,0},{2,3},{3,2},{4,5},{5,4},{6,7},{7,6},{8,9},{9,8},{10,11... | collective-permute-start | bytes 258056 | tf_op jit(solution)/shard_map/ppermute | solution.py:53
  58.5 1.3 collective-permute-start.14
  59.8 1.6 %collective-permute-start.15 = (bf16[48,896]{1,0:T(8,128)(2,1)S(1)}, bf16[48,896]{1,0:T(8,128)(2,1)S(1)}, u32[]{:S(2)}, u32[]{:S(2)}) collective-permute-start(bf16[48,896]{1,0:T(8,128)(2,1)S(1)} %get-tuple-element.109), channel_id=1, source_target_pairs={{0,3},{1,2},{2,1},{3,0},{4,7},{5,6},{6,5},{7,4},{8,11},{9,10},{10,... | collective-permute-start | bytes 258056 | tf_op jit(solution)/shard_map/ppermute | solution.py:53
  62.0 1.5 collective-permute-done.13.refs_3_
  63.5 1.2 collective-permute-start.20
  64.7 1.9 %collective-permute-start.21 = (bf16[48,896]{1,0:T(8,128)(2,1)S(1)}, bf16[48,896]{1,0:T(8,128)(2,1)S(1)}, u32[]{:S(2)}, u32[]{:S(2)}) collective-permute-start(bf16[48,896]{1,0:T(8,128)(2,1)S(1)} %get-tuple-element.102.refs_3_.refs_0_.refs_2_), channel_id=1, source_target_pairs={{3,0},{2,1},{1,2},{0,3},{7,4},{6,5},{5,6},{4,7},{11,8},{10,9},{9,1... | collective-permute-start | bytes 258056 | tf_op jit(solution)/shard_map/ppermute | solution.py:45
  66.7 5.8 %dense_a.1 = (bf16[128,7168]{1,0:T(8,128)(2,1)S(1)}, f32[4,7168]{1,0:T(4,128)S(1)}) custom-call(s32[1,1,2,6]{3,2,1,0:T(2,128)} %refs_1_.7, s32[1,1,2,1]{3,2,1,0:T(2,128)} %copy.16.refs_2_.count_ref, bf16[128,7168]{1,0:T(8,128)(2,1)S(1)} %collective-permute-done.4.hidden_ref, bf16[128,7168]{1,0:T(8,128)(2,1)S(1)} %bitcast.8, ...), custom_call_target="tpu_custom_call" | custom-call | flops 27525120 | bytes 4587520 | tf_op jit(solution)/shard_map/dense_a/pallas_call | solution.py:564
  73.2 1.9 %collective-permute-start.17 = (bf16[48,896]{1,0:T(8,128)(2,1)S(1)}, bf16[48,896]{1,0:T(8,128)(2,1)S(1)}, u32[]{:S(2)}, u32[]{:S(2)}) collective-permute-start(bf16[48,896]{1,0:T(8,128)(2,1)S(1)} %get-tuple-element.110.refs_4_.refs_1_.refs_0_.refs_5_.refs_11_), channel_id=1, source_target_pairs={{2,0},{3,1},{0,2},{1,3},{6,4},{7,5},{4,6},{5,7},{10,8},{11,9},{8,1... | collective-permute-start | bytes 258056 | tf_op jit(solution)/shard_map/ppermute | solution.py:45
  75.1 1.9 %collective-permute-start.18 = (bf16[48,896]{1,0:T(8,128)(2,1)S(1)}, bf16[48,896]{1,0:T(8,128)(2,1)S(1)}, u32[]{:S(2)}, u32[]{:S(2)}) collective-permute-start(bf16[48,896]{1,0:T(8,128)(2,1)S(1)} %get-tuple-element.110.refs_4_.refs_1_.refs_0_.refs_5_.refs_11_), channel_id=1, source_target_pairs={{3,0},{2,1},{1,2},{0,3},{7,4},{6,5},{5,6},{4,7},{11,8},{10,9},{9,1... | collective-permute-start | bytes 258056 | tf_op jit(solution)/shard_map/ppermute | solution.py:45
  77.2 5.2 %fixed_2.1 = (f32[48,1536]{1,0:T(8,128)S(1)}, bf16[48,1536]{1,0:T(8,128)(2,1)S(1)}) custom-call(bf16[48,896]{1,0:T(8,128)(2,1)S(1)} %get-tuple-element.102.refs_3_.refs_0_.refs_2_, bf16[48,896]{1,0:T(8,128)(2,1)S(1)} %collective-permute-done.19.refs_1_.refs_3_, bf16[48,896]{1,0:T(8,128)(2,1)S(1)} %collective-permute-done.20.refs_2_.refs_4_, ...), custom_call_target="tpu_custom_call" | custom-call | flops 528482304 | bytes 11010048 | tf_op jit(solution)/shard_map/fixed_2/pallas_call | solution.py:344
  83.0 4.3 %gate_up_2.1 = (f32[48,1152]{1,0:T(8,128)S(1)}, bf16[48,1152]{1,0:T(8,128)(2,1)S(1)}, bf16[48,3584]{1,0:T(8,128)(2,1)S(1)}) custom-call(s32[2]{0:T(128)S(1)} %copy-done.4, bf16[48,896]{1,0:T(8,128)(2,1)S(1)} %get-tuple-element.110.refs_4_.refs_1_.refs_0_.refs_5_.refs_11_, bf16[48,896]{1,0:T(8,128)(2,1)S(1)} %collective-permute-done.16.refs_2_.refs_1_.refs_6_.refs_12_, ...), custom_call_target="tpu_custom_call" | custom-call | flops 352321536 | bytes 7340032 | tf_op jit(solution)/shard_map/gate_up_2/pallas_call | solution.py:344
  87.3 1.6 %collective-permute-start.22 = (bf16[48,1152]{1,0:T(8,128)(2,1)S(1)}, bf16[48,1152]{1,0:T(8,128)(2,1)S(1)}, u32[]{:S(2)}, u32[]{:S(2)}) collective-permute-start(bf16[48,1152]{1,0:T(8,128)(2,1)S(1)} %get-tuple-element.119.refs_5_), channel_id=1, source_target_pairs={{0,4},{4,0},{1,5},{5,1},{2,6},{6,2},{3,7},{7,3},{8,12},{12,8},{9,1... | collective-permute-start | bytes 331784 | tf_op jit(solution)/shard_map/ppermute | solution.py:19
  88.9 2.3 %prev_down.1 = (f32[48,512]{1,0:T(8,128)S(1)}, bf16[48,512]{1,0:T(8,128)(2,1)S(1)}) custom-call(bf16[48,896]{1,0:T(8,128)(2,1)S(1)} %get-tuple-element.110.refs_4_.refs_1_.refs_0_.refs_5_.refs_11_, bf16[48,896]{1,0:T(8,128)(2,1)S(1)} %collective-permute-done.16.refs_2_.refs_1_.refs_6_.refs_12_, ...), custom_call_target="tpu_custom_call" | custom-call | flops 176160768 | bytes 3670016 | tf_op jit(solution)/shard_map/prev_down/pallas_call | solution.py:344
  91.3 0.8 collective-permute-done.22.refs_1_
  92.1 4.6 %back_rows_2.1 = (bf16[48,512]{1,0:T(8,128)(2,1)S(1)}, bf16[48,512]{1,0:T(8,128)(2,1)S(1)}, bf16[48,512]{1,0:T(8,128)(2,1)S(1)}, f32[48,1]{1,0:T(8,128)S(1)}, f3...) custom-call(f32[48,1152]{1,0:T(8,128)S(1)} %get-tuple-element.118.re, ...), custom_call_target="tpu_custom_call" | custom-call | flops 352321536 | bytes 7340032 | tf_op jit(solution)/shard_map/back_rows_2/pallas_call | solution.py:385
  96.7 1.4 collective-permute-start.24
  98.1 1.3 collective-permute-start.25
  99.4 1.8 %collective-permute-start.26 = (bf16[48,896]{1,0:T(8,128)(2,1)S(1)}, bf16[48,896]{1,0:T(8,128)(2,1)S(1)}, u32[]{:S(2)}, u32[]{:S(2)}) collective-permute-start(bf16[48,896]{1,0:T(8,128)(2,1)S(1)} %get-tuple-element.128), channel_id=1, source_target_pairs={{0,3},{1,2},{2,1},{3,0},{4,7},{5,6},{6,5},{7,4},{8,11},{9,10},{10,... | collective-permute-start | bytes 258056 | tf_op jit(solution)/shard_map/ppermute | solution.py:53
  101.2 1.6 %collective-permute-start.27 = (bf16[48,512]{1,0:T(8,128)(2,1)S(1)}, bf16[48,512]{1,0:T(8,128)(2,1)S(1)}, u32[]{:S(2)}, u32[]{:S(2)}) collective-permute-start(bf16[48,512]{1,0:T(8,128)(2,1)S(1)} %get-tuple-element.130), channel_id=1, source_target_pairs={{0,4},{4,0},{1,5},{5,1},{2,6},{6,2},{3,7},{7,3},{8,12},{12,8},{9,1... | collective-permute-start | bytes 147464 | tf_op jit(solution)/shard_map/ppermute | solution.py:19
  102.8 5.7 %dense_b.1 = (bf16[128,7168]{1,0:T(8,128)(2,1)S(1)}, f32[4,7168]{1,0:T(4,128)S(1)}) custom-call(s32[1,1,2,6]{3,2,1,0:T(2,128)} %refs_1_.7, s32[1,1,2,1]{3,2,1,0:T(2,128)} %copy.16.refs_2_.count_ref, bf16[128,7168]{1,0:T(8,128)(2,1)S(1)} %collective-permute-done.4.hidden_ref, bf16[128,7168]{1,0:T(8,128)(2,1)S(1)} %bitcast.9, ...), custom_call_target="tpu_custom_call", output_to_operand_aliasing={{0}: (7, {})} | custom-call | flops 27525120 | bytes 4587520 | tf_op jit(solution)/shard_map/dense_b/pallas_call | solution.py:564
  108.5 1.1 first_grad.1
  110.8 2.2 %collective-permute-start.31 = (bf16[48,896]{1,0:T(8,128)(2,1)S(1)}, bf16[48,896]{1,0:T(8,128)(2,1)S(1)}, u32[]{:S(2)}, u32[]{:S(2)}) collective-permute-start(bf16[48,896]{1,0:T(8,128)(2,1)S(1)} %get-tuple-element.131.refs_13_.refs_0_.refs_7_), channel_id=1, source_target_pairs={{2,0},{3,1},{0,2},{1,3},{6,4},{7,5},{4,6},{5,7},{10,8},{11,9},{8,1... | collective-permute-start | bytes 258056 | tf_op jit(solution)/shard_map/ppermute | solution.py:45
  113.0 1.8 %collective-permute-start.32 = (bf16[48,896]{1,0:T(8,128)(2,1)S(1)}, bf16[48,896]{1,0:T(8,128)(2,1)S(1)}, u32[]{:S(2)}, u32[]{:S(2)}) collective-permute-start(bf16[48,896]{1,0:T(8,128)(2,1)S(1)} %get-tuple-element.131.refs_13_.refs_0_.refs_7_), channel_id=1, source_target_pairs={{3,0},{2,1},{1,2},{0,3},{7,4},{6,5},{5,6},{4,7},{11,8},{10,9},{9,1... | collective-permute-start | bytes 258056 | tf_op jit(solution)/shard_map/ppermute | solution.py:45
  114.8 4.7 %weight_grad_2.1 = (bf16[1,2,3,3584,512]{4,3,2,1,0:T(8,128)(2,1)}, f32[8,128]{1,0:T(8,128)S(1)}) custom-call(bf16[48,3584]{1,0:T(8,128)(2,1)S(1)} %get-tuple-element.137.refs_0_, f32[48,1]{1,0:T(8,128)S(1)} %get-tuple-element.138.refs_1_, bf16[48,896]{1,0:T(8,128)(2,1)S(1)} %get-tuple-element.102.refs_3_.refs_0_.refs_2_, ...), custom_call_target="tpu_custom_call" | custom-call | flops 528482304 | bytes 11010048 | tf_op jit(solution)/shard_map/weight_grad_2/pallas_call | solution.py:433
  119.6 1.2 collective-permute-done.31.refs_2_.refs_9_
  120.8 2.4 %back_1.1 = (f32[48,640]{1,0:T(8,128)S(1)}, bf16[48,640]{1,0:T(8,128)(2,1)S(1)}) custom-call(bf16[48,896]{1,0:T(8,128)(2,1)S(1)} %get-tuple-element.131.refs_13_.refs_0_.refs_7_, bf16[48,896]{1,0:T(8,128)(2,1)S(1)} %collective-permute-done.30.refs_1_.refs_8_, bf16[48,896]{1,0:T(8,128)(2,1)S(1)} %collective-permute-done.31.refs_2_.refs_9_, ...), custom_call_target="tpu_custom_call" | custom-call | flops 176160768 | bytes 3670016 | tf_op jit(solution)/shard_map/back_1/pallas_call | solution.py:344
  123.2 1.5 collective-permute-start.34
  124.6 1.6 %second_grad.1 = (bf16[6,7296]{1,0:T(8,128)(2,1)S(1)}, f32[4,3584]{1,0:T(4,128)S(1)}, f32[4,3584]{1,0:T(4,128)S(1)}) custom-call(s32[2]{0:T(128)} %pad_add_fusion.refs_0_, s32[1,1,2,6]{3,2,1,0:T(2,128)} %refs_1_.7, s32[1,1,2,1]{3,2,1,0:T(2,128)} %copy.16.refs_2_.count_ref, bf16[6,10880]{1,0:T(8,128)(2,1)S(1)} %collective-permute-done.1.refs_2_.refs_3_, ...), custom_call_target="tpu_custom_call" | custom-call | bytes 2655232 | tf_op jit(solution)/shard_map/second_grad/pallas_call | solution.py:239
  126.3 0.7 collective-permute-start.38
  127.0 1.0 collective-permute-done.34.refs_1_
  128.0 4.7 %back_rows_1.1 = (bf16[48,512]{1,0:T(8,128)(2,1)S(1)}, bf16[48,512]{1,0:T(8,128)(2,1)S(1)}, f32[48,1]{1,0:T(8,128)S(1)}, bf16[48,896]{1,0:T(8,128)(2,1)S(1)}, bf...) custom-call(f32[48,640]{1,0:T(8,128)S(1)} %get-tuple-element.148.refs_0_, ...), custom_call_target="tpu_custom_call" | custom-call | flops 352321536 | bytes 7340032 | tf_op jit(solution)/shard_map/back_rows_1/pallas_call | solution.py:385
  132.7 1.1 collective-permute-start.35
  133.7 1.8 %collective-permute-start.36 = (bf16[48,896]{1,0:T(8,128)(2,1)S(1)}, bf16[48,896]{1,0:T(8,128)(2,1)S(1)}, u32[]{:S(2)}, u32[]{:S(2)}) collective-permute-start(bf16[48,896]{1,0:T(8,128)(2,1)S(1)} %get-tuple-element.158), channel_id=1, source_target_pairs={{0,2},{1,3},{2,0},{3,1},{4,6},{5,7},{6,4},{7,5},{8,10},{9,11},{10,... | collective-permute-start | bytes 258056 | tf_op jit(solution)/shard_map/ppermute | solution.py:53
  135.5 1.6 %collective-permute-start.37 = (bf16[48,896]{1,0:T(8,128)(2,1)S(1)}, bf16[48,896]{1,0:T(8,128)(2,1)S(1)}, u32[]{:S(2)}, u32[]{:S(2)}) collective-permute-start(bf16[48,896]{1,0:T(8,128)(2,1)S(1)} %get-tuple-element.159), channel_id=1, source_target_pairs={{0,3},{1,2},{2,1},{3,0},{4,7},{5,6},{6,5},{7,4},{8,11},{9,10},{10,... | collective-permute-start | bytes 258056 | tf_op jit(solution)/shard_map/ppermute | solution.py:53
  137.1 4.7 %weight_grad_1.1 = (bf16[1,2,3,3584,512]{4,3,2,1,0:T(8,128)(2,1)}, f32[8,128]{1,0:T(8,128)S(1)}) custom-call(f32[48,1]{1,0:T(8,128)S(1)} %get-tuple-element.152.refs_0_.refs_4_, f32[48,1]{1,0:T(8,128)S(1)} %get-tuple-element.147.refs_5_.refs_1_.refs_3_, f32[48,1]{1,0:T(8,128)S(1)} %get-tuple-element.150.refs_6_.refs_2_, ...), custom_call_target="tpu_custom_call", output_to_operand_aliasing={{0}: (18, {})} | custom-call | flops 528482304 | bytes 11010048 | tf_op jit(solution)/shard_map/weight_grad_1/pallas_call | solution.py:433
  141.9 1.1 last_grad.1
  143.0 1.8 %collective-permute-start.39 = (bf16[6,3584]{1,0:T(8,128)(2,1)S(1)}, bf16[6,3584]{1,0:T(8,128)(2,1)S(1)}, u32[]{:S(2)}, u32[]{:S(2)}) collective-permute-start(bf16[6,3584]{1,0:T(8,128)(2,1)S(1)} %get-tuple-element.166), channel_id=1, source_target_pairs={{0,24},{4,28},{8,0},{12,4},{16,8},{20,12},{24,16},{28,20},{1,25},{... | collective-permute-start | bytes 129032 | tf_op jit(solution)/shard_map/ppermute | solution.py:29
  145.4 1.2 collective-permute-start.41
  146.7 1.6 %collective-permute-start.42 = (f32[4,896]{1,0:T(4,128)S(1)}, f32[4,896]{1,0:T(4,128)S(1)}, u32[]{:S(2)}, u32[]{:S(2)}) collective-permute-start(f32[4,896]{1,0:T(4,128)S(1)} %get-tuple-element.172), channel_id=1, source_target_pairs={{0,2},{1,3},{2,0},{3,1},{4,6},{5,7},{6,4},{7,5},{8,10},{9,11},{10,... | collective-permute-start | bytes 43016 | tf_op jit(solution)/shard_map/ppermute | solution.py:53
  148.2 1.6 %collective-permute-start.43 = (f32[4,896]{1,0:T(4,128)S(1)}, f32[4,896]{1,0:T(4,128)S(1)}, u32[]{:S(2)}, u32[]{:S(2)}) collective-permute-start(f32[4,896]{1,0:T(4,128)S(1)} %get-tuple-element.173), channel_id=1, source_target_pairs={{0,3},{1,2},{2,1},{3,0},{4,7},{5,6},{6,5},{7,4},{8,11},{9,10},{10,... | collective-permute-start | bytes 43016 | tf_op jit(solution)/shard_map/ppermute | solution.py:53
  149.8 2.9 %finish.1 = (bf16[128,7168]{1,0:T(8,128)(2,1)}, f32[8,128]{1,0:T(8,128)S(1)}) custom-call(s32[2]{0:T(128)} %pad_add_fusion.refs_0_, s32[1,1,2,6]{3,2,1,0:T(2,128)} %copy-done.5, bf16[128,7168]{1,0:T(8,128)(2,1)S(1)} %collective-permute-done.28.refs_2_, bf16[6,7168]{1,0:T(8,128)(2,1)S(1)} %get-tuple-element.133.refs_3_, ...), custom_call_target="tpu_custom_call" | custom-call | bytes 3933696 | tf_op jit(solution)/shard_map/finish/pallas_call | solution.py:239
  152.7 1.0 collective-permute-done.43.refs_3_
  (62 shorter events, 6.5 us)
Async XLA Ops:
  0.6 4.3 %collective-permute-start = (s32[1,1,2,6]{3,2,1,0:T(2,128)}, s32[1,1,2,6]{3,2,1,0:T(2,128)S(1)}, u32[]{:S(2)}, u32[]{:S(2)}) collective-permute-start(s32[1,1,2,6]{3,2,1,0:T(2,128)} %refs_1_.7), channel_id=1, source_target_pairs={{0,24},{8,0},{16,8},{24,16},{1,25},{9,1},{17,9},{25,17},{2,26},{10... | collective-permute-start | bytes 152 | tf_op jit(solution)/shard_map/ppermute | solution.py:19
  5.0 4.0 %copy-start.5 = (s32[1,1,2,6]{3,2,1,0:T(2,128)}, s32[1,1,2,6]{3,2,1,0:T(2,128)S(1)}, u32[]{:S(2)}) copy-start(s32[1,1,2,6]{3,2,1,0:T(2,128)S(1)} %collective-permute-done.refs_6_.refs_1_) | copy-start | bytes 148
  5.0 5.6 %copy-start.3 = (bf16[1,1,128,7168]{3,2,1,0:T(8,128)(2,1)S(1)}, bf16[1,1,128,7168]{3,2,1,0:T(8,128)(2,1)}, u32[]{:S(2)}) copy-start(bf16[1,1,128,7168]{3,2,1,0:T(8,128)(2,1)} %param.8) | copy-start | bytes 5505028
  9.0 8.5 %copy-start.2 = (f32[2,2,7168]{2,1,0:T(2,128)S(1)}, f32[2,2,7168]{2,1,0:T(2,128)}, u32[]{:S(2)}) copy-start(f32[2,2,7168]{2,1,0:T(2,128)} %refs_9_.1) | copy-start | bytes 344068
  9.0 22.0 %copy-start = (bf16[1,1,128,7168]{3,2,1,0:T(8,128)(2,1)S(1)}, bf16[1,1,128,7168]{3,2,1,0:T(8,128)(2,1)}, u32[]{:S(2)}) copy-start(bf16[1,1,128,7168]{3,2,1,0:T(8,128)(2,1)} %param.9) | copy-start | bytes 5505028
  9.0 8.5 %collective-permute-start.3 = (bf16[22,3712]{1,0:T(8,128)(2,1)S(1)}, bf16[22,3712]{1,0:T(8,128)(2,1)S(1)}, u32[]{:S(2)}, u32[]{:S(2)}) collective-permute-start(bf16[22,3712]{1,0:T(8,128)(2,1)S(1)} %get-tuple-element.92), channel_id=1, source_target_pairs={{0,4},{4,0},{1,5},{5,1},{2,6},{6,2},{3,7},{7,3},{8,12},{12,8},{9,1... | collective-permute-start | bytes 489992 | tf_op jit(solution)/shard_map/ppermute | solution.py:19
  11.9 5.6 %collective-permute-start.1 = (bf16[6,10880]{1,0:T(8,128)(2,1)S(1)}, bf16[6,10880]{1,0:T(8,128)(2,1)S(1)}, u32[]{:S(2)}, u32[]{:S(2)}) collective-permute-start(bf16[6,10880]{1,0:T(8,128)(2,1)S(1)} %get-tuple-element.90), channel_id=1, source_target_pairs={{0,8},{4,12},{8,16},{12,20},{16,24},{20,28},{24,0},{28,4},{1,9},{5... | collective-permute-start | bytes 391688 | tf_op jit(solution)/shard_map/ppermute | solution.py:29
  11.9 5.6 %collective-permute-start.2 = (bf16[6,3712]{1,0:T(8,128)(2,1)S(1)}, bf16[6,3712]{1,0:T(8,128)(2,1)S(1)}, u32[]{:S(2)}, u32[]{:S(2)}) collective-permute-start(bf16[6,3712]{1,0:T(8,128)(2,1)S(1)} %get-tuple-element.91), channel_id=1, source_target_pairs={{0,12},{4,8},{8,20},{12,16},{16,28},{20,24},{24,4},{28,0},{1,13},{... | collective-permute-start | bytes 133640 | tf_op jit(solution)/shard_map/ppermute | solution.py:29
  18.6 46.1 %collective-permute-start.4 = (bf16[128,7168]{1,0:T(8,128)(2,1)S(1)}, bf16[128,7168]{1,0:T(8,128)(2,1)S(1)}, u32[]{:S(2)}, u32[]{:S(2)}) collective-permute-start(bf16[128,7168]{1,0:T(8,128)(2,1)S(1)} %bitcast.15), channel_id=1, source_target_pairs={{0,8},{8,16},{16,24},{24,0},{1,9},{9,17},{17,25},{25,1},{2,10},{10... | collective-permute-start | bytes 5505032 | tf_op jit(solution)/shard_map/ppermute | solution.py:19
  18.7 5.5 %collective-permute-start.8 = (bf16[48,1024]{1,0:T(8,128)(2,1)S(1)}, bf16[48,1024]{1,0:T(8,128)(2,1)S(1)}, u32[]{:S(2)}, u32[]{:S(2)}) collective-permute-start(bf16[48,1024]{1,0:T(8,128)(2,1)S(1)} %get-tuple-element.96.refs_7_), channel_id=1, source_target_pairs={{1,0},{0,1},{3,2},{2,3},{5,4},{4,5},{7,6},{6,7},{9,8},{8,9},{11,10... | collective-permute-start | bytes 294920 | tf_op jit(solution)/shard_map/ppermute | solution.py:45
  20.3 10.7 %collective-permute-start.9 = (bf16[48,1024]{1,0:T(8,128)(2,1)S(1)}, bf16[48,1024]{1,0:T(8,128)(2,1)S(1)}, u32[]{:S(2)}, u32[]{:S(2)}) collective-permute-start(bf16[48,1024]{1,0:T(8,128)(2,1)S(1)} %get-tuple-element.96.refs_7_), channel_id=1, source_target_pairs={{2,0},{3,1},{0,2},{1,3},{6,4},{7,5},{4,6},{5,7},{10,8},{11,9},{8,1... | collective-permute-start | bytes 294920 | tf_op jit(solution)/shard_map/ppermute | solution.py:45
  22.9 8.1 %collective-permute-start.10 = (bf16[48,1024]{1,0:T(8,128)(2,1)S(1)}, bf16[48,1024]{1,0:T(8,128)(2,1)S(1)}, u32[]{:S(2)}, u32[]{:S(2)}) collective-permute-start(bf16[48,1024]{1,0:T(8,128)(2,1)S(1)} %get-tuple-element.96.refs_7_), channel_id=1, source_target_pairs={{3,0},{2,1},{1,2},{0,3},{7,4},{6,5},{5,6},{4,7},{11,8},{10,9},{9,1... | collective-permute-start | bytes 294920 | tf_op jit(solution)/shard_map/ppermute | solution.py:45
  32.8 17.2 %collective-permute-start.12 = (bf16[120,1024]{1,0:T(8,128)(2,1)S(1)}, bf16[120,1024]{1,0:T(8,128)(2,1)S(1)}, u32[]{:S(2)}, u32[]{:S(2)}) collective-permute-start(bf16[120,1024]{1,0:T(8,128)(2,1)S(1)} %get-tuple-element.101), channel_id=1, source_target_pairs={{0,4},{4,0},{1,5},{5,1},{2,6},{6,2},{3,7},{7,3},{8,12},{12,8},{9,1... | collective-permute-start | bytes 737288 | tf_op jit(solution)/shard_map/ppermute | solution.py:19
  34.2 5.1 %collective-permute-start.5 = (bf16[48,896]{1,0:T(8,128)(2,1)S(1)}, bf16[48,896]{1,0:T(8,128)(2,1)S(1)}, u32[]{:S(2)}, u32[]{:S(2)}) collective-permute-start(bf16[48,896]{1,0:T(8,128)(2,1)S(1)} %get-tuple-element.93.refs_11_.refs_0_.refs_1_.refs_3_), channel_id=1, source_target_pairs={{1,0},{0,1},{3,2},{2,3},{5,4},{4,5},{7,6},{6,7},{9,8},{8,9},{11,10... | collective-permute-start | bytes 258056 | tf_op jit(solution)/shard_map/ppermute | solution.py:45
  36.4 9.0 %collective-permute-start.6 = (bf16[48,896]{1,0:T(8,128)(2,1)S(1)}, bf16[48,896]{1,0:T(8,128)(2,1)S(1)}, u32[]{:S(2)}, u32[]{:S(2)}) collective-permute-start(bf16[48,896]{1,0:T(8,128)(2,1)S(1)} %get-tuple-element.93.refs_11_.refs_0_.refs_1_.refs_3_), channel_id=1, source_target_pairs={{2,0},{3,1},{0,2},{1,3},{6,4},{7,5},{4,6},{5,7},{10,8},{11,9},{8,1... | collective-permute-start | bytes 258056 | tf_op jit(solution)/shard_map/ppermute | solution.py:45
  37.5 8.0 %collective-permute-start.7 = (bf16[48,896]{1,0:T(8,128)(2,1)S(1)}, bf16[48,896]{1,0:T(8,128)(2,1)S(1)}, u32[]{:S(2)}, u32[]{:S(2)}) collective-permute-start(bf16[48,896]{1,0:T(8,128)(2,1)S(1)} %get-tuple-element.93.refs_11_.refs_0_.refs_1_.refs_3_), channel_id=1, source_target_pairs={{3,0},{2,1},{1,2},{0,3},{7,4},{6,5},{5,6},{4,7},{11,8},{10,9},{9,1... | collective-permute-start | bytes 258056 | tf_op jit(solution)/shard_map/ppermute | solution.py:45
  49.2 4.7 %collective-permute-start.11 = (bf16[48,1024]{1,0:T(8,128)(2,1)S(1)}, bf16[48,1024]{1,0:T(8,128)(2,1)S(1)}, u32[]{:S(2)}, u32[]{:S(2)}) collective-permute-start(bf16[48,1024]{1,0:T(8,128)(2,1)S(1)} %get-tuple-element.99.refs_3_), channel_id=1, source_target_pairs={{0,4},{4,0},{1,5},{5,1},{2,6},{6,2},{3,7},{7,3},{8,12},{12,8},{9,1... | collective-permute-start | bytes 294920 | tf_op jit(solution)/shard_map/ppermute | solution.py:19
  53.9 12.7 %copy-start.1 = (bf16[1,1,128,7168]{3,2,1,0:T(8,128)(2,1)S(1)}, bf16[1,1,128,7168]{3,2,1,0:T(8,128)(2,1)}, u32[]{:S(2)}) copy-start(bf16[1,1,128,7168]{3,2,1,0:T(8,128)(2,1)} %param.10) | copy-start | bytes 5505028
  57.0 6.6 %collective-permute-start.13 = (bf16[48,896]{1,0:T(8,128)(2,1)S(1)}, bf16[48,896]{1,0:T(8,128)(2,1)S(1)}, u32[]{:S(2)}, u32[]{:S(2)}) collective-permute-start(bf16[48,896]{1,0:T(8,128)(2,1)S(1)} %get-tuple-element.107), channel_id=1, source_target_pairs={{0,1},{1,0},{2,3},{3,2},{4,5},{5,4},{6,7},{7,6},{8,9},{9,8},{10,11... | collective-permute-start | bytes 258056 | tf_op jit(solution)/shard_map/ppermute | solution.py:53
  58.5 13.9 %collective-permute-start.14 = (bf16[48,896]{1,0:T(8,128)(2,1)S(1)}, bf16[48,896]{1,0:T(8,128)(2,1)S(1)}, u32[]{:S(2)}, u32[]{:S(2)}) collective-permute-start(bf16[48,896]{1,0:T(8,128)(2,1)S(1)} %get-tuple-element.108), channel_id=1, source_target_pairs={{0,2},{1,3},{2,0},{3,1},{4,6},{5,7},{6,4},{7,5},{8,10},{9,11},{10,... | collective-permute-start | bytes 258056 | tf_op jit(solution)/shard_map/ppermute | solution.py:53
  59.8 12.6 %collective-permute-start.15 = (bf16[48,896]{1,0:T(8,128)(2,1)S(1)}, bf16[48,896]{1,0:T(8,128)(2,1)S(1)}, u32[]{:S(2)}, u32[]{:S(2)}) collective-permute-start(bf16[48,896]{1,0:T(8,128)(2,1)S(1)} %get-tuple-element.109), channel_id=1, source_target_pairs={{0,3},{1,2},{2,1},{3,0},{4,7},{5,6},{6,5},{7,4},{8,11},{9,10},{10,... | collective-permute-start | bytes 258056 | tf_op jit(solution)/shard_map/ppermute | solution.py:53
  61.4 13.7 %collective-permute-start.19 = (bf16[48,896]{1,0:T(8,128)(2,1)S(1)}, bf16[48,896]{1,0:T(8,128)(2,1)S(1)}, u32[]{:S(2)}, u32[]{:S(2)}) collective-permute-start(bf16[48,896]{1,0:T(8,128)(2,1)S(1)} %get-tuple-element.102.refs_3_.refs_0_.refs_2_), channel_id=1, source_target_pairs={{1,0},{0,1},{3,2},{2,3},{5,4},{4,5},{7,6},{6,7},{9,8},{8,9},{11,10... | collective-permute-start | bytes 258056 | tf_op jit(solution)/shard_map/ppermute | solution.py:45
  63.5 13.6 %collective-permute-start.20 = (bf16[48,896]{1,0:T(8,128)(2,1)S(1)}, bf16[48,896]{1,0:T(8,128)(2,1)S(1)}, u32[]{:S(2)}, u32[]{:S(2)}) collective-permute-start(bf16[48,896]{1,0:T(8,128)(2,1)S(1)} %get-tuple-element.102.refs_3_.refs_0_.refs_2_), channel_id=1, source_target_pairs={{2,0},{3,1},{0,2},{1,3},{6,4},{7,5},{4,6},{5,7},{10,8},{11,9},{8,1... | collective-permute-start | bytes 258056 | tf_op jit(solution)/shard_map/ppermute | solution.py:45
  64.7 12.5 %collective-permute-start.21 = (bf16[48,896]{1,0:T(8,128)(2,1)S(1)}, bf16[48,896]{1,0:T(8,128)(2,1)S(1)}, u32[]{:S(2)}, u32[]{:S(2)}) collective-permute-start(bf16[48,896]{1,0:T(8,128)(2,1)S(1)} %get-tuple-element.102.refs_3_.refs_0_.refs_2_), channel_id=1, source_target_pairs={{3,0},{2,1},{1,2},{0,3},{7,4},{6,5},{5,6},{4,7},{11,8},{10,9},{9,1... | collective-permute-start | bytes 258056 | tf_op jit(solution)/shard_map/ppermute | solution.py:45
  72.6 10.4 %collective-permute-start.16 = (bf16[48,896]{1,0:T(8,128)(2,1)S(1)}, bf16[48,896]{1,0:T(8,128)(2,1)S(1)}, u32[]{:S(2)}, u32[]{:S(2)}) collective-permute-start(bf16[48,896]{1,0:T(8,128)(2,1)S(1)} %get-tuple-element.110.refs_4_.refs_1_.refs_0_.refs_5_.refs_11_), channel_id=1, source_target_pairs={{1,0},{0,1},{3,2},{2,3},{5,4},{4,5},{7,6},{6,7},{9,8},{8,9},{11,10... | collective-permute-start | bytes 258056 | tf_op jit(solution)/shard_map/ppermute | solution.py:45
  73.2 9.8 %collective-permute-start.17 = (bf16[48,896]{1,0:T(8,128)(2,1)S(1)}, bf16[48,896]{1,0:T(8,128)(2,1)S(1)}, u32[]{:S(2)}, u32[]{:S(2)}) collective-permute-start(bf16[48,896]{1,0:T(8,128)(2,1)S(1)} %get-tuple-element.110.refs_4_.refs_1_.refs_0_.refs_5_.refs_11_), channel_id=1, source_target_pairs={{2,0},{3,1},{0,2},{1,3},{6,4},{7,5},{4,6},{5,7},{10,8},{11,9},{8,1... | collective-permute-start | bytes 258056 | tf_op jit(solution)/shard_map/ppermute | solution.py:45
  75.1 7.9 %collective-permute-start.18 = (bf16[48,896]{1,0:T(8,128)(2,1)S(1)}, bf16[48,896]{1,0:T(8,128)(2,1)S(1)}, u32[]{:S(2)}, u32[]{:S(2)}) collective-permute-start(bf16[48,896]{1,0:T(8,128)(2,1)S(1)} %get-tuple-element.110.refs_4_.refs_1_.refs_0_.refs_5_.refs_11_), channel_id=1, source_target_pairs={{3,0},{2,1},{1,2},{0,3},{7,4},{6,5},{5,6},{4,7},{11,8},{10,9},{9,1... | collective-permute-start | bytes 258056 | tf_op jit(solution)/shard_map/ppermute | solution.py:45
  77.2 5.8 %copy-start.4 = (s32[2]{0:T(128)S(1)}, s32[2]{0:T(128)}, u32[]{:S(2)}) copy-start(s32[2]{0:T(128)} %pad_add_fusion.refs_0_) | copy-start | bytes 28
  82.4 8.8 %collective-permute-start.23 = (bf16[48,1536]{1,0:T(8,128)(2,1)S(1)}, bf16[48,1536]{1,0:T(8,128)(2,1)S(1)}, u32[]{:S(2)}, u32[]{:S(2)}) collective-permute-start(bf16[48,1536]{1,0:T(8,128)(2,1)S(1)} %get-tuple-element.120), channel_id=1, source_target_pairs={{0,4},{4,0},{1,5},{5,1},{2,6},{6,2},{3,7},{7,3},{8,12},{12,8},{9,1... | collective-permute-start | bytes 442376 | tf_op jit(solution)/shard_map/ppermute | solution.py:19
  87.3 4.8 %collective-permute-start.22 = (bf16[48,1152]{1,0:T(8,128)(2,1)S(1)}, bf16[48,1152]{1,0:T(8,128)(2,1)S(1)}, u32[]{:S(2)}, u32[]{:S(2)}) collective-permute-start(bf16[48,1152]{1,0:T(8,128)(2,1)S(1)} %get-tuple-element.119.refs_5_), channel_id=1, source_target_pairs={{0,4},{4,0},{1,5},{5,1},{2,6},{6,2},{3,7},{7,3},{8,12},{12,8},{9,1... | collective-permute-start | bytes 331784 | tf_op jit(solution)/shard_map/ppermute | solution.py:19
  96.7 11.7 %collective-permute-start.24 = (bf16[48,896]{1,0:T(8,128)(2,1)S(1)}, bf16[48,896]{1,0:T(8,128)(2,1)S(1)}, u32[]{:S(2)}, u32[]{:S(2)}) collective-permute-start(bf16[48,896]{1,0:T(8,128)(2,1)S(1)} %get-tuple-element.126), channel_id=1, source_target_pairs={{0,1},{1,0},{2,3},{3,2},{4,5},{5,4},{6,7},{7,6},{8,9},{9,8},{10,11... | collective-permute-start | bytes 258056 | tf_op jit(solution)/shard_map/ppermute | solution.py:53
  98.1 10.3 %collective-permute-start.25 = (bf16[48,896]{1,0:T(8,128)(2,1)S(1)}, bf16[48,896]{1,0:T(8,128)(2,1)S(1)}, u32[]{:S(2)}, u32[]{:S(2)}) collective-permute-start(bf16[48,896]{1,0:T(8,128)(2,1)S(1)} %get-tuple-element.127), channel_id=1, source_target_pairs={{0,2},{1,3},{2,0},{3,1},{4,6},{5,7},{6,4},{7,5},{8,10},{9,11},{10,... | collective-permute-start | bytes 258056 | tf_op jit(solution)/shard_map/ppermute | solution.py:53
  99.4 9.0 %collective-permute-start.26 = (bf16[48,896]{1,0:T(8,128)(2,1)S(1)}, bf16[48,896]{1,0:T(8,128)(2,1)S(1)}, u32[]{:S(2)}, u32[]{:S(2)}) collective-permute-start(bf16[48,896]{1,0:T(8,128)(2,1)S(1)} %get-tuple-element.128), channel_id=1, source_target_pairs={{0,3},{1,2},{2,1},{3,0},{4,7},{5,6},{6,5},{7,4},{8,11},{9,10},{10,... | collective-permute-start | bytes 258056 | tf_op jit(solution)/shard_map/ppermute | solution.py:53
  101.2 7.2 %collective-permute-start.27 = (bf16[48,512]{1,0:T(8,128)(2,1)S(1)}, bf16[48,512]{1,0:T(8,128)(2,1)S(1)}, u32[]{:S(2)}, u32[]{:S(2)}) collective-permute-start(bf16[48,512]{1,0:T(8,128)(2,1)S(1)} %get-tuple-element.130), channel_id=1, source_target_pairs={{0,4},{4,0},{1,5},{5,1},{2,6},{6,2},{3,7},{7,3},{8,12},{12,8},{9,1... | collective-permute-start | bytes 147464 | tf_op jit(solution)/shard_map/ppermute | solution.py:19
  109.6 40.3 %collective-permute-start.28 = (bf16[128,7168]{1,0:T(8,128)(2,1)S(1)}, bf16[128,7168]{1,0:T(8,128)(2,1)S(1)}, u32[]{:S(2)}, u32[]{:S(2)}) collective-permute-start(bf16[128,7168]{1,0:T(8,128)(2,1)S(1)} %get-tuple-element.132), channel_id=1, source_target_pairs={{0,24},{8,0},{16,8},{24,16},{1,25},{9,1},{17,9},{25,17},{2,26},{10... | collective-permute-start | bytes 5505032 | tf_op jit(solution)/shard_map/ppermute | solution.py:19
  109.9 4.9 %collective-permute-start.29 = (bf16[6,3584]{1,0:T(8,128)(2,1)S(1)}, bf16[6,3584]{1,0:T(8,128)(2,1)S(1)}, u32[]{:S(2)}, u32[]{:S(2)}) collective-permute-start(bf16[6,3584]{1,0:T(8,128)(2,1)S(1)} %get-tuple-element.136), channel_id=1, source_target_pairs={{0,4},{4,0},{1,5},{5,1},{2,6},{6,2},{3,7},{7,3},{8,12},{12,8},{9,1... | collective-permute-start | bytes 129032 | tf_op jit(solution)/shard_map/ppermute | solution.py:19
  110.4 9.1 %collective-permute-start.30 = (bf16[48,896]{1,0:T(8,128)(2,1)S(1)}, bf16[48,896]{1,0:T(8,128)(2,1)S(1)}, u32[]{:S(2)}, u32[]{:S(2)}) collective-permute-start(bf16[48,896]{1,0:T(8,128)(2,1)S(1)} %get-tuple-element.131.refs_13_.refs_0_.refs_7_), channel_id=1, source_target_pairs={{1,0},{0,1},{3,2},{2,3},{5,4},{4,5},{7,6},{6,7},{9,8},{8,9},{11,10... | collective-permute-start | bytes 258056 | tf_op jit(solution)/shard_map/ppermute | solution.py:45
  110.8 10.0 %collective-permute-start.31 = (bf16[48,896]{1,0:T(8,128)(2,1)S(1)}, bf16[48,896]{1,0:T(8,128)(2,1)S(1)}, u32[]{:S(2)}, u32[]{:S(2)}) collective-permute-start(bf16[48,896]{1,0:T(8,128)(2,1)S(1)} %get-tuple-element.131.refs_13_.refs_0_.refs_7_), channel_id=1, source_target_pairs={{2,0},{3,1},{0,2},{1,3},{6,4},{7,5},{4,6},{5,7},{10,8},{11,9},{8,1... | collective-permute-start | bytes 258056 | tf_op jit(solution)/shard_map/ppermute | solution.py:45
  113.0 7.7 %collective-permute-start.32 = (bf16[48,896]{1,0:T(8,128)(2,1)S(1)}, bf16[48,896]{1,0:T(8,128)(2,1)S(1)}, u32[]{:S(2)}, u32[]{:S(2)}) collective-permute-start(bf16[48,896]{1,0:T(8,128)(2,1)S(1)} %get-tuple-element.131.refs_13_.refs_0_.refs_7_), channel_id=1, source_target_pairs={{3,0},{2,1},{1,2},{0,3},{7,4},{6,5},{5,6},{4,7},{11,8},{10,9},{9,1... | collective-permute-start | bytes 258056 | tf_op jit(solution)/shard_map/ppermute | solution.py:45
  123.2 4.8 %collective-permute-start.34 = (bf16[48,640]{1,0:T(8,128)(2,1)S(1)}, bf16[48,640]{1,0:T(8,128)(2,1)S(1)}, u32[]{:S(2)}, u32[]{:S(2)}) collective-permute-start(bf16[48,640]{1,0:T(8,128)(2,1)S(1)} %get-tuple-element.143.refs_11_), channel_id=1, source_target_pairs={{0,4},{4,0},{1,5},{5,1},{2,6},{6,2},{3,7},{7,3},{8,12},{12,8},{9,1... | collective-permute-start | bytes 184328 | tf_op jit(solution)/shard_map/ppermute | solution.py:19
  126.3 10.8 %collective-permute-start.38 = (f32[4,3584]{1,0:T(4,128)S(1)}, f32[4,3584]{1,0:T(4,128)S(1)}, u32[]{:S(2)}, u32[]{:S(2)}) collective-permute-start(f32[4,3584]{1,0:T(4,128)S(1)} %get-tuple-element.160), channel_id=1, source_target_pairs={{0,4},{4,0},{1,5},{5,1},{2,6},{6,2},{3,7},{7,3},{8,12},{12,8},{9,1... | collective-permute-start | bytes 172040 | tf_op jit(solution)/shard_map/ppermute | solution.py:19
  132.7 9.1 %collective-permute-start.35 = (bf16[48,896]{1,0:T(8,128)(2,1)S(1)}, bf16[48,896]{1,0:T(8,128)(2,1)S(1)}, u32[]{:S(2)}, u32[]{:S(2)}) collective-permute-start(bf16[48,896]{1,0:T(8,128)(2,1)S(1)} %get-tuple-element.157), channel_id=1, source_target_pairs={{0,1},{1,0},{2,3},{3,2},{4,5},{5,4},{6,7},{7,6},{8,9},{9,8},{10,11... | collective-permute-start | bytes 258056 | tf_op jit(solution)/shard_map/ppermute | solution.py:53
  133.7 8.1 %collective-permute-start.36 = (bf16[48,896]{1,0:T(8,128)(2,1)S(1)}, bf16[48,896]{1,0:T(8,128)(2,1)S(1)}, u32[]{:S(2)}, u32[]{:S(2)}) collective-permute-start(bf16[48,896]{1,0:T(8,128)(2,1)S(1)} %get-tuple-element.158), channel_id=1, source_target_pairs={{0,2},{1,3},{2,0},{3,1},{4,6},{5,7},{6,4},{7,5},{8,10},{9,11},{10,... | collective-permute-start | bytes 258056 | tf_op jit(solution)/shard_map/ppermute | solution.py:53
  135.5 6.4 %collective-permute-start.37 = (bf16[48,896]{1,0:T(8,128)(2,1)S(1)}, bf16[48,896]{1,0:T(8,128)(2,1)S(1)}, u32[]{:S(2)}, u32[]{:S(2)}) collective-permute-start(bf16[48,896]{1,0:T(8,128)(2,1)S(1)} %get-tuple-element.159), channel_id=1, source_target_pairs={{0,3},{1,2},{2,1},{3,0},{4,7},{5,6},{6,5},{7,4},{8,11},{9,10},{10,... | collective-permute-start | bytes 258056 | tf_op jit(solution)/shard_map/ppermute | solution.py:53
  137.1 9.6 %collective-permute-start.33 = (bf16[6,7296]{1,0:T(8,128)(2,1)S(1)}, bf16[6,7296]{1,0:T(8,128)(2,1)S(1)}, u32[]{:S(2)}, u32[]{:S(2)}) collective-permute-start(bf16[6,7296]{1,0:T(8,128)(2,1)S(1)} %get-tuple-element.144), channel_id=1, source_target_pairs={{0,24},{8,0},{16,8},{24,16},{1,25},{9,1},{17,9},{25,17},{2,26},{10... | collective-permute-start | bytes 262664 | tf_op jit(solution)/shard_map/ppermute | solution.py:19
  143.0 5.2 %collective-permute-start.39 = (bf16[6,3584]{1,0:T(8,128)(2,1)S(1)}, bf16[6,3584]{1,0:T(8,128)(2,1)S(1)}, u32[]{:S(2)}, u32[]{:S(2)}) collective-permute-start(bf16[6,3584]{1,0:T(8,128)(2,1)S(1)} %get-tuple-element.166), channel_id=1, source_target_pairs={{0,24},{4,28},{8,0},{12,4},{16,8},{20,12},{24,16},{28,20},{1,25},{... | collective-permute-start | bytes 129032 | tf_op jit(solution)/shard_map/ppermute | solution.py:29
  144.8 5.0 %collective-permute-start.40 = (bf16[6,3584]{1,0:T(8,128)(2,1)S(1)}, bf16[6,3584]{1,0:T(8,128)(2,1)S(1)}, u32[]{:S(2)}, u32[]{:S(2)}) collective-permute-start(bf16[6,3584]{1,0:T(8,128)(2,1)S(1)} %get-tuple-element.167), channel_id=1, source_target_pairs={{0,28},{4,24},{8,4},{12,0},{16,12},{20,8},{24,20},{28,16},{1,29},{... | collective-permute-start | bytes 129032 | tf_op jit(solution)/shard_map/ppermute | solution.py:29
  145.4 7.3 %collective-permute-start.41 = (f32[4,896]{1,0:T(4,128)S(1)}, f32[4,896]{1,0:T(4,128)S(1)}, u32[]{:S(2)}, u32[]{:S(2)}) collective-permute-start(f32[4,896]{1,0:T(4,128)S(1)} %get-tuple-element.171), channel_id=1, source_target_pairs={{0,1},{1,0},{2,3},{3,2},{4,5},{5,4},{6,7},{7,6},{8,9},{9,8},{10,11... | collective-permute-start | bytes 43016 | tf_op jit(solution)/shard_map/ppermute | solution.py:53
  146.7 6.1 %collective-permute-start.42 = (f32[4,896]{1,0:T(4,128)S(1)}, f32[4,896]{1,0:T(4,128)S(1)}, u32[]{:S(2)}, u32[]{:S(2)}) collective-permute-start(f32[4,896]{1,0:T(4,128)S(1)} %get-tuple-element.172), channel_id=1, source_target_pairs={{0,2},{1,3},{2,0},{3,1},{4,6},{5,7},{6,4},{7,5},{8,10},{9,11},{10,... | collective-permute-start | bytes 43016 | tf_op jit(solution)/shard_map/ppermute | solution.py:53
  148.2 5.5 %collective-permute-start.43 = (f32[4,896]{1,0:T(4,128)S(1)}, f32[4,896]{1,0:T(4,128)S(1)}, u32[]{:S(2)}, u32[]{:S(2)}) collective-permute-start(f32[4,896]{1,0:T(4,128)S(1)} %get-tuple-element.173), channel_id=1, source_target_pairs={{0,3},{1,2},{2,1},{3,0},{4,7},{5,6},{6,5},{7,4},{8,11},{9,10},{10,... | collective-permute-start | bytes 43016 | tf_op jit(solution)/shard_map/ppermute | solution.py:53

commit v2 on v1

--- a/solution.py
+++ b/solution.py
@@ -248,25 +248,21 @@
     )(*[in_hbm(a) for a in small], *args, *[in_hbm(a) for a in far], *after)
 
 
-def fetch(weight_ref, depth, kinds, buffer, sems, parts, ahead=4):
+def fetch(weight_ref, depth, kinds, buffer, sems, parts):
     step = weight_ref.shape[2] // parts
     copies = [
-        pltpu.make_async_copy(
-            weight_ref.at[depth, kind, pl.ds(g * step, step)], buffer.at[g, k], sems.at[g, k]
-        )
+        [
+            pltpu.make_async_copy(
+                weight_ref.at[depth, kind, pl.ds(g * step, step)], buffer.at[g, k], sems.at[g, k]
+            )
+            for k, kind in enumerate(kinds)
+        ]
         for g in range(parts)
-        for k, kind in enumerate(kinds)
     ]
-    for copy in copies[:ahead]:
-        copy.start()
-
-    def wait(g, k):
-        at = g * len(kinds) + k
-        copies[at].wait()
-        if at + ahead < len(copies):
-            copies[at + ahead].start()
-
-    return wait
+    for row in copies:
+        for copy in row:
+            copy.start()
+    return copies
 
 
 def fetched(weight, kinds, parts):
@@ -301,7 +297,7 @@
         own_ref, send_ref = refs.pop(0), refs.pop(0)
         kept_ref = refs.pop(0) if select is not None else None
         buffer, sems = refs
-        wait = fetch(w_ref, depth, kinds, buffer, sems, parts)
+        copies = fetch(w_ref, depth, kinds, buffer, sems, parts)
         x_all = [r[...] for r in x_refs]
         mate_all = [r[...] for r in mate_refs] if mates is not None else x_all
         if select is not None:
@@ -320,7 +316,7 @@
             for k in range(len(kinds)):
                 if k == len(first_kinds):
                     x = column_part([r[...] for r in other_refs], rows, g)[:, :step]
-                wait(g, k)
+                copies[g][k].wait()
                 sums[k] += jnp.dot(x, buffer[g, k], preferred_element_type=f32)
         for k in range(len(kinds)):
             own_ref[:, k * hidden : (k + 1) * hidden] = sums[k]
@@ -365,14 +361,14 @@
         in_refs, w_ref = refs[:count], refs[count]
         refs = refs[count + 1 + len(after) :]
         saved_refs, out_refs, (buffer, sems) = refs[:kept], refs[kept:-2], refs[-2:]
-        wait = fetch(w_ref, depth, kinds, buffer, sems, parts)
+        copies = fetch(w_ref, depth, kinds, buffer, sems, parts)
         for ref, value in zip(saved_refs, prepare(*[r[...] for r in in_refs])):
             ref[...] = value.astype(ref.dtype)
         out = []
         for g in range(parts):
             part = jnp.zeros((total, step), f32)
             for k in range(len(kinds)):
-                wait(g, k)
+                copies[g][k].wait()
                 part += lax.dot_general(
                     saved_refs[k][...], buffer[g, k], (((1,), (1,)), ((), ())),
                     preferred_element_type=f32,
@@ -656,10 +652,12 @@
         (where, asked_token), source, after=(own_sent[0],),
     )
     start_got = trade_seq(sent, 1)
-    dout_2_sent = gather_dp(dout_2)
+    dout_2, _ = lax.optimization_barrier((dout_2, sent[0]))
+    dout_2_got = gather_dp(dout_2)
 
     def first_mixed(where, gain, *got):
-        start_got, got = got[:seqs], [g.astype(f32) for g in got[seqs:]]
+        start_got, dout = got[:seqs], [g.astype(f32) for g in got[2 * seqs :]]
+        got = [g.astype(f32) for g in got[seqs : 2 * seqs]]
         first = 3 * slots
         block_1, block_2, block_3 = (
             in_order([g[k * slots : (k + 1) * slots] for g in got], where[0], 0) for k in range(3)
@@ -691,16 +689,19 @@
         unit = start[:, :width] * decoded(start[:, width:])
         gain_h, gain_e = (piece_of(gain[0, k : k + 1], where[0], seqs, 0) for k in range(2))
         mixed = (unit * gain_h + units[0] * gain_e).astype(bf16).astype(f32)
-        return payload(mixed * facts[:, 2:3]), unit, *units, block_3[:, :width], facts, follow
-
-    rows_1, unit_1, unit_e1, unit_e2, cot_1, own_facts, next_rows = call(
+        douts = zip(*(blocks_of(block, where[0], seqs) for block in dout))
+        douts = [jnp.concatenate(blocks, 0) for blocks in douts]
+        return payload(mixed * facts[:, 2:3]), unit, *units, block_3[:, :width], facts, follow, *douts
+
+    rows_1, unit_1, unit_e1, unit_e2, cot_1, own_facts, next_rows, *dout_2_sent = call(
         "first_mixed", first_mixed,
-        [packed] + [part_rows] * 4 + [((rows, lanes), f32), ((16, features), bf16)],
-        (where,), norm_gain, *start_got, *own_got,
+        [packed] + [part_rows] * 4 + [((rows, lanes), f32), ((16, features), bf16)]
+        + [((groups * slots * parts, fine), bf16)] * seqs,
+        (where,), norm_gain, *start_got, *own_got, *dout_2_got,
     )
     rows_1_all = gather_dp(rows_1)
 
-    def second_base(where, token, count, start, table, after, gain, *dout):
+    def second_base(where, token, count, start, table, after, gain):
         second = token_column(token, 1)
         start = start[:, width + lanes :].astype(f32)
         ahead_1 = pick_ahead(second + 1, table, after)
@@ -710,40 +711,29 @@
         mixed = mixed.astype(bf16).astype(f32)
         own = mixed * inv_rms(mixed) * gain[1, 0:1] * (1.0 - met_column(token, count))
         out = (own + ahead_2 * inv_rms(ahead_2) * gain[1, 1:2]) * live_column(count, 1, slots)
-        none = jnp.zeros((slots * parts, lanes), f32)
-        bases = [
-            jnp.concatenate([folded(piece, parts), none], 1)
-            for piece in pieces_of(out, where[0], seqs)
-        ]
-        douts = zip(*(blocks_of(block.astype(f32), where[0], seqs) for block in dout))
-        return [jnp.concatenate([base, *more], 0) for base, more in zip(bases, douts)] + [ahead_1, ahead_2]
-
-    *fixed_sent, ahead_21, ahead_22 = call(
+        bases = [folded(piece, parts) for piece in pieces_of(out, where[0], seqs)]
+        return bases + [ahead_1, ahead_2]
+
+    *base_sent, ahead_21, ahead_22 = call(
         "second_base", second_base,
-        [((slots * parts * (1 + groups), fine), bf16)] * seqs + [((slots, features), bf16)] * 2,
-        (where, *facts), start_got[0], embed, next_rows, norm_gain, *dout_2_sent, after=(rows_1,),
-    )
-    fixed_got = trade_seq(fixed_sent)
+        [((slots * parts, width // parts), bf16)] * seqs + [((slots, features), bf16)] * 2,
+        (where, *facts), start_got[0], embed, next_rows, norm_gain, after=(rows_1,),
+    )
+    base_got = trade_seq(base_sent)
 
     first_own, first_send = project(
-        "gate_up_1", rows_1_all, expert_weight, 0, (0, 1), parts, after=(ahead_21,)
+        "gate_up_1", rows_1_all, expert_weight, 0, (0, 1), parts, after=(ahead_21, base_got[-1])
     )
     first = pair_seq(first_own, first_send)
 
-    def fixed_order(where, *got):
-        got = [g.astype(f32) for g in got]
-        size = slots * parts
-        out = []
-        for z in range(1 + groups):
-            blocks = [g[z * size : (z + 1) * size] for g in got]
-            blocks = [from_block(blocks, where[0], j) for j in range(seqs)]
-            pairs = [b[g * slots : (g + 1) * slots] for g in range(parts) for b in blocks]
-            out.append(jnp.concatenate(pairs, 0))
-        return [out[0][:, : width // parts]] + out[1:]
-
-    base_2, *dout_2_all = call(
-        "fixed_order", fixed_order, [packed] + [((rows * parts, fine), bf16)] * groups,
-        (where,), *fixed_got, after=(first_send,),
+    def by_slots(got, place):
+        blocks = [from_block(got, place, j) for j in range(seqs)]
+        pairs = [b[g * slots : (g + 1) * slots] for g in range(parts) for b in blocks]
+        return jnp.concatenate(pairs, 0)
+
+    (base_2,) = call(
+        "base_order", lambda where, *got: [by_slots([g.astype(f32) for g in got], where[0])], [packed],
+        (where,), *base_got, after=(first_send,),
     )
     base_2_all = gather_dp(base_2)
 
@@ -776,20 +766,26 @@
     )
     prev_all = gather_dp(prev)
 
-    def slot_facts(*blocks):
-        facts = jnp.concatenate(
-            [block[:rows].astype(f32)[:, width // parts :] for block in blocks], 0
-        )
+    dout_2_sent = lax.optimization_barrier((*dout_2_sent, out_blocks[0]))[:-1]
+    dout_2_traded = trade_seq(dout_2_sent)
+
+    def slot_facts(where, *got):
+        got, size = [g.astype(f32) for g in got], slots * parts
+        blocks = [
+            by_slots([g[z * size : (z + 1) * size] for g in got], where[0]) for z in range(groups)
+        ]
+        facts = jnp.concatenate([block[:rows, width // parts :] for block in blocks], 0)
         base = (iota((total, 1), 0) // slots * tokens).astype(f32)
         first, second = facts[:, 0:1] + base, facts[:, 1:2] + base
         live = (facts[:, 3:4] > 0) & (as_row(facts[:, 2:3]) > 0)
         same = ((second == as_row(first)) & live).astype(f32)
-        return same, same, same[:rows, :rows], decoded(facts, 4)
-
-    same, same_16, same_own, weight_1 = call(
+        return same, same, same[:rows, :rows], decoded(facts, 4), *blocks
+
+    same, same_16, same_own, weight_1, *dout_2_all = call(
         "slot_facts", slot_facts,
-        [((total, total), f32), ((total, total), bf16), ((rows, rows), f32), ((total, 1), f32)],
-        (), *dout_2_all, after=(prev,),
+        [((total, total), f32), ((total, total), bf16), ((rows, rows), f32), ((total, 1), f32)]
+        + [((rows * parts, fine), bf16)] * groups,
+        (where,), *dout_2_traded, after=(prev,),
     )
     fixed_own, fixed_send = project(
         "fixed_2", base_2_all, expert_weight, 1, (0, 1), parts,

time: 155 us -> 153 us (0.987)
  waiting for transfers between devices: 27.9 us -> 18.5 us
  starting transfers between devices: 55.8 us -> 63.5 us
    ppermute x15, waiting for transfers between devices: 15.7 us -> 7.24 us  [gather_dp(): lax.ppermute(block, 'dp', [(partner(z, i, count), z) for z in range(count)])]
    ppermute x15, starting transfers between devices: 21.7 us -> 27.6 us  [gather_dp(): lax.ppermute(block, 'dp', [(partner(z, i, count), z) for z in range(count)])]
    ppermute x4, waiting for transfers between devices: 4.63 us -> 0.01 us  [hop(): return lax.ppermute(value, ('section', 'seq'), pairs)]
    ppermute x13 -> x14, starting transfers between devices: 12.9 us -> 15.1 us  [ring(): lax.ppermute(value, axis, [(i, (i + steps) % count) for i in range(count)])]
    ppermute x13 -> x14, waiting for transfers between devices: 4.97 us -> 6.96 us  [ring(): lax.ppermute(value, axis, [(i, (i + steps) % count) for i in range(count)])]
    ppermute x12, waiting for transfers between devices: 2.62 us -> 4.3 us  [return_dp(): lax.ppermute(blocks[i], 'dp', [(z, partner(z, i, count)) for z in range(c...]
  transfers between devices with their start and end apart: 44 -> 45, of which waited for: 12 -> 11; matrix products, arithmetic and copies ran while one was open for 1% -> 1% of each run, Pallas kernels for 36% -> 37%
where the time goes in v2:
time: 153 us; the launch traced here: 152 us
  Pallas kernels  67.5 us (44%)
  starting transfers between devices  63.5 us (42%)
  waiting for transfers between devices  18.5 us (12%)
    ppermute x15, starting transfers between devices, gather_dp(): lax.ppermute(block, 'dp', [(partner(z, i, count), z) for z in range(count)])  27.6 us
    ppermute x12, starting transfers between devices, return_dp(): lax.ppermute(blocks[i], 'dp', [(z, partner(z, i, count)) for z in range(c...  17.7 us
    pallas_call x12, Pallas kernels, call(): pl.pallas_call(body, name=name, out_shape=shapes, in_specs=[smem] * n_sma...  17.5 us
    pallas_call x5, Pallas kernels, project(): pl.pallas_call(body, name=name, in_specs=specs + [anywhere] * len(after),...  16.9 us
    ppermute x14, starting transfers between devices, ring(): lax.ppermute(value, axis, [(i, (i + steps) % count) for i in range(count)])  15.1 us
    pallas_call x3, Pallas kernels, expand(): pl.pallas_call(body, name=name, in_specs=[vmem] * count + [anywhere] * (1...  12.3 us
    pallas_call x2, Pallas kernels, dense_rows(): pl.pallas_call(body, name=name, in_specs=[smem] * 2 + [vmem] * (5 + len(e...  11.4 us
    pallas_call x2, Pallas kernels, outer(): pl.pallas_call(body, name=name, in_specs=[vmem] * (count + 3) + [anywhere...  9.41 us
  transfers between devices with their start and end apart: 45, of which 11 were waited for; matrix products, arithmetic and copies ran while one was open for 1% of the time, Pallas kernels for 37%

profile of v2, /device:TPU:0, one launch (start us, length us, event | category | flops | bytes accessed | tf_op | source)
XLA Modules:
  0.0 152.5 jit_solution(11919795883395471775)
XLA Ops:
  0.6 2.4 %collective-permute-start = (s32[1,1,2,6]{3,2,1,0:T(2,128)}, s32[1,1,2,6]{3,2,1,0:T(2,128)S(1)}, u32[]{:S(2)}, u32[]{:S(2)}) collective-permute-start(s32[1,1,2,6]{3,2,1,0:T(2,128)} %refs_1_.7), channel_id=1, source_target_pairs={{0,24},{8,0},{16,8},{24,16},{1,25},{9,1},{17,9},{25,17},{2,26},{10... | collective-permute-start | bytes 152 | tf_op jit(solution)/shard_map/ppermute | solution.py:19
  3.1 1.3 copy.16.refs_2_.count_ref
  5.0 4.0 %own_rows.1 = (bf16[22,3712]{1,0:T(8,128)(2,1)S(1)}, bf16[22,3712]{1,0:T(8,128)(2,1)S(1)}, bf16[48,1024]{1,0:T(8,128)(2,1)S(1)}) custom-call(s32[2]{0:T(128)} %pad_add_fusion.refs_0_, s32[1,1,2,6]{3,2,1,0:T(2,128)} %refs_1_.7, s32[1,1,2,1]{3,2,1,0:T(2,128)} %copy.16.refs_2_.count_ref, f32[1,1,2,6]{3,2,1,0:T(2,128)} %refs_3_.2, bf16[128,7168]{1,0:T(8,128)(2,1)} %bitcast.6, ...), custom_call_target="tpu_custom_call" | custom-call | bytes 4094976 | tf_op jit(solution)/shard_map/own_rows/pallas_call | solution.py:239
  9.0 1.6 %collective-permute-start.3 = (bf16[22,3712]{1,0:T(8,128)(2,1)S(1)}, bf16[22,3712]{1,0:T(8,128)(2,1)S(1)}, u32[]{:S(2)}, u32[]{:S(2)}) collective-permute-start(bf16[22,3712]{1,0:T(8,128)(2,1)S(1)} %get-tuple-element.96), channel_id=1, source_target_pairs={{0,4},{4,0},{1,5},{5,1},{2,6},{6,2},{3,7},{7,3},{8,12},{12,8},{9,1... | collective-permute-start | bytes 489992 | tf_op jit(solution)/shard_map/ppermute | solution.py:19
  10.6 1.3 source_rows.1
  12.7 1.6 %collective-permute-start.4 = (bf16[48,1024]{1,0:T(8,128)(2,1)S(1)}, bf16[48,1024]{1,0:T(8,128)(2,1)S(1)}, u32[]{:S(2)}, u32[]{:S(2)}) collective-permute-start(bf16[48,1024]{1,0:T(8,128)(2,1)S(1)} %get-tuple-element.98.refs_6_), channel_id=1, source_target_pairs={{1,0},{0,1},{3,2},{2,3},{5,4},{4,5},{7,6},{6,7},{9,8},{8,9},{11,10... | collective-permute-start | bytes 294920 | tf_op jit(solution)/shard_map/ppermute | solution.py:45
  14.3 2.6 %collective-permute-start.5 = (bf16[48,1024]{1,0:T(8,128)(2,1)S(1)}, bf16[48,1024]{1,0:T(8,128)(2,1)S(1)}, u32[]{:S(2)}, u32[]{:S(2)}) collective-permute-start(bf16[48,1024]{1,0:T(8,128)(2,1)S(1)} %get-tuple-element.98.refs_6_), channel_id=1, source_target_pairs={{2,0},{3,1},{0,2},{1,3},{6,4},{7,5},{4,6},{5,7},{10,8},{11,9},{8,1... | collective-permute-start | bytes 294920 | tf_op jit(solution)/shard_map/ppermute | solution.py:45
  16.9 3.3 %collective-permute-start.6 = (bf16[48,1024]{1,0:T(8,128)(2,1)S(1)}, bf16[48,1024]{1,0:T(8,128)(2,1)S(1)}, u32[]{:S(2)}, u32[]{:S(2)}) collective-permute-start(bf16[48,1024]{1,0:T(8,128)(2,1)S(1)} %get-tuple-element.98.refs_6_), channel_id=1, source_target_pairs={{3,0},{2,1},{1,2},{0,3},{7,4},{6,5},{5,6},{4,7},{11,8},{10,9},{9,1... | collective-permute-start | bytes 294920 | tf_op jit(solution)/shard_map/ppermute | solution.py:45
  20.1 4.7 %collective-permute-done.5.refs_8_ = bf16[48,1024]{1,0:T(8,128)(2,1)S(1)} collective-permute-done((bf16[48,1024]{1,0:T(8,128)(2,1)S(1)}, bf16[48,1024]{1,0:T(8,128)(2,1)S(1)}, u32[]{:S(2)}, u32[]{:S(2)}) %collective-permute-start.5) | collective-permute-done | bytes 98336 | tf_op jit(solution)/shard_map/ppermute | solution.py:45
  24.9 1.3 first_mixed.1
  26.2 2.7 %collective-permute-start.8 = (bf16[48,896]{1,0:T(8,128)(2,1)S(1)}, bf16[48,896]{1,0:T(8,128)(2,1)S(1)}, u32[]{:S(2)}, u32[]{:S(2)}) collective-permute-start(bf16[48,896]{1,0:T(8,128)(2,1)S(1)} %get-tuple-element.99.refs_7_.refs_0_.refs_1_.refs_3_), channel_id=1, source_target_pairs={{1,0},{0,1},{3,2},{2,3},{5,4},{4,5},{7,6},{6,7},{9,8},{8,9},{11,10... | collective-permute-start | bytes 258056 | tf_op jit(solution)/shard_map/ppermute | solution.py:45
  28.9 1.1 collective-permute-start.9
  30.1 1.4 collective-permute-start.10
  31.4 1.7 %second_base.1 = (bf16[24,896]{1,0:T(8,128)(2,1)S(1)}, bf16[24,896]{1,0:T(8,128)(2,1)S(1)}, bf16[6,7168]{1,0:T(8,128)(2,1)S(1)}, bf16[6,7168]{1,0:T(8,128)(2,1)S(1)}) custom-call(s32[2]{0:T(128)} %pad_add_fusion.refs_0_, s32[1,1,2,6]{3,2,1,0:T(2,128)} %refs_1_.7, s32[1,1,2,1]{3,2,1,0:T(2,128)} %copy.16.refs_2_.count_ref, ...), custom_call_target="tpu_custom_call" | custom-call | bytes 2567680 | tf_op jit(solution)/shard_map/second_base/pallas_call | solution.py:239
  33.1 1.5 collective-permute-start.11
  34.6 2.6 %collective-permute-done.11.refs_6_.refs_2_ = bf16[24,896]{1,0:T(8,128)(2,1)S(1)} collective-permute-done((bf16[24,896]{1,0:T(8,128)(2,1)S(1)}, bf16[24,896]{1,0:T(8,128)(2,1)S(1)}, u32[]{:S(2)}, u32[]{:S(2)}) %collective-permute-start.11) | collective-permute-done | bytes 43040 | tf_op jit(solution)/shard_map/ppermute | solution.py:19
  37.2 1.7 %collective-permute-done.9.refs_2_.refs_5_ = bf16[48,896]{1,0:T(8,128)(2,1)S(1)} collective-permute-done((bf16[48,896]{1,0:T(8,128)(2,1)S(1)}, bf16[48,896]{1,0:T(8,128)(2,1)S(1)}, u32[]{:S(2)}, u32[]{:S(2)}) %collective-permute-start.9) | collective-permute-done | bytes 86048 | tf_op jit(solution)/shard_map/ppermute | solution.py:45
  38.9 3.5 %gate_up_1.1 = (f32[48,1024]{1,0:T(8,128)S(1)}, bf16[48,1024]{1,0:T(8,128)(2,1)S(1)}) custom-call(bf16[48,896]{1,0:T(8,128)(2,1)S(1)} %get-tuple-element.99.refs_7_.refs_0_.refs_1_.refs_3_, bf16[48,896]{1,0:T(8,128)(2,1)S(1)} %collective-permute-done.8.refs_1_.refs_4_, bf16[48,896]{1,0:T(8,128)(2,1)S(1)} %collective-permute-done.9.refs_2_.refs_5_, ...), custom_call_target="tpu_custom_call" | custom-call | flops 352321536 | bytes 7340032 | tf_op jit(solution)/shard_map/gate_up_1/pallas_call | solution.py:340
  42.3 1.5 collective-permute-start.12
  44.5 2.5 %collective-permute-done.12.refs_1_ = bf16[48,1024]{1,0:T(8,128)(2,1)S(1)} collective-permute-done((bf16[48,1024]{1,0:T(8,128)(2,1)S(1)}, bf16[48,1024]{1,0:T(8,128)(2,1)S(1)}, u32[]{:S(2)}, u32[]{:S(2)}) %collective-permute-start.12) | collective-permute-done | bytes 98336 | tf_op jit(solution)/shard_map/ppermute | solution.py:19
  47.0 3.0 %down_1.1 = (bf16[48,512]{1,0:T(8,128)(2,1)S(1)}, f32[48,1024]{1,0:T(8,128)S(1)}, bf16[48,896]{1,0:T(8,128)(2,1)S(1)}, bf16[48,896]{1,0:T(8,128)(2,1)S(1)}, bf16...) custom-call(f32[48,1024]{1,0:T(8,128)S(1)} %get-tuple-element.104.refs_0_, ...), custom_call_target="tpu_custom_call" | custom-call | flops 176160768 | bytes 3670016 | tf_op jit(solution)/shard_map/down_1/pallas_call | solution.py:381
  50.1 1.4 collective-permute-start.19
  51.5 1.9 %collective-permute-start.13 = (bf16[48,896]{1,0:T(8,128)(2,1)S(1)}, bf16[48,896]{1,0:T(8,128)(2,1)S(1)}, u32[]{:S(2)}, u32[]{:S(2)}) collective-permute-start(bf16[48,896]{1,0:T(8,128)(2,1)S(1)} %get-tuple-element.111), channel_id=1, source_target_pairs={{0,1},{1,0},{2,3},{3,2},{4,5},{5,4},{6,7},{7,6},{8,9},{9,8},{10,11... | collective-permute-start | bytes 258056 | tf_op jit(solution)/shard_map/ppermute | solution.py:53
  53.4 1.0 collective-permute-start.14
  54.4 1.5 collective-permute-start.15
  55.9 1.8 %collective-permute-done.13.refs_3_ = bf16[48,896]{1,0:T(8,128)(2,1)S(1)} collective-permute-done((bf16[48,896]{1,0:T(8,128)(2,1)S(1)}, bf16[48,896]{1,0:T(8,128)(2,1)S(1)}, u32[]{:S(2)}, u32[]{:S(2)}) %collective-permute-start.13) | collective-permute-done | bytes 86048 | tf_op jit(solution)/shard_map/ppermute | solution.py:53
  57.7 1.1 collective-permute-start.20
  58.8 1.7 %collective-permute-done.14.refs_4_ = bf16[48,896]{1,0:T(8,128)(2,1)S(1)} collective-permute-done((bf16[48,896]{1,0:T(8,128)(2,1)S(1)}, bf16[48,896]{1,0:T(8,128)(2,1)S(1)}, u32[]{:S(2)}, u32[]{:S(2)}) %collective-permute-start.14) | collective-permute-done | bytes 86048 | tf_op jit(solution)/shard_map/ppermute | solution.py:53
  60.5 1.1 collective-permute-start.21
  61.6 4.0 %collective-permute-start.22 = (bf16[48,896]{1,0:T(8,128)(2,1)S(1)}, bf16[48,896]{1,0:T(8,128)(2,1)S(1)}, u32[]{:S(2)}, u32[]{:S(2)}) collective-permute-start(bf16[48,896]{1,0:T(8,128)(2,1)S(1)} %base_order.1.refs_3_.refs_0_.refs_2_), channel_id=1, source_target_pairs={{3,0},{2,1},{1,2},{0,3},{7,4},{6,5},{5,6},{4,7},{11,8},{10,9},{9,1... | collective-permute-start | bytes 258056 | tf_op jit(solution)/shard_map/ppermute | solution.py:45
  65.6 5.8 %dense_a.1 = (bf16[128,7168]{1,0:T(8,128)(2,1)S(1)}, f32[4,7168]{1,0:T(4,128)S(1)}) custom-call(s32[1,1,2,6]{3,2,1,0:T(2,128)} %refs_1_.7, s32[1,1,2,1]{3,2,1,0:T(2,128)} %copy.16.refs_2_.count_ref, bf16[128,7168]{1,0:T(8,128)(2,1)S(1)} %collective-permute-done.7.hidden_ref, bf16[128,7168]{1,0:T(8,128)(2,1)S(1)} %bitcast.8, ...), custom_call_target="tpu_custom_call" | custom-call | flops 27525120 | bytes 4587520 | tf_op jit(solution)/shard_map/dense_a/pallas_call | solution.py:560
  72.1 1.6 %collective-permute-start.17 = (bf16[48,896]{1,0:T(8,128)(2,1)S(1)}, bf16[48,896]{1,0:T(8,128)(2,1)S(1)}, u32[]{:S(2)}, u32[]{:S(2)}) collective-permute-start(bf16[48,896]{1,0:T(8,128)(2,1)S(1)} %get-tuple-element.114.refs_3_.refs_1_.refs_0_.refs_5_.refs_11_), channel_id=1, source_target_pairs={{2,0},{3,1},{0,2},{1,3},{6,4},{7,5},{4,6},{5,7},{10,8},{11,9},{8,1... | collective-permute-start | bytes 258056 | tf_op jit(solution)/shard_map/ppermute | solution.py:45
  73.7 2.3 %collective-permute-start.18 = (bf16[48,896]{1,0:T(8,128)(2,1)S(1)}, bf16[48,896]{1,0:T(8,128)(2,1)S(1)}, u32[]{:S(2)}, u32[]{:S(2)}) collective-permute-start(bf16[48,896]{1,0:T(8,128)(2,1)S(1)} %get-tuple-element.114.refs_3_.refs_1_.refs_0_.refs_5_.refs_11_), channel_id=1, source_target_pairs={{3,0},{2,1},{1,2},{0,3},{7,4},{6,5},{5,6},{4,7},{11,8},{10,9},{9,1... | collective-permute-start | bytes 258056 | tf_op jit(solution)/shard_map/ppermute | solution.py:45
  76.0 1.0 slot_facts.1
  77.0 4.6 %fixed_2.1 = (f32[48,1536]{1,0:T(8,128)S(1)}, bf16[48,1536]{1,0:T(8,128)(2,1)S(1)}) custom-call(bf16[48,896]{1,0:T(8,128)(2,1)S(1)} %base_order.1.refs_3_.refs_0_.refs_2_, bf16[48,896]{1,0:T(8,128)(2,1)S(1)} %collective-permute-done.20.refs_1_.refs_3_, bf16[48,896]{1,0:T(8,128)(2,1)S(1)} %collective-permute-done.21.refs_2_.refs_4_, ...), custom_call_target="tpu_custom_call" | custom-call | flops 528482304 | bytes 11010048 | tf_op jit(solution)/shard_map/fixed_2/pallas_call | solution.py:340
  82.3 4.2 %gate_up_2.1 = (f32[48,1152]{1,0:T(8,128)S(1)}, bf16[48,1152]{1,0:T(8,128)(2,1)S(1)}, bf16[48,3584]{1,0:T(8,128)(2,1)S(1)}) custom-call(s32[2]{0:T(128)S(1)} %copy-done.4, bf16[48,896]{1,0:T(8,128)(2,1)S(1)} %get-tuple-element.114.refs_3_.refs_1_.refs_0_.refs_5_.refs_11_, bf16[48,896]{1,0:T(8,128)(2,1)S(1)} %collective-permute-done.16.refs_2_.refs_1_.refs_6_.refs_12_, ...), custom_call_target="tpu_custom_call" | custom-call | flops 352321536 | bytes 7340032 | tf_op jit(solution)/shard_map/gate_up_2/pallas_call | solution.py:340
  86.5 1.5 collective-permute-start.23
  88.0 2.3 %prev_down.1 = (f32[48,512]{1,0:T(8,128)S(1)}, bf16[48,512]{1,0:T(8,128)(2,1)S(1)}) custom-call(bf16[48,896]{1,0:T(8,128)(2,1)S(1)} %get-tuple-element.114.refs_3_.refs_1_.refs_0_.refs_5_.refs_11_, bf16[48,896]{1,0:T(8,128)(2,1)S(1)} %collective-permute-done.16.refs_2_.refs_1_.refs_6_.refs_12_, ...), custom_call_target="tpu_custom_call" | custom-call | flops 176160768 | bytes 3670016 | tf_op jit(solution)/shard_map/prev_down/pallas_call | solution.py:340
  90.3 1.0 collective-permute-done.23.refs_1_
  91.3 4.6 %back_rows_2.1 = (bf16[48,512]{1,0:T(8,128)(2,1)S(1)}, bf16[48,512]{1,0:T(8,128)(2,1)S(1)}, bf16[48,512]{1,0:T(8,128)(2,1)S(1)}, f32[48,1]{1,0:T(8,128)S(1)}, f3...) custom-call(f32[48,1152]{1,0:T(8,128)S(1)} %get-tuple-element.126.re, ...), custom_call_target="tpu_custom_call" | custom-call | flops 352321536 | bytes 7340032 | tf_op jit(solution)/shard_map/back_rows_2/pallas_call | solution.py:381
  96.0 2.1 %collective-permute-start.26 = (bf16[48,896]{1,0:T(8,128)(2,1)S(1)}, bf16[48,896]{1,0:T(8,128)(2,1)S(1)}, u32[]{:S(2)}, u32[]{:S(2)}) collective-permute-start(bf16[48,896]{1,0:T(8,128)(2,1)S(1)} %get-tuple-element.135), channel_id=1, source_target_pairs={{0,2},{1,3},{2,0},{3,1},{4,6},{5,7},{6,4},{7,5},{8,10},{9,11},{10,... | collective-permute-start | bytes 258056 | tf_op jit(solution)/shard_map/ppermute | solution.py:53
  98.1 2.3 %collective-permute-start.27 = (bf16[48,896]{1,0:T(8,128)(2,1)S(1)}, bf16[48,896]{1,0:T(8,128)(2,1)S(1)}, u32[]{:S(2)}, u32[]{:S(2)}) collective-permute-start(bf16[48,896]{1,0:T(8,128)(2,1)S(1)} %get-tuple-element.136), channel_id=1, source_target_pairs={{0,3},{1,2},{2,1},{3,0},{4,7},{5,6},{6,5},{7,4},{8,11},{9,10},{10,... | collective-permute-start | bytes 258056 | tf_op jit(solution)/shard_map/ppermute | solution.py:53
  100.4 1.4 collective-permute-start.28
  101.8 5.7 %dense_b.1 = (bf16[128,7168]{1,0:T(8,128)(2,1)S(1)}, f32[4,7168]{1,0:T(4,128)S(1)}) custom-call(s32[1,1,2,6]{3,2,1,0:T(2,128)} %refs_1_.7, s32[1,1,2,1]{3,2,1,0:T(2,128)} %copy.16.refs_2_.count_ref, bf16[128,7168]{1,0:T(8,128)(2,1)S(1)} %collective-permute-done.7.hidden_ref, bf16[128,7168]{1,0:T(8,128)(2,1)S(1)} %bitcast.9, ...), custom_call_target="tpu_custom_call", output_to_operand_aliasing={{0}: (7, {})} | custom-call | flops 27525120 | bytes 4587520 | tf_op jit(solution)/shard_map/dense_b/pallas_call | solution.py:560
  107.5 1.1 first_grad.1
  109.6 2.1 %collective-permute-start.32 = (bf16[48,896]{1,0:T(8,128)(2,1)S(1)}, bf16[48,896]{1,0:T(8,128)(2,1)S(1)}, u32[]{:S(2)}, u32[]{:S(2)}) collective-permute-start(bf16[48,896]{1,0:T(8,128)(2,1)S(1)} %get-tuple-element.139.refs_13_.refs_0_.refs_7_), channel_id=1, source_target_pairs={{2,0},{3,1},{0,2},{1,3},{6,4},{7,5},{4,6},{5,7},{10,8},{11,9},{8,1... | collective-permute-start | bytes 258056 | tf_op jit(solution)/shard_map/ppermute | solution.py:45
  111.7 2.3 %collective-permute-start.33 = (bf16[48,896]{1,0:T(8,128)(2,1)S(1)}, bf16[48,896]{1,0:T(8,128)(2,1)S(1)}, u32[]{:S(2)}, u32[]{:S(2)}) collective-permute-start(bf16[48,896]{1,0:T(8,128)(2,1)S(1)} %get-tuple-element.139.refs_13_.refs_0_.refs_7_), channel_id=1, source_target_pairs={{3,0},{2,1},{1,2},{0,3},{7,4},{6,5},{5,6},{4,7},{11,8},{10,9},{9,1... | collective-permute-start | bytes 258056 | tf_op jit(solution)/shard_map/ppermute | solution.py:45
  114.0 4.7 %weight_grad_2.1 = (bf16[1,2,3,3584,512]{4,3,2,1,0:T(8,128)(2,1)}, f32[8,128]{1,0:T(8,128)S(1)}) custom-call(bf16[48,3584]{1,0:T(8,128)(2,1)S(1)} %get-tuple-element.145.refs_0_, f32[48,1]{1,0:T(8,128)S(1)} %get-tuple-element.146.refs_1_, bf16[48,896]{1,0:T(8,128)(2,1)S(1)} %base_order.1.refs_3_.refs_0_.refs_2_, ...), custom_call_target="tpu_custom_call" | custom-call | flops 528482304 | bytes 11010048 | tf_op jit(solution)/shard_map/weight_grad_2/pallas_call | solution.py:429
  118.8 0.9 collective-permute-done.32.refs_2_.refs_9_
  119.6 2.4 %back_1.1 = (f32[48,640]{1,0:T(8,128)S(1)}, bf16[48,640]{1,0:T(8,128)(2,1)S(1)}) custom-call(bf16[48,896]{1,0:T(8,128)(2,1)S(1)} %get-tuple-element.139.refs_13_.refs_0_.refs_7_, bf16[48,896]{1,0:T(8,128)(2,1)S(1)} %collective-permute-done.31.refs_1_.refs_8_, bf16[48,896]{1,0:T(8,128)(2,1)S(1)} %collective-permute-done.32.refs_2_.refs_9_, ...), custom_call_target="tpu_custom_call" | custom-call | flops 176160768 | bytes 3670016 | tf_op jit(solution)/shard_map/back_1/pallas_call | solution.py:340
  122.0 1.5 collective-permute-start.35
  123.5 1.6 %second_grad.1 = (bf16[6,7296]{1,0:T(8,128)(2,1)S(1)}, f32[4,3584]{1,0:T(4,128)S(1)}, f32[4,3584]{1,0:T(4,128)S(1)}) custom-call(s32[2]{0:T(128)} %pad_add_fusion.refs_0_, s32[1,1,2,6]{3,2,1,0:T(2,128)} %refs_1_.7, s32[1,1,2,1]{3,2,1,0:T(2,128)} %copy.16.refs_2_.count_ref, bf16[6,10880]{1,0:T(8,128)(2,1)S(1)} %collective-permute-done.1.refs_2_.refs_3_, ...), custom_call_target="tpu_custom_call" | custom-call | bytes 2655232 | tf_op jit(solution)/shard_map/second_grad/pallas_call | solution.py:239
  125.8 0.8 collective-permute-done.35.refs_1_
  126.6 4.6 %back_rows_1.1 = (bf16[48,512]{1,0:T(8,128)(2,1)S(1)}, bf16[48,512]{1,0:T(8,128)(2,1)S(1)}, f32[48,1]{1,0:T(8,128)S(1)}, bf16[48,896]{1,0:T(8,128)(2,1)S(1)}, bf...) custom-call(f32[48,640]{1,0:T(8,128)S(1)} %get-tuple-element.156.refs_0_, ...), custom_call_target="tpu_custom_call" | custom-call | flops 352321536 | bytes 7340032 | tf_op jit(solution)/shard_map/back_rows_1/pallas_call | solution.py:381
  131.2 1.4 collective-permute-start.36
  133.4 2.3 %collective-permute-start.38 = (bf16[48,896]{1,0:T(8,128)(2,1)S(1)}, bf16[48,896]{1,0:T(8,128)(2,1)S(1)}, u32[]{:S(2)}, u32[]{:S(2)}) collective-permute-start(bf16[48,896]{1,0:T(8,128)(2,1)S(1)} %get-tuple-element.167), channel_id=1, source_target_pairs={{0,3},{1,2},{2,1},{3,0},{4,7},{5,6},{6,5},{7,4},{8,11},{9,10},{10,... | collective-permute-start | bytes 258056 | tf_op jit(solution)/shard_map/ppermute | solution.py:53
  135.7 4.7 %weight_grad_1.1 = (bf16[1,2,3,3584,512]{4,3,2,1,0:T(8,128)(2,1)}, f32[8,128]{1,0:T(8,128)S(1)}) custom-call(f32[48,1]{1,0:T(8,128)S(1)} %get-tuple-element.160.refs_0_.refs_4_, f32[48,1]{1,0:T(8,128)S(1)} %get-tuple-element.155.refs_5_.refs_1_.refs_3_, f32[48,1]{1,0:T(8,128)S(1)} %get-tuple-element.158.refs_6_.refs_2_, ...), custom_call_target="tpu_custom_call", output_to_operand_aliasing={{0}: (18, {})} | custom-call | flops 528482304 | bytes 11010048 | tf_op jit(solution)/shard_map/weight_grad_1/pallas_call | solution.py:429
  140.4 1.2 last_grad.1
  141.6 1.3 collective-permute-start.40
  142.9 1.0 collective-permute-start.41
  143.9 1.5 collective-permute-start.42
  145.4 1.0 collective-permute-start.43
  146.3 2.0 %collective-permute-start.44 = (f32[4,896]{1,0:T(4,128)S(1)}, f32[4,896]{1,0:T(4,128)S(1)}, u32[]{:S(2)}, u32[]{:S(2)}) collective-permute-start(f32[4,896]{1,0:T(4,128)S(1)} %get-tuple-element.181), channel_id=1, source_target_pairs={{0,3},{1,2},{2,1},{3,0},{4,7},{5,6},{6,5},{7,4},{8,11},{9,10},{10,... | collective-permute-start | bytes 43016 | tf_op jit(solution)/shard_map/ppermute | solution.py:53
  148.3 2.9 %finish.1 = (bf16[128,7168]{1,0:T(8,128)(2,1)}, f32[8,128]{1,0:T(8,128)S(1)}) custom-call(s32[2]{0:T(128)} %pad_add_fusion.refs_0_, s32[1,1,2,6]{3,2,1,0:T(2,128)} %copy-done.5, bf16[128,7168]{1,0:T(8,128)(2,1)S(1)} %collective-permute-done.29.refs_2_, bf16[6,7168]{1,0:T(8,128)(2,1)S(1)} %get-tuple-element.141.refs_3_, ...), custom_call_target="tpu_custom_call" | custom-call | bytes 3933696 | tf_op jit(solution)/shard_map/finish/pallas_call | solution.py:239
  (64 shorter events, 7.6 us)
Async XLA Ops:
  0.6 4.3 %collective-permute-start = (s32[1,1,2,6]{3,2,1,0:T(2,128)}, s32[1,1,2,6]{3,2,1,0:T(2,128)S(1)}, u32[]{:S(2)}, u32[]{:S(2)}) collective-permute-start(s32[1,1,2,6]{3,2,1,0:T(2,128)} %refs_1_.7), channel_id=1, source_target_pairs={{0,24},{8,0},{16,8},{24,16},{1,25},{9,1},{17,9},{25,17},{2,26},{10... | collective-permute-start | bytes 152 | tf_op jit(solution)/shard_map/ppermute | solution.py:19
  5.0 4.0 %copy-start.5 = (s32[1,1,2,6]{3,2,1,0:T(2,128)}, s32[1,1,2,6]{3,2,1,0:T(2,128)S(1)}, u32[]{:S(2)}) copy-start(s32[1,1,2,6]{3,2,1,0:T(2,128)S(1)} %collective-permute-done.refs_6_.refs_1_) | copy-start | bytes 148
  5.0 5.6 %copy-start.3 = (bf16[1,1,128,7168]{3,2,1,0:T(8,128)(2,1)S(1)}, bf16[1,1,128,7168]{3,2,1,0:T(8,128)(2,1)}, u32[]{:S(2)}) copy-start(bf16[1,1,128,7168]{3,2,1,0:T(8,128)(2,1)} %param.8) | copy-start | bytes 5505028
  9.0 15.9 %copy-start.2 = (f32[2,2,7168]{2,1,0:T(2,128)S(1)}, f32[2,2,7168]{2,1,0:T(2,128)}, u32[]{:S(2)}) copy-start(f32[2,2,7168]{2,1,0:T(2,128)} %refs_9_.1) | copy-start | bytes 344068
  9.0 22.4 %copy-start = (bf16[1,1,128,7168]{3,2,1,0:T(8,128)(2,1)S(1)}, bf16[1,1,128,7168]{3,2,1,0:T(8,128)(2,1)}, u32[]{:S(2)}) copy-start(bf16[1,1,128,7168]{3,2,1,0:T(8,128)(2,1)} %param.9) | copy-start | bytes 5505028
  9.0 15.8 %collective-permute-start.3 = (bf16[22,3712]{1,0:T(8,128)(2,1)S(1)}, bf16[22,3712]{1,0:T(8,128)(2,1)S(1)}, u32[]{:S(2)}, u32[]{:S(2)}) collective-permute-start(bf16[22,3712]{1,0:T(8,128)(2,1)S(1)} %get-tuple-element.96), channel_id=1, source_target_pairs={{0,4},{4,0},{1,5},{5,1},{2,6},{6,2},{3,7},{7,3},{8,12},{12,8},{9,1... | collective-permute-start | bytes 489992 | tf_op jit(solution)/shard_map/ppermute | solution.py:19
  11.9 5.0 %collective-permute-start.2 = (bf16[6,3712]{1,0:T(8,128)(2,1)S(1)}, bf16[6,3712]{1,0:T(8,128)(2,1)S(1)}, u32[]{:S(2)}, u32[]{:S(2)}) collective-permute-start(bf16[6,3712]{1,0:T(8,128)(2,1)S(1)} %get-tuple-element.95), channel_id=1, source_target_pairs={{0,12},{4,8},{8,20},{12,16},{16,28},{20,24},{24,4},{28,0},{1,13},{... | collective-permute-start | bytes 133640 | tf_op jit(solution)/shard_map/ppermute | solution.py:29
  12.1 12.7 %collective-permute-start.1 = (bf16[6,10880]{1,0:T(8,128)(2,1)S(1)}, bf16[6,10880]{1,0:T(8,128)(2,1)S(1)}, u32[]{:S(2)}, u32[]{:S(2)}) collective-permute-start(bf16[6,10880]{1,0:T(8,128)(2,1)S(1)} %get-tuple-element.94), channel_id=1, source_target_pairs={{0,8},{4,12},{8,16},{12,20},{16,24},{20,28},{24,0},{28,4},{1,9},{5... | collective-permute-start | bytes 391688 | tf_op jit(solution)/shard_map/ppermute | solution.py:29
  12.7 7.5 %collective-permute-start.4 = (bf16[48,1024]{1,0:T(8,128)(2,1)S(1)}, bf16[48,1024]{1,0:T(8,128)(2,1)S(1)}, u32[]{:S(2)}, u32[]{:S(2)}) collective-permute-start(bf16[48,1024]{1,0:T(8,128)(2,1)S(1)} %get-tuple-element.98.refs_6_), channel_id=1, source_target_pairs={{1,0},{0,1},{3,2},{2,3},{5,4},{4,5},{7,6},{6,7},{9,8},{8,9},{11,10... | collective-permute-start | bytes 294920 | tf_op jit(solution)/shard_map/ppermute | solution.py:45
  14.3 10.6 %collective-permute-start.5 = (bf16[48,1024]{1,0:T(8,128)(2,1)S(1)}, bf16[48,1024]{1,0:T(8,128)(2,1)S(1)}, u32[]{:S(2)}, u32[]{:S(2)}) collective-permute-start(bf16[48,1024]{1,0:T(8,128)(2,1)S(1)} %get-tuple-element.98.refs_6_), channel_id=1, source_target_pairs={{2,0},{3,1},{0,2},{1,3},{6,4},{7,5},{4,6},{5,7},{10,8},{11,9},{8,1... | collective-permute-start | bytes 294920 | tf_op jit(solution)/shard_map/ppermute | solution.py:45
  16.9 8.0 %collective-permute-start.6 = (bf16[48,1024]{1,0:T(8,128)(2,1)S(1)}, bf16[48,1024]{1,0:T(8,128)(2,1)S(1)}, u32[]{:S(2)}, u32[]{:S(2)}) collective-permute-start(bf16[48,1024]{1,0:T(8,128)(2,1)S(1)} %get-tuple-element.98.refs_6_), channel_id=1, source_target_pairs={{3,0},{2,1},{1,2},{0,3},{7,4},{6,5},{5,6},{4,7},{11,8},{10,9},{9,1... | collective-permute-start | bytes 294920 | tf_op jit(solution)/shard_map/ppermute | solution.py:45
  26.2 35.5 %collective-permute-start.7 = (bf16[128,7168]{1,0:T(8,128)(2,1)S(1)}, bf16[128,7168]{1,0:T(8,128)(2,1)S(1)}, u32[]{:S(2)}, u32[]{:S(2)}) collective-permute-start(bf16[128,7168]{1,0:T(8,128)(2,1)S(1)} %bitcast.15), channel_id=1, source_target_pairs={{0,8},{8,16},{16,24},{24,0},{1,9},{9,17},{17,25},{25,1},{2,10},{10... | collective-permute-start | bytes 5505032 | tf_op jit(solution)/shard_map/ppermute | solution.py:19
  26.2 11.0 %collective-permute-start.8 = (bf16[48,896]{1,0:T(8,128)(2,1)S(1)}, bf16[48,896]{1,0:T(8,128)(2,1)S(1)}, u32[]{:S(2)}, u32[]{:S(2)}) collective-permute-start(bf16[48,896]{1,0:T(8,128)(2,1)S(1)} %get-tuple-element.99.refs_7_.refs_0_.refs_1_.refs_3_), channel_id=1, source_target_pairs={{1,0},{0,1},{3,2},{2,3},{5,4},{4,5},{7,6},{6,7},{9,8},{8,9},{11,10... | collective-permute-start | bytes 258056 | tf_op jit(solution)/shard_map/ppermute | solution.py:45
  28.9 10.0 %collective-permute-start.9 = (bf16[48,896]{1,0:T(8,128)(2,1)S(1)}, bf16[48,896]{1,0:T(8,128)(2,1)S(1)}, u32[]{:S(2)}, u32[]{:S(2)}) collective-permute-start(bf16[48,896]{1,0:T(8,128)(2,1)S(1)} %get-tuple-element.99.refs_7_.refs_0_.refs_1_.refs_3_), channel_id=1, source_target_pairs={{2,0},{3,1},{0,2},{1,3},{6,4},{7,5},{4,6},{5,7},{10,8},{11,9},{8,1... | collective-permute-start | bytes 258056 | tf_op jit(solution)/shard_map/ppermute | solution.py:45
  30.1 8.8 %collective-permute-start.10 = (bf16[48,896]{1,0:T(8,128)(2,1)S(1)}, bf16[48,896]{1,0:T(8,128)(2,1)S(1)}, u32[]{:S(2)}, u32[]{:S(2)}) collective-permute-start(bf16[48,896]{1,0:T(8,128)(2,1)S(1)} %get-tuple-element.99.refs_7_.refs_0_.refs_1_.refs_3_), channel_id=1, source_target_pairs={{3,0},{2,1},{1,2},{0,3},{7,4},{6,5},{5,6},{4,7},{11,8},{10,9},{9,1... | collective-permute-start | bytes 258056 | tf_op jit(solution)/shard_map/ppermute | solution.py:45
  33.1 4.1 %collective-permute-start.11 = (bf16[24,896]{1,0:T(8,128)(2,1)S(1)}, bf16[24,896]{1,0:T(8,128)(2,1)S(1)}, u32[]{:S(2)}, u32[]{:S(2)}) collective-permute-start(bf16[24,896]{1,0:T(8,128)(2,1)S(1)} %get-tuple-element.103), channel_id=1, source_target_pairs={{0,4},{4,0},{1,5},{5,1},{2,6},{6,2},{3,7},{7,3},{8,12},{12,8},{9,1... | collective-permute-start | bytes 129032 | tf_op jit(solution)/shard_map/ppermute | solution.py:19
  42.3 4.7 %collective-permute-start.12 = (bf16[48,1024]{1,0:T(8,128)(2,1)S(1)}, bf16[48,1024]{1,0:T(8,128)(2,1)S(1)}, u32[]{:S(2)}, u32[]{:S(2)}) collective-permute-start(bf16[48,1024]{1,0:T(8,128)(2,1)S(1)} %get-tuple-element.105.refs_3_), channel_id=1, source_target_pairs={{0,4},{4,0},{1,5},{5,1},{2,6},{6,2},{3,7},{7,3},{8,12},{12,8},{9,1... | collective-permute-start | bytes 294920 | tf_op jit(solution)/shard_map/ppermute | solution.py:19
  47.0 18.6 %copy-start.1 = (bf16[1,1,128,7168]{3,2,1,0:T(8,128)(2,1)S(1)}, bf16[1,1,128,7168]{3,2,1,0:T(8,128)(2,1)}, u32[]{:S(2)}) copy-start(bf16[1,1,128,7168]{3,2,1,0:T(8,128)(2,1)} %param.10) | copy-start | bytes 5505028
  50.1 23.6 %collective-permute-start.19 = (bf16[96,1024]{1,0:T(8,128)(2,1)S(1)}, bf16[96,1024]{1,0:T(8,128)(2,1)S(1)}, u32[]{:S(2)}, u32[]{:S(2)}) collective-permute-start(bf16[96,1024]{1,0:T(8,128)(2,1)S(1)} %get-tuple-element.118), channel_id=1, source_target_pairs={{0,4},{4,0},{1,5},{5,1},{2,6},{6,2},{3,7},{7,3},{8,12},{12,8},{9,1... | collective-permute-start | bytes 589832 | tf_op jit(solution)/shard_map/ppermute | solution.py:19
  51.5 6.2 %collective-permute-start.13 = (bf16[48,896]{1,0:T(8,128)(2,1)S(1)}, bf16[48,896]{1,0:T(8,128)(2,1)S(1)}, u32[]{:S(2)}, u32[]{:S(2)}) collective-permute-start(bf16[48,896]{1,0:T(8,128)(2,1)S(1)} %get-tuple-element.111), channel_id=1, source_target_pairs={{0,1},{1,0},{2,3},{3,2},{4,5},{5,4},{6,7},{7,6},{8,9},{9,8},{10,11... | collective-permute-start | bytes 258056 | tf_op jit(solution)/shard_map/ppermute | solution.py:53
  53.4 7.1 %collective-permute-start.14 = (bf16[48,896]{1,0:T(8,128)(2,1)S(1)}, bf16[48,896]{1,0:T(8,128)(2,1)S(1)}, u32[]{:S(2)}, u32[]{:S(2)}) collective-permute-start(bf16[48,896]{1,0:T(8,128)(2,1)S(1)} %get-tuple-element.112), channel_id=1, source_target_pairs={{0,2},{1,3},{2,0},{3,1},{4,6},{5,7},{6,4},{7,5},{8,10},{9,11},{10,... | collective-permute-start | bytes 258056 | tf_op jit(solution)/shard_map/ppermute | solution.py:53
  54.4 17.0 %collective-permute-start.15 = (bf16[48,896]{1,0:T(8,128)(2,1)S(1)}, bf16[48,896]{1,0:T(8,128)(2,1)S(1)}, u32[]{:S(2)}, u32[]{:S(2)}) collective-permute-start(bf16[48,896]{1,0:T(8,128)(2,1)S(1)} %get-tuple-element.113), channel_id=1, source_target_pairs={{0,3},{1,2},{2,1},{3,0},{4,7},{5,6},{6,5},{7,4},{8,11},{9,10},{10,... | collective-permute-start | bytes 258056 | tf_op jit(solution)/shard_map/ppermute | solution.py:53
  57.7 14.4 %collective-permute-start.20 = (bf16[48,896]{1,0:T(8,128)(2,1)S(1)}, bf16[48,896]{1,0:T(8,128)(2,1)S(1)}, u32[]{:S(2)}, u32[]{:S(2)}) collective-permute-start(bf16[48,896]{1,0:T(8,128)(2,1)S(1)} %base_order.1.refs_3_.refs_0_.refs_2_), channel_id=1, source_target_pairs={{1,0},{0,1},{3,2},{2,3},{5,4},{4,5},{7,6},{6,7},{9,8},{8,9},{11,10... | collective-permute-start | bytes 258056 | tf_op jit(solution)/shard_map/ppermute | solution.py:45
  60.5 16.4 %collective-permute-start.21 = (bf16[48,896]{1,0:T(8,128)(2,1)S(1)}, bf16[48,896]{1,0:T(8,128)(2,1)S(1)}, u32[]{:S(2)}, u32[]{:S(2)}) collective-permute-start(bf16[48,896]{1,0:T(8,128)(2,1)S(1)} %base_order.1.refs_3_.refs_0_.refs_2_), channel_id=1, source_target_pairs={{2,0},{3,1},{0,2},{1,3},{6,4},{7,5},{4,6},{5,7},{10,8},{11,9},{8,1... | collective-permute-start | bytes 258056 | tf_op jit(solution)/shard_map/ppermute | solution.py:45
  61.6 15.3 %collective-permute-start.22 = (bf16[48,896]{1,0:T(8,128)(2,1)S(1)}, bf16[48,896]{1,0:T(8,128)(2,1)S(1)}, u32[]{:S(2)}, u32[]{:S(2)}) collective-permute-start(bf16[48,896]{1,0:T(8,128)(2,1)S(1)} %base_order.1.refs_3_.refs_0_.refs_2_), channel_id=1, source_target_pairs={{3,0},{2,1},{1,2},{0,3},{7,4},{6,5},{5,6},{4,7},{11,8},{10,9},{9,1... | collective-permute-start | bytes 258056 | tf_op jit(solution)/shard_map/ppermute | solution.py:45
  71.5 10.8 %collective-permute-start.16 = (bf16[48,896]{1,0:T(8,128)(2,1)S(1)}, bf16[48,896]{1,0:T(8,128)(2,1)S(1)}, u32[]{:S(2)}, u32[]{:S(2)}) collective-permute-start(bf16[48,896]{1,0:T(8,128)(2,1)S(1)} %get-tuple-element.114.refs_3_.refs_1_.refs_0_.refs_5_.refs_11_), channel_id=1, source_target_pairs={{1,0},{0,1},{3,2},{2,3},{5,4},{4,5},{7,6},{6,7},{9,8},{8,9},{11,10... | collective-permute-start | bytes 258056 | tf_op jit(solution)/shard_map/ppermute | solution.py:45
  72.1 10.2 %collective-permute-start.17 = (bf16[48,896]{1,0:T(8,128)(2,1)S(1)}, bf16[48,896]{1,0:T(8,128)(2,1)S(1)}, u32[]{:S(2)}, u32[]{:S(2)}) collective-permute-start(bf16[48,896]{1,0:T(8,128)(2,1)S(1)} %get-tuple-element.114.refs_3_.refs_1_.refs_0_.refs_5_.refs_11_), channel_id=1, source_target_pairs={{2,0},{3,1},{0,2},{1,3},{6,4},{7,5},{4,6},{5,7},{10,8},{11,9},{8,1... | collective-permute-start | bytes 258056 | tf_op jit(solution)/shard_map/ppermute | solution.py:45
  73.7 8.6 %collective-permute-start.18 = (bf16[48,896]{1,0:T(8,128)(2,1)S(1)}, bf16[48,896]{1,0:T(8,128)(2,1)S(1)}, u32[]{:S(2)}, u32[]{:S(2)}) collective-permute-start(bf16[48,896]{1,0:T(8,128)(2,1)S(1)} %get-tuple-element.114.refs_3_.refs_1_.refs_0_.refs_5_.refs_11_), channel_id=1, source_target_pairs={{3,0},{2,1},{1,2},{0,3},{7,4},{6,5},{5,6},{4,7},{11,8},{10,9},{9,1... | collective-permute-start | bytes 258056 | tf_op jit(solution)/shard_map/ppermute | solution.py:45
  77.0 5.3 %copy-start.4 = (s32[2]{0:T(128)S(1)}, s32[2]{0:T(128)}, u32[]{:S(2)}) copy-start(s32[2]{0:T(128)} %pad_add_fusion.refs_0_) | copy-start | bytes 28
  81.6 8.7 %collective-permute-start.24 = (bf16[48,1536]{1,0:T(8,128)(2,1)S(1)}, bf16[48,1536]{1,0:T(8,128)(2,1)S(1)}, u32[]{:S(2)}, u32[]{:S(2)}) collective-permute-start(bf16[48,1536]{1,0:T(8,128)(2,1)S(1)} %get-tuple-element.128), channel_id=1, source_target_pairs={{0,4},{4,0},{1,5},{5,1},{2,6},{6,2},{3,7},{7,3},{8,12},{12,8},{9,1... | collective-permute-start | bytes 442376 | tf_op jit(solution)/shard_map/ppermute | solution.py:19
  86.5 4.8 %collective-permute-start.23 = (bf16[48,1152]{1,0:T(8,128)(2,1)S(1)}, bf16[48,1152]{1,0:T(8,128)(2,1)S(1)}, u32[]{:S(2)}, u32[]{:S(2)}) collective-permute-start(bf16[48,1152]{1,0:T(8,128)(2,1)S(1)} %get-tuple-element.127.refs_5_), channel_id=1, source_target_pairs={{0,4},{4,0},{1,5},{5,1},{2,6},{6,2},{3,7},{7,3},{8,12},{12,8},{9,1... | collective-permute-start | bytes 331784 | tf_op jit(solution)/shard_map/ppermute | solution.py:19
  95.9 11.5 %collective-permute-start.25 = (bf16[48,896]{1,0:T(8,128)(2,1)S(1)}, bf16[48,896]{1,0:T(8,128)(2,1)S(1)}, u32[]{:S(2)}, u32[]{:S(2)}) collective-permute-start(bf16[48,896]{1,0:T(8,128)(2,1)S(1)} %get-tuple-element.134), channel_id=1, source_target_pairs={{0,1},{1,0},{2,3},{3,2},{4,5},{5,4},{6,7},{7,6},{8,9},{9,8},{10,11... | collective-permute-start | bytes 258056 | tf_op jit(solution)/shard_map/ppermute | solution.py:53
  96.0 11.5 %collective-permute-start.26 = (bf16[48,896]{1,0:T(8,128)(2,1)S(1)}, bf16[48,896]{1,0:T(8,128)(2,1)S(1)}, u32[]{:S(2)}, u32[]{:S(2)}) collective-permute-start(bf16[48,896]{1,0:T(8,128)(2,1)S(1)} %get-tuple-element.135), channel_id=1, source_target_pairs={{0,2},{1,3},{2,0},{3,1},{4,6},{5,7},{6,4},{7,5},{8,10},{9,11},{10,... | collective-permute-start | bytes 258056 | tf_op jit(solution)/shard_map/ppermute | solution.py:53
  98.1 9.4 %collective-permute-start.27 = (bf16[48,896]{1,0:T(8,128)(2,1)S(1)}, bf16[48,896]{1,0:T(8,128)(2,1)S(1)}, u32[]{:S(2)}, u32[]{:S(2)}) collective-permute-start(bf16[48,896]{1,0:T(8,128)(2,1)S(1)} %get-tuple-element.136), channel_id=1, source_target_pairs={{0,3},{1,2},{2,1},{3,0},{4,7},{5,6},{6,5},{7,4},{8,11},{9,10},{10,... | collective-permute-start | bytes 258056 | tf_op jit(solution)/shard_map/ppermute | solution.py:53
  100.4 7.1 %collective-permute-start.28 = (bf16[48,512]{1,0:T(8,128)(2,1)S(1)}, bf16[48,512]{1,0:T(8,128)(2,1)S(1)}, u32[]{:S(2)}, u32[]{:S(2)}) collective-permute-start(bf16[48,512]{1,0:T(8,128)(2,1)S(1)} %get-tuple-element.138), channel_id=1, source_target_pairs={{0,4},{4,0},{1,5},{5,1},{2,6},{6,2},{3,7},{7,3},{8,12},{12,8},{9,1... | collective-permute-start | bytes 147464 | tf_op jit(solution)/shard_map/ppermute | solution.py:19
  108.6 39.7 %collective-permute-start.29 = (bf16[128,7168]{1,0:T(8,128)(2,1)S(1)}, bf16[128,7168]{1,0:T(8,128)(2,1)S(1)}, u32[]{:S(2)}, u32[]{:S(2)}) collective-permute-start(bf16[128,7168]{1,0:T(8,128)(2,1)S(1)} %get-tuple-element.140), channel_id=1, source_target_pairs={{0,24},{8,0},{16,8},{24,16},{1,25},{9,1},{17,9},{25,17},{2,26},{10... | collective-permute-start | bytes 5505032 | tf_op jit(solution)/shard_map/ppermute | solution.py:19
  108.9 5.1 %collective-permute-start.30 = (bf16[6,3584]{1,0:T(8,128)(2,1)S(1)}, bf16[6,3584]{1,0:T(8,128)(2,1)S(1)}, u32[]{:S(2)}, u32[]{:S(2)}) collective-permute-start(bf16[6,3584]{1,0:T(8,128)(2,1)S(1)} %get-tuple-element.144), channel_id=1, source_target_pairs={{0,4},{4,0},{1,5},{5,1},{2,6},{6,2},{3,7},{7,3},{8,12},{12,8},{9,1... | collective-permute-start | bytes 129032 | tf_op jit(solution)/shard_map/ppermute | solution.py:19
  109.6 9.1 %collective-permute-start.31 = (bf16[48,896]{1,0:T(8,128)(2,1)S(1)}, bf16[48,896]{1,0:T(8,128)(2,1)S(1)}, u32[]{:S(2)}, u32[]{:S(2)}) collective-permute-start(bf16[48,896]{1,0:T(8,128)(2,1)S(1)} %get-tuple-element.139.refs_13_.refs_0_.refs_7_), channel_id=1, source_target_pairs={{1,0},{0,1},{3,2},{2,3},{5,4},{4,5},{7,6},{6,7},{9,8},{8,9},{11,10... | collective-permute-start | bytes 258056 | tf_op jit(solution)/shard_map/ppermute | solution.py:45
  109.6 10.0 %collective-permute-start.32 = (bf16[48,896]{1,0:T(8,128)(2,1)S(1)}, bf16[48,896]{1,0:T(8,128)(2,1)S(1)}, u32[]{:S(2)}, u32[]{:S(2)}) collective-permute-start(bf16[48,896]{1,0:T(8,128)(2,1)S(1)} %get-tuple-element.139.refs_13_.refs_0_.refs_7_), channel_id=1, source_target_pairs={{2,0},{3,1},{0,2},{1,3},{6,4},{7,5},{4,6},{5,7},{10,8},{11,9},{8,1... | collective-permute-start | bytes 258056 | tf_op jit(solution)/shard_map/ppermute | solution.py:45
  111.7 7.9 %collective-permute-start.33 = (bf16[48,896]{1,0:T(8,128)(2,1)S(1)}, bf16[48,896]{1,0:T(8,128)(2,1)S(1)}, u32[]{:S(2)}, u32[]{:S(2)}) collective-permute-start(bf16[48,896]{1,0:T(8,128)(2,1)S(1)} %get-tuple-element.139.refs_13_.refs_0_.refs_7_), channel_id=1, source_target_pairs={{3,0},{2,1},{1,2},{0,3},{7,4},{6,5},{5,6},{4,7},{11,8},{10,9},{9,1... | collective-permute-start | bytes 258056 | tf_op jit(solution)/shard_map/ppermute | solution.py:45
  122.0 4.6 %collective-permute-start.35 = (bf16[48,640]{1,0:T(8,128)(2,1)S(1)}, bf16[48,640]{1,0:T(8,128)(2,1)S(1)}, u32[]{:S(2)}, u32[]{:S(2)}) collective-permute-start(bf16[48,640]{1,0:T(8,128)(2,1)S(1)} %get-tuple-element.151.refs_11_), channel_id=1, source_target_pairs={{0,4},{4,0},{1,5},{5,1},{2,6},{6,2},{3,7},{7,3},{8,12},{12,8},{9,1... | collective-permute-start | bytes 184328 | tf_op jit(solution)/shard_map/ppermute | solution.py:19
  125.1 10.6 %collective-permute-start.39 = (f32[4,3584]{1,0:T(4,128)S(1)}, f32[4,3584]{1,0:T(4,128)S(1)}, u32[]{:S(2)}, u32[]{:S(2)}) collective-permute-start(f32[4,3584]{1,0:T(4,128)S(1)} %get-tuple-element.168), channel_id=1, source_target_pairs={{0,4},{4,0},{1,5},{5,1},{2,6},{6,2},{3,7},{7,3},{8,12},{12,8},{9,1... | collective-permute-start | bytes 172040 | tf_op jit(solution)/shard_map/ppermute | solution.py:19
  131.2 9.1 %collective-permute-start.36 = (bf16[48,896]{1,0:T(8,128)(2,1)S(1)}, bf16[48,896]{1,0:T(8,128)(2,1)S(1)}, u32[]{:S(2)}, u32[]{:S(2)}) collective-permute-start(bf16[48,896]{1,0:T(8,128)(2,1)S(1)} %get-tuple-element.165), channel_id=1, source_target_pairs={{0,1},{1,0},{2,3},{3,2},{4,5},{5,4},{6,7},{7,6},{8,9},{9,8},{10,11... | collective-permute-start | bytes 258056 | tf_op jit(solution)/shard_map/ppermute | solution.py:53
  132.6 7.8 %collective-permute-start.37 = (bf16[48,896]{1,0:T(8,128)(2,1)S(1)}, bf16[48,896]{1,0:T(8,128)(2,1)S(1)}, u32[]{:S(2)}, u32[]{:S(2)}) collective-permute-start(bf16[48,896]{1,0:T(8,128)(2,1)S(1)} %get-tuple-element.166), channel_id=1, source_target_pairs={{0,2},{1,3},{2,0},{3,1},{4,6},{5,7},{6,4},{7,5},{8,10},{9,11},{10,... | collective-permute-start | bytes 258056 | tf_op jit(solution)/shard_map/ppermute | solution.py:53
  133.4 7.0 %collective-permute-start.38 = (bf16[48,896]{1,0:T(8,128)(2,1)S(1)}, bf16[48,896]{1,0:T(8,128)(2,1)S(1)}, u32[]{:S(2)}, u32[]{:S(2)}) collective-permute-start(bf16[48,896]{1,0:T(8,128)(2,1)S(1)} %get-tuple-element.167), channel_id=1, source_target_pairs={{0,3},{1,2},{2,1},{3,0},{4,7},{5,6},{6,5},{7,4},{8,11},{9,10},{10,... | collective-permute-start | bytes 258056 | tf_op jit(solution)/shard_map/ppermute | solution.py:53
  135.7 9.7 %collective-permute-start.34 = (bf16[6,7296]{1,0:T(8,128)(2,1)S(1)}, bf16[6,7296]{1,0:T(8,128)(2,1)S(1)}, u32[]{:S(2)}, u32[]{:S(2)}) collective-permute-start(bf16[6,7296]{1,0:T(8,128)(2,1)S(1)} %get-tuple-element.152), channel_id=1, source_target_pairs={{0,24},{8,0},{16,8},{24,16},{1,25},{9,1},{17,9},{25,17},{2,26},{10... | collective-permute-start | bytes 262664 | tf_op jit(solution)/shard_map/ppermute | solution.py:19
  141.6 4.7 %collective-permute-start.40 = (bf16[6,3584]{1,0:T(8,128)(2,1)S(1)}, bf16[6,3584]{1,0:T(8,128)(2,1)S(1)}, u32[]{:S(2)}, u32[]{:S(2)}) collective-permute-start(bf16[6,3584]{1,0:T(8,128)(2,1)S(1)} %get-tuple-element.174), channel_id=1, source_target_pairs={{0,24},{4,28},{8,0},{12,4},{16,8},{20,12},{24,16},{28,20},{1,25},{... | collective-permute-start | bytes 129032 | tf_op jit(solution)/shard_map/ppermute | solution.py:29
  142.9 5.4 %collective-permute-start.41 = (bf16[6,3584]{1,0:T(8,128)(2,1)S(1)}, bf16[6,3584]{1,0:T(8,128)(2,1)S(1)}, u32[]{:S(2)}, u32[]{:S(2)}) collective-permute-start(bf16[6,3584]{1,0:T(8,128)(2,1)S(1)} %get-tuple-element.175), channel_id=1, source_target_pairs={{0,28},{4,24},{8,4},{12,0},{16,12},{20,8},{24,20},{28,16},{1,29},{... | collective-permute-start | bytes 129032 | tf_op jit(solution)/shard_map/ppermute | solution.py:29
  143.9 7.3 %collective-permute-start.42 = (f32[4,896]{1,0:T(4,128)S(1)}, f32[4,896]{1,0:T(4,128)S(1)}, u32[]{:S(2)}, u32[]{:S(2)}) collective-permute-start(f32[4,896]{1,0:T(4,128)S(1)} %get-tuple-element.179), channel_id=1, source_target_pairs={{0,1},{1,0},{2,3},{3,2},{4,5},{5,4},{6,7},{7,6},{8,9},{9,8},{10,11... | collective-permute-start | bytes 43016 | tf_op jit(solution)/shard_map/ppermute | solution.py:53
  145.4 5.8 %collective-permute-start.43 = (f32[4,896]{1,0:T(4,128)S(1)}, f32[4,896]{1,0:T(4,128)S(1)}, u32[]{:S(2)}, u32[]{:S(2)}) collective-permute-start(f32[4,896]{1,0:T(4,128)S(1)} %get-tuple-element.180), channel_id=1, source_target_pairs={{0,2},{1,3},{2,0},{3,1},{4,6},{5,7},{6,4},{7,5},{8,10},{9,11},{10,... | collective-permute-start | bytes 43016 | tf_op jit(solution)/shard_map/ppermute | solution.py:53
  146.3 5.5 %collective-permute-start.44 = (f32[4,896]{1,0:T(4,128)S(1)}, f32[4,896]{1,0:T(4,128)S(1)}, u32[]{:S(2)}, u32[]{:S(2)}) collective-permute-start(f32[4,896]{1,0:T(4,128)S(1)} %get-tuple-element.181), channel_id=1, source_target_pairs={{0,3},{1,2},{2,1},{3,0},{4,7},{5,6},{6,5},{7,4},{8,11},{9,10},{10,... | collective-permute-start | bytes 43016 | tf_op jit(solution)/shard_map/ppermute | solution.py:53

commit v3 on v2

--- a/solution.py
+++ b/solution.py
@@ -69,6 +69,10 @@
     return lax.broadcasted_iota(jnp.int32, shape, dim)
 
 
+def seq_place():
+    return lax.axis_index("seq").astype(jnp.int32)
+
+
 def token_column(token, depth):
     capacity = token.shape[3]
     out = jnp.full((capacity, 1), token[0, 0, depth, 0], jnp.int32)
@@ -86,7 +90,7 @@
 
 
 def live_column(count, depth, capacity):
-    return (iota((capacity, 1), 0) < count[0, 0, depth, 0]).astype(f32)
+    return (iota((capacity, 1), 0) < count[depth]).astype(f32)
 
 
 def met_column(token, count):
@@ -94,7 +98,7 @@
     second = token_column(token, 1)
     out = jnp.zeros((capacity, 1), f32)
     for c in range(capacity):
-        out += ((second == token[0, 0, 0, c]) & (c < count[0, 0, 0, 0])).astype(f32)
+        out += ((second == token[0, 0, 0, c]) & (c < count[0])).astype(f32)
     return jnp.minimum(out, 1.0)
 
 
@@ -248,35 +252,37 @@
     )(*[in_hbm(a) for a in small], *args, *[in_hbm(a) for a in far], *after)
 
 
-def fetch(weight_ref, depth, kinds, buffer, sems, parts):
-    step = weight_ref.shape[2] // parts
-    copies = [
-        [
-            pltpu.make_async_copy(
-                weight_ref.at[depth, kind, pl.ds(g * step, step)], buffer.at[g, k], sems.at[g, k]
-            )
-            for k, kind in enumerate(kinds)
-        ]
-        for g in range(parts)
-    ]
-    for row in copies:
-        for copy in row:
-            copy.start()
-    return copies
-
-
-def fetched(weight, kinds, parts):
-    hidden = weight.shape[3]
-    return [
-        pltpu.VMEM((parts, len(kinds), weight.shape[2] // parts, hidden), bf16),
-        pltpu.SemaphoreType.DMA((parts, len(kinds))),
-    ]
-
-
-def project(name, blocks, weight, depth, kinds, parts, others=None, select=None, gain=None, mates=None, after=()):
+def held(name, weight, depth, after=()):
+    _, kinds, width, hidden = weight.shape
+
+    def body(*refs):
+        weight_ref, out_ref, tick_ref, sem = refs[0], *refs[-3:]
+        copy = pltpu.make_async_copy(weight_ref.at[depth], out_ref, sem)
+        copy.start()
+        tick_ref[...] = jnp.zeros_like(tick_ref)
+        copy.wait()
+
+    return pl.pallas_call(
+        body,
+        name=name,
+        in_specs=[anywhere] * (1 + len(after)),
+        out_specs=[vmem] * 2,
+        out_shape=[
+            jax.ShapeDtypeStruct((kinds, width, hidden), bf16),
+            jax.ShapeDtypeStruct((8, lanes), f32),
+        ],
+        scratch_shapes=[pltpu.SemaphoreType.DMA],
+        compiler_params=pltpu.CompilerParams(vmem_limit_bytes=2 << 20),
+        cost_estimate=pl.CostEstimate(
+            flops=0, bytes_accessed=4 * kinds * width * hidden, transcendentals=0
+        ),
+    )(in_hbm(weight), *after)
+
+
+def project(name, blocks, weight, kinds, parts, others=None, select=None, gain=None, mates=None, after=()):
     groups = len(blocks)
     rows = blocks[0].shape[0] // parts
-    width, hidden = weight.shape[2:]
+    width, hidden = weight.shape[1:]
     step = width // parts
     other_blocks, other_kinds = others if others is not None else ([], ())
     first_kinds, kinds = kinds, kinds + other_kinds
@@ -286,7 +292,6 @@
 
     def body(*refs):
         refs = list(refs)
-        where_ref = refs.pop(0) if select is not None else None
         x_refs, w_ref, refs = refs[:groups], refs[groups], refs[groups + 1 :]
         other_refs, refs = refs[: len(other_blocks)], refs[len(other_blocks) :]
         if select is not None:
@@ -296,12 +301,10 @@
         refs = refs[len(after) :]
         own_ref, send_ref = refs.pop(0), refs.pop(0)
         kept_ref = refs.pop(0) if select is not None else None
-        buffer, sems = refs
-        copies = fetch(w_ref, depth, kinds, buffer, sems, parts)
         x_all = [r[...] for r in x_refs]
         mate_all = [r[...] for r in mate_refs] if mates is not None else x_all
         if select is not None:
-            gain_all = piece_of(gain_ref[1, 0:1, :], where_ref[0], gain.shape[2] // width, 0)
+            gain_all = piece_of(gain_ref[1, 0:1, :], seq_place(), gain.shape[2] // width, 0)
         sums = [jnp.zeros((total, hidden), f32) for _ in kinds]
         mark = jnp.zeros((total, 1), f32)
         for g in range(parts):
@@ -316,8 +319,8 @@
             for k in range(len(kinds)):
                 if k == len(first_kinds):
                     x = column_part([r[...] for r in other_refs], rows, g)[:, :step]
-                copies[g][k].wait()
-                sums[k] += jnp.dot(x, buffer[g, k], preferred_element_type=f32)
+                part_ref = w_ref.at[kinds[k], pl.ds(g * step, step)]
+                sums[k] += jnp.dot(x, part_ref[...], preferred_element_type=f32)
         for k in range(len(kinds)):
             own_ref[:, k * hidden : (k + 1) * hidden] = sums[k]
             send_ref[:, k * hidden : (k + 1) * hidden] = sums[k].astype(bf16)
@@ -325,15 +328,14 @@
             own_ref[:, many:] = in_lanes([mark])
             send_ref[:, many:] = coded(mark).astype(bf16)
 
-    args = list(blocks) + [in_hbm(weight)]
-    args, specs = args + list(other_blocks), [vmem] * groups + [anywhere] + [vmem] * len(other_blocks)
+    args = list(blocks) + [weight]
+    args, specs = args + list(other_blocks), [vmem] * groups + [vmem] + [vmem] * len(other_blocks)
     outs = [
         jax.ShapeDtypeStruct((total, many + extra), f32),
         jax.ShapeDtypeStruct((total, many + extra), bf16),
     ]
     if select is not None:
-        where, table = select
-        args, specs = [where] + args + [table, gain], [smem] + specs + [vmem, vmem]
+        args, specs = args + [select, gain], specs + [vmem, vmem]
         outs.append(jax.ShapeDtypeStruct((total, width), bf16))
     if mates is not None:
         args, specs = args + list(mates), specs + [vmem] * groups
@@ -343,16 +345,15 @@
         in_specs=specs + [anywhere] * len(after),
         out_specs=[vmem] * len(outs),
         out_shape=outs,
-        scratch_shapes=fetched(weight, kinds, parts),
-        compiler_params=pltpu.CompilerParams(vmem_limit_bytes=16 << 20),
+        compiler_params=pltpu.CompilerParams(vmem_limit_bytes=8 << 20),
         cost_estimate=pl.CostEstimate(
             flops=2 * total * width * many, bytes_accessed=2 * width * many, transcendentals=0
         ),
     )(*args, *after)
 
 
-def expand(name, prepare, args, saved, weight, depth, kinds, groups, parts, after=()):
-    width, hidden = weight.shape[2:]
+def expand(name, prepare, args, saved, weight, kinds, groups, parts, after=()):
+    width, hidden = weight.shape[1:]
     total = saved[0][0][0]
     rows, step = total // groups, width // parts
     count, kept = len(args), len(saved)
@@ -360,17 +361,16 @@
     def body(*refs):
         in_refs, w_ref = refs[:count], refs[count]
         refs = refs[count + 1 + len(after) :]
-        saved_refs, out_refs, (buffer, sems) = refs[:kept], refs[kept:-2], refs[-2:]
-        copies = fetch(w_ref, depth, kinds, buffer, sems, parts)
+        saved_refs, out_refs = refs[:kept], refs[kept:]
         for ref, value in zip(saved_refs, prepare(*[r[...] for r in in_refs])):
             ref[...] = value.astype(ref.dtype)
         out = []
         for g in range(parts):
             part = jnp.zeros((total, step), f32)
             for k in range(len(kinds)):
-                copies[g][k].wait()
+                part_ref = w_ref.at[kinds[k], pl.ds(g * step, step)]
                 part += lax.dot_general(
-                    saved_refs[k][...], buffer[g, k], (((1,), (1,)), ((), ())),
+                    saved_refs[k][...], part_ref[...], (((1,), (1,)), ((), ())),
                     preferred_element_type=f32,
                 )
             out.append(part)
@@ -381,18 +381,17 @@
     results = pl.pallas_call(
         body,
         name=name,
-        in_specs=[vmem] * count + [anywhere] * (1 + len(after)),
+        in_specs=[vmem] * (count + 1) + [anywhere] * len(after),
         out_specs=[vmem] * (kept + groups),
         out_shape=[jax.ShapeDtypeStruct(shape, kind) for shape, kind in saved]
         + [jax.ShapeDtypeStruct((rows * parts, step), bf16)] * groups,
-        scratch_shapes=fetched(weight, kinds, parts),
-        compiler_params=pltpu.CompilerParams(vmem_limit_bytes=16 << 20),
+        compiler_params=pltpu.CompilerParams(vmem_limit_bytes=8 << 20),
         cost_estimate=pl.CostEstimate(
             flops=2 * total * width * hidden * len(kinds),
             bytes_accessed=2 * width * hidden * len(kinds),
             transcendentals=0,
         ),
-    )(*args, in_hbm(weight), *after)
+    )(*args, weight, *after)
     return results[:kept], results[kept:]
 
 
@@ -498,7 +497,7 @@
             keep = jnp.ones((step, 1), f32)
             for k in range(2):
                 for c in range(capacity):
-                    out = (here == token_ref[0, 0, k, c]) & (c < count_ref[0, 0, k, 0])
+                    out = (here == token_ref[0, 0, k, c]) & (c < count_ref[k])
                     keep = jnp.where(out, 0.0, keep)
 
             def ahead(at, hot):
@@ -590,8 +589,8 @@
     share = width // groups
     hidden_units = expert_weight.shape[3]
     parts = folds(rows, width)
-    where = jnp.stack([lax.axis_index("seq"), lax.axis_index("dp")]).astype(jnp.int32)
     source, embed, cot = main_hidden[0, 0], embedded[0, 0], cotangent[0, 0]
+    slot_count = slot_count.reshape(-1)
     facts = (slot_token, slot_count)
     packed = ((rows * parts, width // parts), bf16)
     part_rows = ((rows, width), f32)
@@ -601,7 +600,7 @@
 
     asked_token = ring(slot_token, "section", -1)
 
-    def own_rows(where, token, count, gate, embed, cot):
+    def own_rows(token, count, gate, embed, cot):
         first, second = token_column(token, 0), token_column(token, 1)
         live_1, live_2 = (live_column(count, k, slots) for k in range(2))
         weight_1, weight_2 = gate_column(gate, 0) * live_1, gate_column(gate, 1) * live_2
@@ -624,7 +623,7 @@
         ]
         return [
             jnp.concatenate([jnp.concatenate([piece, notes], 1)] + heads, 0)
-            for piece in pieces_of(block, where[0], seqs)
+            for piece in pieces_of(block, seq_place(), seqs)
         ] + [dout]
 
     fine = width // parts + lanes
@@ -632,15 +631,15 @@
         "own_rows", own_rows,
         [((3 * slots + depths * seqs, width + lanes), bf16)] * seqs
         + [((slots * parts * seqs, fine), bf16)],
-        (where, slot_token, slot_count, route_gate), far=(embed, cot), after=(asked_token,),
+        (slot_token, slot_count, route_gate), far=(embed, cot), after=(asked_token,),
     )
     own_got = trade_seq(own_sent)
 
-    def source_rows(where, asked, source):
+    def source_rows(asked, source):
         first = pick(token_column(asked, 0), source)
         second = pick(token_column(asked, 1), source)
         scale = coded(inv_rms(first))
-        sent = [jnp.concatenate([p, scale], 1) for p in pieces_of(first, where[0], seqs)]
+        sent = [jnp.concatenate([p, scale], 1) for p in pieces_of(first, seq_place(), seqs)]
         sent[0] = jnp.concatenate([sent[0], second], 1)
         return sent + [first]
 
@@ -649,21 +648,49 @@
         [((slots, width + lanes + features), bf16)]
         + [((slots, width + lanes), bf16)] * (seqs - 1)
         + [((slots, features), bf16)],
-        (where, asked_token), source, after=(own_sent[0],),
+        (asked_token,), source, after=(own_sent[0],),
     )
     start_got = trade_seq(sent, 1)
     dout_2, _ = lax.optimization_barrier((dout_2, sent[0]))
     dout_2_got = gather_dp(dout_2)
 
-    def first_mixed(where, gain, *got):
+    def second_base(token, count, start, table, got, gain):
+        after = got[3 * slots :, :width].astype(f32)
+        after = jnp.concatenate([after[p * depths : (p + 1) * depths] for p in range(seqs)], 1)
+        after = jnp.where(seq_place() == seqs - 1, 0.0, after)
+        after = jnp.concatenate([after, jnp.zeros((16 - depths, features), f32)], 0).astype(bf16)
+        second = token_column(token, 1)
+        start = start[:, width + lanes :].astype(f32)
+        ahead_1 = pick_ahead(second + 1, table, after)
+        ahead_2 = pick_ahead(second + 2, table, after)
+        unit = start * inv_rms(start)
+        mixed = unit * gain[0, 0:1] + ahead_1 * inv_rms(ahead_1) * gain[0, 1:2]
+        mixed = mixed.astype(bf16).astype(f32)
+        own = mixed * inv_rms(mixed) * gain[1, 0:1] * (1.0 - met_column(token, count))
+        out = (own + ahead_2 * inv_rms(ahead_2) * gain[1, 1:2]) * live_column(count, 1, slots)
+        bases = [folded(piece, parts) for piece in pieces_of(out, seq_place(), seqs)]
+        return bases + [after, ahead_1, ahead_2]
+
+    *base_sent, next_rows, ahead_21, ahead_22 = call(
+        "second_base", second_base,
+        [((slots * parts, width // parts), bf16)] * seqs
+        + [((16, features), bf16)]
+        + [((slots, features), bf16)] * 2,
+        facts, start_got[0], embed, own_got[-1], norm_gain, after=(start_got[-1],),
+    )
+    base_got = trade_seq(base_sent)
+
+    weight_1st, tick_a = held("held_1", expert_weight, 0, after=(sent[0],))
+
+    def first_mixed(gain, *got):
         start_got, dout = got[:seqs], [g.astype(f32) for g in got[2 * seqs :]]
         got = [g.astype(f32) for g in got[seqs : 2 * seqs]]
         first = 3 * slots
         block_1, block_2, block_3 = (
-            in_order([g[k * slots : (k + 1) * slots] for g in got], where[0], 0) for k in range(3)
+            in_order([g[k * slots : (k + 1) * slots] for g in got], seq_place(), 0) for k in range(3)
         )
         facts = block_3[:, width:]
-        heads = in_order([g[first:] for g in got], where[0], 0)
+        heads = in_order([g[first:] for g in got], seq_place(), 0)
         heads = [heads[j * depths * seqs : (j + 1) * depths * seqs] for j in range(seqs)]
         units = []
         for k, block in ((1, block_1), (2, block_2)):
@@ -676,55 +703,26 @@
                     row = heads[j + 1][i : i + 1]
                     for p in range(1, seqs):
                         at = p * depths + i
-                        row = jnp.where(where[0] == p, heads[j + 1][at : at + 1], row)
+                        row = jnp.where(seq_place() == p, heads[j + 1][at : at + 1], row)
                     row = row[:, :width] * decoded(row[:, width:])
                     add += jnp.where(token == float(tokens + i - k), row, 0.0)
                 after.append(add)
             units.append(unit + jnp.concatenate(after, 0))
-        follow = got[-1][first:, :width]
-        follow = jnp.concatenate([follow[p * depths : (p + 1) * depths] for p in range(seqs)], 1)
-        follow = jnp.where(where[0] == seqs - 1, 0.0, follow)
-        follow = jnp.concatenate([follow, jnp.zeros((16 - depths, features), f32)], 0)
-        start = in_order([g[:, : width + lanes].astype(f32) for g in start_got], where[0], 0)
+        start = in_order([g[:, : width + lanes].astype(f32) for g in start_got], seq_place(), 0)
         unit = start[:, :width] * decoded(start[:, width:])
-        gain_h, gain_e = (piece_of(gain[0, k : k + 1], where[0], seqs, 0) for k in range(2))
+        gain_h, gain_e = (piece_of(gain[0, k : k + 1], seq_place(), seqs, 0) for k in range(2))
         mixed = (unit * gain_h + units[0] * gain_e).astype(bf16).astype(f32)
-        douts = zip(*(blocks_of(block, where[0], seqs) for block in dout))
+        douts = zip(*(blocks_of(block, seq_place(), seqs) for block in dout))
         douts = [jnp.concatenate(blocks, 0) for blocks in douts]
-        return payload(mixed * facts[:, 2:3]), unit, *units, block_3[:, :width], facts, follow, *douts
-
-    rows_1, unit_1, unit_e1, unit_e2, cot_1, own_facts, next_rows, *dout_2_sent = call(
+        return payload(mixed * facts[:, 2:3]), unit, *units, block_3[:, :width], facts, *douts
+
+    rows_1, unit_1, unit_e1, unit_e2, cot_1, own_facts, *dout_2_sent = call(
         "first_mixed", first_mixed,
-        [packed] + [part_rows] * 4 + [((rows, lanes), f32), ((16, features), bf16)]
+        [packed] + [part_rows] * 4 + [((rows, lanes), f32)]
         + [((groups * slots * parts, fine), bf16)] * seqs,
-        (where,), norm_gain, *start_got, *own_got, *dout_2_got,
+        (), norm_gain, *start_got, *own_got, *dout_2_got, after=(ahead_21, tick_a),
     )
     rows_1_all = gather_dp(rows_1)
-
-    def second_base(where, token, count, start, table, after, gain):
-        second = token_column(token, 1)
-        start = start[:, width + lanes :].astype(f32)
-        ahead_1 = pick_ahead(second + 1, table, after)
-        ahead_2 = pick_ahead(second + 2, table, after)
-        unit = start * inv_rms(start)
-        mixed = unit * gain[0, 0:1] + ahead_1 * inv_rms(ahead_1) * gain[0, 1:2]
-        mixed = mixed.astype(bf16).astype(f32)
-        own = mixed * inv_rms(mixed) * gain[1, 0:1] * (1.0 - met_column(token, count))
-        out = (own + ahead_2 * inv_rms(ahead_2) * gain[1, 1:2]) * live_column(count, 1, slots)
-        bases = [folded(piece, parts) for piece in pieces_of(out, where[0], seqs)]
-        return bases + [ahead_1, ahead_2]
-
-    *base_sent, ahead_21, ahead_22 = call(
-        "second_base", second_base,
-        [((slots * parts, width // parts), bf16)] * seqs + [((slots, features), bf16)] * 2,
-        (where, *facts), start_got[0], embed, next_rows, norm_gain, after=(rows_1,),
-    )
-    base_got = trade_seq(base_sent)
-
-    first_own, first_send = project(
-        "gate_up_1", rows_1_all, expert_weight, 0, (0, 1), parts, after=(ahead_21, base_got[-1])
-    )
-    first = pair_seq(first_own, first_send)
 
     def by_slots(got, place):
         blocks = [from_block(got, place, j) for j in range(seqs)]
@@ -732,10 +730,16 @@
         return jnp.concatenate(pairs, 0)
 
     (base_2,) = call(
-        "base_order", lambda where, *got: [by_slots([g.astype(f32) for g in got], where[0])], [packed],
-        (where,), *base_got, after=(first_send,),
+        "base_order", lambda *got: [by_slots([g.astype(f32) for g in got], seq_place())], [packed],
+        (), *base_got, after=(rows_1,),
     )
     base_2_all = gather_dp(base_2)
+
+    weight_2nd, tick_b = held("held_2", expert_weight, 1, after=(rows_1,))
+    first_own, first_send = project(
+        "gate_up_1", rows_1_all, weight_1st, (0, 1), parts, after=(base_2, tick_b)
+    )
+    first = pair_seq(first_own, first_send)
 
     def forward_1(own, other):
         both = own + other.astype(f32)
@@ -745,8 +749,9 @@
     (act_1, both_1), out_blocks = expand(
         "down_1", forward_1, first,
         [((total, hidden_units), bf16), ((total, 2 * hidden_units), f32)],
-        expert_weight, 0, (2,), groups, parts, after=(base_2,),
-    )
+        weight_1st, (2,), groups, parts,
+    )
+    out_blocks = lax.optimization_barrier((*out_blocks, *base_2_all))[:groups]
     out_got = return_dp(out_blocks)
 
     hidden, _ = lax.optimization_barrier((source, rows_1))
@@ -769,10 +774,10 @@
     dout_2_sent = lax.optimization_barrier((*dout_2_sent, out_blocks[0]))[:-1]
     dout_2_traded = trade_seq(dout_2_sent)
 
-    def slot_facts(where, *got):
+    def slot_facts(*got):
         got, size = [g.astype(f32) for g in got], slots * parts
         blocks = [
-            by_slots([g[z * size : (z + 1) * size] for g in got], where[0]) for z in range(groups)
+            by_slots([g[z * size : (z + 1) * size] for g in got], seq_place()) for z in range(groups)
         ]
         facts = jnp.concatenate([block[:rows, width // parts :] for block in blocks], 0)
         base = (iota((total, 1), 0) // slots * tokens).astype(f32)
@@ -785,21 +790,21 @@
         "slot_facts", slot_facts,
         [((total, total), f32), ((total, total), bf16), ((rows, rows), f32), ((total, 1), f32)]
         + [((rows * parts, fine), bf16)] * groups,
-        (where,), *dout_2_traded, after=(prev,),
+        (), *dout_2_traded, after=(prev,),
     )
     fixed_own, fixed_send = project(
-        "fixed_2", base_2_all, expert_weight, 1, (0, 1), parts,
+        "fixed_2", base_2_all, weight_2nd, (0, 1), parts,
         others=(dout_2_all, (2,)), after=(same_own,),
     )
     fixed_pair = pair_seq(fixed_own, fixed_send)
 
     mixed_own, mixed_send, chosen = project(
-        "gate_up_2", prev_all, expert_weight, 1, (0, 1), parts,
-        select=(where, same_16), gain=norm_gain, after=(fixed_own,),
+        "gate_up_2", prev_all, weight_2nd, (0, 1), parts,
+        select=same_16, gain=norm_gain, after=(fixed_own,),
     )
     second = pair_seq(mixed_own, mixed_send)
     prev_w_own, prev_w_send = project(
-        "prev_down", prev_all, expert_weight, 0, (2,), parts, after=(mixed_send,)
+        "prev_down", prev_all, weight_1st, (2,), parts, after=(mixed_send,)
     )
     prev_pair = pair_seq(prev_w_own, prev_w_send)
 
@@ -825,26 +830,26 @@
         "back_rows_2", backward_2,
         second + fixed_pair + (same,),
         [units, units, units, ((total, 1), f32), ((total, 1), f32)],
-        expert_weight, 1, (0, 1), groups, parts, after=(prev_w_own,),
+        weight_2nd, (0, 1), groups, parts, after=(prev_w_own,),
     )
     d_rows_got = return_dp(d_rows_blocks)
     dense, dense_terms = dense_rows(
         "dense_b", *facts, hidden, embed, next_rows, cot, norm_gain, dense, 1, 2,
         after=(d_rows_blocks[0],),
     )
-    def first_grad(where, cot, same, gain, *got):
+    def first_grad(cot, same, gain, *got):
         d_rows = summed(got, parts)
         added = lax.dot_general(
             same, d_rows, (((0,), (0,)), ((), ())),
             precision=lax.Precision.HIGHEST, preferred_element_type=f32,
         )
         d_mixed = cot + added
-        u = d_mixed * piece_of(gain[1, 0:1], where[0], seqs, 0)
-        return [payload(u), d_mixed] + blocks_of(d_rows, where[0], seqs)
+        u = d_mixed * piece_of(gain[1, 0:1], seq_place(), seqs, 0)
+        return [payload(u), d_mixed] + blocks_of(d_rows, seq_place(), seqs)
 
     u, d_mixed_2, *d_rows_back = call(
         "first_grad", first_grad, [packed, part_rows] + [((slots, width), bf16)] * seqs,
-        (where,), cot_1, same_own, norm_gain, *d_rows_got, after=(dense_terms, prev_pair[1]),
+        (), cot_1, same_own, norm_gain, *d_rows_got, after=(dense_terms, prev_pair[1]),
     )
     u_all = gather_dp(u)
     dense, _ = lax.optimization_barrier((dense, u))
@@ -864,12 +869,12 @@
     )
 
     back_1_own, back_1_send = project(
-        "back_1", u_all, expert_weight, 0, (2,), parts, mates=prev_all, after=(tick_2,)
+        "back_1", u_all, weight_1st, (2,), parts, mates=prev_all, after=(tick_2,)
     )
     back_1 = pair_seq(back_1_own, back_1_send)
 
-    def second_grad(where, token, count, start, ahead_1, ahead_2, cot, gain, terms, *got):
-        d_rows = in_order([g.astype(f32) for g in got], where[0], 1)
+    def second_grad(token, count, start, ahead_1, ahead_2, cot, gain, terms, *got):
+        d_rows = in_order([g.astype(f32) for g in got], seq_place(), 1)
         keep = live_column(count, 1, slots) * (1.0 - met_column(token, count))
         grad, more = backward_rows(
             start[:, width + lanes :].astype(f32), ahead_1.astype(f32), ahead_2.astype(f32),
@@ -877,12 +882,12 @@
         )
         notes = in_lanes([live_column(count, 0, slots), keep])
         grad = jnp.concatenate([grad.astype(f32), notes], 1)
-        return [grad] + pieces_of(terms + more, where[0], seqs)
+        return [grad] + pieces_of(terms + more, seq_place(), seqs)
 
     grad_2, *terms_parts = call(
         "second_grad", second_grad,
         [((slots, features + lanes), bf16)] + [((2 * depths, width), f32)] * seqs,
-        (where, *facts), start_got[0], ahead_21, ahead_22, cot, norm_gain, dense_terms, *back_got,
+        facts, start_got[0], ahead_21, ahead_22, cot, norm_gain, dense_terms, *back_got,
         after=(back_1_send,),
     )
     grad_2 = ring(grad_2, "section", -1)
@@ -901,7 +906,7 @@
         "back_rows_1", backward_1,
         back_1 + prev_pair + (both_1, scale_2, weight_1),
         [units, units, ((total, 1), f32)],
-        expert_weight, 0, (0, 1), groups, parts, after=(terms_parts[0],),
+        weight_1st, (0, 1), groups, parts, after=(terms_parts[0],),
     )
     d_rows_got = return_dp(d_rows_blocks)
 
@@ -917,10 +922,10 @@
         d_gate_1, d_up_1, act_1, width, parts, weight_grad, after=(d_rows_blocks[0],),
     )
 
-    def last_grad(where, d_mixed_2, prev, scale, through, unit_1, unit_e1, unit_e2, own_facts, gain, *got):
+    def last_grad(d_mixed_2, prev, scale, through, unit_1, unit_e1, unit_e2, own_facts, gain, *got):
         got, terms = got[:groups], got[groups:]
         d_rows = summed(got, parts)
-        gain_1, gain_2 = (piece_of(gain[k, 0:1], where[0], seqs, 0) for k in range(2))
+        gain_1, gain_2 = (piece_of(gain[k, 0:1], seq_place(), seqs, 0) for k in range(2))
         scale, through = scale[:rows], through[:rows]
         live = own_facts[:, 2:3]
         prev = prev.astype(f32)
@@ -937,21 +942,21 @@
             block = sums[:, :share]
             for z in range(groups):
                 at = partner(z, i, groups) * share
-                block = jnp.where(where[1] == z, sums[:, at : at + share], block)
+                block = jnp.where(lax.axis_index("dp") == z, sums[:, at : at + share], block)
             cut.append(block)
-        return cut + blocks_of(d_mixed_1 * gain_1, where[0], seqs)
+        return cut + blocks_of(d_mixed_1 * gain_1, seq_place(), seqs)
 
     last = call(
         "last_grad", last_grad,
         [((2 * depths, share), f32)] * groups + [((slots, width), bf16)] * seqs,
-        (where,), d_mixed_2, prev_own, scale_2, through_1, unit_1, unit_e1, unit_e2,
+        (), d_mixed_2, prev_own, scale_2, through_1, unit_1, unit_e1, unit_e2,
         own_facts, norm_gain, *d_rows_got, *terms_got, after=(tick_1,),
     )
     last_got = trade_seq(last[groups:], -1)
     sums_got = return_dp(last[:groups])
 
-    def finish(where, token, dense, asked_rows, grad_2, *got):
-        part = in_order([g.astype(f32) for g in got], where[0], 1)
+    def finish(token, dense, asked_rows, grad_2, *got):
+        part = in_order([g.astype(f32) for g in got], seq_place(), 1)
         asked_rows = asked_rows.astype(f32)
         scale = inv_rms(asked_rows)
         unit = asked_rows * scale
@@ -982,7 +987,7 @@
 
     hidden_grad, tick = call(
         "finish", finish, [((tokens, features), bf16), ((8, lanes), f32)],
-        (where, asked_token), dense, asked_rows, grad_2, *last_got, limit=20,
+        (asked_token,), dense, asked_rows, grad_2, *last_got, limit=20,
     )
 
     def gain_sum(*got):

time: 153 us -> 134 us (0.88)
  Pallas kernels: 67.5 us -> 55.6 us
  waiting for transfers between devices: 18.5 us -> 15 us
    pallas_call x5, Pallas kernels: 16.9 us -> 6.63 us  [project(): pl.pallas_call(body, name=name, in_specs=specs + [anywhere] * len(after),...]
    pallas_call x12, Pallas kernels: 17.5 us -> 14 us  [call(): pl.pallas_call(body, name=name, out_shape=shapes, in_specs=[smem] * n_sma...]
    ppermute x12, waiting for transfers between devices: 4.3 us -> 1.51 us  [return_dp(): lax.ppermute(blocks[i], 'dp', [(z, partner(z, i, count)) for z in range(c...]
    ppermute x15, starting transfers between devices: 27.6 us -> 25.5 us  [gather_dp(): lax.ppermute(block, 'dp', [(partner(z, i, count), z) for z in range(count)])]
    pallas_call x3 -> x5, Pallas kernels: 12.3 us -> 14.3 us  [the longest x2 8.27 us: held(): pl.pallas_call(body, name=name, in_specs=[anywhere] * (1 + len(after)), o...]
    ppermute x14, waiting for transfers between devices: 6.96 us -> 4.98 us  [ring(): lax.ppermute(value, axis, [(i, (i + steps) % count) for i in range(count)])]
  transfers between devices with their start and end apart: 45 -> 45, of which waited for: 11 -> 9; matrix products, arithmetic and copies ran while one was open for 1% -> 0% of each run, Pallas kernels for 37% -> 36%
where the time goes in v3:
time: 134 us
  starting transfers between devices  62 us (46%)
  Pallas kernels  55.6 us (41%)
  waiting for transfers between devices  15 us (11%)
    ppermute x15, starting transfers between devices, gather_dp(): lax.ppermute(block, 'dp', [(partner(z, i, count), z) for z in range(count)])  25.5 us
    ppermute x12, starting transfers between devices, return_dp(): lax.ppermute(blocks[i], 'dp', [(z, partner(z, i, count)) for z in range(c...  17.7 us
    ppermute x14, starting transfers between devices, ring(): lax.ppermute(value, axis, [(i, (i + steps) % count) for i in range(count)])  16.2 us
    pallas_call x12, Pallas kernels, call(): pl.pallas_call(body, name=name, out_shape=shapes, in_specs=[smem] * n_sma...  14 us
    pallas_call x2, Pallas kernels, dense_rows(): pl.pallas_call(body, name=name, in_specs=[smem] * 2 + [vmem] * (5 + len(e...  11.2 us
    pallas_call x2, Pallas kernels, outer(): pl.pallas_call(body, name=name, in_specs=[vmem] * (count + 3) + [anywhere...  9.4 us
    ppermute x15, waiting for transfers between devices, gather_dp(): lax.ppermute(block, 'dp', [(partner(z, i, count), z) for z in range(count)])  8.54 us
    pallas_call x2, Pallas kernels, held(): pl.pallas_call(body, name=name, in_specs=[anywhere] * (1 + len(after)), o...  8.27 us
  transfers between devices with their start and end apart: 45, of which 9 were waited for; matrix products, arithmetic and copies ran while one was open for 0% of the time, Pallas kernels for 36%

profile of v3, /device:TPU:0, one launch (start us, length us, event | category | flops | bytes accessed | tf_op | source)
XLA Modules:
  0.0 133.7 jit_solution(5876409587256843676)
XLA Ops:
  0.6 2.4 %collective-permute-start = (s32[1,1,2,6]{3,2,1,0:T(2,128)}, s32[1,1,2,6]{3,2,1,0:T(2,128)S(1)}, u32[]{:S(2)}, u32[]{:S(2)}) collective-permute-start(s32[1,1,2,6]{3,2,1,0:T(2,128)} %refs_0_.11), channel_id=1, source_target_pairs={{0,24},{8,0},{16,8},{24,16},{1,25},{9,1},{17,9},{25,17},{2,26},{10... | collective-permute-start | bytes 152 | tf_op jit(solution)/shard_map/ppermute | solution.py:19
  3.1 1.5 %collective-permute-done.refs_5_.refs_0_ = s32[1,1,2,6]{3,2,1,0:T(2,128)S(1)} collective-permute-done((s32[1,1,2,6]{3,2,1,0:T(2,128)}, s32[1,1,2,6]{3,2,1,0:T(2,128)S(1)}, u32[]{:S(2)}, u32[]{:S(2)}) %collective-permute-start) | collective-permute-done | bytes 80 | tf_op jit(solution)/shard_map/ppermute | solution.py:19
  4.6 4.0 %own_rows.1 = (bf16[22,3712]{1,0:T(8,128)(2,1)S(1)}, bf16[22,3712]{1,0:T(8,128)(2,1)S(1)}, bf16[48,1024]{1,0:T(8,128)(2,1)S(1)}) custom-call(s32[1,1,2,6]{3,2,1,0:T(2,128)} %refs_0_.11, s32[2]{0:T(128)} %bitcast.15, f32[1,1,2,6]{3,2,1,0:T(2,128)} %refs_2_.2, bf16[128,7168]{1,0:T(8,128)(2,1)} %bitcast.5, bf16[128,7168]{1,0:T(8,128)(2,1)} %bitcast.9, ...), custom_call_target="tpu_custom_call" | custom-call | bytes 4094976 | tf_op jit(solution)/shard_map/own_rows/pallas_call | solution.py:243
  8.6 1.6 %collective-permute-start.3 = (bf16[22,3712]{1,0:T(8,128)(2,1)S(1)}, bf16[22,3712]{1,0:T(8,128)(2,1)S(1)}, u32[]{:S(2)}, u32[]{:S(2)}) collective-permute-start(bf16[22,3712]{1,0:T(8,128)(2,1)S(1)} %get-tuple-element.104), channel_id=1, source_target_pairs={{0,4},{4,0},{1,5},{5,1},{2,6},{6,2},{3,7},{7,3},{8,12},{12,8},{9,1... | collective-permute-start | bytes 489992 | tf_op jit(solution)/shard_map/ppermute | solution.py:19
  10.2 1.3 source_rows.1
  12.1 1.6 %collective-permute-start.4 = (bf16[48,1024]{1,0:T(8,128)(2,1)S(1)}, bf16[48,1024]{1,0:T(8,128)(2,1)S(1)}, u32[]{:S(2)}, u32[]{:S(2)}) collective-permute-start(bf16[48,1024]{1,0:T(8,128)(2,1)S(1)} %get-tuple-element.106.refs_5_), channel_id=1, source_target_pairs={{1,0},{0,1},{3,2},{2,3},{5,4},{4,5},{7,6},{6,7},{9,8},{8,9},{11,10... | collective-permute-start | bytes 294920 | tf_op jit(solution)/shard_map/ppermute | solution.py:45
  13.7 2.6 %collective-permute-start.5 = (bf16[48,1024]{1,0:T(8,128)(2,1)S(1)}, bf16[48,1024]{1,0:T(8,128)(2,1)S(1)}, u32[]{:S(2)}, u32[]{:S(2)}) collective-permute-start(bf16[48,1024]{1,0:T(8,128)(2,1)S(1)} %get-tuple-element.106.refs_5_), channel_id=1, source_target_pairs={{2,0},{3,1},{0,2},{1,3},{6,4},{7,5},{4,6},{5,7},{10,8},{11,9},{8,1... | collective-permute-start | bytes 294920 | tf_op jit(solution)/shard_map/ppermute | solution.py:45
  16.3 3.4 %collective-permute-start.6 = (bf16[48,1024]{1,0:T(8,128)(2,1)S(1)}, bf16[48,1024]{1,0:T(8,128)(2,1)S(1)}, u32[]{:S(2)}, u32[]{:S(2)}) collective-permute-start(bf16[48,1024]{1,0:T(8,128)(2,1)S(1)} %get-tuple-element.106.refs_5_), channel_id=1, source_target_pairs={{3,0},{2,1},{1,2},{0,3},{7,4},{6,5},{5,6},{4,7},{11,8},{10,9},{9,1... | collective-permute-start | bytes 294920 | tf_op jit(solution)/shard_map/ppermute | solution.py:45
  19.7 4.1 %held_1.1 = (bf16[3,3584,512]{2,1,0:T(8,128)(2,1)S(1)}, f32[8,128]{1,0:T(8,128)S(1)}) custom-call(bf16[2,3,3584,512]{3,2,1,0:T(8,128)(2,1)} %refs_0_.10, bf16[6,10880]{1,0:T(8,128)(2,1)S(1)} %get-tuple-element.102.refs_1_), custom_call_target="tpu_custom_call" | custom-call | bytes 22020096 | tf_op jit(solution)/shard_map/held_1/pallas_call | solution.py:265
  23.9 1.6 %second_base.1 = (bf16[24,896]{1,0:T(8,128)(2,1)S(1)}, bf16[24,896]{1,0:T(8,128)(2,1)S(1)}, bf16[16,7168]{1,0:T(8,128)(2,1)S(1)}, bf16[6,7168]{1,0:T(8,128)(2,1)S(1)}, bf16[6,7168]{1,0:T(8,128)(2,1)S(1)}) custom-call(s32[1,1,2,6]{3,2,1,0:T(2,128)} %refs_0_.11, s32[2]{0:T(128)} %bitcast.16, bf16[6,10880]{1,0:T(8,128)(2,1)S(1)} %collective-permute-done.1.refs_2_.refs_1_, ...), custom_call_target="tpu_custom_call" | custom-call | bytes 2731008 | tf_op jit(solution)/shard_map/second_base/pallas_call | solution.py:243
  26.1 0.9 collective-permute-start.7
  27.1 0.8 collective-permute-start.8
  27.9 1.1 collective-permute-start.9
  29.0 2.5 %collective-permute-start.10 = (bf16[48,896]{1,0:T(8,128)(2,1)S(1)}, bf16[48,896]{1,0:T(8,128)(2,1)S(1)}, u32[]{:S(2)}, u32[]{:S(2)}) collective-permute-start(bf16[48,896]{1,0:T(8,128)(2,1)S(1)} %get-tuple-element.109.refs_2_.refs_1_.refs_0_.refs_3_), channel_id=1, source_target_pairs={{3,0},{2,1},{1,2},{0,3},{7,4},{6,5},{5,6},{4,7},{11,8},{10,9},{9,1... | collective-permute-start | bytes 258056 | tf_op jit(solution)/shard_map/ppermute | solution.py:45
  31.5 1.5 %collective-permute-start.11 = (bf16[24,896]{1,0:T(8,128)(2,1)S(1)}, bf16[24,896]{1,0:T(8,128)(2,1)S(1)}, u32[]{:S(2)}, u32[]{:S(2)}) collective-permute-start(bf16[24,896]{1,0:T(8,128)(2,1)S(1)} %get-tuple-element.114), channel_id=1, source_target_pairs={{0,4},{4,0},{1,5},{5,1},{2,6},{6,2},{3,7},{7,3},{8,12},{12,8},{9,1... | collective-permute-start | bytes 129032 | tf_op jit(solution)/shard_map/ppermute | solution.py:19
  33.0 4.1 %held_2.1 = (bf16[3,3584,512]{2,1,0:T(8,128)(2,1)S(1)}, f32[8,128]{1,0:T(8,128)S(1)}) custom-call(bf16[2,3,3584,512]{3,2,1,0:T(8,128)(2,1)} %refs_0_.10, bf16[48,896]{1,0:T(8,128)(2,1)S(1)} %get-tuple-element.109.refs_2_.refs_1_.refs_0_.refs_3_), custom_call_target="tpu_custom_call" | custom-call | bytes 22020096 | tf_op jit(solution)/shard_map/held_2/pallas_call | solution.py:265
  37.8 1.4 %gate_up_1.1 = (f32[48,1024]{1,0:T(8,128)S(1)}, bf16[48,1024]{1,0:T(8,128)(2,1)S(1)}) custom-call(bf16[48,896]{1,0:T(8,128)(2,1)S(1)} %get-tuple-element.109.refs_2_.refs_1_.refs_0_.refs_3_, bf16[48,896]{1,0:T(8,128)(2,1)S(1)} %collective-permute-done.8.refs_1_.refs_4_, bf16[48,896]{1,0:T(8,128)(2,1)S(1)} %collective-permute-done.9.refs_2_.refs_5_, ...), custom_call_target="tpu_custom_call" | custom-call | flops 352321536 | bytes 7340032 | tf_op jit(solution)/shard_map/gate_up_1/pallas_call | solution.py:342
  39.1 1.6 %collective-permute-start.12 = (bf16[48,1024]{1,0:T(8,128)(2,1)S(1)}, bf16[48,1024]{1,0:T(8,128)(2,1)S(1)}, u32[]{:S(2)}, u32[]{:S(2)}) collective-permute-start(bf16[48,1024]{1,0:T(8,128)(2,1)S(1)} %get-tuple-element.117), channel_id=1, source_target_pairs={{0,4},{4,0},{1,5},{5,1},{2,6},{6,2},{3,7},{7,3},{8,12},{12,8},{9,1... | collective-permute-start | bytes 294920 | tf_op jit(solution)/shard_map/ppermute | solution.py:19
  40.7 2.1 %collective-permute-start.13 = (bf16[48,896]{1,0:T(8,128)(2,1)S(1)}, bf16[48,896]{1,0:T(8,128)(2,1)S(1)}, u32[]{:S(2)}, u32[]{:S(2)}) collective-permute-start(bf16[48,896]{1,0:T(8,128)(2,1)S(1)} %base_order.1.refs_5_.refs_0_.refs_2_), channel_id=1, source_target_pairs={{1,0},{0,1},{3,2},{2,3},{5,4},{4,5},{7,6},{6,7},{9,8},{8,9},{11,10... | collective-permute-start | bytes 258056 | tf_op jit(solution)/shard_map/ppermute | solution.py:45
  42.9 1.1 collective-permute-start.14
  43.9 1.5 %collective-permute-start.15 = (bf16[48,896]{1,0:T(8,128)(2,1)S(1)}, bf16[48,896]{1,0:T(8,128)(2,1)S(1)}, u32[]{:S(2)}, u32[]{:S(2)}) collective-permute-start(bf16[48,896]{1,0:T(8,128)(2,1)S(1)} %base_order.1.refs_5_.refs_0_.refs_2_), channel_id=1, source_target_pairs={{3,0},{2,1},{1,2},{0,3},{7,4},{6,5},{5,6},{4,7},{11,8},{10,9},{9,1... | collective-permute-start | bytes 258056 | tf_op jit(solution)/shard_map/ppermute | solution.py:45
  45.4 1.2 down_1.1
  46.6 5.5 %collective-permute-done.14.refs_2_.refs_4_ = bf16[48,896]{1,0:T(8,128)(2,1)S(1)} collective-permute-done((bf16[48,896]{1,0:T(8,128)(2,1)S(1)}, bf16[48,896]{1,0:T(8,128)(2,1)S(1)}, u32[]{:S(2)}, u32[]{:S(2)}) %collective-permute-start.14) | collective-permute-done | bytes 86048 | tf_op jit(solution)/shard_map/ppermute | solution.py:45
  52.6 1.5 %collective-permute-start.16 = (bf16[48,896]{1,0:T(8,128)(2,1)S(1)}, bf16[48,896]{1,0:T(8,128)(2,1)S(1)}, u32[]{:S(2)}, u32[]{:S(2)}) collective-permute-start(bf16[48,896]{1,0:T(8,128)(2,1)S(1)} %get-tuple-element.126), channel_id=1, source_target_pairs={{0,1},{1,0},{2,3},{3,2},{4,5},{5,4},{6,7},{7,6},{8,9},{9,8},{10,11... | collective-permute-start | bytes 258056 | tf_op jit(solution)/shard_map/ppermute | solution.py:53
  54.1 1.3 collective-permute-start.17
  55.4 1.6 %collective-permute-start.18 = (bf16[48,896]{1,0:T(8,128)(2,1)S(1)}, bf16[48,896]{1,0:T(8,128)(2,1)S(1)}, u32[]{:S(2)}, u32[]{:S(2)}) collective-permute-start(bf16[48,896]{1,0:T(8,128)(2,1)S(1)} %get-tuple-element.128), channel_id=1, source_target_pairs={{0,3},{1,2},{2,1},{3,0},{4,7},{5,6},{6,5},{7,4},{8,11},{9,10},{10,... | collective-permute-start | bytes 258056 | tf_op jit(solution)/shard_map/ppermute | solution.py:53
  57.0 5.5 %dense_a.1 = (bf16[128,7168]{1,0:T(8,128)(2,1)S(1)}, f32[4,7168]{1,0:T(4,128)S(1)}) custom-call(s32[1,1,2,6]{3,2,1,0:T(2,128)} %refs_0_.11, s32[2]{0:T(128)} %bitcast.17, bf16[128,7168]{1,0:T(8,128)(2,1)S(1)} %collective-permute-done.7.hidden_ref, bf16[128,7168]{1,0:T(8,128)(2,1)S(1)} %bitcast.7, bf16[16,7168]{1,0:T(8,128)(2,1)S(1)} %get-tuple-element.111.next_ref, ...), custom_call_target="tpu_custom_call" | custom-call | flops 27525120 | bytes 4587520 | tf_op jit(solution)/shard_map/dense_a/pallas_call | solution.py:559
  62.7 1.3 collective-permute-start.19
  64.0 1.5 %collective-permute-start.20 = (bf16[48,896]{1,0:T(8,128)(2,1)S(1)}, bf16[48,896]{1,0:T(8,128)(2,1)S(1)}, u32[]{:S(2)}, u32[]{:S(2)}) collective-permute-start(bf16[48,896]{1,0:T(8,128)(2,1)S(1)} %get-tuple-element.129.refs_2_.refs_0_.refs_5_.refs_11_), channel_id=1, source_target_pairs={{2,0},{3,1},{0,2},{1,3},{6,4},{7,5},{4,6},{5,7},{10,8},{11,9},{8,1... | collective-permute-start | bytes 258056 | tf_op jit(solution)/shard_map/ppermute | solution.py:45
  65.5 1.6 %collective-permute-start.21 = (bf16[48,896]{1,0:T(8,128)(2,1)S(1)}, bf16[48,896]{1,0:T(8,128)(2,1)S(1)}, u32[]{:S(2)}, u32[]{:S(2)}) collective-permute-start(bf16[48,896]{1,0:T(8,128)(2,1)S(1)} %get-tuple-element.129.refs_2_.refs_0_.refs_5_.refs_11_), channel_id=1, source_target_pairs={{3,0},{2,1},{1,2},{0,3},{7,4},{6,5},{5,6},{4,7},{11,8},{10,9},{9,1... | collective-permute-start | bytes 258056 | tf_op jit(solution)/shard_map/ppermute | solution.py:45
  67.5 2.0 %fixed_2.1 = (f32[48,1536]{1,0:T(8,128)S(1)}, bf16[48,1536]{1,0:T(8,128)(2,1)S(1)}) custom-call(bf16[48,896]{1,0:T(8,128)(2,1)S(1)} %base_order.1.refs_5_.refs_0_.refs_2_, bf16[48,896]{1,0:T(8,128)(2,1)S(1)} %collective-permute-done.13.refs_1_.refs_3_, bf16[48,896]{1,0:T(8,128)(2,1)S(1)} %collective-permute-done.14.refs_2_.refs_4_, ...), custom_call_target="tpu_custom_call" | custom-call | flops 528482304 | bytes 11010048 | tf_op jit(solution)/shard_map/fixed_2/pallas_call | solution.py:342
  69.5 1.6 %collective-permute-start.24 = (bf16[48,1536]{1,0:T(8,128)(2,1)S(1)}, bf16[48,1536]{1,0:T(8,128)(2,1)S(1)}, u32[]{:S(2)}, u32[]{:S(2)}) collective-permute-start(bf16[48,1536]{1,0:T(8,128)(2,1)S(1)} %get-tuple-element.144), channel_id=1, source_target_pairs={{0,4},{4,0},{1,5},{5,1},{2,6},{6,2},{3,7},{7,3},{8,12},{12,8},{9,1... | collective-permute-start | bytes 442376 | tf_op jit(solution)/shard_map/ppermute | solution.py:19
  71.1 1.2 collective-permute-done.20.refs_2_.refs_7_.refs_13_
  72.3 1.7 %gate_up_2.1 = (f32[48,1152]{1,0:T(8,128)S(1)}, bf16[48,1152]{1,0:T(8,128)(2,1)S(1)}, bf16[48,3584]{1,0:T(8,128)(2,1)S(1)}) custom-call(bf16[48,896]{1,0:T(8,128)(2,1)S(1)} %get-tuple-element.129.refs_2_.refs_0_.refs_5_.refs_11_, bf16[48,896]{1,0:T(8,128)(2,1)S(1)} %collective-permute-done.19.refs_1_.refs_6_.refs_12_, ...), custom_call_target="tpu_custom_call" | custom-call | flops 352321536 | bytes 7340032 | tf_op jit(solution)/shard_map/gate_up_2/pallas_call | solution.py:342
  74.0 1.6 %collective-permute-start.23 = (bf16[48,1152]{1,0:T(8,128)(2,1)S(1)}, bf16[48,1152]{1,0:T(8,128)(2,1)S(1)}, u32[]{:S(2)}, u32[]{:S(2)}) collective-permute-start(bf16[48,1152]{1,0:T(8,128)(2,1)S(1)} %get-tuple-element.143.refs_5_), channel_id=1, source_target_pairs={{0,4},{4,0},{1,5},{5,1},{2,6},{6,2},{3,7},{7,3},{8,12},{12,8},{9,1... | collective-permute-start | bytes 331784 | tf_op jit(solution)/shard_map/ppermute | solution.py:19
  75.6 0.7 prev_down.1
  76.4 2.5 %collective-permute-done.23.refs_1_ = bf16[48,1152]{1,0:T(8,128)(2,1)S(1)} collective-permute-done((bf16[48,1152]{1,0:T(8,128)(2,1)S(1)}, bf16[48,1152]{1,0:T(8,128)(2,1)S(1)}, u32[]{:S(2)}, u32[]{:S(2)}) %collective-permute-start.23) | collective-permute-done | bytes 110624 | tf_op jit(solution)/shard_map/ppermute | solution.py:19
  78.8 2.5 %back_rows_2.1 = (bf16[48,512]{1,0:T(8,128)(2,1)S(1)}, bf16[48,512]{1,0:T(8,128)(2,1)S(1)}, bf16[48,512]{1,0:T(8,128)(2,1)S(1)}, f32[48,1]{1,0:T(8,128)S(1)}, f3...) custom-call(f32[48,1152]{1,0:T(8,128)S(1)} %get-tuple-element.142.re, ...), custom_call_target="tpu_custom_call" | custom-call | flops 352321536 | bytes 7340032 | tf_op jit(solution)/shard_map/back_rows_2/pallas_call | solution.py:381
  81.3 1.5 %collective-permute-start.25 = (bf16[48,896]{1,0:T(8,128)(2,1)S(1)}, bf16[48,896]{1,0:T(8,128)(2,1)S(1)}, u32[]{:S(2)}, u32[]{:S(2)}) collective-permute-start(bf16[48,896]{1,0:T(8,128)(2,1)S(1)} %get-tuple-element.150), channel_id=1, source_target_pairs={{0,1},{1,0},{2,3},{3,2},{4,5},{5,4},{6,7},{7,6},{8,9},{9,8},{10,11... | collective-permute-start | bytes 258056 | tf_op jit(solution)/shard_map/ppermute | solution.py:53
  82.9 1.6 %collective-permute-start.26 = (bf16[48,896]{1,0:T(8,128)(2,1)S(1)}, bf16[48,896]{1,0:T(8,128)(2,1)S(1)}, u32[]{:S(2)}, u32[]{:S(2)}) collective-permute-start(bf16[48,896]{1,0:T(8,128)(2,1)S(1)} %get-tuple-element.151), channel_id=1, source_target_pairs={{0,2},{1,3},{2,0},{3,1},{4,6},{5,7},{6,4},{7,5},{8,10},{9,11},{10,... | collective-permute-start | bytes 258056 | tf_op jit(solution)/shard_map/ppermute | solution.py:53
  84.4 1.3 %collective-permute-start.27 = (bf16[48,896]{1,0:T(8,128)(2,1)S(1)}, bf16[48,896]{1,0:T(8,128)(2,1)S(1)}, u32[]{:S(2)}, u32[]{:S(2)}) collective-permute-start(bf16[48,896]{1,0:T(8,128)(2,1)S(1)} %get-tuple-element.152), channel_id=1, source_target_pairs={{0,3},{1,2},{2,1},{3,0},{4,7},{5,6},{6,5},{7,4},{8,11},{9,10},{10,... | collective-permute-start | bytes 258056 | tf_op jit(solution)/shard_map/ppermute | solution.py:53
  85.8 1.5 %collective-permute-start.28 = (bf16[48,512]{1,0:T(8,128)(2,1)S(1)}, bf16[48,512]{1,0:T(8,128)(2,1)S(1)}, u32[]{:S(2)}, u32[]{:S(2)}) collective-permute-start(bf16[48,512]{1,0:T(8,128)(2,1)S(1)} %get-tuple-element.154), channel_id=1, source_target_pairs={{0,4},{4,0},{1,5},{5,1},{2,6},{6,2},{3,7},{7,3},{8,12},{12,8},{9,1... | collective-permute-start | bytes 147464 | tf_op jit(solution)/shard_map/ppermute | solution.py:19
  87.3 5.7 %dense_b.1 = (bf16[128,7168]{1,0:T(8,128)(2,1)S(1)}, f32[4,7168]{1,0:T(4,128)S(1)}) custom-call(s32[1,1,2,6]{3,2,1,0:T(2,128)} %refs_0_.11, s32[2]{0:T(128)} %bitcast.18, bf16[128,7168]{1,0:T(8,128)(2,1)S(1)} %collective-permute-done.7.hidden_ref, bf16[128,7168]{1,0:T(8,128)(2,1)S(1)} %bitcast.8, ...), custom_call_target="tpu_custom_call", output_to_operand_aliasing={{0}: (7, {})} | custom-call | flops 27525120 | bytes 4587520 | tf_op jit(solution)/shard_map/dense_b/pallas_call | solution.py:559
  94.3 0.6 collective-permute-start.31
  94.9 2.4 %collective-permute-start.32 = (bf16[48,896]{1,0:T(8,128)(2,1)S(1)}, bf16[48,896]{1,0:T(8,128)(2,1)S(1)}, u32[]{:S(2)}, u32[]{:S(2)}) collective-permute-start(bf16[48,896]{1,0:T(8,128)(2,1)S(1)} %get-tuple-element.155.refs_13_.refs_0_.refs_7_), channel_id=1, source_target_pairs={{2,0},{3,1},{0,2},{1,3},{6,4},{7,5},{4,6},{5,7},{10,8},{11,9},{8,1... | collective-permute-start | bytes 258056 | tf_op jit(solution)/shard_map/ppermute | solution.py:45
  97.4 1.3 collective-permute-start.33
  98.7 4.7 %weight_grad_2.1 = (bf16[1,2,3,3584,512]{4,3,2,1,0:T(8,128)(2,1)}, f32[8,128]{1,0:T(8,128)S(1)}) custom-call(bf16[48,3584]{1,0:T(8,128)(2,1)S(1)} %get-tuple-element.161.refs_0_, f32[48,1]{1,0:T(8,128)S(1)} %get-tuple-element.162.refs_1_, bf16[48,896]{1,0:T(8,128)(2,1)S(1)} %base_order.1.refs_5_.refs_0_.refs_2_, ...), custom_call_target="tpu_custom_call" | custom-call | flops 528482304 | bytes 11010048 | tf_op jit(solution)/shard_map/weight_grad_2/pallas_call | solution.py:428
  103.5 1.3 collective-permute-done.32.refs_2_.refs_9_
  104.7 0.8 back_1.1
  105.5 1.6 %collective-permute-start.35 = (bf16[48,640]{1,0:T(8,128)(2,1)S(1)}, bf16[48,640]{1,0:T(8,128)(2,1)S(1)}, u32[]{:S(2)}, u32[]{:S(2)}) collective-permute-start(bf16[48,640]{1,0:T(8,128)(2,1)S(1)} %get-tuple-element.167.refs_10_), channel_id=1, source_target_pairs={{0,4},{4,0},{1,5},{5,1},{2,6},{6,2},{3,7},{7,3},{8,12},{12,8},{9,1... | collective-permute-start | bytes 184328 | tf_op jit(solution)/shard_map/ppermute | solution.py:19
  107.1 1.6 %second_grad.1 = (bf16[6,7296]{1,0:T(8,128)(2,1)S(1)}, f32[4,3584]{1,0:T(4,128)S(1)}, f32[4,3584]{1,0:T(4,128)S(1)}) custom-call(s32[1,1,2,6]{3,2,1,0:T(2,128)} %refs_0_.11, s32[2]{0:T(128)} %bitcast.19, bf16[6,10880]{1,0:T(8,128)(2,1)S(1)} %collective-permute-done.1.refs_2_.refs_1_, bf16[6,7168]{1,0:T(8,128)(2,1)S(1)} %get-tuple-element.107.refs_9_.refs_3_, ...), custom_call_target="tpu_custom_call" | custom-call | bytes 2655232 | tf_op jit(solution)/shard_map/second_grad/pallas_call | solution.py:243
  109.3 1.0 collective-permute-done.35.refs_1_
  110.3 2.4 %back_rows_1.1 = (bf16[48,512]{1,0:T(8,128)(2,1)S(1)}, bf16[48,512]{1,0:T(8,128)(2,1)S(1)}, f32[48,1]{1,0:T(8,128)S(1)}, bf16[48,896]{1,0:T(8,128)(2,1)S(1)}, bf...) custom-call(f32[48,640]{1,0:T(8,128)S(1)} %get-tuple-element.172.refs_0_, ...), custom_call_target="tpu_custom_call" | custom-call | flops 352321536 | bytes 7340032 | tf_op jit(solution)/shard_map/back_rows_1/pallas_call | solution.py:381
  112.7 1.2 collective-permute-start.36
  113.9 2.1 %collective-permute-start.37 = (bf16[48,896]{1,0:T(8,128)(2,1)S(1)}, bf16[48,896]{1,0:T(8,128)(2,1)S(1)}, u32[]{:S(2)}, u32[]{:S(2)}) collective-permute-start(bf16[48,896]{1,0:T(8,128)(2,1)S(1)} %get-tuple-element.182), channel_id=1, source_target_pairs={{0,2},{1,3},{2,0},{3,1},{4,6},{5,7},{6,4},{7,5},{8,10},{9,11},{10,... | collective-permute-start | bytes 258056 | tf_op jit(solution)/shard_map/ppermute | solution.py:53
  116.0 1.2 collective-permute-start.38
  117.1 4.7 %weight_grad_1.1 = (bf16[1,2,3,3584,512]{4,3,2,1,0:T(8,128)(2,1)}, f32[8,128]{1,0:T(8,128)S(1)}) custom-call(f32[48,1]{1,0:T(8,128)S(1)} %get-tuple-element.176.refs_0_.refs_3_, f32[48,1]{1,0:T(8,128)S(1)} %get-tuple-element.171.refs_5_.refs_1_.refs_2_, f32[48,1]{1,0:T(8,128)S(1)} %get-tuple-element.174.refs_6_.refs_2_, ...), custom_call_target="tpu_custom_call", output_to_operand_aliasing={{0}: (18, {})} | custom-call | flops 528482304 | bytes 11010048 | tf_op jit(solution)/shard_map/weight_grad_1/pallas_call | solution.py:428
  122.9 1.0 collective-permute-start.40
  123.9 0.9 collective-permute-start.41
  124.8 1.5 %collective-permute-start.42 = (f32[4,896]{1,0:T(4,128)S(1)}, f32[4,896]{1,0:T(4,128)S(1)}, u32[]{:S(2)}, u32[]{:S(2)}) collective-permute-start(f32[4,896]{1,0:T(4,128)S(1)} %get-tuple-element.195), channel_id=1, source_target_pairs={{0,1},{1,0},{2,3},{3,2},{4,5},{5,4},{6,7},{7,6},{8,9},{9,8},{10,11... | collective-permute-start | bytes 43016 | tf_op jit(solution)/shard_map/ppermute | solution.py:53
  126.3 1.2 collective-permute-start.43
  127.6 1.7 %collective-permute-start.44 = (f32[4,896]{1,0:T(4,128)S(1)}, f32[4,896]{1,0:T(4,128)S(1)}, u32[]{:S(2)}, u32[]{:S(2)}) collective-permute-start(f32[4,896]{1,0:T(4,128)S(1)} %get-tuple-element.197), channel_id=1, source_target_pairs={{0,3},{1,2},{2,1},{3,0},{4,7},{5,6},{6,5},{7,4},{8,11},{9,10},{10,... | collective-permute-start | bytes 43016 | tf_op jit(solution)/shard_map/ppermute | solution.py:53
  129.2 2.9 %finish.1 = (bf16[128,7168]{1,0:T(8,128)(2,1)}, f32[8,128]{1,0:T(8,128)S(1)}) custom-call(s32[1,1,2,6]{3,2,1,0:T(2,128)} %copy-done.4, bf16[128,7168]{1,0:T(8,128)(2,1)S(1)} %collective-permute-done.29.refs_1_, bf16[6,7168]{1,0:T(8,128)(2,1)S(1)} %get-tuple-element.157.refs_2_, bf16[6,7296]{1,0:T(8,128)(2,1)S(1)} %collective-permute-done.34.refs_3_, ...), custom_call_target="tpu_custom_call" | custom-call | bytes 3933696 | tf_op jit(solution)/shard_map/finish/pallas_call | solution.py:243
  132.1 1.0 collective-permute-done.44.refs_3_
  (62 shorter events, 6.4 us)
Async XLA Ops:
  0.6 3.9 %collective-permute-start = (s32[1,1,2,6]{3,2,1,0:T(2,128)}, s32[1,1,2,6]{3,2,1,0:T(2,128)S(1)}, u32[]{:S(2)}, u32[]{:S(2)}) collective-permute-start(s32[1,1,2,6]{3,2,1,0:T(2,128)} %refs_0_.11), channel_id=1, source_target_pairs={{0,24},{8,0},{16,8},{24,16},{1,25},{9,1},{17,9},{25,17},{2,26},{10... | collective-permute-start | bytes 152 | tf_op jit(solution)/shard_map/ppermute | solution.py:19
  4.6 4.0 %copy-start.4 = (s32[1,1,2,6]{3,2,1,0:T(2,128)}, s32[1,1,2,6]{3,2,1,0:T(2,128)S(1)}, u32[]{:S(2)}) copy-start(s32[1,1,2,6]{3,2,1,0:T(2,128)S(1)} %collective-permute-done.refs_5_.refs_0_) | copy-start | bytes 148
  4.6 5.6 %copy-start.3 = (bf16[1,1,128,7168]{3,2,1,0:T(8,128)(2,1)S(1)}, bf16[1,1,128,7168]{3,2,1,0:T(8,128)(2,1)}, u32[]{:S(2)}) copy-start(bf16[1,1,128,7168]{3,2,1,0:T(8,128)(2,1)} %param.8) | copy-start | bytes 5505028
  8.6 15.3 %collective-permute-start.3 = (bf16[22,3712]{1,0:T(8,128)(2,1)S(1)}, bf16[22,3712]{1,0:T(8,128)(2,1)S(1)}, u32[]{:S(2)}, u32[]{:S(2)}) collective-permute-start(bf16[22,3712]{1,0:T(8,128)(2,1)S(1)} %get-tuple-element.104), channel_id=1, source_target_pairs={{0,4},{4,0},{1,5},{5,1},{2,6},{6,2},{3,7},{7,3},{8,12},{12,8},{9,1... | collective-permute-start | bytes 489992 | tf_op jit(solution)/shard_map/ppermute | solution.py:19
  11.4 4.8 %collective-permute-start.2 = (bf16[6,3712]{1,0:T(8,128)(2,1)S(1)}, bf16[6,3712]{1,0:T(8,128)(2,1)S(1)}, u32[]{:S(2)}, u32[]{:S(2)}) collective-permute-start(bf16[6,3712]{1,0:T(8,128)(2,1)S(1)} %get-tuple-element.103), channel_id=1, source_target_pairs={{0,12},{4,8},{8,20},{12,16},{16,28},{20,24},{24,4},{28,0},{1,13},{... | collective-permute-start | bytes 133640 | tf_op jit(solution)/shard_map/ppermute | solution.py:29
  11.9 11.9 %collective-permute-start.1 = (bf16[6,10880]{1,0:T(8,128)(2,1)S(1)}, bf16[6,10880]{1,0:T(8,128)(2,1)S(1)}, u32[]{:S(2)}, u32[]{:S(2)}) collective-permute-start(bf16[6,10880]{1,0:T(8,128)(2,1)S(1)} %get-tuple-element.102.refs_1_), channel_id=1, source_target_pairs={{0,8},{4,12},{8,16},{12,20},{16,24},{20,28},{24,0},{28,4},{1,9},{5... | collective-permute-start | bytes 391688 | tf_op jit(solution)/shard_map/ppermute | solution.py:29
  12.1 11.8 %copy-start = (bf16[1,1,128,7168]{3,2,1,0:T(8,128)(2,1)S(1)}, bf16[1,1,128,7168]{3,2,1,0:T(8,128)(2,1)}, u32[]{:S(2)}) copy-start(bf16[1,1,128,7168]{3,2,1,0:T(8,128)(2,1)} %param.9) | copy-start | bytes 5505028
  12.1 11.8 %copy-start.2 = (f32[2,2,7168]{2,1,0:T(2,128)S(1)}, f32[2,2,7168]{2,1,0:T(2,128)}, u32[]{:S(2)}) copy-start(f32[2,2,7168]{2,1,0:T(2,128)} %refs_8_.1) | copy-start | bytes 344068
  12.1 13.4 %collective-permute-start.4 = (bf16[48,1024]{1,0:T(8,128)(2,1)S(1)}, bf16[48,1024]{1,0:T(8,128)(2,1)S(1)}, u32[]{:S(2)}, u32[]{:S(2)}) collective-permute-start(bf16[48,1024]{1,0:T(8,128)(2,1)S(1)} %get-tuple-element.106.refs_5_), channel_id=1, source_target_pairs={{1,0},{0,1},{3,2},{2,3},{5,4},{4,5},{7,6},{6,7},{9,8},{8,9},{11,10... | collective-permute-start | bytes 294920 | tf_op jit(solution)/shard_map/ppermute | solution.py:45
  13.7 11.9 %collective-permute-start.5 = (bf16[48,1024]{1,0:T(8,128)(2,1)S(1)}, bf16[48,1024]{1,0:T(8,128)(2,1)S(1)}, u32[]{:S(2)}, u32[]{:S(2)}) collective-permute-start(bf16[48,1024]{1,0:T(8,128)(2,1)S(1)} %get-tuple-element.106.refs_5_), channel_id=1, source_target_pairs={{2,0},{3,1},{0,2},{1,3},{6,4},{7,5},{4,6},{5,7},{10,8},{11,9},{8,1... | collective-permute-start | bytes 294920 | tf_op jit(solution)/shard_map/ppermute | solution.py:45
  16.3 9.3 %collective-permute-start.6 = (bf16[48,1024]{1,0:T(8,128)(2,1)S(1)}, bf16[48,1024]{1,0:T(8,128)(2,1)S(1)}, u32[]{:S(2)}, u32[]{:S(2)}) collective-permute-start(bf16[48,1024]{1,0:T(8,128)(2,1)S(1)} %get-tuple-element.106.refs_5_), channel_id=1, source_target_pairs={{3,0},{2,1},{1,2},{0,3},{7,4},{6,5},{5,6},{4,7},{11,8},{10,9},{9,1... | collective-permute-start | bytes 294920 | tf_op jit(solution)/shard_map/ppermute | solution.py:45
  26.1 30.9 %collective-permute-start.7 = (bf16[128,7168]{1,0:T(8,128)(2,1)S(1)}, bf16[128,7168]{1,0:T(8,128)(2,1)S(1)}, u32[]{:S(2)}, u32[]{:S(2)}) collective-permute-start(bf16[128,7168]{1,0:T(8,128)(2,1)S(1)} %bitcast.14), channel_id=1, source_target_pairs={{0,8},{8,16},{16,24},{24,0},{1,9},{9,17},{17,25},{25,1},{2,10},{10... | collective-permute-start | bytes 5505032 | tf_op jit(solution)/shard_map/ppermute | solution.py:19
  27.1 10.1 %collective-permute-start.8 = (bf16[48,896]{1,0:T(8,128)(2,1)S(1)}, bf16[48,896]{1,0:T(8,128)(2,1)S(1)}, u32[]{:S(2)}, u32[]{:S(2)}) collective-permute-start(bf16[48,896]{1,0:T(8,128)(2,1)S(1)} %get-tuple-element.109.refs_2_.refs_1_.refs_0_.refs_3_), channel_id=1, source_target_pairs={{1,0},{0,1},{3,2},{2,3},{5,4},{4,5},{7,6},{6,7},{9,8},{8,9},{11,10... | collective-permute-start | bytes 258056 | tf_op jit(solution)/shard_map/ppermute | solution.py:45
  27.9 9.9 %collective-permute-start.9 = (bf16[48,896]{1,0:T(8,128)(2,1)S(1)}, bf16[48,896]{1,0:T(8,128)(2,1)S(1)}, u32[]{:S(2)}, u32[]{:S(2)}) collective-permute-start(bf16[48,896]{1,0:T(8,128)(2,1)S(1)} %get-tuple-element.109.refs_2_.refs_1_.refs_0_.refs_3_), channel_id=1, source_target_pairs={{2,0},{3,1},{0,2},{1,3},{6,4},{7,5},{4,6},{5,7},{10,8},{11,9},{8,1... | collective-permute-start | bytes 258056 | tf_op jit(solution)/shard_map/ppermute | solution.py:45
  29.0 8.8 %collective-permute-start.10 = (bf16[48,896]{1,0:T(8,128)(2,1)S(1)}, bf16[48,896]{1,0:T(8,128)(2,1)S(1)}, u32[]{:S(2)}, u32[]{:S(2)}) collective-permute-start(bf16[48,896]{1,0:T(8,128)(2,1)S(1)} %get-tuple-element.109.refs_2_.refs_1_.refs_0_.refs_3_), channel_id=1, source_target_pairs={{3,0},{2,1},{1,2},{0,3},{7,4},{6,5},{5,6},{4,7},{11,8},{10,9},{9,1... | collective-permute-start | bytes 258056 | tf_op jit(solution)/shard_map/ppermute | solution.py:45
  31.5 5.7 %collective-permute-start.11 = (bf16[24,896]{1,0:T(8,128)(2,1)S(1)}, bf16[24,896]{1,0:T(8,128)(2,1)S(1)}, u32[]{:S(2)}, u32[]{:S(2)}) collective-permute-start(bf16[24,896]{1,0:T(8,128)(2,1)S(1)} %get-tuple-element.114), channel_id=1, source_target_pairs={{0,4},{4,0},{1,5},{5,1},{2,6},{6,2},{3,7},{7,3},{8,12},{12,8},{9,1... | collective-permute-start | bytes 129032 | tf_op jit(solution)/shard_map/ppermute | solution.py:19
  39.1 6.3 %collective-permute-start.12 = (bf16[48,1024]{1,0:T(8,128)(2,1)S(1)}, bf16[48,1024]{1,0:T(8,128)(2,1)S(1)}, u32[]{:S(2)}, u32[]{:S(2)}) collective-permute-start(bf16[48,1024]{1,0:T(8,128)(2,1)S(1)} %get-tuple-element.117), channel_id=1, source_target_pairs={{0,4},{4,0},{1,5},{5,1},{2,6},{6,2},{3,7},{7,3},{8,12},{12,8},{9,1... | collective-permute-start | bytes 294920 | tf_op jit(solution)/shard_map/ppermute | solution.py:19
  40.7 5.9 %collective-permute-start.13 = (bf16[48,896]{1,0:T(8,128)(2,1)S(1)}, bf16[48,896]{1,0:T(8,128)(2,1)S(1)}, u32[]{:S(2)}, u32[]{:S(2)}) collective-permute-start(bf16[48,896]{1,0:T(8,128)(2,1)S(1)} %base_order.1.refs_5_.refs_0_.refs_2_), channel_id=1, source_target_pairs={{1,0},{0,1},{3,2},{2,3},{5,4},{4,5},{7,6},{6,7},{9,8},{8,9},{11,10... | collective-permute-start | bytes 258056 | tf_op jit(solution)/shard_map/ppermute | solution.py:45
  42.9 9.2 %collective-permute-start.14 = (bf16[48,896]{1,0:T(8,128)(2,1)S(1)}, bf16[48,896]{1,0:T(8,128)(2,1)S(1)}, u32[]{:S(2)}, u32[]{:S(2)}) collective-permute-start(bf16[48,896]{1,0:T(8,128)(2,1)S(1)} %base_order.1.refs_5_.refs_0_.refs_2_), channel_id=1, source_target_pairs={{2,0},{3,1},{0,2},{1,3},{6,4},{7,5},{4,6},{5,7},{10,8},{11,9},{8,1... | collective-permute-start | bytes 258056 | tf_op jit(solution)/shard_map/ppermute | solution.py:45
  43.9 8.2 %collective-permute-start.15 = (bf16[48,896]{1,0:T(8,128)(2,1)S(1)}, bf16[48,896]{1,0:T(8,128)(2,1)S(1)}, u32[]{:S(2)}, u32[]{:S(2)}) collective-permute-start(bf16[48,896]{1,0:T(8,128)(2,1)S(1)} %base_order.1.refs_5_.refs_0_.refs_2_), channel_id=1, source_target_pairs={{3,0},{2,1},{1,2},{0,3},{7,4},{6,5},{5,6},{4,7},{11,8},{10,9},{9,1... | collective-permute-start | bytes 258056 | tf_op jit(solution)/shard_map/ppermute | solution.py:45
  45.4 11.6 %copy-start.1 = (bf16[1,1,128,7168]{3,2,1,0:T(8,128)(2,1)S(1)}, bf16[1,1,128,7168]{3,2,1,0:T(8,128)(2,1)}, u32[]{:S(2)}) copy-start(bf16[1,1,128,7168]{3,2,1,0:T(8,128)(2,1)} %param.10) | copy-start | bytes 5505028
  52.1 15.1 %collective-permute-start.22 = (bf16[96,1024]{1,0:T(8,128)(2,1)S(1)}, bf16[96,1024]{1,0:T(8,128)(2,1)S(1)}, u32[]{:S(2)}, u32[]{:S(2)}) collective-permute-start(bf16[96,1024]{1,0:T(8,128)(2,1)S(1)} %get-tuple-element.134), channel_id=1, source_target_pairs={{0,4},{4,0},{1,5},{5,1},{2,6},{6,2},{3,7},{7,3},{8,12},{12,8},{9,1... | collective-permute-start | bytes 589832 | tf_op jit(solution)/shard_map/ppermute | solution.py:19
  52.6 9.9 %collective-permute-start.16 = (bf16[48,896]{1,0:T(8,128)(2,1)S(1)}, bf16[48,896]{1,0:T(8,128)(2,1)S(1)}, u32[]{:S(2)}, u32[]{:S(2)}) collective-permute-start(bf16[48,896]{1,0:T(8,128)(2,1)S(1)} %get-tuple-element.126), channel_id=1, source_target_pairs={{0,1},{1,0},{2,3},{3,2},{4,5},{5,4},{6,7},{7,6},{8,9},{9,8},{10,11... | collective-permute-start | bytes 258056 | tf_op jit(solution)/shard_map/ppermute | solution.py:53
  54.1 8.5 %collective-permute-start.17 = (bf16[48,896]{1,0:T(8,128)(2,1)S(1)}, bf16[48,896]{1,0:T(8,128)(2,1)S(1)}, u32[]{:S(2)}, u32[]{:S(2)}) collective-permute-start(bf16[48,896]{1,0:T(8,128)(2,1)S(1)} %get-tuple-element.127), channel_id=1, source_target_pairs={{0,2},{1,3},{2,0},{3,1},{4,6},{5,7},{6,4},{7,5},{8,10},{9,11},{10,... | collective-permute-start | bytes 258056 | tf_op jit(solution)/shard_map/ppermute | solution.py:53
  55.4 7.2 %collective-permute-start.18 = (bf16[48,896]{1,0:T(8,128)(2,1)S(1)}, bf16[48,896]{1,0:T(8,128)(2,1)S(1)}, u32[]{:S(2)}, u32[]{:S(2)}) collective-permute-start(bf16[48,896]{1,0:T(8,128)(2,1)S(1)} %get-tuple-element.128), channel_id=1, source_target_pairs={{0,3},{1,2},{2,1},{3,0},{4,7},{5,6},{6,5},{7,4},{8,11},{9,10},{10,... | collective-permute-start | bytes 258056 | tf_op jit(solution)/shard_map/ppermute | solution.py:53
  62.7 8.4 %collective-permute-start.19 = (bf16[48,896]{1,0:T(8,128)(2,1)S(1)}, bf16[48,896]{1,0:T(8,128)(2,1)S(1)}, u32[]{:S(2)}, u32[]{:S(2)}) collective-permute-start(bf16[48,896]{1,0:T(8,128)(2,1)S(1)} %get-tuple-element.129.refs_2_.refs_0_.refs_5_.refs_11_), channel_id=1, source_target_pairs={{1,0},{0,1},{3,2},{2,3},{5,4},{4,5},{7,6},{6,7},{9,8},{8,9},{11,10... | collective-permute-start | bytes 258056 | tf_op jit(solution)/shard_map/ppermute | solution.py:45
  64.0 8.3 %collective-permute-start.20 = (bf16[48,896]{1,0:T(8,128)(2,1)S(1)}, bf16[48,896]{1,0:T(8,128)(2,1)S(1)}, u32[]{:S(2)}, u32[]{:S(2)}) collective-permute-start(bf16[48,896]{1,0:T(8,128)(2,1)S(1)} %get-tuple-element.129.refs_2_.refs_0_.refs_5_.refs_11_), channel_id=1, source_target_pairs={{2,0},{3,1},{0,2},{1,3},{6,4},{7,5},{4,6},{5,7},{10,8},{11,9},{8,1... | collective-permute-start | bytes 258056 | tf_op jit(solution)/shard_map/ppermute | solution.py:45
  65.5 6.8 %collective-permute-start.21 = (bf16[48,896]{1,0:T(8,128)(2,1)S(1)}, bf16[48,896]{1,0:T(8,128)(2,1)S(1)}, u32[]{:S(2)}, u32[]{:S(2)}) collective-permute-start(bf16[48,896]{1,0:T(8,128)(2,1)S(1)} %get-tuple-element.129.refs_2_.refs_0_.refs_5_.refs_11_), channel_id=1, source_target_pairs={{3,0},{2,1},{1,2},{0,3},{7,4},{6,5},{5,6},{4,7},{11,8},{10,9},{9,1... | collective-permute-start | bytes 258056 | tf_op jit(solution)/shard_map/ppermute | solution.py:45
  69.5 6.8 %collective-permute-start.24 = (bf16[48,1536]{1,0:T(8,128)(2,1)S(1)}, bf16[48,1536]{1,0:T(8,128)(2,1)S(1)}, u32[]{:S(2)}, u32[]{:S(2)}) collective-permute-start(bf16[48,1536]{1,0:T(8,128)(2,1)S(1)} %get-tuple-element.144), channel_id=1, source_target_pairs={{0,4},{4,0},{1,5},{5,1},{2,6},{6,2},{3,7},{7,3},{8,12},{12,8},{9,1... | collective-permute-start | bytes 442376 | tf_op jit(solution)/shard_map/ppermute | solution.py:19
  74.0 4.8 %collective-permute-start.23 = (bf16[48,1152]{1,0:T(8,128)(2,1)S(1)}, bf16[48,1152]{1,0:T(8,128)(2,1)S(1)}, u32[]{:S(2)}, u32[]{:S(2)}) collective-permute-start(bf16[48,1152]{1,0:T(8,128)(2,1)S(1)} %get-tuple-element.143.refs_5_), channel_id=1, source_target_pairs={{0,4},{4,0},{1,5},{5,1},{2,6},{6,2},{3,7},{7,3},{8,12},{12,8},{9,1... | collective-permute-start | bytes 331784 | tf_op jit(solution)/shard_map/ppermute | solution.py:19
  81.3 11.6 %collective-permute-start.25 = (bf16[48,896]{1,0:T(8,128)(2,1)S(1)}, bf16[48,896]{1,0:T(8,128)(2,1)S(1)}, u32[]{:S(2)}, u32[]{:S(2)}) collective-permute-start(bf16[48,896]{1,0:T(8,128)(2,1)S(1)} %get-tuple-element.150), channel_id=1, source_target_pairs={{0,1},{1,0},{2,3},{3,2},{4,5},{5,4},{6,7},{7,6},{8,9},{9,8},{10,11... | collective-permute-start | bytes 258056 | tf_op jit(solution)/shard_map/ppermute | solution.py:53
  82.9 10.1 %collective-permute-start.26 = (bf16[48,896]{1,0:T(8,128)(2,1)S(1)}, bf16[48,896]{1,0:T(8,128)(2,1)S(1)}, u32[]{:S(2)}, u32[]{:S(2)}) collective-permute-start(bf16[48,896]{1,0:T(8,128)(2,1)S(1)} %get-tuple-element.151), channel_id=1, source_target_pairs={{0,2},{1,3},{2,0},{3,1},{4,6},{5,7},{6,4},{7,5},{8,10},{9,11},{10,... | collective-permute-start | bytes 258056 | tf_op jit(solution)/shard_map/ppermute | solution.py:53
  84.4 8.6 %collective-permute-start.27 = (bf16[48,896]{1,0:T(8,128)(2,1)S(1)}, bf16[48,896]{1,0:T(8,128)(2,1)S(1)}, u32[]{:S(2)}, u32[]{:S(2)}) collective-permute-start(bf16[48,896]{1,0:T(8,128)(2,1)S(1)} %get-tuple-element.152), channel_id=1, source_target_pairs={{0,3},{1,2},{2,1},{3,0},{4,7},{5,6},{6,5},{7,4},{8,11},{9,10},{10,... | collective-permute-start | bytes 258056 | tf_op jit(solution)/shard_map/ppermute | solution.py:53
  85.8 7.2 %collective-permute-start.28 = (bf16[48,512]{1,0:T(8,128)(2,1)S(1)}, bf16[48,512]{1,0:T(8,128)(2,1)S(1)}, u32[]{:S(2)}, u32[]{:S(2)}) collective-permute-start(bf16[48,512]{1,0:T(8,128)(2,1)S(1)} %get-tuple-element.154), channel_id=1, source_target_pairs={{0,4},{4,0},{1,5},{5,1},{2,6},{6,2},{3,7},{7,3},{8,12},{12,8},{9,1... | collective-permute-start | bytes 147464 | tf_op jit(solution)/shard_map/ppermute | solution.py:19
  93.5 35.8 %collective-permute-start.29 = (bf16[128,7168]{1,0:T(8,128)(2,1)S(1)}, bf16[128,7168]{1,0:T(8,128)(2,1)S(1)}, u32[]{:S(2)}, u32[]{:S(2)}) collective-permute-start(bf16[128,7168]{1,0:T(8,128)(2,1)S(1)} %get-tuple-element.156), channel_id=1, source_target_pairs={{0,24},{8,0},{16,8},{24,16},{1,25},{9,1},{17,9},{25,17},{2,26},{10... | collective-permute-start | bytes 5505032 | tf_op jit(solution)/shard_map/ppermute | solution.py:19
  93.7 5.0 %collective-permute-start.30 = (bf16[6,3584]{1,0:T(8,128)(2,1)S(1)}, bf16[6,3584]{1,0:T(8,128)(2,1)S(1)}, u32[]{:S(2)}, u32[]{:S(2)}) collective-permute-start(bf16[6,3584]{1,0:T(8,128)(2,1)S(1)} %get-tuple-element.160), channel_id=1, source_target_pairs={{0,4},{4,0},{1,5},{5,1},{2,6},{6,2},{3,7},{7,3},{8,12},{12,8},{9,1... | collective-permute-start | bytes 129032 | tf_op jit(solution)/shard_map/ppermute | solution.py:19
  94.3 9.1 %collective-permute-start.31 = (bf16[48,896]{1,0:T(8,128)(2,1)S(1)}, bf16[48,896]{1,0:T(8,128)(2,1)S(1)}, u32[]{:S(2)}, u32[]{:S(2)}) collective-permute-start(bf16[48,896]{1,0:T(8,128)(2,1)S(1)} %get-tuple-element.155.refs_13_.refs_0_.refs_7_), channel_id=1, source_target_pairs={{1,0},{0,1},{3,2},{2,3},{5,4},{4,5},{7,6},{6,7},{9,8},{8,9},{11,10... | collective-permute-start | bytes 258056 | tf_op jit(solution)/shard_map/ppermute | solution.py:45
  94.9 9.8 %collective-permute-start.32 = (bf16[48,896]{1,0:T(8,128)(2,1)S(1)}, bf16[48,896]{1,0:T(8,128)(2,1)S(1)}, u32[]{:S(2)}, u32[]{:S(2)}) collective-permute-start(bf16[48,896]{1,0:T(8,128)(2,1)S(1)} %get-tuple-element.155.refs_13_.refs_0_.refs_7_), channel_id=1, source_target_pairs={{2,0},{3,1},{0,2},{1,3},{6,4},{7,5},{4,6},{5,7},{10,8},{11,9},{8,1... | collective-permute-start | bytes 258056 | tf_op jit(solution)/shard_map/ppermute | solution.py:45
  97.4 7.4 %collective-permute-start.33 = (bf16[48,896]{1,0:T(8,128)(2,1)S(1)}, bf16[48,896]{1,0:T(8,128)(2,1)S(1)}, u32[]{:S(2)}, u32[]{:S(2)}) collective-permute-start(bf16[48,896]{1,0:T(8,128)(2,1)S(1)} %get-tuple-element.155.refs_13_.refs_0_.refs_7_), channel_id=1, source_target_pairs={{3,0},{2,1},{1,2},{0,3},{7,4},{6,5},{5,6},{4,7},{11,8},{10,9},{9,1... | collective-permute-start | bytes 258056 | tf_op jit(solution)/shard_map/ppermute | solution.py:45
  105.5 4.8 %collective-permute-start.35 = (bf16[48,640]{1,0:T(8,128)(2,1)S(1)}, bf16[48,640]{1,0:T(8,128)(2,1)S(1)}, u32[]{:S(2)}, u32[]{:S(2)}) collective-permute-start(bf16[48,640]{1,0:T(8,128)(2,1)S(1)} %get-tuple-element.167.refs_10_), channel_id=1, source_target_pairs={{0,4},{4,0},{1,5},{5,1},{2,6},{6,2},{3,7},{7,3},{8,12},{12,8},{9,1... | collective-permute-start | bytes 184328 | tf_op jit(solution)/shard_map/ppermute | solution.py:19
  108.7 8.4 %collective-permute-start.39 = (f32[4,3584]{1,0:T(4,128)S(1)}, f32[4,3584]{1,0:T(4,128)S(1)}, u32[]{:S(2)}, u32[]{:S(2)}) collective-permute-start(f32[4,3584]{1,0:T(4,128)S(1)} %get-tuple-element.184), channel_id=1, source_target_pairs={{0,4},{4,0},{1,5},{5,1},{2,6},{6,2},{3,7},{7,3},{8,12},{12,8},{9,1... | collective-permute-start | bytes 172040 | tf_op jit(solution)/shard_map/ppermute | solution.py:19
  112.7 9.1 %collective-permute-start.36 = (bf16[48,896]{1,0:T(8,128)(2,1)S(1)}, bf16[48,896]{1,0:T(8,128)(2,1)S(1)}, u32[]{:S(2)}, u32[]{:S(2)}) collective-permute-start(bf16[48,896]{1,0:T(8,128)(2,1)S(1)} %get-tuple-element.181), channel_id=1, source_target_pairs={{0,1},{1,0},{2,3},{3,2},{4,5},{5,4},{6,7},{7,6},{8,9},{9,8},{10,11... | collective-permute-start | bytes 258056 | tf_op jit(solution)/shard_map/ppermute | solution.py:53
  113.9 8.0 %collective-permute-start.37 = (bf16[48,896]{1,0:T(8,128)(2,1)S(1)}, bf16[48,896]{1,0:T(8,128)(2,1)S(1)}, u32[]{:S(2)}, u32[]{:S(2)}) collective-permute-start(bf16[48,896]{1,0:T(8,128)(2,1)S(1)} %get-tuple-element.182), channel_id=1, source_target_pairs={{0,2},{1,3},{2,0},{3,1},{4,6},{5,7},{6,4},{7,5},{8,10},{9,11},{10,... | collective-permute-start | bytes 258056 | tf_op jit(solution)/shard_map/ppermute | solution.py:53
  116.0 6.4 %collective-permute-start.38 = (bf16[48,896]{1,0:T(8,128)(2,1)S(1)}, bf16[48,896]{1,0:T(8,128)(2,1)S(1)}, u32[]{:S(2)}, u32[]{:S(2)}) collective-permute-start(bf16[48,896]{1,0:T(8,128)(2,1)S(1)} %get-tuple-element.183), channel_id=1, source_target_pairs={{0,3},{1,2},{2,1},{3,0},{4,7},{5,6},{6,5},{7,4},{8,11},{9,10},{10,... | collective-permute-start | bytes 258056 | tf_op jit(solution)/shard_map/ppermute | solution.py:53
  117.1 9.2 %collective-permute-start.34 = (bf16[6,7296]{1,0:T(8,128)(2,1)S(1)}, bf16[6,7296]{1,0:T(8,128)(2,1)S(1)}, u32[]{:S(2)}, u32[]{:S(2)}) collective-permute-start(bf16[6,7296]{1,0:T(8,128)(2,1)S(1)} %get-tuple-element.168), channel_id=1, source_target_pairs={{0,24},{8,0},{16,8},{24,16},{1,25},{9,1},{17,9},{25,17},{2,26},{10... | collective-permute-start | bytes 262664 | tf_op jit(solution)/shard_map/ppermute | solution.py:19
  122.9 4.7 %collective-permute-start.40 = (bf16[6,3584]{1,0:T(8,128)(2,1)S(1)}, bf16[6,3584]{1,0:T(8,128)(2,1)S(1)}, u32[]{:S(2)}, u32[]{:S(2)}) collective-permute-start(bf16[6,3584]{1,0:T(8,128)(2,1)S(1)} %get-tuple-element.190), channel_id=1, source_target_pairs={{0,24},{4,28},{8,0},{12,4},{16,8},{20,12},{24,16},{28,20},{1,25},{... | collective-permute-start | bytes 129032 | tf_op jit(solution)/shard_map/ppermute | solution.py:29
  123.9 5.3 %collective-permute-start.41 = (bf16[6,3584]{1,0:T(8,128)(2,1)S(1)}, bf16[6,3584]{1,0:T(8,128)(2,1)S(1)}, u32[]{:S(2)}, u32[]{:S(2)}) collective-permute-start(bf16[6,3584]{1,0:T(8,128)(2,1)S(1)} %get-tuple-element.191), channel_id=1, source_target_pairs={{0,28},{4,24},{8,4},{12,0},{16,12},{20,8},{24,20},{28,16},{1,29},{... | collective-permute-start | bytes 129032 | tf_op jit(solution)/shard_map/ppermute | solution.py:29
  124.8 7.3 %collective-permute-start.42 = (f32[4,896]{1,0:T(4,128)S(1)}, f32[4,896]{1,0:T(4,128)S(1)}, u32[]{:S(2)}, u32[]{:S(2)}) collective-permute-start(f32[4,896]{1,0:T(4,128)S(1)} %get-tuple-element.195), channel_id=1, source_target_pairs={{0,1},{1,0},{2,3},{3,2},{4,5},{5,4},{6,7},{7,6},{8,9},{9,8},{10,11... | collective-permute-start | bytes 43016 | tf_op jit(solution)/shard_map/ppermute | solution.py:53
  126.3 5.8 %collective-permute-start.43 = (f32[4,896]{1,0:T(4,128)S(1)}, f32[4,896]{1,0:T(4,128)S(1)}, u32[]{:S(2)}, u32[]{:S(2)}) collective-permute-start(f32[4,896]{1,0:T(4,128)S(1)} %get-tuple-element.196), channel_id=1, source_target_pairs={{0,2},{1,3},{2,0},{3,1},{4,6},{5,7},{6,4},{7,5},{8,10},{9,11},{10,... | collective-permute-start | bytes 43016 | tf_op jit(solution)/shard_map/ppermute | solution.py:53
  127.6 5.5 %collective-permute-start.44 = (f32[4,896]{1,0:T(4,128)S(1)}, f32[4,896]{1,0:T(4,128)S(1)}, u32[]{:S(2)}, u32[]{:S(2)}) collective-permute-start(f32[4,896]{1,0:T(4,128)S(1)} %get-tuple-element.197), channel_id=1, source_target_pairs={{0,3},{1,2},{2,1},{3,0},{4,7},{5,6},{6,5},{7,4},{8,11},{9,10},{10,... | collective-permute-start | bytes 43016 | tf_op jit(solution)/shard_map/ppermute | solution.py:53

commit v4 on v3

--- a/solution.py
+++ b/solution.py
@@ -39,12 +39,14 @@
     return place ^ step if count & (count - 1) == 0 else (place - step) % count
 
 
-def gather_dp(block):
+def gather_dp(block, before_last=None):
     count = lax.axis_size("dp")
-    return [block] + [
-        lax.ppermute(block, "dp", [(partner(z, i, count), z) for z in range(count)])
-        for i in range(1, count)
-    ]
+    got = [block]
+    for i in range(1, count):
+        if i == count - 1 and before_last is not None:
+            block, _ = lax.optimization_barrier((block, before_last))
+        got.append(lax.ppermute(block, "dp", [(partner(z, i, count), z) for z in range(count)]))
+    return got
 
 
 def return_dp(blocks):
@@ -216,9 +218,10 @@
     return pltpu.with_memory_space_constraint(value, pltpu.HBM)
 
 
-def call(name, fn, outs, small, *args, far=(), after=(), flops=0, limit=12):
+def call(name, fn, outs, small, *args, far=(), hold=(), after=(), flops=0, limit=12):
+    outs = list(outs) + [(weight.shape[2:], bf16) for weight, _, _ in hold]
     shapes = [jax.ShapeDtypeStruct(shape, kind) for shape, kind in outs]
-    n_small, n_args, n_far, n_outs = len(small), len(args), len(far), len(shapes)
+    n_small, n_args, n_far, n_outs = len(small), len(args), len(far), len(shapes) - len(hold)
 
     def body(*refs):
         refs = list(refs)
@@ -228,71 +231,53 @@
             return taken
 
         small_refs, arg_refs, far_refs = take(n_small), take(n_args), take(n_far)
+        hold_refs = take(len(hold))
         take(len(after))
-        out_refs, buffers, sems = take(n_outs), take(n_far), take(n_far)
-        copies = [pltpu.make_async_copy(*trio) for trio in zip(far_refs, buffers, sems)]
-        for copy in copies:
+        out_refs, held_refs, buffers = take(n_outs), take(len(hold)), take(n_far)
+        copies = [pltpu.make_async_copy(*trio) for trio in zip(far_refs, buffers, take(n_far))]
+        holds = [
+            pltpu.make_async_copy(ref.at[depth, kind], held_ref, sem)
+            for ref, (_, depth, kind), held_ref, sem in zip(hold_refs, hold, held_refs, refs)
+        ]
+        for copy in copies + holds:
             copy.start()
         for copy in copies:
             copy.wait()
         values = small_refs + [r[...] for r in arg_refs + buffers]
         for ref, value in zip(out_refs, fn(*values)):
             ref[...] = value.astype(ref.dtype)
+        for copy in holds:
+            copy.wait()
 
     size = sum(a.size * a.dtype.itemsize for a in list(args) + list(far) + shapes)
     return pl.pallas_call(
         body,
         name=name,
         out_shape=shapes,
-        in_specs=[smem] * n_small + [vmem] * n_args + [anywhere] * (n_far + len(after)),
-        out_specs=[vmem] * n_outs,
-        scratch_shapes=[pltpu.VMEM(a.shape, a.dtype) for a in far] + [pltpu.SemaphoreType.DMA] * n_far,
+        in_specs=[smem] * n_small + [vmem] * n_args + [anywhere] * (n_far + len(hold) + len(after)),
+        out_specs=[vmem] * len(shapes),
+        scratch_shapes=[pltpu.VMEM(a.shape, a.dtype) for a in far]
+        + [pltpu.SemaphoreType.DMA] * (n_far + len(hold)),
         compiler_params=pltpu.CompilerParams(vmem_limit_bytes=limit << 20),
         cost_estimate=pl.CostEstimate(flops=flops, bytes_accessed=size, transcendentals=0),
-    )(*[in_hbm(a) for a in small], *args, *[in_hbm(a) for a in far], *after)
-
-
-def held(name, weight, depth, after=()):
-    _, kinds, width, hidden = weight.shape
-
-    def body(*refs):
-        weight_ref, out_ref, tick_ref, sem = refs[0], *refs[-3:]
-        copy = pltpu.make_async_copy(weight_ref.at[depth], out_ref, sem)
-        copy.start()
-        tick_ref[...] = jnp.zeros_like(tick_ref)
-        copy.wait()
-
-    return pl.pallas_call(
-        body,
-        name=name,
-        in_specs=[anywhere] * (1 + len(after)),
-        out_specs=[vmem] * 2,
-        out_shape=[
-            jax.ShapeDtypeStruct((kinds, width, hidden), bf16),
-            jax.ShapeDtypeStruct((8, lanes), f32),
-        ],
-        scratch_shapes=[pltpu.SemaphoreType.DMA],
-        compiler_params=pltpu.CompilerParams(vmem_limit_bytes=2 << 20),
-        cost_estimate=pl.CostEstimate(
-            flops=0, bytes_accessed=4 * kinds * width * hidden, transcendentals=0
-        ),
-    )(in_hbm(weight), *after)
-
-
-def project(name, blocks, weight, kinds, parts, others=None, select=None, gain=None, mates=None, after=()):
+    )(*[in_hbm(a) for a in small], *args, *[in_hbm(a) for a in far], *[in_hbm(a) for a, _, _ in hold], *after)
+
+
+def project(name, blocks, weights, kinds, parts, others=None, select=None, gain=None, mates=None, after=()):
     groups = len(blocks)
     rows = blocks[0].shape[0] // parts
-    width, hidden = weight.shape[1:]
+    width, hidden = weights[0].shape
     step = width // parts
     other_blocks, other_kinds = others if others is not None else ([], ())
     first_kinds, kinds = kinds, kinds + other_kinds
+    many_kinds = len(kinds)
     total, many = rows * groups, len(kinds) * hidden
     marked = select is not None or mates is not None
     extra = lanes if marked else 0
 
     def body(*refs):
         refs = list(refs)
-        x_refs, w_ref, refs = refs[:groups], refs[groups], refs[groups + 1 :]
+        x_refs, w_refs, refs = refs[:groups], refs[groups : groups + many_kinds], refs[groups + many_kinds :]
         other_refs, refs = refs[: len(other_blocks)], refs[len(other_blocks) :]
         if select is not None:
             select_ref, gain_ref = refs.pop(0), refs.pop(0)
@@ -319,7 +304,7 @@
             for k in range(len(kinds)):
                 if k == len(first_kinds):
                     x = column_part([r[...] for r in other_refs], rows, g)[:, :step]
-                part_ref = w_ref.at[kinds[k], pl.ds(g * step, step)]
+                part_ref = w_refs[k].at[pl.ds(g * step, step)]
                 sums[k] += jnp.dot(x, part_ref[...], preferred_element_type=f32)
         for k in range(len(kinds)):
             own_ref[:, k * hidden : (k + 1) * hidden] = sums[k]
@@ -328,8 +313,8 @@
             own_ref[:, many:] = in_lanes([mark])
             send_ref[:, many:] = coded(mark).astype(bf16)
 
-    args = list(blocks) + [weight]
-    args, specs = args + list(other_blocks), [vmem] * groups + [vmem] + [vmem] * len(other_blocks)
+    args = list(blocks) + [weights[k] for k in kinds]
+    args, specs = args + list(other_blocks), [vmem] * (groups + many_kinds) + [vmem] * len(other_blocks)
     outs = [
         jax.ShapeDtypeStruct((total, many + extra), f32),
         jax.ShapeDtypeStruct((total, many + extra), bf16),
@@ -352,15 +337,15 @@
     )(*args, *after)
 
 
-def expand(name, prepare, args, saved, weight, kinds, groups, parts, after=()):
-    width, hidden = weight.shape[1:]
+def expand(name, prepare, args, saved, weights, kinds, groups, parts, after=()):
+    width, hidden = weights[0].shape
     total = saved[0][0][0]
     rows, step = total // groups, width // parts
     count, kept = len(args), len(saved)
 
     def body(*refs):
-        in_refs, w_ref = refs[:count], refs[count]
-        refs = refs[count + 1 + len(after) :]
+        in_refs, w_refs = refs[:count], refs[count : count + len(kinds)]
+        refs = refs[count + len(kinds) + len(after) :]
         saved_refs, out_refs = refs[:kept], refs[kept:]
         for ref, value in zip(saved_refs, prepare(*[r[...] for r in in_refs])):
             ref[...] = value.astype(ref.dtype)
@@ -368,7 +353,7 @@
         for g in range(parts):
             part = jnp.zeros((total, step), f32)
             for k in range(len(kinds)):
-                part_ref = w_ref.at[kinds[k], pl.ds(g * step, step)]
+                part_ref = w_refs[k].at[pl.ds(g * step, step)]
                 part += lax.dot_general(
                     saved_refs[k][...], part_ref[...], (((1,), (1,)), ((), ())),
                     preferred_element_type=f32,
@@ -381,7 +366,7 @@
     results = pl.pallas_call(
         body,
         name=name,
-        in_specs=[vmem] * (count + 1) + [anywhere] * len(after),
+        in_specs=[vmem] * (count + len(kinds)) + [anywhere] * len(after),
         out_specs=[vmem] * (kept + groups),
         out_shape=[jax.ShapeDtypeStruct(shape, kind) for shape, kind in saved]
         + [jax.ShapeDtypeStruct((rows * parts, step), bf16)] * groups,
@@ -391,7 +376,7 @@
             bytes_accessed=2 * width * hidden * len(kinds),
             transcendentals=0,
         ),
-    )(*args, weight, *after)
+    )(*args, *[weights[k] for k in kinds], *after)
     return results[:kept], results[kept:]
 
 
@@ -466,7 +451,7 @@
     return grad_0.astype(bf16), jnp.concatenate(terms, 0)
 
 
-def dense_rows(name, token, count, hidden, embed, next_rows, cotangent, gain, before, half, halves, after=()):
+def dense_rows(name, token, count, hidden, embed, next_rows, cotangent, gain, before, half, halves, hold=(), after=()):
     tokens, width = hidden.shape
     step = next_rows.shape[0]
     blocks = tokens // step // halves
@@ -476,7 +461,17 @@
     earlier = [] if before is None else list(before)
 
     def body(token_ref, count_ref, hidden_ref, embed_ref, next_ref, cot_ref, gain_ref, *refs):
-        out_ref, terms_ref, mixed_ref, sums_ref = refs[-4:]
+        skip, kept = len(earlier), len(hold)
+        hold_refs, refs = refs[skip : skip + kept], refs[:skip] + refs[skip + kept :]
+        held_refs, sems = refs[len(refs) - 2 * kept - 2 : len(refs) - kept - 2], refs[len(refs) - kept :]
+        out_ref, terms_ref = refs[skip + len(after) : skip + len(after) + 2]
+        mixed_ref, sums_ref = refs[len(refs) - kept - 2 : len(refs) - kept]
+        holds = [
+            pltpu.make_async_copy(ref.at[depth, kind], held_ref, sem)
+            for ref, (_, depth, kind), held_ref, sem in zip(hold_refs, hold, held_refs, sems)
+        ]
+        for copy in holds:
+            copy.start()
         sums_ref[...] = jnp.zeros_like(sums_ref)
         row, column = (iota((2 * step, 2 * step), dim) for dim in range(2))
         shift = (column == jnp.where(row < step, row + 1, row + 2 - step)).astype(bf16)
@@ -555,25 +550,29 @@
         for k in range(4):
             term = jnp.sum(sums_ref[k], axis=0, keepdims=True)
             terms_ref[k : k + 1] = term + refs[1][k : k + 1] if earlier else term
+        for copy in holds:
+            copy.wait()
 
     return pl.pallas_call(
         body,
         name=name,
-        in_specs=[smem] * 2 + [vmem] * (5 + len(earlier)) + [anywhere] * len(after),
-        out_specs=[vmem] * 2,
+        in_specs=[smem] * 2 + [vmem] * (5 + len(earlier)) + [anywhere] * (len(hold) + len(after)),
+        out_specs=[vmem] * (2 + len(hold)),
         out_shape=[
             jax.ShapeDtypeStruct((tokens, width), bf16),
             jax.ShapeDtypeStruct((4, width), f32),
-        ],
+        ]
+        + [jax.ShapeDtypeStruct(weight.shape[2:], bf16) for weight, _, _ in hold],
         input_output_aliases={7: 0} if earlier else {},
-        scratch_shapes=[pltpu.VMEM((step, width), bf16), pltpu.VMEM((4, 8, width), f32)],
+        scratch_shapes=[pltpu.VMEM((step, width), bf16), pltpu.VMEM((4, 8, width), f32)]
+        + [pltpu.SemaphoreType.DMA] * len(hold),
         compiler_params=pltpu.CompilerParams(vmem_limit_bytes=8 << 20),
         cost_estimate=pl.CostEstimate(
             flops=60 * tokens * width // halves,
             bytes_accessed=10 * tokens * width // halves,
             transcendentals=0,
         ),
-    )(in_hbm(token), in_hbm(count), hidden, embed, next_rows, cotangent, gain, *earlier, *after)
+    )(in_hbm(token), in_hbm(count), hidden, embed, next_rows, cotangent, gain, *earlier, *[in_hbm(a) for a, _, _ in hold], *after)
 
 
 def local(
@@ -627,11 +626,12 @@
         ] + [dout]
 
     fine = width // parts + lanes
-    *own_sent, dout_2 = call(
+    *own_sent, dout_2, gate_1st = call(
         "own_rows", own_rows,
         [((3 * slots + depths * seqs, width + lanes), bf16)] * seqs
         + [((slots * parts * seqs, fine), bf16)],
-        (slot_token, slot_count, route_gate), far=(embed, cot), after=(asked_token,),
+        (slot_token, slot_count, route_gate), far=(embed, cot),
+        hold=((expert_weight, 0, 0),), after=(asked_token,),
     )
     own_got = trade_seq(own_sent)
 
@@ -643,16 +643,15 @@
         sent[0] = jnp.concatenate([sent[0], second], 1)
         return sent + [first]
 
-    *sent, asked_rows = call(
+    *sent, asked_rows, up_1st = call(
         "source_rows", source_rows,
         [((slots, width + lanes + features), bf16)]
         + [((slots, width + lanes), bf16)] * (seqs - 1)
         + [((slots, features), bf16)],
-        (asked_token,), source, after=(own_sent[0],),
+        (asked_token,), source, hold=((expert_weight, 0, 1),), after=(own_sent[0],),
     )
     start_got = trade_seq(sent, 1)
     dout_2, _ = lax.optimization_barrier((dout_2, sent[0]))
-    dout_2_got = gather_dp(dout_2)
 
     def second_base(token, count, start, table, got, gain):
         after = got[3 * slots :, :width].astype(f32)
@@ -671,16 +670,17 @@
         bases = [folded(piece, parts) for piece in pieces_of(out, seq_place(), seqs)]
         return bases + [after, ahead_1, ahead_2]
 
-    *base_sent, next_rows, ahead_21, ahead_22 = call(
+    *base_sent, next_rows, ahead_21, ahead_22, down_1st = call(
         "second_base", second_base,
         [((slots * parts, width // parts), bf16)] * seqs
         + [((16, features), bf16)]
         + [((slots, features), bf16)] * 2,
-        facts, start_got[0], embed, own_got[-1], norm_gain, after=(start_got[-1],),
+        facts, start_got[0], embed, own_got[-1], norm_gain,
+        hold=((expert_weight, 0, 2),), after=(start_got[-1],),
     )
     base_got = trade_seq(base_sent)
 
-    weight_1st, tick_a = held("held_1", expert_weight, 0, after=(sent[0],))
+    dout_2_got = gather_dp(dout_2, ahead_21)
 
     def first_mixed(gain, *got):
         start_got, dout = got[:seqs], [g.astype(f32) for g in got[2 * seqs :]]
@@ -720,7 +720,7 @@
         "first_mixed", first_mixed,
         [packed] + [part_rows] * 4 + [((rows, lanes), f32)]
         + [((groups * slots * parts, fine), bf16)] * seqs,
-        (), norm_gain, *start_got, *own_got, *dout_2_got, after=(ahead_21, tick_a),
+        (), norm_gain, *start_got, *own_got, *dout_2_got, after=(ahead_21,),
     )
     rows_1_all = gather_dp(rows_1)
 
@@ -735,9 +735,9 @@
     )
     base_2_all = gather_dp(base_2)
 
-    weight_2nd, tick_b = held("held_2", expert_weight, 1, after=(rows_1,))
+    weight_1st = (gate_1st, up_1st, down_1st)
     first_own, first_send = project(
-        "gate_up_1", rows_1_all, weight_1st, (0, 1), parts, after=(base_2, tick_b)
+        "gate_up_1", rows_1_all, weight_1st, (0, 1), parts, after=(base_2,)
     )
     first = pair_seq(first_own, first_send)
 
@@ -756,10 +756,11 @@
 
     hidden, _ = lax.optimization_barrier((source, rows_1))
     hidden = ring(hidden, "section", 1)
-    dense = dense_rows(
+    *dense, gate_2nd, up_2nd, down_2nd = dense_rows(
         "dense_a", *facts, hidden, embed, next_rows, cot, norm_gain, None, 0, 2,
-        after=(out_blocks[0],),
-    )
+        hold=tuple((expert_weight, 1, k) for k in range(3)), after=(out_blocks[0],),
+    )
+    weight_2nd = (gate_2nd, up_2nd, down_2nd)
 
     def second_prev(own_facts, rows_1, *got):
         value = unfolded(rows_1.astype(f32), parts) + summed(got, parts) * decoded(own_facts, 4)

time: 134 us -> 138 us (1.030)
  waiting for transfers between devices: 15 us -> 25.4 us
  Pallas kernels: 55.6 us -> 51.2 us
  starting transfers between devices: 62 us -> 60.3 us
    pallas_call x5 -> x3, Pallas kernels: 14.3 us -> 6.05 us  [expand(): pl.pallas_call(body, name=name, in_specs=[vmem] * (count + len(kinds)) +...]
    ppermute x15, waiting for transfers between devices: 8.54 us -> 15 us  [gather_dp(): lax.ppermute(block, 'dp', [(partner(z, i, count), z) for z in range(count)])]
    pallas_call x12, Pallas kernels: 14 us -> 17.8 us  [call(): pl.pallas_call(body, name=name, out_shape=shapes, in_specs=[smem] * n_sma...]
    ppermute x14, waiting for transfers between devices: 4.98 us -> 8.34 us  [ring(): lax.ppermute(value, axis, [(i, (i + steps) % count) for i in range(count)])]
    ppermute x14, starting transfers between devices: 16.2 us -> 14.2 us  [ring(): lax.ppermute(value, axis, [(i, (i + steps) % count) for i in range(count)])]
  transfers between devices with their start and end apart: 45 -> 45, of which waited for: 9 -> 13; matrix products, arithmetic and copies ran while one was open for 0% -> 0% of each run, Pallas kernels for 36% -> 31%
where the time goes in v4:
time: 138 us
  starting transfers between devices  60.3 us (44%)
  Pallas kernels  51.2 us (37%)
  waiting for transfers between devices  25.4 us (18%)
    ppermute x15, starting transfers between devices, gather_dp(): lax.ppermute(block, 'dp', [(partner(z, i, count), z) for z in range(count)])  25.5 us
    ppermute x12, starting transfers between devices, return_dp(): lax.ppermute(blocks[i], 'dp', [(z, partner(z, i, count)) for z in range(c...  17.9 us
    pallas_call x12, Pallas kernels, call(): pl.pallas_call(body, name=name, out_shape=shapes, in_specs=[smem] * n_sma...  17.8 us
    ppermute x15, waiting for transfers between devices, gather_dp(): lax.ppermute(block, 'dp', [(partner(z, i, count), z) for z in range(count)])  15 us
    ppermute x14, starting transfers between devices, ring(): lax.ppermute(value, axis, [(i, (i + steps) % count) for i in range(count)])  14.2 us
    pallas_call x2, Pallas kernels, dense_rows(): pl.pallas_call(body, name=name, in_specs=[smem] * 2 + [vmem] * (5 + len(e...  11.3 us
    pallas_call x2, Pallas kernels, outer(): pl.pallas_call(body, name=name, in_specs=[vmem] * (count + 3) + [anywhere...  9.4 us
    ppermute x14, waiting for transfers between devices, ring(): lax.ppermute(value, axis, [(i, (i + steps) % count) for i in range(count)])  8.34 us
  transfers between devices with their start and end apart: 45, of which 13 were waited for; matrix products, arithmetic and copies ran while one was open for 0% of the time, Pallas kernels for 31%

profile of v4, /device:TPU:0, one launch (start us, length us, event | category | flops | bytes accessed | tf_op | source)
XLA Modules:
  0.0 137.8 jit_solution(5566475958546644537)
XLA Ops:
  0.6 2.4 %collective-permute-start = (s32[1,1,2,6]{3,2,1,0:T(2,128)}, s32[1,1,2,6]{3,2,1,0:T(2,128)S(1)}, u32[]{:S(2)}, u32[]{:S(2)}) collective-permute-start(s32[1,1,2,6]{3,2,1,0:T(2,128)} %refs_0_.9), channel_id=1, source_target_pairs={{0,24},{8,0},{16,8},{24,16},{1,25},{9,1},{17,9},{25,17},{2,26},{10... | collective-permute-start | bytes 152 | tf_op jit(solution)/shard_map/ppermute | solution.py:19
  3.1 1.5 %collective-permute-done.refs_6_.refs_0_ = s32[1,1,2,6]{3,2,1,0:T(2,128)S(1)} collective-permute-done((s32[1,1,2,6]{3,2,1,0:T(2,128)}, s32[1,1,2,6]{3,2,1,0:T(2,128)S(1)}, u32[]{:S(2)}, u32[]{:S(2)}) %collective-permute-start) | collective-permute-done | bytes 80 | tf_op jit(solution)/shard_map/ppermute | solution.py:19
  4.6 4.0 %own_rows.1 = (bf16[22,3712]{1,0:T(8,128)(2,1)S(1)}, bf16[22,3712]{1,0:T(8,128)(2,1)S(1)}, bf16[48,1024]{1,0:T(8,128)(2,1)S(1)}, bf16[3584,512]{1,0:T(8,128)(2,1)S(1)}) custom-call(s32[1,1,2,6]{3,2,1,0:T(2,128)} %refs_0_.9, s32[2]{0:T(128)} %bitcast.15, f32[1,1,2,6]{3,2,1,0:T(2,128)} %refs_2_.4, bf16[128,7168]{1,0:T(8,128)(2,1)} %bitcast.5, ...), custom_call_target="tpu_custom_call" | custom-call | bytes 7764992 | tf_op jit(solution)/shard_map/own_rows/pallas_call | solution.py:253
  8.6 1.6 %collective-permute-start.3 = (bf16[22,3712]{1,0:T(8,128)(2,1)S(1)}, bf16[22,3712]{1,0:T(8,128)(2,1)S(1)}, u32[]{:S(2)}, u32[]{:S(2)}) collective-permute-start(bf16[22,3712]{1,0:T(8,128)(2,1)S(1)} %get-tuple-element.107), channel_id=1, source_target_pairs={{0,4},{4,0},{1,5},{5,1},{2,6},{6,2},{3,7},{7,3},{8,12},{12,8},{9,1... | collective-permute-start | bytes 489992 | tf_op jit(solution)/shard_map/ppermute | solution.py:19
  10.2 3.1 %source_rows.1 = (bf16[6,10880]{1,0:T(8,128)(2,1)S(1)}, bf16[6,3712]{1,0:T(8,128)(2,1)S(1)}, bf16[6,7168]{1,0:T(8,128)(2,1)S(1)}, bf16[3584,512]{1,0:T(8,128)(2,1)S(1)}) custom-call(s32[1,1,2,6]{3,2,1,0:T(2,128)} %copy-done.4, bf16[128,7168]{1,0:T(8,128)(2,1)S(1)} %bitcast.13, bf16[2,3,3584,512]{3,2,1,0:T(8,128)(2,1)} %refs_2_.6, ...), custom_call_target="tpu_custom_call" | custom-call | bytes 5766144 | tf_op jit(solution)/shard_map/source_rows/pallas_call | solution.py:253
  14.2 1.6 %collective-permute-start.4 = (bf16[48,1024]{1,0:T(8,128)(2,1)S(1)}, bf16[48,1024]{1,0:T(8,128)(2,1)S(1)}, u32[]{:S(2)}, u32[]{:S(2)}) collective-permute-start(bf16[48,1024]{1,0:T(8,128)(2,1)S(1)} %get-tuple-element.111.refs_5_), channel_id=1, source_target_pairs={{1,0},{0,1},{3,2},{2,3},{5,4},{4,5},{7,6},{6,7},{9,8},{8,9},{11,10... | collective-permute-start | bytes 294920 | tf_op jit(solution)/shard_map/ppermute | solution.py:48
  15.7 2.6 %collective-permute-start.5 = (bf16[48,1024]{1,0:T(8,128)(2,1)S(1)}, bf16[48,1024]{1,0:T(8,128)(2,1)S(1)}, u32[]{:S(2)}, u32[]{:S(2)}) collective-permute-start(bf16[48,1024]{1,0:T(8,128)(2,1)S(1)} %get-tuple-element.111.refs_5_), channel_id=1, source_target_pairs={{2,0},{3,1},{0,2},{1,3},{6,4},{7,5},{4,6},{5,7},{10,8},{11,9},{8,1... | collective-permute-start | bytes 294920 | tf_op jit(solution)/shard_map/ppermute | solution.py:48
  18.8 3.6 %second_base.1 = (bf16[24,896]{1,0:T(8,128)(2,1)S(1)}, bf16[24,896]{1,0:T(8,128)(2,1)S(1)}, bf16[16,7168]{1,0:T(8,128)(2,1)S(1)}, bf16[6,7168]{1,0:T(8,128)(2,1)...) custom-call(s32[1,1,2,6]{3,2,1,0:T(2,128)} %refs_0_.9, s32[2]{0:T(128)} %bitcast.16, ...), custom_call_target="tpu_custom_call" | custom-call | bytes 6401024 | tf_op jit(solution)/shard_map/second_base/pallas_call | solution.py:253
  22.4 3.7 %collective-permute-start.6 = (bf16[48,1024]{1,0:T(8,128)(2,1)S(1)}, bf16[48,1024]{1,0:T(8,128)(2,1)S(1)}, u32[]{:S(2)}, u32[]{:S(2)}) collective-permute-start(bf16[48,1024]{1,0:T(8,128)(2,1)S(1)} %get-tuple-element.111.refs_5_), channel_id=1, source_target_pairs={{3,0},{2,1},{1,2},{0,3},{7,4},{6,5},{5,6},{4,7},{11,8},{10,9},{9,1... | collective-permute-start | bytes 294920 | tf_op jit(solution)/shard_map/ppermute | solution.py:48
  26.1 3.0 %collective-permute-done.6.refs_8_ = bf16[48,1024]{1,0:T(8,128)(2,1)S(1)} collective-permute-done((bf16[48,1024]{1,0:T(8,128)(2,1)S(1)}, bf16[48,1024]{1,0:T(8,128)(2,1)S(1)}, u32[]{:S(2)}, u32[]{:S(2)}) %collective-permute-start.6) | collective-permute-done | bytes 98336 | tf_op jit(solution)/shard_map/ppermute | solution.py:48
  29.1 0.6 first_mixed.1
  29.9 1.6 %collective-permute-start.8 = (bf16[48,896]{1,0:T(8,128)(2,1)S(1)}, bf16[48,896]{1,0:T(8,128)(2,1)S(1)}, u32[]{:S(2)}, u32[]{:S(2)}) collective-permute-start(bf16[48,896]{1,0:T(8,128)(2,1)S(1)} %get-tuple-element.112.refs_2_.refs_0_.refs_1_.refs_3_), channel_id=1, source_target_pairs={{1,0},{0,1},{3,2},{2,3},{5,4},{4,5},{7,6},{6,7},{9,8},{8,9},{11,10... | collective-permute-start | bytes 258056 | tf_op jit(solution)/shard_map/ppermute | solution.py:48
  31.5 2.5 %collective-permute-start.9 = (bf16[48,896]{1,0:T(8,128)(2,1)S(1)}, bf16[48,896]{1,0:T(8,128)(2,1)S(1)}, u32[]{:S(2)}, u32[]{:S(2)}) collective-permute-start(bf16[48,896]{1,0:T(8,128)(2,1)S(1)} %get-tuple-element.112.refs_2_.refs_0_.refs_1_.refs_3_), channel_id=1, source_target_pairs={{2,0},{3,1},{0,2},{1,3},{6,4},{7,5},{4,6},{5,7},{10,8},{11,9},{8,1... | collective-permute-start | bytes 258056 | tf_op jit(solution)/shard_map/ppermute | solution.py:48
  34.4 1.5 %collective-permute-start.11 = (bf16[24,896]{1,0:T(8,128)(2,1)S(1)}, bf16[24,896]{1,0:T(8,128)(2,1)S(1)}, u32[]{:S(2)}, u32[]{:S(2)}) collective-permute-start(bf16[24,896]{1,0:T(8,128)(2,1)S(1)} %get-tuple-element.118), channel_id=1, source_target_pairs={{0,4},{4,0},{1,5},{5,1},{2,6},{6,2},{3,7},{7,3},{8,12},{12,8},{9,1... | collective-permute-start | bytes 129032 | tf_op jit(solution)/shard_map/ppermute | solution.py:19
  35.9 2.6 %collective-permute-done.11.refs_1_ = bf16[24,896]{1,0:T(8,128)(2,1)S(1)} collective-permute-done((bf16[24,896]{1,0:T(8,128)(2,1)S(1)}, bf16[24,896]{1,0:T(8,128)(2,1)S(1)}, u32[]{:S(2)}, u32[]{:S(2)}) %collective-permute-start.11) | collective-permute-done | bytes 43040 | tf_op jit(solution)/shard_map/ppermute | solution.py:19
  38.5 2.8 %collective-permute-done.10.refs_3_.refs_6_ = bf16[48,896]{1,0:T(8,128)(2,1)S(1)} collective-permute-done((bf16[48,896]{1,0:T(8,128)(2,1)S(1)}, bf16[48,896]{1,0:T(8,128)(2,1)S(1)}, u32[]{:S(2)}, u32[]{:S(2)}) %collective-permute-start.10) | collective-permute-done | bytes 86048 | tf_op jit(solution)/shard_map/ppermute | solution.py:48
  41.3 1.4 gate_up_1.1
  42.7 1.8 %collective-permute-start.12 = (bf16[48,1024]{1,0:T(8,128)(2,1)S(1)}, bf16[48,1024]{1,0:T(8,128)(2,1)S(1)}, u32[]{:S(2)}, u32[]{:S(2)}) collective-permute-start(bf16[48,1024]{1,0:T(8,128)(2,1)S(1)} %get-tuple-element.120), channel_id=1, source_target_pairs={{0,4},{4,0},{1,5},{5,1},{2,6},{6,2},{3,7},{7,3},{8,12},{12,8},{9,1... | collective-permute-start | bytes 294920 | tf_op jit(solution)/shard_map/ppermute | solution.py:19
  44.4 1.8 %collective-permute-start.13 = (bf16[48,896]{1,0:T(8,128)(2,1)S(1)}, bf16[48,896]{1,0:T(8,128)(2,1)S(1)}, u32[]{:S(2)}, u32[]{:S(2)}) collective-permute-start(bf16[48,896]{1,0:T(8,128)(2,1)S(1)} %base_order.1.refs_6_.refs_0_.refs_2_), channel_id=1, source_target_pairs={{1,0},{0,1},{3,2},{2,3},{5,4},{4,5},{7,6},{6,7},{9,8},{8,9},{11,10... | collective-permute-start | bytes 258056 | tf_op jit(solution)/shard_map/ppermute | solution.py:48
  46.2 0.7 collective-permute-start.14
  46.9 1.9 %collective-permute-start.15 = (bf16[48,896]{1,0:T(8,128)(2,1)S(1)}, bf16[48,896]{1,0:T(8,128)(2,1)S(1)}, u32[]{:S(2)}, u32[]{:S(2)}) collective-permute-start(bf16[48,896]{1,0:T(8,128)(2,1)S(1)} %base_order.1.refs_6_.refs_0_.refs_2_), channel_id=1, source_target_pairs={{3,0},{2,1},{1,2},{0,3},{7,4},{6,5},{5,6},{4,7},{11,8},{10,9},{9,1... | collective-permute-start | bytes 258056 | tf_op jit(solution)/shard_map/ppermute | solution.py:48
  48.8 1.2 down_1.1
  50.0 5.3 %collective-permute-done.14.refs_2_.refs_4_ = bf16[48,896]{1,0:T(8,128)(2,1)S(1)} collective-permute-done((bf16[48,896]{1,0:T(8,128)(2,1)S(1)}, bf16[48,896]{1,0:T(8,128)(2,1)S(1)}, u32[]{:S(2)}, u32[]{:S(2)}) %collective-permute-start.14) | collective-permute-done | bytes 86048 | tf_op jit(solution)/shard_map/ppermute | solution.py:48
  55.3 1.5 %collective-permute-start.22 = (bf16[96,1024]{1,0:T(8,128)(2,1)S(1)}, bf16[96,1024]{1,0:T(8,128)(2,1)S(1)}, u32[]{:S(2)}, u32[]{:S(2)}) collective-permute-start(bf16[96,1024]{1,0:T(8,128)(2,1)S(1)} %get-tuple-element.139), channel_id=1, source_target_pairs={{0,4},{4,0},{1,5},{5,1},{2,6},{6,2},{3,7},{7,3},{8,12},{12,8},{9,1... | collective-permute-start | bytes 589832 | tf_op jit(solution)/shard_map/ppermute | solution.py:19
  56.8 1.6 %collective-permute-start.16 = (bf16[48,896]{1,0:T(8,128)(2,1)S(1)}, bf16[48,896]{1,0:T(8,128)(2,1)S(1)}, u32[]{:S(2)}, u32[]{:S(2)}) collective-permute-start(bf16[48,896]{1,0:T(8,128)(2,1)S(1)} %get-tuple-element.130), channel_id=1, source_target_pairs={{0,1},{1,0},{2,3},{3,2},{4,5},{5,4},{6,7},{7,6},{8,9},{9,8},{10,11... | collective-permute-start | bytes 258056 | tf_op jit(solution)/shard_map/ppermute | solution.py:55
  58.4 1.2 collective-permute-start.17
  59.7 1.5 %collective-permute-start.18 = (bf16[48,896]{1,0:T(8,128)(2,1)S(1)}, bf16[48,896]{1,0:T(8,128)(2,1)S(1)}, u32[]{:S(2)}, u32[]{:S(2)}) collective-permute-start(bf16[48,896]{1,0:T(8,128)(2,1)S(1)} %get-tuple-element.132), channel_id=1, source_target_pairs={{0,3},{1,2},{2,1},{3,0},{4,7},{5,6},{6,5},{7,4},{8,11},{9,10},{10,... | collective-permute-start | bytes 258056 | tf_op jit(solution)/shard_map/ppermute | solution.py:55
  61.2 5.6 %dense_a.1 = (bf16[128,7168]{1,0:T(8,128)(2,1)S(1)}, f32[4,7168]{1,0:T(4,128)S(1)}, bf16[3584,512]{1,0:T(8,128)(2,1)S(1)}, bf16[3584,512]{1,0:T(8,128)(2,1)S(1)}, bf16[3584,512]{1,0:T(8,128)(2,1)S(1)}) custom-call(s32[1,1,2,6]{3,2,1,0:T(2,128)} %refs_0_.9, s32[2]{0:T(128)} %bitcast.17, bf16[128,7168]{1,0:T(8,128)(2,1)S(1)} %collective-permute-done.7.hidden_ref, ...), custom_call_target="tpu_custom_call" | custom-call | flops 27525120 | bytes 4587520 | tf_op jit(solution)/shard_map/dense_a/pallas_call | solution.py:556
  67.3 1.5 %collective-permute-start.19 = (bf16[48,896]{1,0:T(8,128)(2,1)S(1)}, bf16[48,896]{1,0:T(8,128)(2,1)S(1)}, u32[]{:S(2)}, u32[]{:S(2)}) collective-permute-start(bf16[48,896]{1,0:T(8,128)(2,1)S(1)} %get-tuple-element.133.refs_2_.refs_0_.refs_5_.refs_11_), channel_id=1, source_target_pairs={{1,0},{0,1},{3,2},{2,3},{5,4},{4,5},{7,6},{6,7},{9,8},{8,9},{11,10... | collective-permute-start | bytes 258056 | tf_op jit(solution)/shard_map/ppermute | solution.py:48
  68.8 1.3 collective-permute-start.20
  70.1 1.6 %collective-permute-start.21 = (bf16[48,896]{1,0:T(8,128)(2,1)S(1)}, bf16[48,896]{1,0:T(8,128)(2,1)S(1)}, u32[]{:S(2)}, u32[]{:S(2)}) collective-permute-start(bf16[48,896]{1,0:T(8,128)(2,1)S(1)} %get-tuple-element.133.refs_2_.refs_0_.refs_5_.refs_11_), channel_id=1, source_target_pairs={{3,0},{2,1},{1,2},{0,3},{7,4},{6,5},{5,6},{4,7},{11,8},{10,9},{9,1... | collective-permute-start | bytes 258056 | tf_op jit(solution)/shard_map/ppermute | solution.py:48
  72.1 2.0 %fixed_2.1 = (f32[48,1536]{1,0:T(8,128)S(1)}, bf16[48,1536]{1,0:T(8,128)(2,1)S(1)}) custom-call(bf16[48,896]{1,0:T(8,128)(2,1)S(1)} %base_order.1.refs_6_.refs_0_.refs_2_, bf16[48,896]{1,0:T(8,128)(2,1)S(1)} %collective-permute-done.13.refs_1_.refs_3_, bf16[48,896]{1,0:T(8,128)(2,1)S(1)} %collective-permute-done.14.refs_2_.refs_4_, ...), custom_call_target="tpu_custom_call" | custom-call | flops 528482304 | bytes 11010048 | tf_op jit(solution)/shard_map/fixed_2/pallas_call | solution.py:327
  74.4 2.7 %collective-permute-done.20.refs_2_.refs_7_.refs_13_ = bf16[48,896]{1,0:T(8,128)(2,1)S(1)} collective-permute-done((bf16[48,896]{1,0:T(8,128)(2,1)S(1)}, bf16[48,896]{1,0:T(8,128)(2,1)S(1)}, u32[]{:S(2)}, u32[]{:S(2)}) %collective-permute-start.20) | collective-permute-done | bytes 86048 | tf_op jit(solution)/shard_map/ppermute | solution.py:48
  77.1 1.7 %gate_up_2.1 = (f32[48,1152]{1,0:T(8,128)S(1)}, bf16[48,1152]{1,0:T(8,128)(2,1)S(1)}, bf16[48,3584]{1,0:T(8,128)(2,1)S(1)}) custom-call(bf16[48,896]{1,0:T(8,128)(2,1)S(1)} %get-tuple-element.133.refs_2_.refs_0_.refs_5_.refs_11_, bf16[48,896]{1,0:T(8,128)(2,1)S(1)} %collective-permute-done.19.refs_1_.refs_6_.refs_12_, ...), custom_call_target="tpu_custom_call" | custom-call | flops 352321536 | bytes 7340032 | tf_op jit(solution)/shard_map/gate_up_2/pallas_call | solution.py:327
  79.1 0.7 prev_down.1
  79.9 3.7 %collective-permute-done.23.refs_1_ = bf16[48,1152]{1,0:T(8,128)(2,1)S(1)} collective-permute-done((bf16[48,1152]{1,0:T(8,128)(2,1)S(1)}, bf16[48,1152]{1,0:T(8,128)(2,1)S(1)}, u32[]{:S(2)}, u32[]{:S(2)}) %collective-permute-start.23) | collective-permute-done | bytes 110624 | tf_op jit(solution)/shard_map/ppermute | solution.py:19
  83.6 2.5 %back_rows_2.1 = (bf16[48,512]{1,0:T(8,128)(2,1)S(1)}, bf16[48,512]{1,0:T(8,128)(2,1)S(1)}, bf16[48,512]{1,0:T(8,128)(2,1)S(1)}, f32[48,1]{1,0:T(8,128)S(1)}, f3...) custom-call(f32[48,1152]{1,0:T(8,128)S(1)} %get-tuple-element.148.re, ...), custom_call_target="tpu_custom_call" | custom-call | flops 352321536 | bytes 7340032 | tf_op jit(solution)/shard_map/back_rows_2/pallas_call | solution.py:366
  86.1 1.6 %collective-permute-start.25 = (bf16[48,896]{1,0:T(8,128)(2,1)S(1)}, bf16[48,896]{1,0:T(8,128)(2,1)S(1)}, u32[]{:S(2)}, u32[]{:S(2)}) collective-permute-start(bf16[48,896]{1,0:T(8,128)(2,1)S(1)} %get-tuple-element.156), channel_id=1, source_target_pairs={{0,1},{1,0},{2,3},{3,2},{4,5},{5,4},{6,7},{7,6},{8,9},{9,8},{10,11... | collective-permute-start | bytes 258056 | tf_op jit(solution)/shard_map/ppermute | solution.py:55
  87.7 1.4 %collective-permute-start.26 = (bf16[48,896]{1,0:T(8,128)(2,1)S(1)}, bf16[48,896]{1,0:T(8,128)(2,1)S(1)}, u32[]{:S(2)}, u32[]{:S(2)}) collective-permute-start(bf16[48,896]{1,0:T(8,128)(2,1)S(1)} %get-tuple-element.157), channel_id=1, source_target_pairs={{0,2},{1,3},{2,0},{3,1},{4,6},{5,7},{6,4},{7,5},{8,10},{9,11},{10,... | collective-permute-start | bytes 258056 | tf_op jit(solution)/shard_map/ppermute | solution.py:55
  89.1 1.5 %collective-permute-start.27 = (bf16[48,896]{1,0:T(8,128)(2,1)S(1)}, bf16[48,896]{1,0:T(8,128)(2,1)S(1)}, u32[]{:S(2)}, u32[]{:S(2)}) collective-permute-start(bf16[48,896]{1,0:T(8,128)(2,1)S(1)} %get-tuple-element.158), channel_id=1, source_target_pairs={{0,3},{1,2},{2,1},{3,0},{4,7},{5,6},{6,5},{7,4},{8,11},{9,10},{10,... | collective-permute-start | bytes 258056 | tf_op jit(solution)/shard_map/ppermute | solution.py:55
  90.8 5.7 %dense_b.1 = (bf16[128,7168]{1,0:T(8,128)(2,1)S(1)}, f32[4,7168]{1,0:T(4,128)S(1)}) custom-call(s32[1,1,2,6]{3,2,1,0:T(2,128)} %refs_0_.9, s32[2]{0:T(128)} %bitcast.18, bf16[128,7168]{1,0:T(8,128)(2,1)S(1)} %collective-permute-done.7.hidden_ref, bf16[128,7168]{1,0:T(8,128)(2,1)S(1)} %bitcast.8, ...), custom_call_target="tpu_custom_call", output_to_operand_aliasing={{0}: (7, {})} | custom-call | flops 27525120 | bytes 4587520 | tf_op jit(solution)/shard_map/dense_b/pallas_call | solution.py:556
  97.3 1.9 %collective-permute-start.30 = (bf16[6,3584]{1,0:T(8,128)(2,1)S(1)}, bf16[6,3584]{1,0:T(8,128)(2,1)S(1)}, u32[]{:S(2)}, u32[]{:S(2)}) collective-permute-start(bf16[6,3584]{1,0:T(8,128)(2,1)S(1)} %get-tuple-element.166), channel_id=1, source_target_pairs={{0,4},{4,0},{1,5},{5,1},{2,6},{6,2},{3,7},{7,3},{8,12},{12,8},{9,1... | collective-permute-start | bytes 129032 | tf_op jit(solution)/shard_map/ppermute | solution.py:19
  99.2 0.6 collective-permute-start.31
  99.8 2.3 %collective-permute-start.32 = (bf16[48,896]{1,0:T(8,128)(2,1)S(1)}, bf16[48,896]{1,0:T(8,128)(2,1)S(1)}, u32[]{:S(2)}, u32[]{:S(2)}) collective-permute-start(bf16[48,896]{1,0:T(8,128)(2,1)S(1)} %get-tuple-element.161.refs_13_.refs_0_.refs_7_), channel_id=1, source_target_pairs={{2,0},{3,1},{0,2},{1,3},{6,4},{7,5},{4,6},{5,7},{10,8},{11,9},{8,1... | collective-permute-start | bytes 258056 | tf_op jit(solution)/shard_map/ppermute | solution.py:48
  102.0 1.5 %collective-permute-start.33 = (bf16[48,896]{1,0:T(8,128)(2,1)S(1)}, bf16[48,896]{1,0:T(8,128)(2,1)S(1)}, u32[]{:S(2)}, u32[]{:S(2)}) collective-permute-start(bf16[48,896]{1,0:T(8,128)(2,1)S(1)} %get-tuple-element.161.refs_13_.refs_0_.refs_7_), channel_id=1, source_target_pairs={{3,0},{2,1},{1,2},{0,3},{7,4},{6,5},{5,6},{4,7},{11,8},{10,9},{9,1... | collective-permute-start | bytes 258056 | tf_op jit(solution)/shard_map/ppermute | solution.py:48
  103.6 4.7 %weight_grad_2.1 = (bf16[1,2,3,3584,512]{4,3,2,1,0:T(8,128)(2,1)}, f32[8,128]{1,0:T(8,128)S(1)}) custom-call(bf16[48,3584]{1,0:T(8,128)(2,1)S(1)} %get-tuple-element.167.refs_0_, f32[48,1]{1,0:T(8,128)S(1)} %get-tuple-element.168.refs_1_, bf16[48,896]{1,0:T(8,128)(2,1)S(1)} %base_order.1.refs_6_.refs_0_.refs_2_, ...), custom_call_target="tpu_custom_call" | custom-call | flops 528482304 | bytes 11010048 | tf_op jit(solution)/shard_map/weight_grad_2/pallas_call | solution.py:413
  108.3 1.3 collective-permute-done.32.refs_2_.refs_9_
  109.6 0.8 back_1.1
  110.7 1.6 %second_grad.1 = (bf16[6,7296]{1,0:T(8,128)(2,1)S(1)}, f32[4,3584]{1,0:T(4,128)S(1)}, f32[4,3584]{1,0:T(4,128)S(1)}) custom-call(s32[1,1,2,6]{3,2,1,0:T(2,128)} %refs_0_.9, s32[2]{0:T(128)} %bitcast.19, bf16[6,10880]{1,0:T(8,128)(2,1)S(1)} %collective-permute-done.1.refs_2_.refs_1_, bf16[6,7168]{1,0:T(8,128)(2,1)S(1)} %get-tuple-element.110.refs_9_.refs_3_, ...), custom_call_target="tpu_custom_call" | custom-call | bytes 2655232 | tf_op jit(solution)/shard_map/second_grad/pallas_call | solution.py:253
  112.3 1.9 %collective-permute-start.39 = (f32[4,3584]{1,0:T(4,128)S(1)}, f32[4,3584]{1,0:T(4,128)S(1)}, u32[]{:S(2)}, u32[]{:S(2)}) collective-permute-start(f32[4,3584]{1,0:T(4,128)S(1)} %get-tuple-element.190), channel_id=1, source_target_pairs={{0,4},{4,0},{1,5},{5,1},{2,6},{6,2},{3,7},{7,3},{8,12},{12,8},{9,1... | collective-permute-start | bytes 172040 | tf_op jit(solution)/shard_map/ppermute | solution.py:19
  114.2 0.5 collective-permute-done.35.refs_1_
  114.7 2.4 %back_rows_1.1 = (bf16[48,512]{1,0:T(8,128)(2,1)S(1)}, bf16[48,512]{1,0:T(8,128)(2,1)S(1)}, f32[48,1]{1,0:T(8,128)S(1)}, bf16[48,896]{1,0:T(8,128)(2,1)S(1)}, bf...) custom-call(f32[48,640]{1,0:T(8,128)S(1)} %get-tuple-element.178.refs_0_, ...), custom_call_target="tpu_custom_call" | custom-call | flops 352321536 | bytes 7340032 | tf_op jit(solution)/shard_map/back_rows_1/pallas_call | solution.py:366
  117.1 2.2 %collective-permute-start.36 = (bf16[48,896]{1,0:T(8,128)(2,1)S(1)}, bf16[48,896]{1,0:T(8,128)(2,1)S(1)}, u32[]{:S(2)}, u32[]{:S(2)}) collective-permute-start(bf16[48,896]{1,0:T(8,128)(2,1)S(1)} %get-tuple-element.187), channel_id=1, source_target_pairs={{0,1},{1,0},{2,3},{3,2},{4,5},{5,4},{6,7},{7,6},{8,9},{9,8},{10,11... | collective-permute-start | bytes 258056 | tf_op jit(solution)/shard_map/ppermute | solution.py:55
  119.3 0.9 collective-permute-start.37
  120.2 1.6 %collective-permute-start.38 = (bf16[48,896]{1,0:T(8,128)(2,1)S(1)}, bf16[48,896]{1,0:T(8,128)(2,1)S(1)}, u32[]{:S(2)}, u32[]{:S(2)}) collective-permute-start(bf16[48,896]{1,0:T(8,128)(2,1)S(1)} %get-tuple-element.189), channel_id=1, source_target_pairs={{0,3},{1,2},{2,1},{3,0},{4,7},{5,6},{6,5},{7,4},{8,11},{9,10},{10,... | collective-permute-start | bytes 258056 | tf_op jit(solution)/shard_map/ppermute | solution.py:55
  121.7 4.7 %weight_grad_1.1 = (bf16[1,2,3,3584,512]{4,3,2,1,0:T(8,128)(2,1)}, f32[8,128]{1,0:T(8,128)S(1)}) custom-call(f32[48,1]{1,0:T(8,128)S(1)} %get-tuple-element.182.refs_0_.refs_3_, f32[48,1]{1,0:T(8,128)S(1)} %get-tuple-element.177.refs_5_.refs_1_.refs_2_, f32[48,1]{1,0:T(8,128)S(1)} %get-tuple-element.180.refs_6_.refs_2_, ...), custom_call_target="tpu_custom_call", output_to_operand_aliasing={{0}: (18, {})} | custom-call | flops 528482304 | bytes 11010048 | tf_op jit(solution)/shard_map/weight_grad_1/pallas_call | solution.py:413
  126.6 0.5 last_grad.1
  127.4 1.6 %collective-permute-start.41 = (bf16[6,3584]{1,0:T(8,128)(2,1)S(1)}, bf16[6,3584]{1,0:T(8,128)(2,1)S(1)}, u32[]{:S(2)}, u32[]{:S(2)}) collective-permute-start(bf16[6,3584]{1,0:T(8,128)(2,1)S(1)} %get-tuple-element.197), channel_id=1, source_target_pairs={{0,28},{4,24},{8,4},{12,0},{16,12},{20,8},{24,20},{28,16},{1,29},{... | collective-permute-start | bytes 129032 | tf_op jit(solution)/shard_map/ppermute | solution.py:29
  128.9 1.4 collective-permute-start.42
  130.3 1.4 %collective-permute-start.43 = (f32[4,896]{1,0:T(4,128)S(1)}, f32[4,896]{1,0:T(4,128)S(1)}, u32[]{:S(2)}, u32[]{:S(2)}) collective-permute-start(f32[4,896]{1,0:T(4,128)S(1)} %get-tuple-element.202), channel_id=1, source_target_pairs={{0,2},{1,3},{2,0},{3,1},{4,6},{5,7},{6,4},{7,5},{8,10},{9,11},{10,... | collective-permute-start | bytes 43016 | tf_op jit(solution)/shard_map/ppermute | solution.py:55
  131.7 1.6 %collective-permute-start.44 = (f32[4,896]{1,0:T(4,128)S(1)}, f32[4,896]{1,0:T(4,128)S(1)}, u32[]{:S(2)}, u32[]{:S(2)}) collective-permute-start(f32[4,896]{1,0:T(4,128)S(1)} %get-tuple-element.203), channel_id=1, source_target_pairs={{0,3},{1,2},{2,1},{3,0},{4,7},{5,6},{6,5},{7,4},{8,11},{9,10},{10,... | collective-permute-start | bytes 43016 | tf_op jit(solution)/shard_map/ppermute | solution.py:55
  133.4 2.9 %finish.1 = (bf16[128,7168]{1,0:T(8,128)(2,1)}, f32[8,128]{1,0:T(8,128)S(1)}) custom-call(s32[1,1,2,6]{3,2,1,0:T(2,128)} %copy-done.4, bf16[128,7168]{1,0:T(8,128)(2,1)S(1)} %collective-permute-done.29.refs_1_, bf16[6,7168]{1,0:T(8,128)(2,1)S(1)} %get-tuple-element.163.refs_2_, bf16[6,7296]{1,0:T(8,128)(2,1)S(1)} %collective-permute-done.34.refs_3_, ...), custom_call_target="tpu_custom_call" | custom-call | bytes 3933696 | tf_op jit(solution)/shard_map/finish/pallas_call | solution.py:253
  136.2 1.0 collective-permute-done.44.refs_3_
  137.2 0.6 gain_sum.1
  (60 shorter events, 5.2 us)
Async XLA Ops:
  0.6 3.9 %collective-permute-start = (s32[1,1,2,6]{3,2,1,0:T(2,128)}, s32[1,1,2,6]{3,2,1,0:T(2,128)S(1)}, u32[]{:S(2)}, u32[]{:S(2)}) collective-permute-start(s32[1,1,2,6]{3,2,1,0:T(2,128)} %refs_0_.9), channel_id=1, source_target_pairs={{0,24},{8,0},{16,8},{24,16},{1,25},{9,1},{17,9},{25,17},{2,26},{10... | collective-permute-start | bytes 152 | tf_op jit(solution)/shard_map/ppermute | solution.py:19
  4.6 4.0 %copy-start.4 = (s32[1,1,2,6]{3,2,1,0:T(2,128)}, s32[1,1,2,6]{3,2,1,0:T(2,128)S(1)}, u32[]{:S(2)}) copy-start(s32[1,1,2,6]{3,2,1,0:T(2,128)S(1)} %collective-permute-done.refs_6_.refs_0_) | copy-start | bytes 148
  4.6 5.6 %copy-start.3 = (bf16[1,1,128,7168]{3,2,1,0:T(8,128)(2,1)S(1)}, bf16[1,1,128,7168]{3,2,1,0:T(8,128)(2,1)}, u32[]{:S(2)}) copy-start(bf16[1,1,128,7168]{3,2,1,0:T(8,128)(2,1)} %param.8) | copy-start | bytes 5505028
  8.6 10.2 %collective-permute-start.3 = (bf16[22,3712]{1,0:T(8,128)(2,1)S(1)}, bf16[22,3712]{1,0:T(8,128)(2,1)S(1)}, u32[]{:S(2)}, u32[]{:S(2)}) collective-permute-start(bf16[22,3712]{1,0:T(8,128)(2,1)S(1)} %get-tuple-element.107), channel_id=1, source_target_pairs={{0,4},{4,0},{1,5},{5,1},{2,6},{6,2},{3,7},{7,3},{8,12},{12,8},{9,1... | collective-permute-start | bytes 489992 | tf_op jit(solution)/shard_map/ppermute | solution.py:19
  10.2 8.6 %copy-start = (bf16[1,1,128,7168]{3,2,1,0:T(8,128)(2,1)S(1)}, bf16[1,1,128,7168]{3,2,1,0:T(8,128)(2,1)}, u32[]{:S(2)}) copy-start(bf16[1,1,128,7168]{3,2,1,0:T(8,128)(2,1)} %param.9) | copy-start | bytes 5505028
  10.2 8.6 %copy-start.2 = (f32[2,2,7168]{2,1,0:T(2,128)S(1)}, f32[2,2,7168]{2,1,0:T(2,128)}, u32[]{:S(2)}) copy-start(f32[2,2,7168]{2,1,0:T(2,128)} %refs_8_.1) | copy-start | bytes 344068
  13.3 5.5 %collective-permute-start.1 = (bf16[6,10880]{1,0:T(8,128)(2,1)S(1)}, bf16[6,10880]{1,0:T(8,128)(2,1)S(1)}, u32[]{:S(2)}, u32[]{:S(2)}) collective-permute-start(bf16[6,10880]{1,0:T(8,128)(2,1)S(1)} %get-tuple-element.105), channel_id=1, source_target_pairs={{0,8},{4,12},{8,16},{12,20},{16,24},{20,28},{24,0},{28,4},{1,9},{5... | collective-permute-start | bytes 391688 | tf_op jit(solution)/shard_map/ppermute | solution.py:29
  13.7 5.1 %collective-permute-start.2 = (bf16[6,3712]{1,0:T(8,128)(2,1)S(1)}, bf16[6,3712]{1,0:T(8,128)(2,1)S(1)}, u32[]{:S(2)}, u32[]{:S(2)}) collective-permute-start(bf16[6,3712]{1,0:T(8,128)(2,1)S(1)} %get-tuple-element.106), channel_id=1, source_target_pairs={{0,12},{4,8},{8,20},{12,16},{16,28},{20,24},{24,4},{28,0},{1,13},{... | collective-permute-start | bytes 133640 | tf_op jit(solution)/shard_map/ppermute | solution.py:29
  14.2 11.9 %collective-permute-start.4 = (bf16[48,1024]{1,0:T(8,128)(2,1)S(1)}, bf16[48,1024]{1,0:T(8,128)(2,1)S(1)}, u32[]{:S(2)}, u32[]{:S(2)}) collective-permute-start(bf16[48,1024]{1,0:T(8,128)(2,1)S(1)} %get-tuple-element.111.refs_5_), channel_id=1, source_target_pairs={{1,0},{0,1},{3,2},{2,3},{5,4},{4,5},{7,6},{6,7},{9,8},{8,9},{11,10... | collective-permute-start | bytes 294920 | tf_op jit(solution)/shard_map/ppermute | solution.py:48
  15.7 10.3 %collective-permute-start.5 = (bf16[48,1024]{1,0:T(8,128)(2,1)S(1)}, bf16[48,1024]{1,0:T(8,128)(2,1)S(1)}, u32[]{:S(2)}, u32[]{:S(2)}) collective-permute-start(bf16[48,1024]{1,0:T(8,128)(2,1)S(1)} %get-tuple-element.111.refs_5_), channel_id=1, source_target_pairs={{2,0},{3,1},{0,2},{1,3},{6,4},{7,5},{4,6},{5,7},{10,8},{11,9},{8,1... | collective-permute-start | bytes 294920 | tf_op jit(solution)/shard_map/ppermute | solution.py:48
  22.4 6.7 %collective-permute-start.6 = (bf16[48,1024]{1,0:T(8,128)(2,1)S(1)}, bf16[48,1024]{1,0:T(8,128)(2,1)S(1)}, u32[]{:S(2)}, u32[]{:S(2)}) collective-permute-start(bf16[48,1024]{1,0:T(8,128)(2,1)S(1)} %get-tuple-element.111.refs_5_), channel_id=1, source_target_pairs={{3,0},{2,1},{1,2},{0,3},{7,4},{6,5},{5,6},{4,7},{11,8},{10,9},{9,1... | collective-permute-start | bytes 294920 | tf_op jit(solution)/shard_map/ppermute | solution.py:48
  29.7 31.5 %collective-permute-start.7 = (bf16[128,7168]{1,0:T(8,128)(2,1)S(1)}, bf16[128,7168]{1,0:T(8,128)(2,1)S(1)}, u32[]{:S(2)}, u32[]{:S(2)}) collective-permute-start(bf16[128,7168]{1,0:T(8,128)(2,1)S(1)} %bitcast.14), channel_id=1, source_target_pairs={{0,8},{8,16},{16,24},{24,0},{1,9},{9,17},{17,25},{25,1},{2,10},{10... | collective-permute-start | bytes 5505032 | tf_op jit(solution)/shard_map/ppermute | solution.py:19
  29.9 8.6 %collective-permute-start.8 = (bf16[48,896]{1,0:T(8,128)(2,1)S(1)}, bf16[48,896]{1,0:T(8,128)(2,1)S(1)}, u32[]{:S(2)}, u32[]{:S(2)}) collective-permute-start(bf16[48,896]{1,0:T(8,128)(2,1)S(1)} %get-tuple-element.112.refs_2_.refs_0_.refs_1_.refs_3_), channel_id=1, source_target_pairs={{1,0},{0,1},{3,2},{2,3},{5,4},{4,5},{7,6},{6,7},{9,8},{8,9},{11,10... | collective-permute-start | bytes 258056 | tf_op jit(solution)/shard_map/ppermute | solution.py:48
  31.5 7.0 %collective-permute-start.9 = (bf16[48,896]{1,0:T(8,128)(2,1)S(1)}, bf16[48,896]{1,0:T(8,128)(2,1)S(1)}, u32[]{:S(2)}, u32[]{:S(2)}) collective-permute-start(bf16[48,896]{1,0:T(8,128)(2,1)S(1)} %get-tuple-element.112.refs_2_.refs_0_.refs_1_.refs_3_), channel_id=1, source_target_pairs={{2,0},{3,1},{0,2},{1,3},{6,4},{7,5},{4,6},{5,7},{10,8},{11,9},{8,1... | collective-permute-start | bytes 258056 | tf_op jit(solution)/shard_map/ppermute | solution.py:48
  34.0 7.3 %collective-permute-start.10 = (bf16[48,896]{1,0:T(8,128)(2,1)S(1)}, bf16[48,896]{1,0:T(8,128)(2,1)S(1)}, u32[]{:S(2)}, u32[]{:S(2)}) collective-permute-start(bf16[48,896]{1,0:T(8,128)(2,1)S(1)} %get-tuple-element.112.refs_2_.refs_0_.refs_1_.refs_3_), channel_id=1, source_target_pairs={{3,0},{2,1},{1,2},{0,3},{7,4},{6,5},{5,6},{4,7},{11,8},{10,9},{9,1... | collective-permute-start | bytes 258056 | tf_op jit(solution)/shard_map/ppermute | solution.py:48
  34.4 4.1 %collective-permute-start.11 = (bf16[24,896]{1,0:T(8,128)(2,1)S(1)}, bf16[24,896]{1,0:T(8,128)(2,1)S(1)}, u32[]{:S(2)}, u32[]{:S(2)}) collective-permute-start(bf16[24,896]{1,0:T(8,128)(2,1)S(1)} %get-tuple-element.118), channel_id=1, source_target_pairs={{0,4},{4,0},{1,5},{5,1},{2,6},{6,2},{3,7},{7,3},{8,12},{12,8},{9,1... | collective-permute-start | bytes 129032 | tf_op jit(solution)/shard_map/ppermute | solution.py:19
  42.7 18.5 %copy-start.1 = (bf16[1,1,128,7168]{3,2,1,0:T(8,128)(2,1)S(1)}, bf16[1,1,128,7168]{3,2,1,0:T(8,128)(2,1)}, u32[]{:S(2)}) copy-start(bf16[1,1,128,7168]{3,2,1,0:T(8,128)(2,1)} %param.10) | copy-start | bytes 5505028
  42.7 6.1 %collective-permute-start.12 = (bf16[48,1024]{1,0:T(8,128)(2,1)S(1)}, bf16[48,1024]{1,0:T(8,128)(2,1)S(1)}, u32[]{:S(2)}, u32[]{:S(2)}) collective-permute-start(bf16[48,1024]{1,0:T(8,128)(2,1)S(1)} %get-tuple-element.120), channel_id=1, source_target_pairs={{0,4},{4,0},{1,5},{5,1},{2,6},{6,2},{3,7},{7,3},{8,12},{12,8},{9,1... | collective-permute-start | bytes 294920 | tf_op jit(solution)/shard_map/ppermute | solution.py:19
  44.4 5.6 %collective-permute-start.13 = (bf16[48,896]{1,0:T(8,128)(2,1)S(1)}, bf16[48,896]{1,0:T(8,128)(2,1)S(1)}, u32[]{:S(2)}, u32[]{:S(2)}) collective-permute-start(bf16[48,896]{1,0:T(8,128)(2,1)S(1)} %base_order.1.refs_6_.refs_0_.refs_2_), channel_id=1, source_target_pairs={{1,0},{0,1},{3,2},{2,3},{5,4},{4,5},{7,6},{6,7},{9,8},{8,9},{11,10... | collective-permute-start | bytes 258056 | tf_op jit(solution)/shard_map/ppermute | solution.py:48
  46.2 9.1 %collective-permute-start.14 = (bf16[48,896]{1,0:T(8,128)(2,1)S(1)}, bf16[48,896]{1,0:T(8,128)(2,1)S(1)}, u32[]{:S(2)}, u32[]{:S(2)}) collective-permute-start(bf16[48,896]{1,0:T(8,128)(2,1)S(1)} %base_order.1.refs_6_.refs_0_.refs_2_), channel_id=1, source_target_pairs={{2,0},{3,1},{0,2},{1,3},{6,4},{7,5},{4,6},{5,7},{10,8},{11,9},{8,1... | collective-permute-start | bytes 258056 | tf_op jit(solution)/shard_map/ppermute | solution.py:48
  46.9 8.3 %collective-permute-start.15 = (bf16[48,896]{1,0:T(8,128)(2,1)S(1)}, bf16[48,896]{1,0:T(8,128)(2,1)S(1)}, u32[]{:S(2)}, u32[]{:S(2)}) collective-permute-start(bf16[48,896]{1,0:T(8,128)(2,1)S(1)} %base_order.1.refs_6_.refs_0_.refs_2_), channel_id=1, source_target_pairs={{3,0},{2,1},{1,2},{0,3},{7,4},{6,5},{5,6},{4,7},{11,8},{10,9},{9,1... | collective-permute-start | bytes 258056 | tf_op jit(solution)/shard_map/ppermute | solution.py:48
  55.3 16.4 %collective-permute-start.22 = (bf16[96,1024]{1,0:T(8,128)(2,1)S(1)}, bf16[96,1024]{1,0:T(8,128)(2,1)S(1)}, u32[]{:S(2)}, u32[]{:S(2)}) collective-permute-start(bf16[96,1024]{1,0:T(8,128)(2,1)S(1)} %get-tuple-element.139), channel_id=1, source_target_pairs={{0,4},{4,0},{1,5},{5,1},{2,6},{6,2},{3,7},{7,3},{8,12},{12,8},{9,1... | collective-permute-start | bytes 589832 | tf_op jit(solution)/shard_map/ppermute | solution.py:19
  56.8 10.0 %collective-permute-start.16 = (bf16[48,896]{1,0:T(8,128)(2,1)S(1)}, bf16[48,896]{1,0:T(8,128)(2,1)S(1)}, u32[]{:S(2)}, u32[]{:S(2)}) collective-permute-start(bf16[48,896]{1,0:T(8,128)(2,1)S(1)} %get-tuple-element.130), channel_id=1, source_target_pairs={{0,1},{1,0},{2,3},{3,2},{4,5},{5,4},{6,7},{7,6},{8,9},{9,8},{10,11... | collective-permute-start | bytes 258056 | tf_op jit(solution)/shard_map/ppermute | solution.py:55
  58.4 8.7 %collective-permute-start.17 = (bf16[48,896]{1,0:T(8,128)(2,1)S(1)}, bf16[48,896]{1,0:T(8,128)(2,1)S(1)}, u32[]{:S(2)}, u32[]{:S(2)}) collective-permute-start(bf16[48,896]{1,0:T(8,128)(2,1)S(1)} %get-tuple-element.131), channel_id=1, source_target_pairs={{0,2},{1,3},{2,0},{3,1},{4,6},{5,7},{6,4},{7,5},{8,10},{9,11},{10,... | collective-permute-start | bytes 258056 | tf_op jit(solution)/shard_map/ppermute | solution.py:55
  59.7 7.5 %collective-permute-start.18 = (bf16[48,896]{1,0:T(8,128)(2,1)S(1)}, bf16[48,896]{1,0:T(8,128)(2,1)S(1)}, u32[]{:S(2)}, u32[]{:S(2)}) collective-permute-start(bf16[48,896]{1,0:T(8,128)(2,1)S(1)} %get-tuple-element.132), channel_id=1, source_target_pairs={{0,3},{1,2},{2,1},{3,0},{4,7},{5,6},{6,5},{7,4},{8,11},{9,10},{10,... | collective-permute-start | bytes 258056 | tf_op jit(solution)/shard_map/ppermute | solution.py:55
  67.3 7.2 %collective-permute-start.19 = (bf16[48,896]{1,0:T(8,128)(2,1)S(1)}, bf16[48,896]{1,0:T(8,128)(2,1)S(1)}, u32[]{:S(2)}, u32[]{:S(2)}) collective-permute-start(bf16[48,896]{1,0:T(8,128)(2,1)S(1)} %get-tuple-element.133.refs_2_.refs_0_.refs_5_.refs_11_), channel_id=1, source_target_pairs={{1,0},{0,1},{3,2},{2,3},{5,4},{4,5},{7,6},{6,7},{9,8},{8,9},{11,10... | collective-permute-start | bytes 258056 | tf_op jit(solution)/shard_map/ppermute | solution.py:48
  68.8 8.3 %collective-permute-start.20 = (bf16[48,896]{1,0:T(8,128)(2,1)S(1)}, bf16[48,896]{1,0:T(8,128)(2,1)S(1)}, u32[]{:S(2)}, u32[]{:S(2)}) collective-permute-start(bf16[48,896]{1,0:T(8,128)(2,1)S(1)} %get-tuple-element.133.refs_2_.refs_0_.refs_5_.refs_11_), channel_id=1, source_target_pairs={{2,0},{3,1},{0,2},{1,3},{6,4},{7,5},{4,6},{5,7},{10,8},{11,9},{8,1... | collective-permute-start | bytes 258056 | tf_op jit(solution)/shard_map/ppermute | solution.py:48
  70.1 6.9 %collective-permute-start.21 = (bf16[48,896]{1,0:T(8,128)(2,1)S(1)}, bf16[48,896]{1,0:T(8,128)(2,1)S(1)}, u32[]{:S(2)}, u32[]{:S(2)}) collective-permute-start(bf16[48,896]{1,0:T(8,128)(2,1)S(1)} %get-tuple-element.133.refs_2_.refs_0_.refs_5_.refs_11_), channel_id=1, source_target_pairs={{3,0},{2,1},{1,2},{0,3},{7,4},{6,5},{5,6},{4,7},{11,8},{10,9},{9,1... | collective-permute-start | bytes 258056 | tf_op jit(solution)/shard_map/ppermute | solution.py:48
  74.1 5.8 %collective-permute-start.24 = (bf16[48,1536]{1,0:T(8,128)(2,1)S(1)}, bf16[48,1536]{1,0:T(8,128)(2,1)S(1)}, u32[]{:S(2)}, u32[]{:S(2)}) collective-permute-start(bf16[48,1536]{1,0:T(8,128)(2,1)S(1)} %get-tuple-element.150), channel_id=1, source_target_pairs={{0,4},{4,0},{1,5},{5,1},{2,6},{6,2},{3,7},{7,3},{8,12},{12,8},{9,1... | collective-permute-start | bytes 442376 | tf_op jit(solution)/shard_map/ppermute | solution.py:19
  78.8 4.8 %collective-permute-start.23 = (bf16[48,1152]{1,0:T(8,128)(2,1)S(1)}, bf16[48,1152]{1,0:T(8,128)(2,1)S(1)}, u32[]{:S(2)}, u32[]{:S(2)}) collective-permute-start(bf16[48,1152]{1,0:T(8,128)(2,1)S(1)} %get-tuple-element.149.refs_5_), channel_id=1, source_target_pairs={{0,4},{4,0},{1,5},{5,1},{2,6},{6,2},{3,7},{7,3},{8,12},{12,8},{9,1... | collective-permute-start | bytes 331784 | tf_op jit(solution)/shard_map/ppermute | solution.py:19
  86.1 10.4 %collective-permute-start.25 = (bf16[48,896]{1,0:T(8,128)(2,1)S(1)}, bf16[48,896]{1,0:T(8,128)(2,1)S(1)}, u32[]{:S(2)}, u32[]{:S(2)}) collective-permute-start(bf16[48,896]{1,0:T(8,128)(2,1)S(1)} %get-tuple-element.156), channel_id=1, source_target_pairs={{0,1},{1,0},{2,3},{3,2},{4,5},{5,4},{6,7},{7,6},{8,9},{9,8},{10,11... | collective-permute-start | bytes 258056 | tf_op jit(solution)/shard_map/ppermute | solution.py:55
  87.7 8.9 %collective-permute-start.26 = (bf16[48,896]{1,0:T(8,128)(2,1)S(1)}, bf16[48,896]{1,0:T(8,128)(2,1)S(1)}, u32[]{:S(2)}, u32[]{:S(2)}) collective-permute-start(bf16[48,896]{1,0:T(8,128)(2,1)S(1)} %get-tuple-element.157), channel_id=1, source_target_pairs={{0,2},{1,3},{2,0},{3,1},{4,6},{5,7},{6,4},{7,5},{8,10},{9,11},{10,... | collective-permute-start | bytes 258056 | tf_op jit(solution)/shard_map/ppermute | solution.py:55
  89.1 7.5 %collective-permute-start.27 = (bf16[48,896]{1,0:T(8,128)(2,1)S(1)}, bf16[48,896]{1,0:T(8,128)(2,1)S(1)}, u32[]{:S(2)}, u32[]{:S(2)}) collective-permute-start(bf16[48,896]{1,0:T(8,128)(2,1)S(1)} %get-tuple-element.158), channel_id=1, source_target_pairs={{0,3},{1,2},{2,1},{3,0},{4,7},{5,6},{6,5},{7,4},{8,11},{9,10},{10,... | collective-permute-start | bytes 258056 | tf_op jit(solution)/shard_map/ppermute | solution.py:55
  90.6 5.9 %collective-permute-start.28 = (bf16[48,512]{1,0:T(8,128)(2,1)S(1)}, bf16[48,512]{1,0:T(8,128)(2,1)S(1)}, u32[]{:S(2)}, u32[]{:S(2)}) collective-permute-start(bf16[48,512]{1,0:T(8,128)(2,1)S(1)} %get-tuple-element.160), channel_id=1, source_target_pairs={{0,4},{4,0},{1,5},{5,1},{2,6},{6,2},{3,7},{7,3},{8,12},{12,8},{9,1... | collective-permute-start | bytes 147464 | tf_op jit(solution)/shard_map/ppermute | solution.py:19
  97.0 36.3 %collective-permute-start.29 = (bf16[128,7168]{1,0:T(8,128)(2,1)S(1)}, bf16[128,7168]{1,0:T(8,128)(2,1)S(1)}, u32[]{:S(2)}, u32[]{:S(2)}) collective-permute-start(bf16[128,7168]{1,0:T(8,128)(2,1)S(1)} %get-tuple-element.162), channel_id=1, source_target_pairs={{0,24},{8,0},{16,8},{24,16},{1,25},{9,1},{17,9},{25,17},{2,26},{10... | collective-permute-start | bytes 5505032 | tf_op jit(solution)/shard_map/ppermute | solution.py:19
  97.3 6.3 %collective-permute-start.30 = (bf16[6,3584]{1,0:T(8,128)(2,1)S(1)}, bf16[6,3584]{1,0:T(8,128)(2,1)S(1)}, u32[]{:S(2)}, u32[]{:S(2)}) collective-permute-start(bf16[6,3584]{1,0:T(8,128)(2,1)S(1)} %get-tuple-element.166), channel_id=1, source_target_pairs={{0,4},{4,0},{1,5},{5,1},{2,6},{6,2},{3,7},{7,3},{8,12},{12,8},{9,1... | collective-permute-start | bytes 129032 | tf_op jit(solution)/shard_map/ppermute | solution.py:19
  99.2 9.1 %collective-permute-start.31 = (bf16[48,896]{1,0:T(8,128)(2,1)S(1)}, bf16[48,896]{1,0:T(8,128)(2,1)S(1)}, u32[]{:S(2)}, u32[]{:S(2)}) collective-permute-start(bf16[48,896]{1,0:T(8,128)(2,1)S(1)} %get-tuple-element.161.refs_13_.refs_0_.refs_7_), channel_id=1, source_target_pairs={{1,0},{0,1},{3,2},{2,3},{5,4},{4,5},{7,6},{6,7},{9,8},{8,9},{11,10... | collective-permute-start | bytes 258056 | tf_op jit(solution)/shard_map/ppermute | solution.py:48
  99.8 9.8 %collective-permute-start.32 = (bf16[48,896]{1,0:T(8,128)(2,1)S(1)}, bf16[48,896]{1,0:T(8,128)(2,1)S(1)}, u32[]{:S(2)}, u32[]{:S(2)}) collective-permute-start(bf16[48,896]{1,0:T(8,128)(2,1)S(1)} %get-tuple-element.161.refs_13_.refs_0_.refs_7_), channel_id=1, source_target_pairs={{2,0},{3,1},{0,2},{1,3},{6,4},{7,5},{4,6},{5,7},{10,8},{11,9},{8,1... | collective-permute-start | bytes 258056 | tf_op jit(solution)/shard_map/ppermute | solution.py:48
  102.0 7.6 %collective-permute-start.33 = (bf16[48,896]{1,0:T(8,128)(2,1)S(1)}, bf16[48,896]{1,0:T(8,128)(2,1)S(1)}, u32[]{:S(2)}, u32[]{:S(2)}) collective-permute-start(bf16[48,896]{1,0:T(8,128)(2,1)S(1)} %get-tuple-element.161.refs_13_.refs_0_.refs_7_), channel_id=1, source_target_pairs={{3,0},{2,1},{1,2},{0,3},{7,4},{6,5},{5,6},{4,7},{11,8},{10,9},{9,1... | collective-permute-start | bytes 258056 | tf_op jit(solution)/shard_map/ppermute | solution.py:48
  110.4 4.3 %collective-permute-start.35 = (bf16[48,640]{1,0:T(8,128)(2,1)S(1)}, bf16[48,640]{1,0:T(8,128)(2,1)S(1)}, u32[]{:S(2)}, u32[]{:S(2)}) collective-permute-start(bf16[48,640]{1,0:T(8,128)(2,1)S(1)} %get-tuple-element.173.refs_10_), channel_id=1, source_target_pairs={{0,4},{4,0},{1,5},{5,1},{2,6},{6,2},{3,7},{7,3},{8,12},{12,8},{9,1... | collective-permute-start | bytes 184328 | tf_op jit(solution)/shard_map/ppermute | solution.py:19
  112.3 9.4 %collective-permute-start.39 = (f32[4,3584]{1,0:T(4,128)S(1)}, f32[4,3584]{1,0:T(4,128)S(1)}, u32[]{:S(2)}, u32[]{:S(2)}) collective-permute-start(f32[4,3584]{1,0:T(4,128)S(1)} %get-tuple-element.190), channel_id=1, source_target_pairs={{0,4},{4,0},{1,5},{5,1},{2,6},{6,2},{3,7},{7,3},{8,12},{12,8},{9,1... | collective-permute-start | bytes 172040 | tf_op jit(solution)/shard_map/ppermute | solution.py:19
  117.1 9.3 %collective-permute-start.36 = (bf16[48,896]{1,0:T(8,128)(2,1)S(1)}, bf16[48,896]{1,0:T(8,128)(2,1)S(1)}, u32[]{:S(2)}, u32[]{:S(2)}) collective-permute-start(bf16[48,896]{1,0:T(8,128)(2,1)S(1)} %get-tuple-element.187), channel_id=1, source_target_pairs={{0,1},{1,0},{2,3},{3,2},{4,5},{5,4},{6,7},{7,6},{8,9},{9,8},{10,11... | collective-permute-start | bytes 258056 | tf_op jit(solution)/shard_map/ppermute | solution.py:55
  119.3 7.3 %collective-permute-start.37 = (bf16[48,896]{1,0:T(8,128)(2,1)S(1)}, bf16[48,896]{1,0:T(8,128)(2,1)S(1)}, u32[]{:S(2)}, u32[]{:S(2)}) collective-permute-start(bf16[48,896]{1,0:T(8,128)(2,1)S(1)} %get-tuple-element.188), channel_id=1, source_target_pairs={{0,2},{1,3},{2,0},{3,1},{4,6},{5,7},{6,4},{7,5},{8,10},{9,11},{10,... | collective-permute-start | bytes 258056 | tf_op jit(solution)/shard_map/ppermute | solution.py:55
  120.2 6.4 %collective-permute-start.38 = (bf16[48,896]{1,0:T(8,128)(2,1)S(1)}, bf16[48,896]{1,0:T(8,128)(2,1)S(1)}, u32[]{:S(2)}, u32[]{:S(2)}) collective-permute-start(bf16[48,896]{1,0:T(8,128)(2,1)S(1)} %get-tuple-element.189), channel_id=1, source_target_pairs={{0,3},{1,2},{2,1},{3,0},{4,7},{5,6},{6,5},{7,4},{8,11},{9,10},{10,... | collective-permute-start | bytes 258056 | tf_op jit(solution)/shard_map/ppermute | solution.py:55
  121.7 8.6 %collective-permute-start.34 = (bf16[6,7296]{1,0:T(8,128)(2,1)S(1)}, bf16[6,7296]{1,0:T(8,128)(2,1)S(1)}, u32[]{:S(2)}, u32[]{:S(2)}) collective-permute-start(bf16[6,7296]{1,0:T(8,128)(2,1)S(1)} %get-tuple-element.174), channel_id=1, source_target_pairs={{0,24},{8,0},{16,8},{24,16},{1,25},{9,1},{17,9},{25,17},{2,26},{10... | collective-permute-start | bytes 262664 | tf_op jit(solution)/shard_map/ppermute | solution.py:19
  127.1 4.6 %collective-permute-start.40 = (bf16[6,3584]{1,0:T(8,128)(2,1)S(1)}, bf16[6,3584]{1,0:T(8,128)(2,1)S(1)}, u32[]{:S(2)}, u32[]{:S(2)}) collective-permute-start(bf16[6,3584]{1,0:T(8,128)(2,1)S(1)} %get-tuple-element.196), channel_id=1, source_target_pairs={{0,24},{4,28},{8,0},{12,4},{16,8},{20,12},{24,16},{28,20},{1,25},{... | collective-permute-start | bytes 129032 | tf_op jit(solution)/shard_map/ppermute | solution.py:29
  127.4 6.0 %collective-permute-start.41 = (bf16[6,3584]{1,0:T(8,128)(2,1)S(1)}, bf16[6,3584]{1,0:T(8,128)(2,1)S(1)}, u32[]{:S(2)}, u32[]{:S(2)}) collective-permute-start(bf16[6,3584]{1,0:T(8,128)(2,1)S(1)} %get-tuple-element.197), channel_id=1, source_target_pairs={{0,28},{4,24},{8,4},{12,0},{16,12},{20,8},{24,20},{28,16},{1,29},{... | collective-permute-start | bytes 129032 | tf_op jit(solution)/shard_map/ppermute | solution.py:29
  128.9 7.3 %collective-permute-start.42 = (f32[4,896]{1,0:T(4,128)S(1)}, f32[4,896]{1,0:T(4,128)S(1)}, u32[]{:S(2)}, u32[]{:S(2)}) collective-permute-start(f32[4,896]{1,0:T(4,128)S(1)} %get-tuple-element.201), channel_id=1, source_target_pairs={{0,1},{1,0},{2,3},{3,2},{4,5},{5,4},{6,7},{7,6},{8,9},{9,8},{10,11... | collective-permute-start | bytes 43016 | tf_op jit(solution)/shard_map/ppermute | solution.py:55
  130.3 5.9 %collective-permute-start.43 = (f32[4,896]{1,0:T(4,128)S(1)}, f32[4,896]{1,0:T(4,128)S(1)}, u32[]{:S(2)}, u32[]{:S(2)}) collective-permute-start(f32[4,896]{1,0:T(4,128)S(1)} %get-tuple-element.202), channel_id=1, source_target_pairs={{0,2},{1,3},{2,0},{3,1},{4,6},{5,7},{6,4},{7,5},{8,10},{9,11},{10,... | collective-permute-start | bytes 43016 | tf_op jit(solution)/shard_map/ppermute | solution.py:55
  131.7 5.5 %collective-permute-start.44 = (f32[4,896]{1,0:T(4,128)S(1)}, f32[4,896]{1,0:T(4,128)S(1)}, u32[]{:S(2)}, u32[]{:S(2)}) collective-permute-start(f32[4,896]{1,0:T(4,128)S(1)} %get-tuple-element.203), channel_id=1, source_target_pairs={{0,3},{1,2},{2,1},{3,0},{4,7},{5,6},{6,5},{7,4},{8,11},{9,10},{10,... | collective-permute-start | bytes 43016 | tf_op jit(solution)/shard_map/ppermute | solution.py:55

commit v5 on v4

--- a/solution.py
+++ b/solution.py
@@ -39,14 +39,12 @@
     return place ^ step if count & (count - 1) == 0 else (place - step) % count
 
 
-def gather_dp(block, before_last=None):
+def gather_dp(block):
     count = lax.axis_size("dp")
-    got = [block]
-    for i in range(1, count):
-        if i == count - 1 and before_last is not None:
-            block, _ = lax.optimization_barrier((block, before_last))
-        got.append(lax.ppermute(block, "dp", [(partner(z, i, count), z) for z in range(count)]))
-    return got
+    return [block] + [
+        lax.ppermute(block, "dp", [(partner(z, i, count), z) for z in range(count)])
+        for i in range(1, count)
+    ]
 
 
 def return_dp(blocks):
@@ -631,8 +629,9 @@
         [((3 * slots + depths * seqs, width + lanes), bf16)] * seqs
         + [((slots * parts * seqs, fine), bf16)],
         (slot_token, slot_count, route_gate), far=(embed, cot),
-        hold=((expert_weight, 0, 0),), after=(asked_token,),
-    )
+        hold=((expert_weight, 0, 0),),
+    )
+    own_sent = lax.optimization_barrier((*own_sent, asked_token))[:-1]
     own_got = trade_seq(own_sent)
 
     def source_rows(asked, source):
@@ -643,12 +642,12 @@
         sent[0] = jnp.concatenate([sent[0], second], 1)
         return sent + [first]
 
-    *sent, asked_rows, up_1st = call(
+    *sent, asked_rows = call(
         "source_rows", source_rows,
         [((slots, width + lanes + features), bf16)]
         + [((slots, width + lanes), bf16)] * (seqs - 1)
         + [((slots, features), bf16)],
-        (asked_token,), source, hold=((expert_weight, 0, 1),), after=(own_sent[0],),
+        (asked_token,), source, after=(own_sent[0],),
     )
     start_got = trade_seq(sent, 1)
     dout_2, _ = lax.optimization_barrier((dout_2, sent[0]))
@@ -670,17 +669,16 @@
         bases = [folded(piece, parts) for piece in pieces_of(out, seq_place(), seqs)]
         return bases + [after, ahead_1, ahead_2]
 
-    *base_sent, next_rows, ahead_21, ahead_22, down_1st = call(
+    *base_sent, next_rows, ahead_21, ahead_22 = call(
         "second_base", second_base,
         [((slots * parts, width // parts), bf16)] * seqs
         + [((16, features), bf16)]
         + [((slots, features), bf16)] * 2,
-        facts, start_got[0], embed, own_got[-1], norm_gain,
-        hold=((expert_weight, 0, 2),), after=(start_got[-1],),
+        facts, start_got[0], embed, own_got[-1], norm_gain, after=(start_got[-1],),
     )
     base_got = trade_seq(base_sent)
 
-    dout_2_got = gather_dp(dout_2, ahead_21)
+    dout_2_got = gather_dp(dout_2)
 
     def first_mixed(gain, *got):
         start_got, dout = got[:seqs], [g.astype(f32) for g in got[2 * seqs :]]
@@ -735,6 +733,10 @@
     )
     base_2_all = gather_dp(base_2)
 
+    up_1st, down_1st = call(
+        "held_1", lambda: [], [], (),
+        hold=((expert_weight, 0, 1), (expert_weight, 0, 2)), after=(rows_1,), limit=2,
+    )
     weight_1st = (gate_1st, up_1st, down_1st)
     first_own, first_send = project(
         "gate_up_1", rows_1_all, weight_1st, (0, 1), parts, after=(base_2,)

time: 138 us -> 132 us (0.957)
  waiting for transfers between devices: 25.4 us -> 19.1 us
    ppermute x14, waiting for transfers between devices: 8.34 us -> 3.41 us  [ring(): lax.ppermute(value, axis, [(i, (i + steps) % count) for i in range(count)])]
    pallas_call x12 -> x13, Pallas kernels: 17.8 us -> 17.5 us  [call(): pl.pallas_call(body, name=name, out_shape=shapes, in_specs=[smem] * n_sma...]
  transfers between devices with their start and end apart: 45 -> 45, of which waited for: 13 -> 9; matrix products, arithmetic and copies ran while one was open for 0% -> 0% of each run, Pallas kernels for 31% -> 36%
where the time goes in v5:
time: 132 us
  starting transfers between devices  60.6 us (46%)
  Pallas kernels  50.9 us (39%)
  waiting for transfers between devices  19.1 us (14%)
    ppermute x15, starting transfers between devices, gather_dp(): lax.ppermute(block, 'dp', [(partner(z, i, count), z) for z in range(count)])  25.8 us
    ppermute x12, starting transfers between devices, return_dp(): lax.ppermute(blocks[i], 'dp', [(z, partner(z, i, count)) for z in range(c...  17.7 us
    pallas_call x13, Pallas kernels, call(): pl.pallas_call(body, name=name, out_shape=shapes, in_specs=[smem] * n_sma...  17.5 us
    ppermute x14, starting transfers between devices, ring(): lax.ppermute(value, axis, [(i, (i + steps) % count) for i in range(count)])  15.1 us
    ppermute x15, waiting for transfers between devices, gather_dp(): lax.ppermute(block, 'dp', [(partner(z, i, count), z) for z in range(count)])  14.4 us
    pallas_call x2, Pallas kernels, dense_rows(): pl.pallas_call(body, name=name, in_specs=[smem] * 2 + [vmem] * (5 + len(e...  11.3 us
    pallas_call x2, Pallas kernels, outer(): pl.pallas_call(body, name=name, in_specs=[vmem] * (count + 3) + [anywhere...  9.4 us
    pallas_call x5, Pallas kernels, project(): pl.pallas_call(body, name=name, in_specs=specs + [anywhere] * len(after),...  6.64 us
  transfers between devices with their start and end apart: 45, of which 9 were waited for; matrix products, arithmetic and copies ran while one was open for 0% of the time, Pallas kernels for 36%

profile of v5, /device:TPU:0, one launch (start us, length us, event | category | flops | bytes accessed | tf_op | source)
XLA Modules:
  0.0 131.6 jit_solution(3530450217592022680)
XLA Ops:
  0.6 2.4 %collective-permute-start = (s32[1,1,2,6]{3,2,1,0:T(2,128)}, s32[1,1,2,6]{3,2,1,0:T(2,128)S(1)}, u32[]{:S(2)}, u32[]{:S(2)}) collective-permute-start(s32[1,1,2,6]{3,2,1,0:T(2,128)} %refs_0_.11), channel_id=1, source_target_pairs={{0,24},{8,0},{16,8},{24,16},{1,25},{9,1},{17,9},{25,17},{2,26},{10... | collective-permute-start | bytes 152 | tf_op jit(solution)/shard_map/ppermute | solution.py:19
  3.1 4.3 %own_rows.1 = (bf16[22,3712]{1,0:T(8,128)(2,1)S(1)}, bf16[22,3712]{1,0:T(8,128)(2,1)S(1)}, bf16[48,1024]{1,0:T(8,128)(2,1)S(1)}, bf16[3584,512]{1,0:T(8,128)(2,1)S(1)}) custom-call(s32[1,1,2,6]{3,2,1,0:T(2,128)} %refs_0_.11, s32[2]{0:T(128)} %bitcast.15, f32[1,1,2,6]{3,2,1,0:T(2,128)} %refs_2_.3, bf16[128,7168]{1,0:T(8,128)(2,1)} %bitcast.5, ...), custom_call_target="tpu_custom_call" | custom-call | bytes 7764992 | tf_op jit(solution)/shard_map/own_rows/pallas_call | solution.py:251
  7.4 1.6 %collective-permute-start.3 = (bf16[22,3712]{1,0:T(8,128)(2,1)S(1)}, bf16[22,3712]{1,0:T(8,128)(2,1)S(1)}, u32[]{:S(2)}, u32[]{:S(2)}) collective-permute-start(bf16[22,3712]{1,0:T(8,128)(2,1)S(1)} %get-tuple-element.110), channel_id=1, source_target_pairs={{0,4},{4,0},{1,5},{5,1},{2,6},{6,2},{3,7},{7,3},{8,12},{12,8},{9,1... | collective-permute-start | bytes 489992 | tf_op jit(solution)/shard_map/ppermute | solution.py:19
  9.0 1.3 source_rows.1
  10.3 0.6 collective-permute-start.1
  10.9 1.6 %collective-permute-start.4 = (bf16[48,1024]{1,0:T(8,128)(2,1)S(1)}, bf16[48,1024]{1,0:T(8,128)(2,1)S(1)}, u32[]{:S(2)}, u32[]{:S(2)}) collective-permute-start(bf16[48,1024]{1,0:T(8,128)(2,1)S(1)} %get-tuple-element.112.refs_5_), channel_id=1, source_target_pairs={{1,0},{0,1},{3,2},{2,3},{5,4},{4,5},{7,6},{6,7},{9,8},{8,9},{11,10... | collective-permute-start | bytes 294920 | tf_op jit(solution)/shard_map/ppermute | solution.py:45
  12.5 2.6 %collective-permute-start.5 = (bf16[48,1024]{1,0:T(8,128)(2,1)S(1)}, bf16[48,1024]{1,0:T(8,128)(2,1)S(1)}, u32[]{:S(2)}, u32[]{:S(2)}) collective-permute-start(bf16[48,1024]{1,0:T(8,128)(2,1)S(1)} %get-tuple-element.112.refs_5_), channel_id=1, source_target_pairs={{2,0},{3,1},{0,2},{1,3},{6,4},{7,5},{4,6},{5,7},{10,8},{11,9},{8,1... | collective-permute-start | bytes 294920 | tf_op jit(solution)/shard_map/ppermute | solution.py:45
  15.1 3.3 %collective-permute-start.6 = (bf16[48,1024]{1,0:T(8,128)(2,1)S(1)}, bf16[48,1024]{1,0:T(8,128)(2,1)S(1)}, u32[]{:S(2)}, u32[]{:S(2)}) collective-permute-start(bf16[48,1024]{1,0:T(8,128)(2,1)S(1)} %get-tuple-element.112.refs_5_), channel_id=1, source_target_pairs={{3,0},{2,1},{1,2},{0,3},{7,4},{6,5},{5,6},{4,7},{11,8},{10,9},{9,1... | collective-permute-start | bytes 294920 | tf_op jit(solution)/shard_map/ppermute | solution.py:45
  18.4 1.7 %second_base.1 = (bf16[24,896]{1,0:T(8,128)(2,1)S(1)}, bf16[24,896]{1,0:T(8,128)(2,1)S(1)}, bf16[16,7168]{1,0:T(8,128)(2,1)S(1)}, bf16[6,7168]{1,0:T(8,128)(2,1)S(1)}, bf16[6,7168]{1,0:T(8,128)(2,1)S(1)}) custom-call(s32[1,1,2,6]{3,2,1,0:T(2,128)} %refs_0_.11, s32[2]{0:T(128)} %bitcast.16, bf16[6,10880]{1,0:T(8,128)(2,1)S(1)} %collective-permute-done.1.refs_2_.refs_1_, ...), custom_call_target="tpu_custom_call" | custom-call | bytes 2731008 | tf_op jit(solution)/shard_map/second_base/pallas_call | solution.py:251
  20.1 3.1 %collective-permute-done.5.refs_7_ = bf16[48,1024]{1,0:T(8,128)(2,1)S(1)} collective-permute-done((bf16[48,1024]{1,0:T(8,128)(2,1)S(1)}, bf16[48,1024]{1,0:T(8,128)(2,1)S(1)}, u32[]{:S(2)}, u32[]{:S(2)}) %collective-permute-start.5) | collective-permute-done | bytes 98336 | tf_op jit(solution)/shard_map/ppermute | solution.py:45
  24.0 2.2 %collective-permute-start.8 = (bf16[48,896]{1,0:T(8,128)(2,1)S(1)}, bf16[48,896]{1,0:T(8,128)(2,1)S(1)}, u32[]{:S(2)}, u32[]{:S(2)}) collective-permute-start(bf16[48,896]{1,0:T(8,128)(2,1)S(1)} %get-tuple-element.114.refs_2_.refs_0_.refs_1_.refs_3_), channel_id=1, source_target_pairs={{1,0},{0,1},{3,2},{2,3},{5,4},{4,5},{7,6},{6,7},{9,8},{8,9},{11,10... | collective-permute-start | bytes 258056 | tf_op jit(solution)/shard_map/ppermute | solution.py:45
  26.2 1.1 collective-permute-start.9
  27.4 1.4 %collective-permute-start.10 = (bf16[48,896]{1,0:T(8,128)(2,1)S(1)}, bf16[48,896]{1,0:T(8,128)(2,1)S(1)}, u32[]{:S(2)}, u32[]{:S(2)}) collective-permute-start(bf16[48,896]{1,0:T(8,128)(2,1)S(1)} %get-tuple-element.114.refs_2_.refs_0_.refs_1_.refs_3_), channel_id=1, source_target_pairs={{3,0},{2,1},{1,2},{0,3},{7,4},{6,5},{5,6},{4,7},{11,8},{10,9},{9,1... | collective-permute-start | bytes 258056 | tf_op jit(solution)/shard_map/ppermute | solution.py:45
  28.7 1.3 collective-permute-start.11
  30.0 3.2 %held_1.1 = (bf16[3584,512]{1,0:T(8,128)(2,1)S(1)}, bf16[3584,512]{1,0:T(8,128)(2,1)S(1)}) custom-call(bf16[2,3,3584,512]{3,2,1,0:T(8,128)(2,1)} %refs_2_.4, bf16[2,3,3584,512]{3,2,1,0:T(8,128)(2,1)} %refs_2_.4, bf16[48,896]{1,0:T(8,128)(2,1)S(1)} %get-tuple-element.114.refs_2_.refs_0_.refs_1_.refs_3_), custom_call_target="tpu_custom_call" | custom-call | bytes 7340032 | tf_op jit(solution)/shard_map/held_1/pallas_call | solution.py:251
  33.3 2.9 %collective-permute-done.9.refs_2_.refs_5_ = bf16[48,896]{1,0:T(8,128)(2,1)S(1)} collective-permute-done((bf16[48,896]{1,0:T(8,128)(2,1)S(1)}, bf16[48,896]{1,0:T(8,128)(2,1)S(1)}, u32[]{:S(2)}, u32[]{:S(2)}) %collective-permute-start.9) | collective-permute-done | bytes 86048 | tf_op jit(solution)/shard_map/ppermute | solution.py:45
  36.2 1.4 %gate_up_1.1 = (f32[48,1024]{1,0:T(8,128)S(1)}, bf16[48,1024]{1,0:T(8,128)(2,1)S(1)}) custom-call(bf16[48,896]{1,0:T(8,128)(2,1)S(1)} %get-tuple-element.114.refs_2_.refs_0_.refs_1_.refs_3_, bf16[48,896]{1,0:T(8,128)(2,1)S(1)} %collective-permute-done.8.refs_1_.refs_4_, bf16[48,896]{1,0:T(8,128)(2,1)S(1)} %collective-permute-done.9.refs_2_.refs_5_, ...), custom_call_target="tpu_custom_call" | custom-call | flops 352321536 | bytes 7340032 | tf_op jit(solution)/shard_map/gate_up_1/pallas_call | solution.py:325
  37.6 1.3 %collective-permute-start.12 = (bf16[48,1024]{1,0:T(8,128)(2,1)S(1)}, bf16[48,1024]{1,0:T(8,128)(2,1)S(1)}, u32[]{:S(2)}, u32[]{:S(2)}) collective-permute-start(bf16[48,1024]{1,0:T(8,128)(2,1)S(1)} %get-tuple-element.122), channel_id=1, source_target_pairs={{0,4},{4,0},{1,5},{5,1},{2,6},{6,2},{3,7},{7,3},{8,12},{12,8},{9,1... | collective-permute-start | bytes 294920 | tf_op jit(solution)/shard_map/ppermute | solution.py:19
  38.9 2.3 %collective-permute-start.13 = (bf16[48,896]{1,0:T(8,128)(2,1)S(1)}, bf16[48,896]{1,0:T(8,128)(2,1)S(1)}, u32[]{:S(2)}, u32[]{:S(2)}) collective-permute-start(bf16[48,896]{1,0:T(8,128)(2,1)S(1)} %base_order.1.refs_6_.refs_0_.refs_2_), channel_id=1, source_target_pairs={{1,0},{0,1},{3,2},{2,3},{5,4},{4,5},{7,6},{6,7},{9,8},{8,9},{11,10... | collective-permute-start | bytes 258056 | tf_op jit(solution)/shard_map/ppermute | solution.py:45
  41.2 1.0 collective-permute-start.14
  42.2 1.5 %collective-permute-start.15 = (bf16[48,896]{1,0:T(8,128)(2,1)S(1)}, bf16[48,896]{1,0:T(8,128)(2,1)S(1)}, u32[]{:S(2)}, u32[]{:S(2)}) collective-permute-start(bf16[48,896]{1,0:T(8,128)(2,1)S(1)} %base_order.1.refs_6_.refs_0_.refs_2_), channel_id=1, source_target_pairs={{3,0},{2,1},{1,2},{0,3},{7,4},{6,5},{5,6},{4,7},{11,8},{10,9},{9,1... | collective-permute-start | bytes 258056 | tf_op jit(solution)/shard_map/ppermute | solution.py:45
  43.7 1.2 down_1.1
  44.9 5.7 %collective-permute-done.14.refs_2_.refs_4_ = bf16[48,896]{1,0:T(8,128)(2,1)S(1)} collective-permute-done((bf16[48,896]{1,0:T(8,128)(2,1)S(1)}, bf16[48,896]{1,0:T(8,128)(2,1)S(1)}, u32[]{:S(2)}, u32[]{:S(2)}) %collective-permute-start.14) | collective-permute-done | bytes 86048 | tf_op jit(solution)/shard_map/ppermute | solution.py:45
  51.2 1.5 %collective-permute-start.16 = (bf16[48,896]{1,0:T(8,128)(2,1)S(1)}, bf16[48,896]{1,0:T(8,128)(2,1)S(1)}, u32[]{:S(2)}, u32[]{:S(2)}) collective-permute-start(bf16[48,896]{1,0:T(8,128)(2,1)S(1)} %get-tuple-element.132), channel_id=1, source_target_pairs={{0,1},{1,0},{2,3},{3,2},{4,5},{5,4},{6,7},{7,6},{8,9},{9,8},{10,11... | collective-permute-start | bytes 258056 | tf_op jit(solution)/shard_map/ppermute | solution.py:53
  52.6 1.1 collective-permute-start.17
  53.8 1.8 %collective-permute-start.18 = (bf16[48,896]{1,0:T(8,128)(2,1)S(1)}, bf16[48,896]{1,0:T(8,128)(2,1)S(1)}, u32[]{:S(2)}, u32[]{:S(2)}) collective-permute-start(bf16[48,896]{1,0:T(8,128)(2,1)S(1)} %get-tuple-element.134), channel_id=1, source_target_pairs={{0,3},{1,2},{2,1},{3,0},{4,7},{5,6},{6,5},{7,4},{8,11},{9,10},{10,... | collective-permute-start | bytes 258056 | tf_op jit(solution)/shard_map/ppermute | solution.py:53
  55.6 5.6 %dense_a.1 = (bf16[128,7168]{1,0:T(8,128)(2,1)S(1)}, f32[4,7168]{1,0:T(4,128)S(1)}, bf16[3584,512]{1,0:T(8,128)(2,1)S(1)}, bf16[3584,512]{1,0:T(8,128)(2,1)S(1)}, bf16[3584,512]{1,0:T(8,128)(2,1)S(1)}) custom-call(s32[1,1,2,6]{3,2,1,0:T(2,128)} %refs_0_.11, s32[2]{0:T(128)} %bitcast.17, bf16[128,7168]{1,0:T(8,128)(2,1)S(1)} %collective-permute-done.7.hidden_ref, ...), custom_call_target="tpu_custom_call" | custom-call | flops 27525120 | bytes 4587520 | tf_op jit(solution)/shard_map/dense_a/pallas_call | solution.py:554
  61.3 1.3 collective-permute-start.19
  62.6 1.4 %collective-permute-start.20 = (bf16[48,896]{1,0:T(8,128)(2,1)S(1)}, bf16[48,896]{1,0:T(8,128)(2,1)S(1)}, u32[]{:S(2)}, u32[]{:S(2)}) collective-permute-start(bf16[48,896]{1,0:T(8,128)(2,1)S(1)} %get-tuple-element.135.refs_2_.refs_0_.refs_5_.refs_11_), channel_id=1, source_target_pairs={{2,0},{3,1},{0,2},{1,3},{6,4},{7,5},{4,6},{5,7},{10,8},{11,9},{8,1... | collective-permute-start | bytes 258056 | tf_op jit(solution)/shard_map/ppermute | solution.py:45
  64.0 1.7 %collective-permute-start.21 = (bf16[48,896]{1,0:T(8,128)(2,1)S(1)}, bf16[48,896]{1,0:T(8,128)(2,1)S(1)}, u32[]{:S(2)}, u32[]{:S(2)}) collective-permute-start(bf16[48,896]{1,0:T(8,128)(2,1)S(1)} %get-tuple-element.135.refs_2_.refs_0_.refs_5_.refs_11_), channel_id=1, source_target_pairs={{3,0},{2,1},{1,2},{0,3},{7,4},{6,5},{5,6},{4,7},{11,8},{10,9},{9,1... | collective-permute-start | bytes 258056 | tf_op jit(solution)/shard_map/ppermute | solution.py:45
  66.1 2.0 %fixed_2.1 = (f32[48,1536]{1,0:T(8,128)S(1)}, bf16[48,1536]{1,0:T(8,128)(2,1)S(1)}) custom-call(bf16[48,896]{1,0:T(8,128)(2,1)S(1)} %base_order.1.refs_6_.refs_0_.refs_2_, bf16[48,896]{1,0:T(8,128)(2,1)S(1)} %collective-permute-done.13.refs_1_.refs_3_, bf16[48,896]{1,0:T(8,128)(2,1)S(1)} %collective-permute-done.14.refs_2_.refs_4_, ...), custom_call_target="tpu_custom_call" | custom-call | flops 528482304 | bytes 11010048 | tf_op jit(solution)/shard_map/fixed_2/pallas_call | solution.py:325
  68.1 1.6 %collective-permute-start.24 = (bf16[48,1536]{1,0:T(8,128)(2,1)S(1)}, bf16[48,1536]{1,0:T(8,128)(2,1)S(1)}, u32[]{:S(2)}, u32[]{:S(2)}) collective-permute-start(bf16[48,1536]{1,0:T(8,128)(2,1)S(1)} %get-tuple-element.152), channel_id=1, source_target_pairs={{0,4},{4,0},{1,5},{5,1},{2,6},{6,2},{3,7},{7,3},{8,12},{12,8},{9,1... | collective-permute-start | bytes 442376 | tf_op jit(solution)/shard_map/ppermute | solution.py:19
  69.7 1.4 %collective-permute-done.20.refs_2_.refs_7_.refs_13_ = bf16[48,896]{1,0:T(8,128)(2,1)S(1)} collective-permute-done((bf16[48,896]{1,0:T(8,128)(2,1)S(1)}, bf16[48,896]{1,0:T(8,128)(2,1)S(1)}, u32[]{:S(2)}, u32[]{:S(2)}) %collective-permute-start.20) | collective-permute-done | bytes 86048 | tf_op jit(solution)/shard_map/ppermute | solution.py:45
  71.1 1.7 %gate_up_2.1 = (f32[48,1152]{1,0:T(8,128)S(1)}, bf16[48,1152]{1,0:T(8,128)(2,1)S(1)}, bf16[48,3584]{1,0:T(8,128)(2,1)S(1)}) custom-call(bf16[48,896]{1,0:T(8,128)(2,1)S(1)} %get-tuple-element.135.refs_2_.refs_0_.refs_5_.refs_11_, bf16[48,896]{1,0:T(8,128)(2,1)S(1)} %collective-permute-done.19.refs_1_.refs_6_.refs_12_, ...), custom_call_target="tpu_custom_call" | custom-call | flops 352321536 | bytes 7340032 | tf_op jit(solution)/shard_map/gate_up_2/pallas_call | solution.py:325
  72.8 1.6 %collective-permute-start.23 = (bf16[48,1152]{1,0:T(8,128)(2,1)S(1)}, bf16[48,1152]{1,0:T(8,128)(2,1)S(1)}, u32[]{:S(2)}, u32[]{:S(2)}) collective-permute-start(bf16[48,1152]{1,0:T(8,128)(2,1)S(1)} %get-tuple-element.151.refs_5_), channel_id=1, source_target_pairs={{0,4},{4,0},{1,5},{5,1},{2,6},{6,2},{3,7},{7,3},{8,12},{12,8},{9,1... | collective-permute-start | bytes 331784 | tf_op jit(solution)/shard_map/ppermute | solution.py:19
  74.4 0.7 prev_down.1
  75.2 2.4 %collective-permute-done.23.refs_1_ = bf16[48,1152]{1,0:T(8,128)(2,1)S(1)} collective-permute-done((bf16[48,1152]{1,0:T(8,128)(2,1)S(1)}, bf16[48,1152]{1,0:T(8,128)(2,1)S(1)}, u32[]{:S(2)}, u32[]{:S(2)}) %collective-permute-start.23) | collective-permute-done | bytes 110624 | tf_op jit(solution)/shard_map/ppermute | solution.py:19
  77.6 2.5 %back_rows_2.1 = (bf16[48,512]{1,0:T(8,128)(2,1)S(1)}, bf16[48,512]{1,0:T(8,128)(2,1)S(1)}, bf16[48,512]{1,0:T(8,128)(2,1)S(1)}, f32[48,1]{1,0:T(8,128)S(1)}, f3...) custom-call(f32[48,1152]{1,0:T(8,128)S(1)} %get-tuple-element.150.re, ...), custom_call_target="tpu_custom_call" | custom-call | flops 352321536 | bytes 7340032 | tf_op jit(solution)/shard_map/back_rows_2/pallas_call | solution.py:364
  80.1 1.6 %collective-permute-start.25 = (bf16[48,896]{1,0:T(8,128)(2,1)S(1)}, bf16[48,896]{1,0:T(8,128)(2,1)S(1)}, u32[]{:S(2)}, u32[]{:S(2)}) collective-permute-start(bf16[48,896]{1,0:T(8,128)(2,1)S(1)} %get-tuple-element.158), channel_id=1, source_target_pairs={{0,1},{1,0},{2,3},{3,2},{4,5},{5,4},{6,7},{7,6},{8,9},{9,8},{10,11... | collective-permute-start | bytes 258056 | tf_op jit(solution)/shard_map/ppermute | solution.py:53
  81.6 1.4 %collective-permute-start.26 = (bf16[48,896]{1,0:T(8,128)(2,1)S(1)}, bf16[48,896]{1,0:T(8,128)(2,1)S(1)}, u32[]{:S(2)}, u32[]{:S(2)}) collective-permute-start(bf16[48,896]{1,0:T(8,128)(2,1)S(1)} %get-tuple-element.159), channel_id=1, source_target_pairs={{0,2},{1,3},{2,0},{3,1},{4,6},{5,7},{6,4},{7,5},{8,10},{9,11},{10,... | collective-permute-start | bytes 258056 | tf_op jit(solution)/shard_map/ppermute | solution.py:53
  83.1 1.5 %collective-permute-start.27 = (bf16[48,896]{1,0:T(8,128)(2,1)S(1)}, bf16[48,896]{1,0:T(8,128)(2,1)S(1)}, u32[]{:S(2)}, u32[]{:S(2)}) collective-permute-start(bf16[48,896]{1,0:T(8,128)(2,1)S(1)} %get-tuple-element.160), channel_id=1, source_target_pairs={{0,3},{1,2},{2,1},{3,0},{4,7},{5,6},{6,5},{7,4},{8,11},{9,10},{10,... | collective-permute-start | bytes 258056 | tf_op jit(solution)/shard_map/ppermute | solution.py:53
  84.6 1.5 %collective-permute-start.28 = (bf16[48,512]{1,0:T(8,128)(2,1)S(1)}, bf16[48,512]{1,0:T(8,128)(2,1)S(1)}, u32[]{:S(2)}, u32[]{:S(2)}) collective-permute-start(bf16[48,512]{1,0:T(8,128)(2,1)S(1)} %get-tuple-element.162), channel_id=1, source_target_pairs={{0,4},{4,0},{1,5},{5,1},{2,6},{6,2},{3,7},{7,3},{8,12},{12,8},{9,1... | collective-permute-start | bytes 147464 | tf_op jit(solution)/shard_map/ppermute | solution.py:19
  86.1 5.7 %dense_b.1 = (bf16[128,7168]{1,0:T(8,128)(2,1)S(1)}, f32[4,7168]{1,0:T(4,128)S(1)}) custom-call(s32[1,1,2,6]{3,2,1,0:T(2,128)} %refs_0_.11, s32[2]{0:T(128)} %bitcast.18, bf16[128,7168]{1,0:T(8,128)(2,1)S(1)} %collective-permute-done.7.hidden_ref, bf16[128,7168]{1,0:T(8,128)(2,1)S(1)} %bitcast.8, ...), custom_call_target="tpu_custom_call", output_to_operand_aliasing={{0}: (7, {})} | custom-call | flops 27525120 | bytes 4587520 | tf_op jit(solution)/shard_map/dense_b/pallas_call | solution.py:554
  93.7 2.3 %collective-permute-start.32 = (bf16[48,896]{1,0:T(8,128)(2,1)S(1)}, bf16[48,896]{1,0:T(8,128)(2,1)S(1)}, u32[]{:S(2)}, u32[]{:S(2)}) collective-permute-start(bf16[48,896]{1,0:T(8,128)(2,1)S(1)} %get-tuple-element.163.refs_13_.refs_0_.refs_7_), channel_id=1, source_target_pairs={{2,0},{3,1},{0,2},{1,3},{6,4},{7,5},{4,6},{5,7},{10,8},{11,9},{8,1... | collective-permute-start | bytes 258056 | tf_op jit(solution)/shard_map/ppermute | solution.py:45
  96.0 1.5 %collective-permute-start.33 = (bf16[48,896]{1,0:T(8,128)(2,1)S(1)}, bf16[48,896]{1,0:T(8,128)(2,1)S(1)}, u32[]{:S(2)}, u32[]{:S(2)}) collective-permute-start(bf16[48,896]{1,0:T(8,128)(2,1)S(1)} %get-tuple-element.163.refs_13_.refs_0_.refs_7_), channel_id=1, source_target_pairs={{3,0},{2,1},{1,2},{0,3},{7,4},{6,5},{5,6},{4,7},{11,8},{10,9},{9,1... | collective-permute-start | bytes 258056 | tf_op jit(solution)/shard_map/ppermute | solution.py:45
  97.5 4.7 %weight_grad_2.1 = (bf16[1,2,3,3584,512]{4,3,2,1,0:T(8,128)(2,1)}, f32[8,128]{1,0:T(8,128)S(1)}) custom-call(bf16[48,3584]{1,0:T(8,128)(2,1)S(1)} %get-tuple-element.169.refs_0_, f32[48,1]{1,0:T(8,128)S(1)} %get-tuple-element.170.refs_1_, bf16[48,896]{1,0:T(8,128)(2,1)S(1)} %base_order.1.refs_6_.refs_0_.refs_2_, ...), custom_call_target="tpu_custom_call" | custom-call | flops 528482304 | bytes 11010048 | tf_op jit(solution)/shard_map/weight_grad_2/pallas_call | solution.py:411
  102.3 1.2 collective-permute-done.32.refs_2_.refs_9_
  103.5 0.8 back_1.1
  104.3 1.6 %collective-permute-start.35 = (bf16[48,640]{1,0:T(8,128)(2,1)S(1)}, bf16[48,640]{1,0:T(8,128)(2,1)S(1)}, u32[]{:S(2)}, u32[]{:S(2)}) collective-permute-start(bf16[48,640]{1,0:T(8,128)(2,1)S(1)} %get-tuple-element.175.refs_10_), channel_id=1, source_target_pairs={{0,4},{4,0},{1,5},{5,1},{2,6},{6,2},{3,7},{7,3},{8,12},{12,8},{9,1... | collective-permute-start | bytes 184328 | tf_op jit(solution)/shard_map/ppermute | solution.py:19
  105.9 1.6 %second_grad.1 = (bf16[6,7296]{1,0:T(8,128)(2,1)S(1)}, f32[4,3584]{1,0:T(4,128)S(1)}, f32[4,3584]{1,0:T(4,128)S(1)}) custom-call(s32[1,1,2,6]{3,2,1,0:T(2,128)} %refs_0_.11, s32[2]{0:T(128)} %bitcast.19, bf16[6,10880]{1,0:T(8,128)(2,1)S(1)} %collective-permute-done.1.refs_2_.refs_1_, bf16[6,7168]{1,0:T(8,128)(2,1)S(1)} %get-tuple-element.113.refs_9_.refs_3_, ...), custom_call_target="tpu_custom_call" | custom-call | bytes 2655232 | tf_op jit(solution)/shard_map/second_grad/pallas_call | solution.py:251
  108.1 0.9 collective-permute-done.35.refs_1_
  109.1 2.4 %back_rows_1.1 = (bf16[48,512]{1,0:T(8,128)(2,1)S(1)}, bf16[48,512]{1,0:T(8,128)(2,1)S(1)}, f32[48,1]{1,0:T(8,128)S(1)}, bf16[48,896]{1,0:T(8,128)(2,1)S(1)}, bf...) custom-call(f32[48,640]{1,0:T(8,128)S(1)} %get-tuple-element.180.refs_0_, ...), custom_call_target="tpu_custom_call" | custom-call | flops 352321536 | bytes 7340032 | tf_op jit(solution)/shard_map/back_rows_1/pallas_call | solution.py:364
  111.5 1.2 collective-permute-start.36
  112.7 1.8 %collective-permute-start.37 = (bf16[48,896]{1,0:T(8,128)(2,1)S(1)}, bf16[48,896]{1,0:T(8,128)(2,1)S(1)}, u32[]{:S(2)}, u32[]{:S(2)}) collective-permute-start(bf16[48,896]{1,0:T(8,128)(2,1)S(1)} %get-tuple-element.190), channel_id=1, source_target_pairs={{0,2},{1,3},{2,0},{3,1},{4,6},{5,7},{6,4},{7,5},{8,10},{9,11},{10,... | collective-permute-start | bytes 258056 | tf_op jit(solution)/shard_map/ppermute | solution.py:53
  114.4 1.5 %collective-permute-start.38 = (bf16[48,896]{1,0:T(8,128)(2,1)S(1)}, bf16[48,896]{1,0:T(8,128)(2,1)S(1)}, u32[]{:S(2)}, u32[]{:S(2)}) collective-permute-start(bf16[48,896]{1,0:T(8,128)(2,1)S(1)} %get-tuple-element.191), channel_id=1, source_target_pairs={{0,3},{1,2},{2,1},{3,0},{4,7},{5,6},{6,5},{7,4},{8,11},{9,10},{10,... | collective-permute-start | bytes 258056 | tf_op jit(solution)/shard_map/ppermute | solution.py:53
  115.9 4.7 %weight_grad_1.1 = (bf16[1,2,3,3584,512]{4,3,2,1,0:T(8,128)(2,1)}, f32[8,128]{1,0:T(8,128)S(1)}) custom-call(f32[48,1]{1,0:T(8,128)S(1)} %get-tuple-element.184.refs_0_.refs_3_, f32[48,1]{1,0:T(8,128)S(1)} %get-tuple-element.179.refs_5_.refs_1_.refs_2_, f32[48,1]{1,0:T(8,128)S(1)} %get-tuple-element.182.refs_6_.refs_2_, ...), custom_call_target="tpu_custom_call", output_to_operand_aliasing={{0}: (18, {})} | custom-call | flops 528482304 | bytes 11010048 | tf_op jit(solution)/shard_map/weight_grad_1/pallas_call | solution.py:411
  121.3 0.8 collective-permute-start.40
  122.1 0.6 collective-permute-start.41
  122.7 1.5 %collective-permute-start.42 = (f32[4,896]{1,0:T(4,128)S(1)}, f32[4,896]{1,0:T(4,128)S(1)}, u32[]{:S(2)}, u32[]{:S(2)}) collective-permute-start(f32[4,896]{1,0:T(4,128)S(1)} %get-tuple-element.203), channel_id=1, source_target_pairs={{0,1},{1,0},{2,3},{3,2},{4,5},{5,4},{6,7},{7,6},{8,9},{9,8},{10,11... | collective-permute-start | bytes 43016 | tf_op jit(solution)/shard_map/ppermute | solution.py:53
  124.2 1.3 collective-permute-start.43
  125.5 1.6 %collective-permute-start.44 = (f32[4,896]{1,0:T(4,128)S(1)}, f32[4,896]{1,0:T(4,128)S(1)}, u32[]{:S(2)}, u32[]{:S(2)}) collective-permute-start(f32[4,896]{1,0:T(4,128)S(1)} %get-tuple-element.205), channel_id=1, source_target_pairs={{0,3},{1,2},{2,1},{3,0},{4,7},{5,6},{6,5},{7,4},{8,11},{9,10},{10,... | collective-permute-start | bytes 43016 | tf_op jit(solution)/shard_map/ppermute | solution.py:53
  127.1 2.9 %finish.1 = (bf16[128,7168]{1,0:T(8,128)(2,1)}, f32[8,128]{1,0:T(8,128)S(1)}) custom-call(s32[1,1,2,6]{3,2,1,0:T(2,128)} %copy-done.4, bf16[128,7168]{1,0:T(8,128)(2,1)S(1)} %collective-permute-done.29.refs_1_, bf16[6,7168]{1,0:T(8,128)(2,1)S(1)} %get-tuple-element.165.refs_2_, bf16[6,7296]{1,0:T(8,128)(2,1)S(1)} %collective-permute-done.34.refs_3_, ...), custom_call_target="tpu_custom_call" | custom-call | bytes 3933696 | tf_op jit(solution)/shard_map/finish/pallas_call | solution.py:251
  130.0 1.0 collective-permute-done.44.refs_3_
  131.0 0.6 gain_sum.1
  (61 shorter events, 5.1 us)
Async XLA Ops:
  0.6 6.7 %collective-permute-start = (s32[1,1,2,6]{3,2,1,0:T(2,128)}, s32[1,1,2,6]{3,2,1,0:T(2,128)S(1)}, u32[]{:S(2)}, u32[]{:S(2)}) collective-permute-start(s32[1,1,2,6]{3,2,1,0:T(2,128)} %refs_0_.11), channel_id=1, source_target_pairs={{0,24},{8,0},{16,8},{24,16},{1,25},{9,1},{17,9},{25,17},{2,26},{10... | collective-permute-start | bytes 152 | tf_op jit(solution)/shard_map/ppermute | solution.py:19
  3.1 5.9 %copy-start.3 = (bf16[1,1,128,7168]{3,2,1,0:T(8,128)(2,1)S(1)}, bf16[1,1,128,7168]{3,2,1,0:T(8,128)(2,1)}, u32[]{:S(2)}) copy-start(bf16[1,1,128,7168]{3,2,1,0:T(8,128)(2,1)} %param.8) | copy-start | bytes 5505028
  3.1 15.4 %copy-start = (bf16[1,1,128,7168]{3,2,1,0:T(8,128)(2,1)S(1)}, bf16[1,1,128,7168]{3,2,1,0:T(8,128)(2,1)}, u32[]{:S(2)}) copy-start(bf16[1,1,128,7168]{3,2,1,0:T(8,128)(2,1)} %param.9) | copy-start | bytes 5505028
  3.1 15.4 %copy-start.2 = (f32[2,2,7168]{2,1,0:T(2,128)S(1)}, f32[2,2,7168]{2,1,0:T(2,128)}, u32[]{:S(2)}) copy-start(f32[2,2,7168]{2,1,0:T(2,128)} %refs_8_.1) | copy-start | bytes 344068
  7.4 1.6 %copy-start.4 = (s32[1,1,2,6]{3,2,1,0:T(2,128)}, s32[1,1,2,6]{3,2,1,0:T(2,128)S(1)}, u32[]{:S(2)}) copy-start(s32[1,1,2,6]{3,2,1,0:T(2,128)S(1)} %collective-permute-done.refs_0_) | copy-start | bytes 148
  7.4 11.0 %collective-permute-start.3 = (bf16[22,3712]{1,0:T(8,128)(2,1)S(1)}, bf16[22,3712]{1,0:T(8,128)(2,1)S(1)}, u32[]{:S(2)}, u32[]{:S(2)}) collective-permute-start(bf16[22,3712]{1,0:T(8,128)(2,1)S(1)} %get-tuple-element.110), channel_id=1, source_target_pairs={{0,4},{4,0},{1,5},{5,1},{2,6},{6,2},{3,7},{7,3},{8,12},{12,8},{9,1... | collective-permute-start | bytes 489992 | tf_op jit(solution)/shard_map/ppermute | solution.py:19
  10.3 4.8 %collective-permute-start.2 = (bf16[6,3712]{1,0:T(8,128)(2,1)S(1)}, bf16[6,3712]{1,0:T(8,128)(2,1)S(1)}, u32[]{:S(2)}, u32[]{:S(2)}) collective-permute-start(bf16[6,3712]{1,0:T(8,128)(2,1)S(1)} %get-tuple-element.109), channel_id=1, source_target_pairs={{0,12},{4,8},{8,20},{12,16},{16,28},{20,24},{24,4},{28,0},{1,13},{... | collective-permute-start | bytes 133640 | tf_op jit(solution)/shard_map/ppermute | solution.py:29
  10.3 8.1 %collective-permute-start.1 = (bf16[6,10880]{1,0:T(8,128)(2,1)S(1)}, bf16[6,10880]{1,0:T(8,128)(2,1)S(1)}, u32[]{:S(2)}, u32[]{:S(2)}) collective-permute-start(bf16[6,10880]{1,0:T(8,128)(2,1)S(1)} %get-tuple-element.108), channel_id=1, source_target_pairs={{0,8},{4,12},{8,16},{12,20},{16,24},{20,28},{24,0},{28,4},{1,9},{5... | collective-permute-start | bytes 391688 | tf_op jit(solution)/shard_map/ppermute | solution.py:29
  10.9 9.2 %collective-permute-start.4 = (bf16[48,1024]{1,0:T(8,128)(2,1)S(1)}, bf16[48,1024]{1,0:T(8,128)(2,1)S(1)}, u32[]{:S(2)}, u32[]{:S(2)}) collective-permute-start(bf16[48,1024]{1,0:T(8,128)(2,1)S(1)} %get-tuple-element.112.refs_5_), channel_id=1, source_target_pairs={{1,0},{0,1},{3,2},{2,3},{5,4},{4,5},{7,6},{6,7},{9,8},{8,9},{11,10... | collective-permute-start | bytes 294920 | tf_op jit(solution)/shard_map/ppermute | solution.py:45
  12.5 10.7 %collective-permute-start.5 = (bf16[48,1024]{1,0:T(8,128)(2,1)S(1)}, bf16[48,1024]{1,0:T(8,128)(2,1)S(1)}, u32[]{:S(2)}, u32[]{:S(2)}) collective-permute-start(bf16[48,1024]{1,0:T(8,128)(2,1)S(1)} %get-tuple-element.112.refs_5_), channel_id=1, source_target_pairs={{2,0},{3,1},{0,2},{1,3},{6,4},{7,5},{4,6},{5,7},{10,8},{11,9},{8,1... | collective-permute-start | bytes 294920 | tf_op jit(solution)/shard_map/ppermute | solution.py:45
  15.1 8.1 %collective-permute-start.6 = (bf16[48,1024]{1,0:T(8,128)(2,1)S(1)}, bf16[48,1024]{1,0:T(8,128)(2,1)S(1)}, u32[]{:S(2)}, u32[]{:S(2)}) collective-permute-start(bf16[48,1024]{1,0:T(8,128)(2,1)S(1)} %get-tuple-element.112.refs_5_), channel_id=1, source_target_pairs={{3,0},{2,1},{1,2},{0,3},{7,4},{6,5},{5,6},{4,7},{11,8},{10,9},{9,1... | collective-permute-start | bytes 294920 | tf_op jit(solution)/shard_map/ppermute | solution.py:45
  23.8 31.8 %collective-permute-start.7 = (bf16[128,7168]{1,0:T(8,128)(2,1)S(1)}, bf16[128,7168]{1,0:T(8,128)(2,1)S(1)}, u32[]{:S(2)}, u32[]{:S(2)}) collective-permute-start(bf16[128,7168]{1,0:T(8,128)(2,1)S(1)} %bitcast.14), channel_id=1, source_target_pairs={{0,8},{8,16},{16,24},{24,0},{1,9},{9,17},{17,25},{25,1},{2,10},{10... | collective-permute-start | bytes 5505032 | tf_op jit(solution)/shard_map/ppermute | solution.py:19
  24.0 9.2 %collective-permute-start.8 = (bf16[48,896]{1,0:T(8,128)(2,1)S(1)}, bf16[48,896]{1,0:T(8,128)(2,1)S(1)}, u32[]{:S(2)}, u32[]{:S(2)}) collective-permute-start(bf16[48,896]{1,0:T(8,128)(2,1)S(1)} %get-tuple-element.114.refs_2_.refs_0_.refs_1_.refs_3_), channel_id=1, source_target_pairs={{1,0},{0,1},{3,2},{2,3},{5,4},{4,5},{7,6},{6,7},{9,8},{8,9},{11,10... | collective-permute-start | bytes 258056 | tf_op jit(solution)/shard_map/ppermute | solution.py:45
  26.2 10.0 %collective-permute-start.9 = (bf16[48,896]{1,0:T(8,128)(2,1)S(1)}, bf16[48,896]{1,0:T(8,128)(2,1)S(1)}, u32[]{:S(2)}, u32[]{:S(2)}) collective-permute-start(bf16[48,896]{1,0:T(8,128)(2,1)S(1)} %get-tuple-element.114.refs_2_.refs_0_.refs_1_.refs_3_), channel_id=1, source_target_pairs={{2,0},{3,1},{0,2},{1,3},{6,4},{7,5},{4,6},{5,7},{10,8},{11,9},{8,1... | collective-permute-start | bytes 258056 | tf_op jit(solution)/shard_map/ppermute | solution.py:45
  27.4 8.9 %collective-permute-start.10 = (bf16[48,896]{1,0:T(8,128)(2,1)S(1)}, bf16[48,896]{1,0:T(8,128)(2,1)S(1)}, u32[]{:S(2)}, u32[]{:S(2)}) collective-permute-start(bf16[48,896]{1,0:T(8,128)(2,1)S(1)} %get-tuple-element.114.refs_2_.refs_0_.refs_1_.refs_3_), channel_id=1, source_target_pairs={{3,0},{2,1},{1,2},{0,3},{7,4},{6,5},{5,6},{4,7},{11,8},{10,9},{9,1... | collective-permute-start | bytes 258056 | tf_op jit(solution)/shard_map/ppermute | solution.py:45
  28.7 4.4 %collective-permute-start.11 = (bf16[24,896]{1,0:T(8,128)(2,1)S(1)}, bf16[24,896]{1,0:T(8,128)(2,1)S(1)}, u32[]{:S(2)}, u32[]{:S(2)}) collective-permute-start(bf16[24,896]{1,0:T(8,128)(2,1)S(1)} %get-tuple-element.120), channel_id=1, source_target_pairs={{0,4},{4,0},{1,5},{5,1},{2,6},{6,2},{3,7},{7,3},{8,12},{12,8},{9,1... | collective-permute-start | bytes 129032 | tf_op jit(solution)/shard_map/ppermute | solution.py:19
  37.6 18.0 %copy-start.1 = (bf16[1,1,128,7168]{3,2,1,0:T(8,128)(2,1)S(1)}, bf16[1,1,128,7168]{3,2,1,0:T(8,128)(2,1)}, u32[]{:S(2)}) copy-start(bf16[1,1,128,7168]{3,2,1,0:T(8,128)(2,1)} %param.10) | copy-start | bytes 5505028
  37.6 6.1 %collective-permute-start.12 = (bf16[48,1024]{1,0:T(8,128)(2,1)S(1)}, bf16[48,1024]{1,0:T(8,128)(2,1)S(1)}, u32[]{:S(2)}, u32[]{:S(2)}) collective-permute-start(bf16[48,1024]{1,0:T(8,128)(2,1)S(1)} %get-tuple-element.122), channel_id=1, source_target_pairs={{0,4},{4,0},{1,5},{5,1},{2,6},{6,2},{3,7},{7,3},{8,12},{12,8},{9,1... | collective-permute-start | bytes 294920 | tf_op jit(solution)/shard_map/ppermute | solution.py:19
  38.9 6.0 %collective-permute-start.13 = (bf16[48,896]{1,0:T(8,128)(2,1)S(1)}, bf16[48,896]{1,0:T(8,128)(2,1)S(1)}, u32[]{:S(2)}, u32[]{:S(2)}) collective-permute-start(bf16[48,896]{1,0:T(8,128)(2,1)S(1)} %base_order.1.refs_6_.refs_0_.refs_2_), channel_id=1, source_target_pairs={{1,0},{0,1},{3,2},{2,3},{5,4},{4,5},{7,6},{6,7},{9,8},{8,9},{11,10... | collective-permute-start | bytes 258056 | tf_op jit(solution)/shard_map/ppermute | solution.py:45
  41.2 9.4 %collective-permute-start.14 = (bf16[48,896]{1,0:T(8,128)(2,1)S(1)}, bf16[48,896]{1,0:T(8,128)(2,1)S(1)}, u32[]{:S(2)}, u32[]{:S(2)}) collective-permute-start(bf16[48,896]{1,0:T(8,128)(2,1)S(1)} %base_order.1.refs_6_.refs_0_.refs_2_), channel_id=1, source_target_pairs={{2,0},{3,1},{0,2},{1,3},{6,4},{7,5},{4,6},{5,7},{10,8},{11,9},{8,1... | collective-permute-start | bytes 258056 | tf_op jit(solution)/shard_map/ppermute | solution.py:45
  42.2 8.4 %collective-permute-start.15 = (bf16[48,896]{1,0:T(8,128)(2,1)S(1)}, bf16[48,896]{1,0:T(8,128)(2,1)S(1)}, u32[]{:S(2)}, u32[]{:S(2)}) collective-permute-start(bf16[48,896]{1,0:T(8,128)(2,1)S(1)} %base_order.1.refs_6_.refs_0_.refs_2_), channel_id=1, source_target_pairs={{3,0},{2,1},{1,2},{0,3},{7,4},{6,5},{5,6},{4,7},{11,8},{10,9},{9,1... | collective-permute-start | bytes 258056 | tf_op jit(solution)/shard_map/ppermute | solution.py:45
  50.7 15.1 %collective-permute-start.22 = (bf16[96,1024]{1,0:T(8,128)(2,1)S(1)}, bf16[96,1024]{1,0:T(8,128)(2,1)S(1)}, u32[]{:S(2)}, u32[]{:S(2)}) collective-permute-start(bf16[96,1024]{1,0:T(8,128)(2,1)S(1)} %get-tuple-element.141), channel_id=1, source_target_pairs={{0,4},{4,0},{1,5},{5,1},{2,6},{6,2},{3,7},{7,3},{8,12},{12,8},{9,1... | collective-permute-start | bytes 589832 | tf_op jit(solution)/shard_map/ppermute | solution.py:19
  51.2 10.0 %collective-permute-start.16 = (bf16[48,896]{1,0:T(8,128)(2,1)S(1)}, bf16[48,896]{1,0:T(8,128)(2,1)S(1)}, u32[]{:S(2)}, u32[]{:S(2)}) collective-permute-start(bf16[48,896]{1,0:T(8,128)(2,1)S(1)} %get-tuple-element.132), channel_id=1, source_target_pairs={{0,1},{1,0},{2,3},{3,2},{4,5},{5,4},{6,7},{7,6},{8,9},{9,8},{10,11... | collective-permute-start | bytes 258056 | tf_op jit(solution)/shard_map/ppermute | solution.py:53
  52.6 8.5 %collective-permute-start.17 = (bf16[48,896]{1,0:T(8,128)(2,1)S(1)}, bf16[48,896]{1,0:T(8,128)(2,1)S(1)}, u32[]{:S(2)}, u32[]{:S(2)}) collective-permute-start(bf16[48,896]{1,0:T(8,128)(2,1)S(1)} %get-tuple-element.133), channel_id=1, source_target_pairs={{0,2},{1,3},{2,0},{3,1},{4,6},{5,7},{6,4},{7,5},{8,10},{9,11},{10,... | collective-permute-start | bytes 258056 | tf_op jit(solution)/shard_map/ppermute | solution.py:53
  53.8 7.4 %collective-permute-start.18 = (bf16[48,896]{1,0:T(8,128)(2,1)S(1)}, bf16[48,896]{1,0:T(8,128)(2,1)S(1)}, u32[]{:S(2)}, u32[]{:S(2)}) collective-permute-start(bf16[48,896]{1,0:T(8,128)(2,1)S(1)} %get-tuple-element.134), channel_id=1, source_target_pairs={{0,3},{1,2},{2,1},{3,0},{4,7},{5,6},{6,5},{7,4},{8,11},{9,10},{10,... | collective-permute-start | bytes 258056 | tf_op jit(solution)/shard_map/ppermute | solution.py:53
  61.3 8.4 %collective-permute-start.19 = (bf16[48,896]{1,0:T(8,128)(2,1)S(1)}, bf16[48,896]{1,0:T(8,128)(2,1)S(1)}, u32[]{:S(2)}, u32[]{:S(2)}) collective-permute-start(bf16[48,896]{1,0:T(8,128)(2,1)S(1)} %get-tuple-element.135.refs_2_.refs_0_.refs_5_.refs_11_), channel_id=1, source_target_pairs={{1,0},{0,1},{3,2},{2,3},{5,4},{4,5},{7,6},{6,7},{9,8},{8,9},{11,10... | collective-permute-start | bytes 258056 | tf_op jit(solution)/shard_map/ppermute | solution.py:45
  62.6 8.5 %collective-permute-start.20 = (bf16[48,896]{1,0:T(8,128)(2,1)S(1)}, bf16[48,896]{1,0:T(8,128)(2,1)S(1)}, u32[]{:S(2)}, u32[]{:S(2)}) collective-permute-start(bf16[48,896]{1,0:T(8,128)(2,1)S(1)} %get-tuple-element.135.refs_2_.refs_0_.refs_5_.refs_11_), channel_id=1, source_target_pairs={{2,0},{3,1},{0,2},{1,3},{6,4},{7,5},{4,6},{5,7},{10,8},{11,9},{8,1... | collective-permute-start | bytes 258056 | tf_op jit(solution)/shard_map/ppermute | solution.py:45
  64.0 7.0 %collective-permute-start.21 = (bf16[48,896]{1,0:T(8,128)(2,1)S(1)}, bf16[48,896]{1,0:T(8,128)(2,1)S(1)}, u32[]{:S(2)}, u32[]{:S(2)}) collective-permute-start(bf16[48,896]{1,0:T(8,128)(2,1)S(1)} %get-tuple-element.135.refs_2_.refs_0_.refs_5_.refs_11_), channel_id=1, source_target_pairs={{3,0},{2,1},{1,2},{0,3},{7,4},{6,5},{5,6},{4,7},{11,8},{10,9},{9,1... | collective-permute-start | bytes 258056 | tf_op jit(solution)/shard_map/ppermute | solution.py:45
  68.1 7.1 %collective-permute-start.24 = (bf16[48,1536]{1,0:T(8,128)(2,1)S(1)}, bf16[48,1536]{1,0:T(8,128)(2,1)S(1)}, u32[]{:S(2)}, u32[]{:S(2)}) collective-permute-start(bf16[48,1536]{1,0:T(8,128)(2,1)S(1)} %get-tuple-element.152), channel_id=1, source_target_pairs={{0,4},{4,0},{1,5},{5,1},{2,6},{6,2},{3,7},{7,3},{8,12},{12,8},{9,1... | collective-permute-start | bytes 442376 | tf_op jit(solution)/shard_map/ppermute | solution.py:19
  72.8 4.8 %collective-permute-start.23 = (bf16[48,1152]{1,0:T(8,128)(2,1)S(1)}, bf16[48,1152]{1,0:T(8,128)(2,1)S(1)}, u32[]{:S(2)}, u32[]{:S(2)}) collective-permute-start(bf16[48,1152]{1,0:T(8,128)(2,1)S(1)} %get-tuple-element.151.refs_5_), channel_id=1, source_target_pairs={{0,4},{4,0},{1,5},{5,1},{2,6},{6,2},{3,7},{7,3},{8,12},{12,8},{9,1... | collective-permute-start | bytes 331784 | tf_op jit(solution)/shard_map/ppermute | solution.py:19
  80.1 11.7 %collective-permute-start.25 = (bf16[48,896]{1,0:T(8,128)(2,1)S(1)}, bf16[48,896]{1,0:T(8,128)(2,1)S(1)}, u32[]{:S(2)}, u32[]{:S(2)}) collective-permute-start(bf16[48,896]{1,0:T(8,128)(2,1)S(1)} %get-tuple-element.158), channel_id=1, source_target_pairs={{0,1},{1,0},{2,3},{3,2},{4,5},{5,4},{6,7},{7,6},{8,9},{9,8},{10,11... | collective-permute-start | bytes 258056 | tf_op jit(solution)/shard_map/ppermute | solution.py:53
  81.6 10.2 %collective-permute-start.26 = (bf16[48,896]{1,0:T(8,128)(2,1)S(1)}, bf16[48,896]{1,0:T(8,128)(2,1)S(1)}, u32[]{:S(2)}, u32[]{:S(2)}) collective-permute-start(bf16[48,896]{1,0:T(8,128)(2,1)S(1)} %get-tuple-element.159), channel_id=1, source_target_pairs={{0,2},{1,3},{2,0},{3,1},{4,6},{5,7},{6,4},{7,5},{8,10},{9,11},{10,... | collective-permute-start | bytes 258056 | tf_op jit(solution)/shard_map/ppermute | solution.py:53
  83.1 8.8 %collective-permute-start.27 = (bf16[48,896]{1,0:T(8,128)(2,1)S(1)}, bf16[48,896]{1,0:T(8,128)(2,1)S(1)}, u32[]{:S(2)}, u32[]{:S(2)}) collective-permute-start(bf16[48,896]{1,0:T(8,128)(2,1)S(1)} %get-tuple-element.160), channel_id=1, source_target_pairs={{0,3},{1,2},{2,1},{3,0},{4,7},{5,6},{6,5},{7,4},{8,11},{9,10},{10,... | collective-permute-start | bytes 258056 | tf_op jit(solution)/shard_map/ppermute | solution.py:53
  84.6 7.3 %collective-permute-start.28 = (bf16[48,512]{1,0:T(8,128)(2,1)S(1)}, bf16[48,512]{1,0:T(8,128)(2,1)S(1)}, u32[]{:S(2)}, u32[]{:S(2)}) collective-permute-start(bf16[48,512]{1,0:T(8,128)(2,1)S(1)} %get-tuple-element.162), channel_id=1, source_target_pairs={{0,4},{4,0},{1,5},{5,1},{2,6},{6,2},{3,7},{7,3},{8,12},{12,8},{9,1... | collective-permute-start | bytes 147464 | tf_op jit(solution)/shard_map/ppermute | solution.py:19
  92.3 34.8 %collective-permute-start.29 = (bf16[128,7168]{1,0:T(8,128)(2,1)S(1)}, bf16[128,7168]{1,0:T(8,128)(2,1)S(1)}, u32[]{:S(2)}, u32[]{:S(2)}) collective-permute-start(bf16[128,7168]{1,0:T(8,128)(2,1)S(1)} %get-tuple-element.164), channel_id=1, source_target_pairs={{0,24},{8,0},{16,8},{24,16},{1,25},{9,1},{17,9},{25,17},{2,26},{10... | collective-permute-start | bytes 5505032 | tf_op jit(solution)/shard_map/ppermute | solution.py:19
  92.6 5.0 %collective-permute-start.30 = (bf16[6,3584]{1,0:T(8,128)(2,1)S(1)}, bf16[6,3584]{1,0:T(8,128)(2,1)S(1)}, u32[]{:S(2)}, u32[]{:S(2)}) collective-permute-start(bf16[6,3584]{1,0:T(8,128)(2,1)S(1)} %get-tuple-element.168), channel_id=1, source_target_pairs={{0,4},{4,0},{1,5},{5,1},{2,6},{6,2},{3,7},{7,3},{8,12},{12,8},{9,1... | collective-permute-start | bytes 129032 | tf_op jit(solution)/shard_map/ppermute | solution.py:19
  93.2 9.1 %collective-permute-start.31 = (bf16[48,896]{1,0:T(8,128)(2,1)S(1)}, bf16[48,896]{1,0:T(8,128)(2,1)S(1)}, u32[]{:S(2)}, u32[]{:S(2)}) collective-permute-start(bf16[48,896]{1,0:T(8,128)(2,1)S(1)} %get-tuple-element.163.refs_13_.refs_0_.refs_7_), channel_id=1, source_target_pairs={{1,0},{0,1},{3,2},{2,3},{5,4},{4,5},{7,6},{6,7},{9,8},{8,9},{11,10... | collective-permute-start | bytes 258056 | tf_op jit(solution)/shard_map/ppermute | solution.py:45
  93.7 9.8 %collective-permute-start.32 = (bf16[48,896]{1,0:T(8,128)(2,1)S(1)}, bf16[48,896]{1,0:T(8,128)(2,1)S(1)}, u32[]{:S(2)}, u32[]{:S(2)}) collective-permute-start(bf16[48,896]{1,0:T(8,128)(2,1)S(1)} %get-tuple-element.163.refs_13_.refs_0_.refs_7_), channel_id=1, source_target_pairs={{2,0},{3,1},{0,2},{1,3},{6,4},{7,5},{4,6},{5,7},{10,8},{11,9},{8,1... | collective-permute-start | bytes 258056 | tf_op jit(solution)/shard_map/ppermute | solution.py:45
  96.0 7.5 %collective-permute-start.33 = (bf16[48,896]{1,0:T(8,128)(2,1)S(1)}, bf16[48,896]{1,0:T(8,128)(2,1)S(1)}, u32[]{:S(2)}, u32[]{:S(2)}) collective-permute-start(bf16[48,896]{1,0:T(8,128)(2,1)S(1)} %get-tuple-element.163.refs_13_.refs_0_.refs_7_), channel_id=1, source_target_pairs={{3,0},{2,1},{1,2},{0,3},{7,4},{6,5},{5,6},{4,7},{11,8},{10,9},{9,1... | collective-permute-start | bytes 258056 | tf_op jit(solution)/shard_map/ppermute | solution.py:45
  104.3 4.7 %collective-permute-start.35 = (bf16[48,640]{1,0:T(8,128)(2,1)S(1)}, bf16[48,640]{1,0:T(8,128)(2,1)S(1)}, u32[]{:S(2)}, u32[]{:S(2)}) collective-permute-start(bf16[48,640]{1,0:T(8,128)(2,1)S(1)} %get-tuple-element.175.refs_10_), channel_id=1, source_target_pairs={{0,4},{4,0},{1,5},{5,1},{2,6},{6,2},{3,7},{7,3},{8,12},{12,8},{9,1... | collective-permute-start | bytes 184328 | tf_op jit(solution)/shard_map/ppermute | solution.py:19
  107.6 8.4 %collective-permute-start.39 = (f32[4,3584]{1,0:T(4,128)S(1)}, f32[4,3584]{1,0:T(4,128)S(1)}, u32[]{:S(2)}, u32[]{:S(2)}) collective-permute-start(f32[4,3584]{1,0:T(4,128)S(1)} %get-tuple-element.192), channel_id=1, source_target_pairs={{0,4},{4,0},{1,5},{5,1},{2,6},{6,2},{3,7},{7,3},{8,12},{12,8},{9,1... | collective-permute-start | bytes 172040 | tf_op jit(solution)/shard_map/ppermute | solution.py:19
  111.5 9.1 %collective-permute-start.36 = (bf16[48,896]{1,0:T(8,128)(2,1)S(1)}, bf16[48,896]{1,0:T(8,128)(2,1)S(1)}, u32[]{:S(2)}, u32[]{:S(2)}) collective-permute-start(bf16[48,896]{1,0:T(8,128)(2,1)S(1)} %get-tuple-element.189), channel_id=1, source_target_pairs={{0,1},{1,0},{2,3},{3,2},{4,5},{5,4},{6,7},{7,6},{8,9},{9,8},{10,11... | collective-permute-start | bytes 258056 | tf_op jit(solution)/shard_map/ppermute | solution.py:53
  112.7 7.9 %collective-permute-start.37 = (bf16[48,896]{1,0:T(8,128)(2,1)S(1)}, bf16[48,896]{1,0:T(8,128)(2,1)S(1)}, u32[]{:S(2)}, u32[]{:S(2)}) collective-permute-start(bf16[48,896]{1,0:T(8,128)(2,1)S(1)} %get-tuple-element.190), channel_id=1, source_target_pairs={{0,2},{1,3},{2,0},{3,1},{4,6},{5,7},{6,4},{7,5},{8,10},{9,11},{10,... | collective-permute-start | bytes 258056 | tf_op jit(solution)/shard_map/ppermute | solution.py:53
  114.4 6.4 %collective-permute-start.38 = (bf16[48,896]{1,0:T(8,128)(2,1)S(1)}, bf16[48,896]{1,0:T(8,128)(2,1)S(1)}, u32[]{:S(2)}, u32[]{:S(2)}) collective-permute-start(bf16[48,896]{1,0:T(8,128)(2,1)S(1)} %get-tuple-element.191), channel_id=1, source_target_pairs={{0,3},{1,2},{2,1},{3,0},{4,7},{5,6},{6,5},{7,4},{8,11},{9,10},{10,... | collective-permute-start | bytes 258056 | tf_op jit(solution)/shard_map/ppermute | solution.py:53
  115.9 8.3 %collective-permute-start.34 = (bf16[6,7296]{1,0:T(8,128)(2,1)S(1)}, bf16[6,7296]{1,0:T(8,128)(2,1)S(1)}, u32[]{:S(2)}, u32[]{:S(2)}) collective-permute-start(bf16[6,7296]{1,0:T(8,128)(2,1)S(1)} %get-tuple-element.176), channel_id=1, source_target_pairs={{0,24},{8,0},{16,8},{24,16},{1,25},{9,1},{17,9},{25,17},{2,26},{10... | collective-permute-start | bytes 262664 | tf_op jit(solution)/shard_map/ppermute | solution.py:19
  121.3 4.2 %collective-permute-start.40 = (bf16[6,3584]{1,0:T(8,128)(2,1)S(1)}, bf16[6,3584]{1,0:T(8,128)(2,1)S(1)}, u32[]{:S(2)}, u32[]{:S(2)}) collective-permute-start(bf16[6,3584]{1,0:T(8,128)(2,1)S(1)} %get-tuple-element.198), channel_id=1, source_target_pairs={{0,24},{4,28},{8,0},{12,4},{16,8},{20,12},{24,16},{28,20},{1,25},{... | collective-permute-start | bytes 129032 | tf_op jit(solution)/shard_map/ppermute | solution.py:29
  122.1 5.0 %collective-permute-start.41 = (bf16[6,3584]{1,0:T(8,128)(2,1)S(1)}, bf16[6,3584]{1,0:T(8,128)(2,1)S(1)}, u32[]{:S(2)}, u32[]{:S(2)}) collective-permute-start(bf16[6,3584]{1,0:T(8,128)(2,1)S(1)} %get-tuple-element.199), channel_id=1, source_target_pairs={{0,28},{4,24},{8,4},{12,0},{16,12},{20,8},{24,20},{28,16},{1,29},{... | collective-permute-start | bytes 129032 | tf_op jit(solution)/shard_map/ppermute | solution.py:29
  122.7 7.3 %collective-permute-start.42 = (f32[4,896]{1,0:T(4,128)S(1)}, f32[4,896]{1,0:T(4,128)S(1)}, u32[]{:S(2)}, u32[]{:S(2)}) collective-permute-start(f32[4,896]{1,0:T(4,128)S(1)} %get-tuple-element.203), channel_id=1, source_target_pairs={{0,1},{1,0},{2,3},{3,2},{4,5},{5,4},{6,7},{7,6},{8,9},{9,8},{10,11... | collective-permute-start | bytes 43016 | tf_op jit(solution)/shard_map/ppermute | solution.py:53
  124.2 5.8 %collective-permute-start.43 = (f32[4,896]{1,0:T(4,128)S(1)}, f32[4,896]{1,0:T(4,128)S(1)}, u32[]{:S(2)}, u32[]{:S(2)}) collective-permute-start(f32[4,896]{1,0:T(4,128)S(1)} %get-tuple-element.204), channel_id=1, source_target_pairs={{0,2},{1,3},{2,0},{3,1},{4,6},{5,7},{6,4},{7,5},{8,10},{9,11},{10,... | collective-permute-start | bytes 43016 | tf_op jit(solution)/shard_map/ppermute | solution.py:53
  125.5 5.5 %collective-permute-start.44 = (f32[4,896]{1,0:T(4,128)S(1)}, f32[4,896]{1,0:T(4,128)S(1)}, u32[]{:S(2)}, u32[]{:S(2)}) collective-permute-start(f32[4,896]{1,0:T(4,128)S(1)} %get-tuple-element.205), channel_id=1, source_target_pairs={{0,3},{1,2},{2,1},{3,0},{4,7},{5,6},{6,5},{7,4},{8,11},{9,10},{10,... | collective-permute-start | bytes 43016 | tf_op jit(solution)/shard_map/ppermute | solution.py:53

commit v6 on v5

--- a/solution.py
+++ b/solution.py
@@ -216,7 +216,7 @@
     return pltpu.with_memory_space_constraint(value, pltpu.HBM)
 
 
-def call(name, fn, outs, small, *args, far=(), hold=(), after=(), flops=0, limit=12):
+def call(name, fn, outs, small, *args, far=(), hold=(), after=(), stream=False, flops=0, limit=12):
     outs = list(outs) + [(weight.shape[2:], bf16) for weight, _, _ in hold]
     shapes = [jax.ShapeDtypeStruct(shape, kind) for shape, kind in outs]
     n_small, n_args, n_far, n_outs = len(small), len(args), len(far), len(shapes) - len(hold)
@@ -232,6 +232,8 @@
         hold_refs = take(len(hold))
         take(len(after))
         out_refs, held_refs, buffers = take(n_outs), take(len(hold)), take(n_far)
+        if stream:
+            stage_ref, stage_sem = refs.pop(), refs.pop()
         copies = [pltpu.make_async_copy(*trio) for trio in zip(far_refs, buffers, take(n_far))]
         holds = [
             pltpu.make_async_copy(ref.at[depth, kind], held_ref, sem)
@@ -242,7 +244,17 @@
         for copy in copies:
             copy.wait()
         values = small_refs + [r[...] for r in arg_refs + buffers]
-        for ref, value in zip(out_refs, fn(*values)):
+        results = fn(*values)
+        if stream:
+            chunks, results, target = results[0], results[1:], out_refs.pop(0)
+            width = target.shape[1] // len(chunks)
+            for k, chunk in enumerate(chunks):
+                at = pl.ds(k * width, width)
+                stage_ref[:, at] = chunk.astype(target.dtype)
+                copy = pltpu.make_async_copy(stage_ref.at[:, at], target.at[:, at], stage_sem.at[k])
+                copy.start()
+                holds.append(copy)
+        for ref, value in zip(out_refs, results):
             ref[...] = value.astype(ref.dtype)
         for copy in holds:
             copy.wait()
@@ -253,9 +265,10 @@
         name=name,
         out_shape=shapes,
         in_specs=[smem] * n_small + [vmem] * n_args + [anywhere] * (n_far + len(hold) + len(after)),
-        out_specs=[vmem] * len(shapes),
+        out_specs=[anywhere if stream and k == 0 else vmem for k in range(len(shapes))],
         scratch_shapes=[pltpu.VMEM(a.shape, a.dtype) for a in far]
-        + [pltpu.SemaphoreType.DMA] * (n_far + len(hold)),
+        + [pltpu.SemaphoreType.DMA] * (n_far + len(hold))
+        + ([pltpu.SemaphoreType.DMA((stream,)), pltpu.VMEM(*outs[0])] if stream else []),
         compiler_params=pltpu.CompilerParams(vmem_limit_bytes=limit << 20),
         cost_estimate=pl.CostEstimate(flops=flops, bytes_accessed=size, transcendentals=0),
     )(*[in_hbm(a) for a in small], *args, *[in_hbm(a) for a in far], *[in_hbm(a) for a, _, _ in hold], *after)
@@ -674,14 +687,14 @@
         [((slots * parts, width // parts), bf16)] * seqs
         + [((16, features), bf16)]
         + [((slots, features), bf16)] * 2,
-        facts, start_got[0], embed, own_got[-1], norm_gain, after=(start_got[-1],),
+        facts, start_got[0], embed, own_got[-1], norm_gain,
     )
     base_got = trade_seq(base_sent)
 
     dout_2_got = gather_dp(dout_2)
 
     def first_mixed(gain, *got):
-        start_got, dout = got[:seqs], [g.astype(f32) for g in got[2 * seqs :]]
+        start_got = got[:seqs]
         got = [g.astype(f32) for g in got[seqs : 2 * seqs]]
         first = 3 * slots
         block_1, block_2, block_3 = (
@@ -710,15 +723,12 @@
         unit = start[:, :width] * decoded(start[:, width:])
         gain_h, gain_e = (piece_of(gain[0, k : k + 1], seq_place(), seqs, 0) for k in range(2))
         mixed = (unit * gain_h + units[0] * gain_e).astype(bf16).astype(f32)
-        douts = zip(*(blocks_of(block, seq_place(), seqs) for block in dout))
-        douts = [jnp.concatenate(blocks, 0) for blocks in douts]
-        return payload(mixed * facts[:, 2:3]), unit, *units, block_3[:, :width], facts, *douts
-
-    rows_1, unit_1, unit_e1, unit_e2, cot_1, own_facts, *dout_2_sent = call(
+        return payload(mixed * facts[:, 2:3]), unit, *units, block_3[:, :width], facts
+
+    rows_1, unit_1, unit_e1, unit_e2, cot_1, own_facts = call(
         "first_mixed", first_mixed,
-        [packed] + [part_rows] * 4 + [((rows, lanes), f32)]
-        + [((groups * slots * parts, fine), bf16)] * seqs,
-        (), norm_gain, *start_got, *own_got, *dout_2_got, after=(ahead_21,),
+        [packed] + [part_rows] * 4 + [((rows, lanes), f32)],
+        (), norm_gain, *start_got, *own_got, after=(ahead_21, *dout_2_got[1:-1]),
     )
     rows_1_all = gather_dp(rows_1)
 
@@ -733,9 +743,17 @@
     )
     base_2_all = gather_dp(base_2)
 
+    def dout_pieces(*dout):
+        pieces = zip(*(blocks_of(block.astype(f32), seq_place(), seqs) for block in dout))
+        return [jnp.concatenate(blocks, 0) for blocks in pieces]
+
+    dout_2_sent = call(
+        "dout_pieces", dout_pieces, [((groups * slots * parts, fine), bf16)] * seqs,
+        (), *dout_2_got, after=(rows_1,),
+    )
     up_1st, down_1st = call(
         "held_1", lambda: [], [], (),
-        hold=((expert_weight, 0, 1), (expert_weight, 0, 2)), after=(rows_1,), limit=2,
+        hold=((expert_weight, 0, 1), (expert_weight, 0, 2)), after=(dout_2_sent[0],), limit=2,
     )
     weight_1st = (gate_1st, up_1st, down_1st)
     first_own, first_send = project(
@@ -986,11 +1004,12 @@
                 preferred_element_type=f32,
             )
             out.append(jnp.where(taken > 0, placed, dense[:, at : at + step].astype(f32)).astype(bf16))
-        return [jnp.concatenate(out, 1), jnp.zeros((8, lanes), f32)]
+        return [out, jnp.zeros((8, lanes), f32)]
 
     hidden_grad, tick = call(
         "finish", finish, [((tokens, features), bf16), ((8, lanes), f32)],
-        (asked_token,), dense, asked_rows, grad_2, *last_got, limit=20,
+        (asked_token,), dense, asked_rows, grad_2, *last_got,
+        stream=features // chunk_of(features), limit=20,
     )
 
     def gain_sum(*got):

time: 132 us -> 130 us (0.985)
  starting transfers between devices: 60.6 us -> 57.4 us
  waiting for transfers between devices: 19.1 us -> 20.6 us
    ppermute x4, waiting for transfers between devices: 0.01 us -> 2.71 us  [hop(): return lax.ppermute(value, ('section', 'seq'), pairs)]
    ppermute x15, waiting for transfers between devices: 14.4 us -> 12 us  [gather_dp(): lax.ppermute(block, 'dp', [(partner(z, i, count), z) for z in range(count)])]
    ppermute x14, starting transfers between devices: 15.1 us -> 13.3 us  [ring(): lax.ppermute(value, axis, [(i, (i + steps) % count) for i in range(count)])]
    pallas_call x13 -> x14, Pallas kernels: 17.5 us -> 17.1 us  [call(): pl.pallas_call(body, name=name, out_shape=shapes, in_specs=[smem] * n_sma...]
  transfers between devices with their start and end apart: 45 -> 45, of which waited for: 9 -> 14; matrix products, arithmetic and copies ran while one was open for 0% -> 0% of each run, Pallas kernels for 36% -> 36%
where the time goes in v6:
time: 130 us
  starting transfers between devices  57.4 us (44%)
  Pallas kernels  50.5 us (39%)
  waiting for transfers between devices  20.6 us (16%)
    ppermute x15, starting transfers between devices, gather_dp(): lax.ppermute(block, 'dp', [(partner(z, i, count), z) for z in range(count)])  24.8 us
    ppermute x12, starting transfers between devices, return_dp(): lax.ppermute(blocks[i], 'dp', [(z, partner(z, i, count)) for z in range(c...  17.7 us
    pallas_call x14, Pallas kernels, call(): pl.pallas_call(body, name=name, out_shape=shapes, in_specs=[smem] * n_sma...  17.1 us
    ppermute x14, starting transfers between devices, ring(): lax.ppermute(value, axis, [(i, (i + steps) % count) for i in range(count)])  13.3 us
    ppermute x15, waiting for transfers between devices, gather_dp(): lax.ppermute(block, 'dp', [(partner(z, i, count), z) for z in range(count)])  12 us
    pallas_call x2, Pallas kernels, dense_rows(): pl.pallas_call(body, name=name, in_specs=[smem] * 2 + [vmem] * (5 + len(e...  11.2 us
    pallas_call x2, Pallas kernels, outer(): pl.pallas_call(body, name=name, in_specs=[vmem] * (count + 3) + [anywhere...  9.4 us
    pallas_call x5, Pallas kernels, project(): pl.pallas_call(body, name=name, in_specs=specs + [anywhere] * len(after),...  6.64 us
  transfers between devices with their start and end apart: 45, of which 14 were waited for; matrix products, arithmetic and copies ran while one was open for 0% of the time, Pallas kernels for 36%

profile of v6, /device:TPU:0, one launch (start us, length us, event | category | flops | bytes accessed | tf_op | source)
XLA Modules:
  0.0 129.6 jit_solution(13168835084275228777)
XLA Ops:
  0.6 2.4 %collective-permute-start = (s32[1,1,2,6]{3,2,1,0:T(2,128)}, s32[1,1,2,6]{3,2,1,0:T(2,128)S(1)}, u32[]{:S(2)}, u32[]{:S(2)}) collective-permute-start(s32[1,1,2,6]{3,2,1,0:T(2,128)} %refs_0_.11), channel_id=1, source_target_pairs={{0,24},{8,0},{16,8},{24,16},{1,25},{9,1},{17,9},{25,17},{2,26},{10... | collective-permute-start | bytes 152 | tf_op jit(solution)/shard_map/ppermute | solution.py:19
  3.1 4.3 %own_rows.1 = (bf16[22,3712]{1,0:T(8,128)(2,1)S(1)}, bf16[22,3712]{1,0:T(8,128)(2,1)S(1)}, bf16[48,1024]{1,0:T(8,128)(2,1)S(1)}, bf16[3584,512]{1,0:T(8,128)(2,1)S(1)}) custom-call(s32[1,1,2,6]{3,2,1,0:T(2,128)} %refs_0_.11, s32[2]{0:T(128)} %bitcast.15, f32[1,1,2,6]{3,2,1,0:T(2,128)} %refs_2_.3, bf16[128,7168]{1,0:T(8,128)(2,1)} %bitcast.5, ...), custom_call_target="tpu_custom_call" | custom-call | bytes 7764992 | tf_op jit(solution)/shard_map/own_rows/pallas_call | solution.py:263
  7.4 1.6 %collective-permute-start.3 = (bf16[22,3712]{1,0:T(8,128)(2,1)S(1)}, bf16[22,3712]{1,0:T(8,128)(2,1)S(1)}, u32[]{:S(2)}, u32[]{:S(2)}) collective-permute-start(bf16[22,3712]{1,0:T(8,128)(2,1)S(1)} %get-tuple-element.110), channel_id=1, source_target_pairs={{0,4},{4,0},{1,5},{5,1},{2,6},{6,2},{3,7},{7,3},{8,12},{12,8},{9,1... | collective-permute-start | bytes 489992 | tf_op jit(solution)/shard_map/ppermute | solution.py:19
  9.0 1.3 source_rows.1
  10.3 1.6 %collective-permute-start.4 = (bf16[48,1024]{1,0:T(8,128)(2,1)S(1)}, bf16[48,1024]{1,0:T(8,128)(2,1)S(1)}, u32[]{:S(2)}, u32[]{:S(2)}) collective-permute-start(bf16[48,1024]{1,0:T(8,128)(2,1)S(1)} %get-tuple-element.113.refs_0_), channel_id=1, source_target_pairs={{1,0},{0,1},{3,2},{2,3},{5,4},{4,5},{7,6},{6,7},{9,8},{8,9},{11,10... | collective-permute-start | bytes 294920 | tf_op jit(solution)/shard_map/ppermute | solution.py:45
  11.9 2.6 %collective-permute-start.5 = (bf16[48,1024]{1,0:T(8,128)(2,1)S(1)}, bf16[48,1024]{1,0:T(8,128)(2,1)S(1)}, u32[]{:S(2)}, u32[]{:S(2)}) collective-permute-start(bf16[48,1024]{1,0:T(8,128)(2,1)S(1)} %get-tuple-element.113.refs_0_), channel_id=1, source_target_pairs={{2,0},{3,1},{0,2},{1,3},{6,4},{7,5},{4,6},{5,7},{10,8},{11,9},{8,1... | collective-permute-start | bytes 294920 | tf_op jit(solution)/shard_map/ppermute | solution.py:45
  15.1 1.6 %second_base.1 = (bf16[24,896]{1,0:T(8,128)(2,1)S(1)}, bf16[24,896]{1,0:T(8,128)(2,1)S(1)}, bf16[16,7168]{1,0:T(8,128)(2,1)S(1)}, bf16[6,7168]{1,0:T(8,128)(2,1)S(1)}, bf16[6,7168]{1,0:T(8,128)(2,1)S(1)}) custom-call(s32[1,1,2,6]{3,2,1,0:T(2,128)} %refs_0_.11, s32[2]{0:T(128)} %bitcast.16, bf16[6,10880]{1,0:T(8,128)(2,1)S(1)} %collective-permute-done.1.refs_2_.refs_1_, ...), custom_call_target="tpu_custom_call" | custom-call | bytes 2731008 | tf_op jit(solution)/shard_map/second_base/pallas_call | solution.py:263
  16.8 2.3 %collective-permute-done.2.refs_2_ = bf16[6,3712]{1,0:T(8,128)(2,1)S(1)} collective-permute-done((bf16[6,3712]{1,0:T(8,128)(2,1)S(1)}, bf16[6,3712]{1,0:T(8,128)(2,1)S(1)}, u32[]{:S(2)}, u32[]{:S(2)}) %collective-permute-start.2) | collective-permute-done | bytes 44576 | tf_op jit(solution)/shard_map/ppermute | solution.py:29
  19.1 0.9 collective-permute-done.5.refs_7_.refs_2_
  20.7 2.6 %collective-permute-start.10 = (bf16[48,1024]{1,0:T(8,128)(2,1)S(1)}, bf16[48,1024]{1,0:T(8,128)(2,1)S(1)}, u32[]{:S(2)}, u32[]{:S(2)}) collective-permute-start(bf16[48,1024]{1,0:T(8,128)(2,1)S(1)} %get-tuple-element.113.refs_0_), channel_id=1, source_target_pairs={{3,0},{2,1},{1,2},{0,3},{7,4},{6,5},{5,6},{4,7},{11,8},{10,9},{9,1... | collective-permute-start | bytes 294920 | tf_op jit(solution)/shard_map/ppermute | solution.py:45
  23.3 1.9 %collective-permute-start.8 = (bf16[48,896]{1,0:T(8,128)(2,1)S(1)}, bf16[48,896]{1,0:T(8,128)(2,1)S(1)}, u32[]{:S(2)}, u32[]{:S(2)}) collective-permute-start(bf16[48,896]{1,0:T(8,128)(2,1)S(1)} %get-tuple-element.114.refs_4_.refs_2_.refs_0_.refs_1_.refs_3_), channel_id=1, source_target_pairs={{2,0},{3,1},{0,2},{1,3},{6,4},{7,5},{4,6},{5,7},{10,8},{11,9},{8,1... | collective-permute-start | bytes 258056 | tf_op jit(solution)/shard_map/ppermute | solution.py:45
  25.1 2.5 %collective-permute-start.9 = (bf16[48,896]{1,0:T(8,128)(2,1)S(1)}, bf16[48,896]{1,0:T(8,128)(2,1)S(1)}, u32[]{:S(2)}, u32[]{:S(2)}) collective-permute-start(bf16[48,896]{1,0:T(8,128)(2,1)S(1)} %get-tuple-element.114.refs_4_.refs_2_.refs_0_.refs_1_.refs_3_), channel_id=1, source_target_pairs={{3,0},{2,1},{1,2},{0,3},{7,4},{6,5},{5,6},{4,7},{11,8},{10,9},{9,1... | collective-permute-start | bytes 258056 | tf_op jit(solution)/shard_map/ppermute | solution.py:45
  28.6 3.2 %held_1.1 = (bf16[3584,512]{1,0:T(8,128)(2,1)S(1)}, bf16[3584,512]{1,0:T(8,128)(2,1)S(1)}) custom-call(bf16[2,3,3584,512]{3,2,1,0:T(8,128)(2,1)} %refs_2_.4, bf16[2,3,3584,512]{3,2,1,0:T(8,128)(2,1)} %refs_2_.4, bf16[96,1024]{1,0:T(8,128)(2,1)S(1)} %get-tuple-element.140.refs_2_.refs_0_), custom_call_target="tpu_custom_call" | custom-call | bytes 7340032 | tf_op jit(solution)/shard_map/held_1/pallas_call | solution.py:263
  32.2 1.3 %collective-permute-done.9.refs_3_.refs_6_ = bf16[48,896]{1,0:T(8,128)(2,1)S(1)} collective-permute-done((bf16[48,896]{1,0:T(8,128)(2,1)S(1)}, bf16[48,896]{1,0:T(8,128)(2,1)S(1)}, u32[]{:S(2)}, u32[]{:S(2)}) %collective-permute-start.9) | collective-permute-done | bytes 86048 | tf_op jit(solution)/shard_map/ppermute | solution.py:45
  33.5 1.4 %gate_up_1.1 = (f32[48,1024]{1,0:T(8,128)S(1)}, bf16[48,1024]{1,0:T(8,128)(2,1)S(1)}) custom-call(bf16[48,896]{1,0:T(8,128)(2,1)S(1)} %get-tuple-element.114.refs_4_.refs_2_.refs_0_.refs_1_.refs_3_, bf16[48,896]{1,0:T(8,128)(2,1)S(1)} %collective-permute-done.7.refs_1_.refs_4_, bf16[48,896]{1,0:T(8,128)(2,1)S(1)} %collective-permute-done.8.refs_2_.refs_5_, ...), custom_call_target="tpu_custom_call" | custom-call | flops 352321536 | bytes 7340032 | tf_op jit(solution)/shard_map/gate_up_1/pallas_call | solution.py:338
  34.9 0.9 collective-permute-start.12
  35.8 2.4 %collective-permute-start.13 = (bf16[48,896]{1,0:T(8,128)(2,1)S(1)}, bf16[48,896]{1,0:T(8,128)(2,1)S(1)}, u32[]{:S(2)}, u32[]{:S(2)}) collective-permute-start(bf16[48,896]{1,0:T(8,128)(2,1)S(1)} %base_order.1.refs_6_.refs_0_.refs_2_), channel_id=1, source_target_pairs={{1,0},{0,1},{3,2},{2,3},{5,4},{4,5},{7,6},{6,7},{9,8},{8,9},{11,10... | collective-permute-start | bytes 258056 | tf_op jit(solution)/shard_map/ppermute | solution.py:45
  38.3 0.9 collective-permute-start.14
  39.2 1.5 %collective-permute-start.15 = (bf16[48,896]{1,0:T(8,128)(2,1)S(1)}, bf16[48,896]{1,0:T(8,128)(2,1)S(1)}, u32[]{:S(2)}, u32[]{:S(2)}) collective-permute-start(bf16[48,896]{1,0:T(8,128)(2,1)S(1)} %base_order.1.refs_6_.refs_0_.refs_2_), channel_id=1, source_target_pairs={{3,0},{2,1},{1,2},{0,3},{7,4},{6,5},{5,6},{4,7},{11,8},{10,9},{9,1... | collective-permute-start | bytes 258056 | tf_op jit(solution)/shard_map/ppermute | solution.py:45
  40.6 1.2 down_1.1
  41.9 6.0 %collective-permute-done.14.refs_2_.refs_4_ = bf16[48,896]{1,0:T(8,128)(2,1)S(1)} collective-permute-done((bf16[48,896]{1,0:T(8,128)(2,1)S(1)}, bf16[48,896]{1,0:T(8,128)(2,1)S(1)}, u32[]{:S(2)}, u32[]{:S(2)}) %collective-permute-start.14) | collective-permute-done | bytes 86048 | tf_op jit(solution)/shard_map/ppermute | solution.py:45
  47.8 1.4 %collective-permute-start.22 = (bf16[96,1024]{1,0:T(8,128)(2,1)S(1)}, bf16[96,1024]{1,0:T(8,128)(2,1)S(1)}, u32[]{:S(2)}, u32[]{:S(2)}) collective-permute-start(bf16[96,1024]{1,0:T(8,128)(2,1)S(1)} %get-tuple-element.141), channel_id=1, source_target_pairs={{0,4},{4,0},{1,5},{5,1},{2,6},{6,2},{3,7},{7,3},{8,12},{12,8},{9,1... | collective-permute-start | bytes 589832 | tf_op jit(solution)/shard_map/ppermute | solution.py:19
  49.2 1.5 %collective-permute-start.16 = (bf16[48,896]{1,0:T(8,128)(2,1)S(1)}, bf16[48,896]{1,0:T(8,128)(2,1)S(1)}, u32[]{:S(2)}, u32[]{:S(2)}) collective-permute-start(bf16[48,896]{1,0:T(8,128)(2,1)S(1)} %get-tuple-element.133), channel_id=1, source_target_pairs={{0,1},{1,0},{2,3},{3,2},{4,5},{5,4},{6,7},{7,6},{8,9},{9,8},{10,11... | collective-permute-start | bytes 258056 | tf_op jit(solution)/shard_map/ppermute | solution.py:53
  50.7 1.2 collective-permute-start.17
  51.9 1.8 %collective-permute-start.18 = (bf16[48,896]{1,0:T(8,128)(2,1)S(1)}, bf16[48,896]{1,0:T(8,128)(2,1)S(1)}, u32[]{:S(2)}, u32[]{:S(2)}) collective-permute-start(bf16[48,896]{1,0:T(8,128)(2,1)S(1)} %get-tuple-element.135), channel_id=1, source_target_pairs={{0,3},{1,2},{2,1},{3,0},{4,7},{5,6},{6,5},{7,4},{8,11},{9,10},{10,... | collective-permute-start | bytes 258056 | tf_op jit(solution)/shard_map/ppermute | solution.py:53
  53.6 5.6 %dense_a.1 = (bf16[128,7168]{1,0:T(8,128)(2,1)S(1)}, f32[4,7168]{1,0:T(4,128)S(1)}, bf16[3584,512]{1,0:T(8,128)(2,1)S(1)}, bf16[3584,512]{1,0:T(8,128)(2,1)S(1)}, bf16[3584,512]{1,0:T(8,128)(2,1)S(1)}) custom-call(s32[1,1,2,6]{3,2,1,0:T(2,128)} %refs_0_.11, s32[2]{0:T(128)} %bitcast.17, bf16[128,7168]{1,0:T(8,128)(2,1)S(1)} %collective-permute-done.6.hidden_ref, ...), custom_call_target="tpu_custom_call" | custom-call | flops 27525120 | bytes 4587520 | tf_op jit(solution)/shard_map/dense_a/pallas_call | solution.py:567
  59.4 1.4 %collective-permute-start.19 = (bf16[48,896]{1,0:T(8,128)(2,1)S(1)}, bf16[48,896]{1,0:T(8,128)(2,1)S(1)}, u32[]{:S(2)}, u32[]{:S(2)}) collective-permute-start(bf16[48,896]{1,0:T(8,128)(2,1)S(1)} %get-tuple-element.136.refs_2_.refs_0_.refs_5_.refs_11_), channel_id=1, source_target_pairs={{1,0},{0,1},{3,2},{2,3},{5,4},{4,5},{7,6},{6,7},{9,8},{8,9},{11,10... | collective-permute-start | bytes 258056 | tf_op jit(solution)/shard_map/ppermute | solution.py:45
  60.7 1.4 %collective-permute-start.20 = (bf16[48,896]{1,0:T(8,128)(2,1)S(1)}, bf16[48,896]{1,0:T(8,128)(2,1)S(1)}, u32[]{:S(2)}, u32[]{:S(2)}) collective-permute-start(bf16[48,896]{1,0:T(8,128)(2,1)S(1)} %get-tuple-element.136.refs_2_.refs_0_.refs_5_.refs_11_), channel_id=1, source_target_pairs={{2,0},{3,1},{0,2},{1,3},{6,4},{7,5},{4,6},{5,7},{10,8},{11,9},{8,1... | collective-permute-start | bytes 258056 | tf_op jit(solution)/shard_map/ppermute | solution.py:45
  62.2 1.6 %collective-permute-start.21 = (bf16[48,896]{1,0:T(8,128)(2,1)S(1)}, bf16[48,896]{1,0:T(8,128)(2,1)S(1)}, u32[]{:S(2)}, u32[]{:S(2)}) collective-permute-start(bf16[48,896]{1,0:T(8,128)(2,1)S(1)} %get-tuple-element.136.refs_2_.refs_0_.refs_5_.refs_11_), channel_id=1, source_target_pairs={{3,0},{2,1},{1,2},{0,3},{7,4},{6,5},{5,6},{4,7},{11,8},{10,9},{9,1... | collective-permute-start | bytes 258056 | tf_op jit(solution)/shard_map/ppermute | solution.py:45
  64.2 2.0 %fixed_2.1 = (f32[48,1536]{1,0:T(8,128)S(1)}, bf16[48,1536]{1,0:T(8,128)(2,1)S(1)}) custom-call(bf16[48,896]{1,0:T(8,128)(2,1)S(1)} %base_order.1.refs_6_.refs_0_.refs_2_, bf16[48,896]{1,0:T(8,128)(2,1)S(1)} %collective-permute-done.13.refs_1_.refs_3_, bf16[48,896]{1,0:T(8,128)(2,1)S(1)} %collective-permute-done.14.refs_2_.refs_4_, ...), custom_call_target="tpu_custom_call" | custom-call | flops 528482304 | bytes 11010048 | tf_op jit(solution)/shard_map/fixed_2/pallas_call | solution.py:338
  66.2 0.8 collective-permute-start.24
  66.9 2.0 %collective-permute-done.20.refs_2_.refs_7_.refs_13_ = bf16[48,896]{1,0:T(8,128)(2,1)S(1)} collective-permute-done((bf16[48,896]{1,0:T(8,128)(2,1)S(1)}, bf16[48,896]{1,0:T(8,128)(2,1)S(1)}, u32[]{:S(2)}, u32[]{:S(2)}) %collective-permute-start.20) | collective-permute-done | bytes 86048 | tf_op jit(solution)/shard_map/ppermute | solution.py:45
  69.0 1.7 %gate_up_2.1 = (f32[48,1152]{1,0:T(8,128)S(1)}, bf16[48,1152]{1,0:T(8,128)(2,1)S(1)}, bf16[48,3584]{1,0:T(8,128)(2,1)S(1)}) custom-call(bf16[48,896]{1,0:T(8,128)(2,1)S(1)} %get-tuple-element.136.refs_2_.refs_0_.refs_5_.refs_11_, bf16[48,896]{1,0:T(8,128)(2,1)S(1)} %collective-permute-done.19.refs_1_.refs_6_.refs_12_, ...), custom_call_target="tpu_custom_call" | custom-call | flops 352321536 | bytes 7340032 | tf_op jit(solution)/shard_map/gate_up_2/pallas_call | solution.py:338
  70.7 1.0 collective-permute-start.23
  71.8 0.7 prev_down.1
  72.5 3.0 %collective-permute-done.23.refs_1_ = bf16[48,1152]{1,0:T(8,128)(2,1)S(1)} collective-permute-done((bf16[48,1152]{1,0:T(8,128)(2,1)S(1)}, bf16[48,1152]{1,0:T(8,128)(2,1)S(1)}, u32[]{:S(2)}, u32[]{:S(2)}) %collective-permute-start.23) | collective-permute-done | bytes 110624 | tf_op jit(solution)/shard_map/ppermute | solution.py:19
  75.5 2.5 %back_rows_2.1 = (bf16[48,512]{1,0:T(8,128)(2,1)S(1)}, bf16[48,512]{1,0:T(8,128)(2,1)S(1)}, bf16[48,512]{1,0:T(8,128)(2,1)S(1)}, f32[48,1]{1,0:T(8,128)S(1)}, f3...) custom-call(f32[48,1152]{1,0:T(8,128)S(1)} %get-tuple-element.150.re, ...), custom_call_target="tpu_custom_call" | custom-call | flops 352321536 | bytes 7340032 | tf_op jit(solution)/shard_map/back_rows_2/pallas_call | solution.py:377
  78.0 1.5 %collective-permute-start.25 = (bf16[48,896]{1,0:T(8,128)(2,1)S(1)}, bf16[48,896]{1,0:T(8,128)(2,1)S(1)}, u32[]{:S(2)}, u32[]{:S(2)}) collective-permute-start(bf16[48,896]{1,0:T(8,128)(2,1)S(1)} %get-tuple-element.158), channel_id=1, source_target_pairs={{0,1},{1,0},{2,3},{3,2},{4,5},{5,4},{6,7},{7,6},{8,9},{9,8},{10,11... | collective-permute-start | bytes 258056 | tf_op jit(solution)/shard_map/ppermute | solution.py:53
  79.6 1.6 %collective-permute-start.26 = (bf16[48,896]{1,0:T(8,128)(2,1)S(1)}, bf16[48,896]{1,0:T(8,128)(2,1)S(1)}, u32[]{:S(2)}, u32[]{:S(2)}) collective-permute-start(bf16[48,896]{1,0:T(8,128)(2,1)S(1)} %get-tuple-element.159), channel_id=1, source_target_pairs={{0,2},{1,3},{2,0},{3,1},{4,6},{5,7},{6,4},{7,5},{8,10},{9,11},{10,... | collective-permute-start | bytes 258056 | tf_op jit(solution)/shard_map/ppermute | solution.py:53
  81.1 1.3 %collective-permute-start.27 = (bf16[48,896]{1,0:T(8,128)(2,1)S(1)}, bf16[48,896]{1,0:T(8,128)(2,1)S(1)}, u32[]{:S(2)}, u32[]{:S(2)}) collective-permute-start(bf16[48,896]{1,0:T(8,128)(2,1)S(1)} %get-tuple-element.160), channel_id=1, source_target_pairs={{0,3},{1,2},{2,1},{3,0},{4,7},{5,6},{6,5},{7,4},{8,11},{9,10},{10,... | collective-permute-start | bytes 258056 | tf_op jit(solution)/shard_map/ppermute | solution.py:53
  82.5 1.0 collective-permute-start.28
  83.4 5.7 %dense_b.1 = (bf16[128,7168]{1,0:T(8,128)(2,1)S(1)}, f32[4,7168]{1,0:T(4,128)S(1)}) custom-call(s32[1,1,2,6]{3,2,1,0:T(2,128)} %refs_0_.11, s32[2]{0:T(128)} %bitcast.18, bf16[128,7168]{1,0:T(8,128)(2,1)S(1)} %collective-permute-done.6.hidden_ref, bf16[128,7168]{1,0:T(8,128)(2,1)S(1)} %bitcast.8, ...), custom_call_target="tpu_custom_call", output_to_operand_aliasing={{0}: (7, {})} | custom-call | flops 27525120 | bytes 4587520 | tf_op jit(solution)/shard_map/dense_b/pallas_call | solution.py:567
  89.9 1.1 collective-permute-start.30
  91.6 2.5 %collective-permute-start.32 = (bf16[48,896]{1,0:T(8,128)(2,1)S(1)}, bf16[48,896]{1,0:T(8,128)(2,1)S(1)}, u32[]{:S(2)}, u32[]{:S(2)}) collective-permute-start(bf16[48,896]{1,0:T(8,128)(2,1)S(1)} %get-tuple-element.163.refs_13_.refs_0_.refs_7_), channel_id=1, source_target_pairs={{2,0},{3,1},{0,2},{1,3},{6,4},{7,5},{4,6},{5,7},{10,8},{11,9},{8,1... | collective-permute-start | bytes 258056 | tf_op jit(solution)/shard_map/ppermute | solution.py:45
  94.1 1.3 %collective-permute-start.33 = (bf16[48,896]{1,0:T(8,128)(2,1)S(1)}, bf16[48,896]{1,0:T(8,128)(2,1)S(1)}, u32[]{:S(2)}, u32[]{:S(2)}) collective-permute-start(bf16[48,896]{1,0:T(8,128)(2,1)S(1)} %get-tuple-element.163.refs_13_.refs_0_.refs_7_), channel_id=1, source_target_pairs={{3,0},{2,1},{1,2},{0,3},{7,4},{6,5},{5,6},{4,7},{11,8},{10,9},{9,1... | collective-permute-start | bytes 258056 | tf_op jit(solution)/shard_map/ppermute | solution.py:45
  95.4 4.7 %weight_grad_2.1 = (bf16[1,2,3,3584,512]{4,3,2,1,0:T(8,128)(2,1)}, f32[8,128]{1,0:T(8,128)S(1)}) custom-call(bf16[48,3584]{1,0:T(8,128)(2,1)S(1)} %get-tuple-element.169.refs_0_, f32[48,1]{1,0:T(8,128)S(1)} %get-tuple-element.170.refs_1_, bf16[48,896]{1,0:T(8,128)(2,1)S(1)} %base_order.1.refs_6_.refs_0_.refs_2_, ...), custom_call_target="tpu_custom_call" | custom-call | flops 528482304 | bytes 11010048 | tf_op jit(solution)/shard_map/weight_grad_2/pallas_call | solution.py:424
  100.2 1.2 collective-permute-done.32.refs_2_.refs_9_
  101.4 0.8 back_1.1
  102.2 1.0 collective-permute-start.35
  103.2 1.6 %second_grad.1 = (bf16[6,7296]{1,0:T(8,128)(2,1)S(1)}, f32[4,3584]{1,0:T(4,128)S(1)}, f32[4,3584]{1,0:T(4,128)S(1)}) custom-call(s32[1,1,2,6]{3,2,1,0:T(2,128)} %refs_0_.11, s32[2]{0:T(128)} %bitcast.19, bf16[6,10880]{1,0:T(8,128)(2,1)S(1)} %collective-permute-done.1.refs_2_.refs_1_, bf16[6,7168]{1,0:T(8,128)(2,1)S(1)} %get-tuple-element.111.refs_5_.refs_3_, ...), custom_call_target="tpu_custom_call" | custom-call | bytes 2655232 | tf_op jit(solution)/shard_map/second_grad/pallas_call | solution.py:263
  104.9 1.1 collective-permute-start.39
  106.0 0.8 collective-permute-done.35.refs_1_
  106.8 2.4 %back_rows_1.1 = (bf16[48,512]{1,0:T(8,128)(2,1)S(1)}, bf16[48,512]{1,0:T(8,128)(2,1)S(1)}, f32[48,1]{1,0:T(8,128)S(1)}, bf16[48,896]{1,0:T(8,128)(2,1)S(1)}, bf...) custom-call(f32[48,640]{1,0:T(8,128)S(1)} %get-tuple-element.180.refs_0_, ...), custom_call_target="tpu_custom_call" | custom-call | flops 352321536 | bytes 7340032 | tf_op jit(solution)/shard_map/back_rows_1/pallas_call | solution.py:377
  109.2 1.4 %collective-permute-start.36 = (bf16[48,896]{1,0:T(8,128)(2,1)S(1)}, bf16[48,896]{1,0:T(8,128)(2,1)S(1)}, u32[]{:S(2)}, u32[]{:S(2)}) collective-permute-start(bf16[48,896]{1,0:T(8,128)(2,1)S(1)} %get-tuple-element.189), channel_id=1, source_target_pairs={{0,1},{1,0},{2,3},{3,2},{4,5},{5,4},{6,7},{7,6},{8,9},{9,8},{10,11... | collective-permute-start | bytes 258056 | tf_op jit(solution)/shard_map/ppermute | solution.py:53
  110.5 1.8 %collective-permute-start.37 = (bf16[48,896]{1,0:T(8,128)(2,1)S(1)}, bf16[48,896]{1,0:T(8,128)(2,1)S(1)}, u32[]{:S(2)}, u32[]{:S(2)}) collective-permute-start(bf16[48,896]{1,0:T(8,128)(2,1)S(1)} %get-tuple-element.190), channel_id=1, source_target_pairs={{0,2},{1,3},{2,0},{3,1},{4,6},{5,7},{6,4},{7,5},{8,10},{9,11},{10,... | collective-permute-start | bytes 258056 | tf_op jit(solution)/shard_map/ppermute | solution.py:53
  112.3 1.3 collective-permute-start.38
  113.6 4.7 %weight_grad_1.1 = (bf16[1,2,3,3584,512]{4,3,2,1,0:T(8,128)(2,1)}, f32[8,128]{1,0:T(8,128)S(1)}) custom-call(f32[48,1]{1,0:T(8,128)S(1)} %get-tuple-element.184.refs_0_.refs_3_, f32[48,1]{1,0:T(8,128)S(1)} %get-tuple-element.179.refs_5_.refs_1_.refs_2_, f32[48,1]{1,0:T(8,128)S(1)} %get-tuple-element.182.refs_6_.refs_2_, ...), custom_call_target="tpu_custom_call", output_to_operand_aliasing={{0}: (18, {})} | custom-call | flops 528482304 | bytes 11010048 | tf_op jit(solution)/shard_map/weight_grad_1/pallas_call | solution.py:424
  119.8 0.9 collective-permute-start.41
  120.7 0.9 collective-permute-start.42
  121.6 1.8 %collective-permute-start.43 = (f32[4,896]{1,0:T(4,128)S(1)}, f32[4,896]{1,0:T(4,128)S(1)}, u32[]{:S(2)}, u32[]{:S(2)}) collective-permute-start(f32[4,896]{1,0:T(4,128)S(1)} %get-tuple-element.204), channel_id=1, source_target_pairs={{0,2},{1,3},{2,0},{3,1},{4,6},{5,7},{6,4},{7,5},{8,10},{9,11},{10,... | collective-permute-start | bytes 43016 | tf_op jit(solution)/shard_map/ppermute | solution.py:53
  123.5 1.6 %collective-permute-start.44 = (f32[4,896]{1,0:T(4,128)S(1)}, f32[4,896]{1,0:T(4,128)S(1)}, u32[]{:S(2)}, u32[]{:S(2)}) collective-permute-start(f32[4,896]{1,0:T(4,128)S(1)} %get-tuple-element.205), channel_id=1, source_target_pairs={{0,3},{1,2},{2,1},{3,0},{4,7},{5,6},{6,5},{7,4},{8,11},{9,10},{10,... | collective-permute-start | bytes 43016 | tf_op jit(solution)/shard_map/ppermute | solution.py:53
  125.1 2.5 %finish.1 = (bf16[128,7168]{1,0:T(8,128)(2,1)}, f32[8,128]{1,0:T(8,128)S(1)}) custom-call(s32[1,1,2,6]{3,2,1,0:T(2,128)} %copy-done.4, bf16[128,7168]{1,0:T(8,128)(2,1)S(1)} %collective-permute-done.29.refs_1_, bf16[6,7168]{1,0:T(8,128)(2,1)S(1)} %get-tuple-element.165.refs_2_, bf16[6,7296]{1,0:T(8,128)(2,1)S(1)} %collective-permute-done.34.refs_3_, ...), custom_call_target="tpu_custom_call" | custom-call | bytes 3933696 | tf_op jit(solution)/shard_map/finish/pallas_call | solution.py:263
  127.6 1.3 %collective-permute-done.44.refs_3_ = f32[4,896]{1,0:T(4,128)S(1)} collective-permute-done((f32[4,896]{1,0:T(4,128)S(1)}, f32[4,896]{1,0:T(4,128)S(1)}, u32[]{:S(2)}, u32[]{:S(2)}) %collective-permute-start.44) | collective-permute-done | bytes 14368 | tf_op jit(solution)/shard_map/ppermute | solution.py:53
  129.0 0.6 gain_sum.1
  (62 shorter events, 6.1 us)
Async XLA Ops:
  0.6 6.7 %collective-permute-start = (s32[1,1,2,6]{3,2,1,0:T(2,128)}, s32[1,1,2,6]{3,2,1,0:T(2,128)S(1)}, u32[]{:S(2)}, u32[]{:S(2)}) collective-permute-start(s32[1,1,2,6]{3,2,1,0:T(2,128)} %refs_0_.11), channel_id=1, source_target_pairs={{0,24},{8,0},{16,8},{24,16},{1,25},{9,1},{17,9},{25,17},{2,26},{10... | collective-permute-start | bytes 152 | tf_op jit(solution)/shard_map/ppermute | solution.py:19
  3.1 5.9 %copy-start.3 = (bf16[1,1,128,7168]{3,2,1,0:T(8,128)(2,1)S(1)}, bf16[1,1,128,7168]{3,2,1,0:T(8,128)(2,1)}, u32[]{:S(2)}) copy-start(bf16[1,1,128,7168]{3,2,1,0:T(8,128)(2,1)} %param.8) | copy-start | bytes 5505028
  3.1 12.1 %copy-start = (bf16[1,1,128,7168]{3,2,1,0:T(8,128)(2,1)S(1)}, bf16[1,1,128,7168]{3,2,1,0:T(8,128)(2,1)}, u32[]{:S(2)}) copy-start(bf16[1,1,128,7168]{3,2,1,0:T(8,128)(2,1)} %param.9) | copy-start | bytes 5505028
  3.1 12.1 %copy-start.2 = (f32[2,2,7168]{2,1,0:T(2,128)S(1)}, f32[2,2,7168]{2,1,0:T(2,128)}, u32[]{:S(2)}) copy-start(f32[2,2,7168]{2,1,0:T(2,128)} %refs_8_.1) | copy-start | bytes 344068
  7.4 1.6 %copy-start.4 = (s32[1,1,2,6]{3,2,1,0:T(2,128)}, s32[1,1,2,6]{3,2,1,0:T(2,128)S(1)}, u32[]{:S(2)}) copy-start(s32[1,1,2,6]{3,2,1,0:T(2,128)S(1)} %collective-permute-done.refs_0_) | copy-start | bytes 148
  7.4 7.7 %collective-permute-start.3 = (bf16[22,3712]{1,0:T(8,128)(2,1)S(1)}, bf16[22,3712]{1,0:T(8,128)(2,1)S(1)}, u32[]{:S(2)}, u32[]{:S(2)}) collective-permute-start(bf16[22,3712]{1,0:T(8,128)(2,1)S(1)} %get-tuple-element.110), channel_id=1, source_target_pairs={{0,4},{4,0},{1,5},{5,1},{2,6},{6,2},{3,7},{7,3},{8,12},{12,8},{9,1... | collective-permute-start | bytes 489992 | tf_op jit(solution)/shard_map/ppermute | solution.py:19
  10.3 4.9 %collective-permute-start.1 = (bf16[6,10880]{1,0:T(8,128)(2,1)S(1)}, bf16[6,10880]{1,0:T(8,128)(2,1)S(1)}, u32[]{:S(2)}, u32[]{:S(2)}) collective-permute-start(bf16[6,10880]{1,0:T(8,128)(2,1)S(1)} %get-tuple-element.108), channel_id=1, source_target_pairs={{0,8},{4,12},{8,16},{12,20},{16,24},{20,28},{24,0},{28,4},{1,9},{5... | collective-permute-start | bytes 391688 | tf_op jit(solution)/shard_map/ppermute | solution.py:29
  10.3 8.8 %collective-permute-start.4 = (bf16[48,1024]{1,0:T(8,128)(2,1)S(1)}, bf16[48,1024]{1,0:T(8,128)(2,1)S(1)}, u32[]{:S(2)}, u32[]{:S(2)}) collective-permute-start(bf16[48,1024]{1,0:T(8,128)(2,1)S(1)} %get-tuple-element.113.refs_0_), channel_id=1, source_target_pairs={{1,0},{0,1},{3,2},{2,3},{5,4},{4,5},{7,6},{6,7},{9,8},{8,9},{11,10... | collective-permute-start | bytes 294920 | tf_op jit(solution)/shard_map/ppermute | solution.py:45
  11.9 8.0 %collective-permute-start.5 = (bf16[48,1024]{1,0:T(8,128)(2,1)S(1)}, bf16[48,1024]{1,0:T(8,128)(2,1)S(1)}, u32[]{:S(2)}, u32[]{:S(2)}) collective-permute-start(bf16[48,1024]{1,0:T(8,128)(2,1)S(1)} %get-tuple-element.113.refs_0_), channel_id=1, source_target_pairs={{2,0},{3,1},{0,2},{1,3},{6,4},{7,5},{4,6},{5,7},{10,8},{11,9},{8,1... | collective-permute-start | bytes 294920 | tf_op jit(solution)/shard_map/ppermute | solution.py:45
  14.5 4.5 %collective-permute-start.2 = (bf16[6,3712]{1,0:T(8,128)(2,1)S(1)}, bf16[6,3712]{1,0:T(8,128)(2,1)S(1)}, u32[]{:S(2)}, u32[]{:S(2)}) collective-permute-start(bf16[6,3712]{1,0:T(8,128)(2,1)S(1)} %get-tuple-element.109), channel_id=1, source_target_pairs={{0,12},{4,8},{8,20},{12,16},{16,28},{20,24},{24,4},{28,0},{1,13},{... | collective-permute-start | bytes 133640 | tf_op jit(solution)/shard_map/ppermute | solution.py:29
  20.4 33.2 %collective-permute-start.6 = (bf16[128,7168]{1,0:T(8,128)(2,1)S(1)}, bf16[128,7168]{1,0:T(8,128)(2,1)S(1)}, u32[]{:S(2)}, u32[]{:S(2)}) collective-permute-start(bf16[128,7168]{1,0:T(8,128)(2,1)S(1)} %bitcast.14), channel_id=1, source_target_pairs={{0,8},{8,16},{16,24},{24,0},{1,9},{9,17},{17,25},{25,1},{2,10},{10... | collective-permute-start | bytes 5505032 | tf_op jit(solution)/shard_map/ppermute | solution.py:19
  20.7 7.4 %collective-permute-start.10 = (bf16[48,1024]{1,0:T(8,128)(2,1)S(1)}, bf16[48,1024]{1,0:T(8,128)(2,1)S(1)}, u32[]{:S(2)}, u32[]{:S(2)}) collective-permute-start(bf16[48,1024]{1,0:T(8,128)(2,1)S(1)} %get-tuple-element.113.refs_0_), channel_id=1, source_target_pairs={{3,0},{2,1},{1,2},{0,3},{7,4},{6,5},{5,6},{4,7},{11,8},{10,9},{9,1... | collective-permute-start | bytes 294920 | tf_op jit(solution)/shard_map/ppermute | solution.py:45
  23.3 9.0 %collective-permute-start.7 = (bf16[48,896]{1,0:T(8,128)(2,1)S(1)}, bf16[48,896]{1,0:T(8,128)(2,1)S(1)}, u32[]{:S(2)}, u32[]{:S(2)}) collective-permute-start(bf16[48,896]{1,0:T(8,128)(2,1)S(1)} %get-tuple-element.114.refs_4_.refs_2_.refs_0_.refs_1_.refs_3_), channel_id=1, source_target_pairs={{1,0},{0,1},{3,2},{2,3},{5,4},{4,5},{7,6},{6,7},{9,8},{8,9},{11,10... | collective-permute-start | bytes 258056 | tf_op jit(solution)/shard_map/ppermute | solution.py:45
  23.3 9.0 %collective-permute-start.8 = (bf16[48,896]{1,0:T(8,128)(2,1)S(1)}, bf16[48,896]{1,0:T(8,128)(2,1)S(1)}, u32[]{:S(2)}, u32[]{:S(2)}) collective-permute-start(bf16[48,896]{1,0:T(8,128)(2,1)S(1)} %get-tuple-element.114.refs_4_.refs_2_.refs_0_.refs_1_.refs_3_), channel_id=1, source_target_pairs={{2,0},{3,1},{0,2},{1,3},{6,4},{7,5},{4,6},{5,7},{10,8},{11,9},{8,1... | collective-permute-start | bytes 258056 | tf_op jit(solution)/shard_map/ppermute | solution.py:45
  25.1 8.4 %collective-permute-start.9 = (bf16[48,896]{1,0:T(8,128)(2,1)S(1)}, bf16[48,896]{1,0:T(8,128)(2,1)S(1)}, u32[]{:S(2)}, u32[]{:S(2)}) collective-permute-start(bf16[48,896]{1,0:T(8,128)(2,1)S(1)} %get-tuple-element.114.refs_4_.refs_2_.refs_0_.refs_1_.refs_3_), channel_id=1, source_target_pairs={{3,0},{2,1},{1,2},{0,3},{7,4},{6,5},{5,6},{4,7},{11,8},{10,9},{9,1... | collective-permute-start | bytes 258056 | tf_op jit(solution)/shard_map/ppermute | solution.py:45
  28.1 4.0 %collective-permute-start.11 = (bf16[24,896]{1,0:T(8,128)(2,1)S(1)}, bf16[24,896]{1,0:T(8,128)(2,1)S(1)}, u32[]{:S(2)}, u32[]{:S(2)}) collective-permute-start(bf16[24,896]{1,0:T(8,128)(2,1)S(1)} %get-tuple-element.121), channel_id=1, source_target_pairs={{0,4},{4,0},{1,5},{5,1},{2,6},{6,2},{3,7},{7,3},{8,12},{12,8},{9,1... | collective-permute-start | bytes 129032 | tf_op jit(solution)/shard_map/ppermute | solution.py:19
  34.9 18.7 %copy-start.1 = (bf16[1,1,128,7168]{3,2,1,0:T(8,128)(2,1)S(1)}, bf16[1,1,128,7168]{3,2,1,0:T(8,128)(2,1)}, u32[]{:S(2)}) copy-start(bf16[1,1,128,7168]{3,2,1,0:T(8,128)(2,1)} %param.10) | copy-start | bytes 5505028
  34.9 5.7 %collective-permute-start.12 = (bf16[48,1024]{1,0:T(8,128)(2,1)S(1)}, bf16[48,1024]{1,0:T(8,128)(2,1)S(1)}, u32[]{:S(2)}, u32[]{:S(2)}) collective-permute-start(bf16[48,1024]{1,0:T(8,128)(2,1)S(1)} %get-tuple-element.123), channel_id=1, source_target_pairs={{0,4},{4,0},{1,5},{5,1},{2,6},{6,2},{3,7},{7,3},{8,12},{12,8},{9,1... | collective-permute-start | bytes 294920 | tf_op jit(solution)/shard_map/ppermute | solution.py:19
  35.8 6.0 %collective-permute-start.13 = (bf16[48,896]{1,0:T(8,128)(2,1)S(1)}, bf16[48,896]{1,0:T(8,128)(2,1)S(1)}, u32[]{:S(2)}, u32[]{:S(2)}) collective-permute-start(bf16[48,896]{1,0:T(8,128)(2,1)S(1)} %base_order.1.refs_6_.refs_0_.refs_2_), channel_id=1, source_target_pairs={{1,0},{0,1},{3,2},{2,3},{5,4},{4,5},{7,6},{6,7},{9,8},{8,9},{11,10... | collective-permute-start | bytes 258056 | tf_op jit(solution)/shard_map/ppermute | solution.py:45
  38.3 9.6 %collective-permute-start.14 = (bf16[48,896]{1,0:T(8,128)(2,1)S(1)}, bf16[48,896]{1,0:T(8,128)(2,1)S(1)}, u32[]{:S(2)}, u32[]{:S(2)}) collective-permute-start(bf16[48,896]{1,0:T(8,128)(2,1)S(1)} %base_order.1.refs_6_.refs_0_.refs_2_), channel_id=1, source_target_pairs={{2,0},{3,1},{0,2},{1,3},{6,4},{7,5},{4,6},{5,7},{10,8},{11,9},{8,1... | collective-permute-start | bytes 258056 | tf_op jit(solution)/shard_map/ppermute | solution.py:45
  39.2 8.6 %collective-permute-start.15 = (bf16[48,896]{1,0:T(8,128)(2,1)S(1)}, bf16[48,896]{1,0:T(8,128)(2,1)S(1)}, u32[]{:S(2)}, u32[]{:S(2)}) collective-permute-start(bf16[48,896]{1,0:T(8,128)(2,1)S(1)} %base_order.1.refs_6_.refs_0_.refs_2_), channel_id=1, source_target_pairs={{3,0},{2,1},{1,2},{0,3},{7,4},{6,5},{5,6},{4,7},{11,8},{10,9},{9,1... | collective-permute-start | bytes 258056 | tf_op jit(solution)/shard_map/ppermute | solution.py:45
  47.8 16.0 %collective-permute-start.22 = (bf16[96,1024]{1,0:T(8,128)(2,1)S(1)}, bf16[96,1024]{1,0:T(8,128)(2,1)S(1)}, u32[]{:S(2)}, u32[]{:S(2)}) collective-permute-start(bf16[96,1024]{1,0:T(8,128)(2,1)S(1)} %get-tuple-element.141), channel_id=1, source_target_pairs={{0,4},{4,0},{1,5},{5,1},{2,6},{6,2},{3,7},{7,3},{8,12},{12,8},{9,1... | collective-permute-start | bytes 589832 | tf_op jit(solution)/shard_map/ppermute | solution.py:19
  49.2 10.0 %collective-permute-start.16 = (bf16[48,896]{1,0:T(8,128)(2,1)S(1)}, bf16[48,896]{1,0:T(8,128)(2,1)S(1)}, u32[]{:S(2)}, u32[]{:S(2)}) collective-permute-start(bf16[48,896]{1,0:T(8,128)(2,1)S(1)} %get-tuple-element.133), channel_id=1, source_target_pairs={{0,1},{1,0},{2,3},{3,2},{4,5},{5,4},{6,7},{7,6},{8,9},{9,8},{10,11... | collective-permute-start | bytes 258056 | tf_op jit(solution)/shard_map/ppermute | solution.py:53
  50.7 8.5 %collective-permute-start.17 = (bf16[48,896]{1,0:T(8,128)(2,1)S(1)}, bf16[48,896]{1,0:T(8,128)(2,1)S(1)}, u32[]{:S(2)}, u32[]{:S(2)}) collective-permute-start(bf16[48,896]{1,0:T(8,128)(2,1)S(1)} %get-tuple-element.134), channel_id=1, source_target_pairs={{0,2},{1,3},{2,0},{3,1},{4,6},{5,7},{6,4},{7,5},{8,10},{9,11},{10,... | collective-permute-start | bytes 258056 | tf_op jit(solution)/shard_map/ppermute | solution.py:53
  51.9 7.4 %collective-permute-start.18 = (bf16[48,896]{1,0:T(8,128)(2,1)S(1)}, bf16[48,896]{1,0:T(8,128)(2,1)S(1)}, u32[]{:S(2)}, u32[]{:S(2)}) collective-permute-start(bf16[48,896]{1,0:T(8,128)(2,1)S(1)} %get-tuple-element.135), channel_id=1, source_target_pairs={{0,3},{1,2},{2,1},{3,0},{4,7},{5,6},{6,5},{7,4},{8,11},{9,10},{10,... | collective-permute-start | bytes 258056 | tf_op jit(solution)/shard_map/ppermute | solution.py:53
  59.4 7.6 %collective-permute-start.19 = (bf16[48,896]{1,0:T(8,128)(2,1)S(1)}, bf16[48,896]{1,0:T(8,128)(2,1)S(1)}, u32[]{:S(2)}, u32[]{:S(2)}) collective-permute-start(bf16[48,896]{1,0:T(8,128)(2,1)S(1)} %get-tuple-element.136.refs_2_.refs_0_.refs_5_.refs_11_), channel_id=1, source_target_pairs={{1,0},{0,1},{3,2},{2,3},{5,4},{4,5},{7,6},{6,7},{9,8},{8,9},{11,10... | collective-permute-start | bytes 258056 | tf_op jit(solution)/shard_map/ppermute | solution.py:45
  60.7 8.2 %collective-permute-start.20 = (bf16[48,896]{1,0:T(8,128)(2,1)S(1)}, bf16[48,896]{1,0:T(8,128)(2,1)S(1)}, u32[]{:S(2)}, u32[]{:S(2)}) collective-permute-start(bf16[48,896]{1,0:T(8,128)(2,1)S(1)} %get-tuple-element.136.refs_2_.refs_0_.refs_5_.refs_11_), channel_id=1, source_target_pairs={{2,0},{3,1},{0,2},{1,3},{6,4},{7,5},{4,6},{5,7},{10,8},{11,9},{8,1... | collective-permute-start | bytes 258056 | tf_op jit(solution)/shard_map/ppermute | solution.py:45
  62.2 6.8 %collective-permute-start.21 = (bf16[48,896]{1,0:T(8,128)(2,1)S(1)}, bf16[48,896]{1,0:T(8,128)(2,1)S(1)}, u32[]{:S(2)}, u32[]{:S(2)}) collective-permute-start(bf16[48,896]{1,0:T(8,128)(2,1)S(1)} %get-tuple-element.136.refs_2_.refs_0_.refs_5_.refs_11_), channel_id=1, source_target_pairs={{3,0},{2,1},{1,2},{0,3},{7,4},{6,5},{5,6},{4,7},{11,8},{10,9},{9,1... | collective-permute-start | bytes 258056 | tf_op jit(solution)/shard_map/ppermute | solution.py:45
  66.2 6.3 %collective-permute-start.24 = (bf16[48,1536]{1,0:T(8,128)(2,1)S(1)}, bf16[48,1536]{1,0:T(8,128)(2,1)S(1)}, u32[]{:S(2)}, u32[]{:S(2)}) collective-permute-start(bf16[48,1536]{1,0:T(8,128)(2,1)S(1)} %get-tuple-element.152), channel_id=1, source_target_pairs={{0,4},{4,0},{1,5},{5,1},{2,6},{6,2},{3,7},{7,3},{8,12},{12,8},{9,1... | collective-permute-start | bytes 442376 | tf_op jit(solution)/shard_map/ppermute | solution.py:19
  70.7 4.8 %collective-permute-start.23 = (bf16[48,1152]{1,0:T(8,128)(2,1)S(1)}, bf16[48,1152]{1,0:T(8,128)(2,1)S(1)}, u32[]{:S(2)}, u32[]{:S(2)}) collective-permute-start(bf16[48,1152]{1,0:T(8,128)(2,1)S(1)} %get-tuple-element.151.refs_5_), channel_id=1, source_target_pairs={{0,4},{4,0},{1,5},{5,1},{2,6},{6,2},{3,7},{7,3},{8,12},{12,8},{9,1... | collective-permute-start | bytes 331784 | tf_op jit(solution)/shard_map/ppermute | solution.py:19
  78.0 11.1 %collective-permute-start.25 = (bf16[48,896]{1,0:T(8,128)(2,1)S(1)}, bf16[48,896]{1,0:T(8,128)(2,1)S(1)}, u32[]{:S(2)}, u32[]{:S(2)}) collective-permute-start(bf16[48,896]{1,0:T(8,128)(2,1)S(1)} %get-tuple-element.158), channel_id=1, source_target_pairs={{0,1},{1,0},{2,3},{3,2},{4,5},{5,4},{6,7},{7,6},{8,9},{9,8},{10,11... | collective-permute-start | bytes 258056 | tf_op jit(solution)/shard_map/ppermute | solution.py:53
  79.6 9.6 %collective-permute-start.26 = (bf16[48,896]{1,0:T(8,128)(2,1)S(1)}, bf16[48,896]{1,0:T(8,128)(2,1)S(1)}, u32[]{:S(2)}, u32[]{:S(2)}) collective-permute-start(bf16[48,896]{1,0:T(8,128)(2,1)S(1)} %get-tuple-element.159), channel_id=1, source_target_pairs={{0,2},{1,3},{2,0},{3,1},{4,6},{5,7},{6,4},{7,5},{8,10},{9,11},{10,... | collective-permute-start | bytes 258056 | tf_op jit(solution)/shard_map/ppermute | solution.py:53
  81.1 8.0 %collective-permute-start.27 = (bf16[48,896]{1,0:T(8,128)(2,1)S(1)}, bf16[48,896]{1,0:T(8,128)(2,1)S(1)}, u32[]{:S(2)}, u32[]{:S(2)}) collective-permute-start(bf16[48,896]{1,0:T(8,128)(2,1)S(1)} %get-tuple-element.160), channel_id=1, source_target_pairs={{0,3},{1,2},{2,1},{3,0},{4,7},{5,6},{6,5},{7,4},{8,11},{9,10},{10,... | collective-permute-start | bytes 258056 | tf_op jit(solution)/shard_map/ppermute | solution.py:53
  82.5 6.7 %collective-permute-start.28 = (bf16[48,512]{1,0:T(8,128)(2,1)S(1)}, bf16[48,512]{1,0:T(8,128)(2,1)S(1)}, u32[]{:S(2)}, u32[]{:S(2)}) collective-permute-start(bf16[48,512]{1,0:T(8,128)(2,1)S(1)} %get-tuple-element.162), channel_id=1, source_target_pairs={{0,4},{4,0},{1,5},{5,1},{2,6},{6,2},{3,7},{7,3},{8,12},{12,8},{9,1... | collective-permute-start | bytes 147464 | tf_op jit(solution)/shard_map/ppermute | solution.py:19
  89.6 35.4 %collective-permute-start.29 = (bf16[128,7168]{1,0:T(8,128)(2,1)S(1)}, bf16[128,7168]{1,0:T(8,128)(2,1)S(1)}, u32[]{:S(2)}, u32[]{:S(2)}) collective-permute-start(bf16[128,7168]{1,0:T(8,128)(2,1)S(1)} %get-tuple-element.164), channel_id=1, source_target_pairs={{0,24},{8,0},{16,8},{24,16},{1,25},{9,1},{17,9},{25,17},{2,26},{10... | collective-permute-start | bytes 5505032 | tf_op jit(solution)/shard_map/ppermute | solution.py:19
  89.9 5.5 %collective-permute-start.30 = (bf16[6,3584]{1,0:T(8,128)(2,1)S(1)}, bf16[6,3584]{1,0:T(8,128)(2,1)S(1)}, u32[]{:S(2)}, u32[]{:S(2)}) collective-permute-start(bf16[6,3584]{1,0:T(8,128)(2,1)S(1)} %get-tuple-element.168), channel_id=1, source_target_pairs={{0,4},{4,0},{1,5},{5,1},{2,6},{6,2},{3,7},{7,3},{8,12},{12,8},{9,1... | collective-permute-start | bytes 129032 | tf_op jit(solution)/shard_map/ppermute | solution.py:19
  91.0 9.1 %collective-permute-start.31 = (bf16[48,896]{1,0:T(8,128)(2,1)S(1)}, bf16[48,896]{1,0:T(8,128)(2,1)S(1)}, u32[]{:S(2)}, u32[]{:S(2)}) collective-permute-start(bf16[48,896]{1,0:T(8,128)(2,1)S(1)} %get-tuple-element.163.refs_13_.refs_0_.refs_7_), channel_id=1, source_target_pairs={{1,0},{0,1},{3,2},{2,3},{5,4},{4,5},{7,6},{6,7},{9,8},{8,9},{11,10... | collective-permute-start | bytes 258056 | tf_op jit(solution)/shard_map/ppermute | solution.py:45
  91.6 9.8 %collective-permute-start.32 = (bf16[48,896]{1,0:T(8,128)(2,1)S(1)}, bf16[48,896]{1,0:T(8,128)(2,1)S(1)}, u32[]{:S(2)}, u32[]{:S(2)}) collective-permute-start(bf16[48,896]{1,0:T(8,128)(2,1)S(1)} %get-tuple-element.163.refs_13_.refs_0_.refs_7_), channel_id=1, source_target_pairs={{2,0},{3,1},{0,2},{1,3},{6,4},{7,5},{4,6},{5,7},{10,8},{11,9},{8,1... | collective-permute-start | bytes 258056 | tf_op jit(solution)/shard_map/ppermute | solution.py:45
  94.1 7.3 %collective-permute-start.33 = (bf16[48,896]{1,0:T(8,128)(2,1)S(1)}, bf16[48,896]{1,0:T(8,128)(2,1)S(1)}, u32[]{:S(2)}, u32[]{:S(2)}) collective-permute-start(bf16[48,896]{1,0:T(8,128)(2,1)S(1)} %get-tuple-element.163.refs_13_.refs_0_.refs_7_), channel_id=1, source_target_pairs={{3,0},{2,1},{1,2},{0,3},{7,4},{6,5},{5,6},{4,7},{11,8},{10,9},{9,1... | collective-permute-start | bytes 258056 | tf_op jit(solution)/shard_map/ppermute | solution.py:45
  102.2 4.6 %collective-permute-start.35 = (bf16[48,640]{1,0:T(8,128)(2,1)S(1)}, bf16[48,640]{1,0:T(8,128)(2,1)S(1)}, u32[]{:S(2)}, u32[]{:S(2)}) collective-permute-start(bf16[48,640]{1,0:T(8,128)(2,1)S(1)} %get-tuple-element.175.refs_10_), channel_id=1, source_target_pairs={{0,4},{4,0},{1,5},{5,1},{2,6},{6,2},{3,7},{7,3},{8,12},{12,8},{9,1... | collective-permute-start | bytes 184328 | tf_op jit(solution)/shard_map/ppermute | solution.py:19
  104.9 8.8 %collective-permute-start.39 = (f32[4,3584]{1,0:T(4,128)S(1)}, f32[4,3584]{1,0:T(4,128)S(1)}, u32[]{:S(2)}, u32[]{:S(2)}) collective-permute-start(f32[4,3584]{1,0:T(4,128)S(1)} %get-tuple-element.192), channel_id=1, source_target_pairs={{0,4},{4,0},{1,5},{5,1},{2,6},{6,2},{3,7},{7,3},{8,12},{12,8},{9,1... | collective-permute-start | bytes 172040 | tf_op jit(solution)/shard_map/ppermute | solution.py:19
  109.2 9.1 %collective-permute-start.36 = (bf16[48,896]{1,0:T(8,128)(2,1)S(1)}, bf16[48,896]{1,0:T(8,128)(2,1)S(1)}, u32[]{:S(2)}, u32[]{:S(2)}) collective-permute-start(bf16[48,896]{1,0:T(8,128)(2,1)S(1)} %get-tuple-element.189), channel_id=1, source_target_pairs={{0,1},{1,0},{2,3},{3,2},{4,5},{5,4},{6,7},{7,6},{8,9},{9,8},{10,11... | collective-permute-start | bytes 258056 | tf_op jit(solution)/shard_map/ppermute | solution.py:53
  110.5 7.8 %collective-permute-start.37 = (bf16[48,896]{1,0:T(8,128)(2,1)S(1)}, bf16[48,896]{1,0:T(8,128)(2,1)S(1)}, u32[]{:S(2)}, u32[]{:S(2)}) collective-permute-start(bf16[48,896]{1,0:T(8,128)(2,1)S(1)} %get-tuple-element.190), channel_id=1, source_target_pairs={{0,2},{1,3},{2,0},{3,1},{4,6},{5,7},{6,4},{7,5},{8,10},{9,11},{10,... | collective-permute-start | bytes 258056 | tf_op jit(solution)/shard_map/ppermute | solution.py:53
  112.3 6.4 %collective-permute-start.38 = (bf16[48,896]{1,0:T(8,128)(2,1)S(1)}, bf16[48,896]{1,0:T(8,128)(2,1)S(1)}, u32[]{:S(2)}, u32[]{:S(2)}) collective-permute-start(bf16[48,896]{1,0:T(8,128)(2,1)S(1)} %get-tuple-element.191), channel_id=1, source_target_pairs={{0,3},{1,2},{2,1},{3,0},{4,7},{5,6},{6,5},{7,4},{8,11},{9,10},{10,... | collective-permute-start | bytes 258056 | tf_op jit(solution)/shard_map/ppermute | solution.py:53
  113.6 8.0 %collective-permute-start.34 = (bf16[6,7296]{1,0:T(8,128)(2,1)S(1)}, bf16[6,7296]{1,0:T(8,128)(2,1)S(1)}, u32[]{:S(2)}, u32[]{:S(2)}) collective-permute-start(bf16[6,7296]{1,0:T(8,128)(2,1)S(1)} %get-tuple-element.176), channel_id=1, source_target_pairs={{0,24},{8,0},{16,8},{24,16},{1,25},{9,1},{17,9},{25,17},{2,26},{10... | collective-permute-start | bytes 262664 | tf_op jit(solution)/shard_map/ppermute | solution.py:19
  119.2 4.2 %collective-permute-start.40 = (bf16[6,3584]{1,0:T(8,128)(2,1)S(1)}, bf16[6,3584]{1,0:T(8,128)(2,1)S(1)}, u32[]{:S(2)}, u32[]{:S(2)}) collective-permute-start(bf16[6,3584]{1,0:T(8,128)(2,1)S(1)} %get-tuple-element.198), channel_id=1, source_target_pairs={{0,24},{4,28},{8,0},{12,4},{16,8},{20,12},{24,16},{28,20},{1,25},{... | collective-permute-start | bytes 129032 | tf_op jit(solution)/shard_map/ppermute | solution.py:29
  119.8 5.3 %collective-permute-start.41 = (bf16[6,3584]{1,0:T(8,128)(2,1)S(1)}, bf16[6,3584]{1,0:T(8,128)(2,1)S(1)}, u32[]{:S(2)}, u32[]{:S(2)}) collective-permute-start(bf16[6,3584]{1,0:T(8,128)(2,1)S(1)} %get-tuple-element.199), channel_id=1, source_target_pairs={{0,28},{4,24},{8,4},{12,0},{16,12},{20,8},{24,20},{28,16},{1,29},{... | collective-permute-start | bytes 129032 | tf_op jit(solution)/shard_map/ppermute | solution.py:29
  120.7 6.9 %collective-permute-start.42 = (f32[4,896]{1,0:T(4,128)S(1)}, f32[4,896]{1,0:T(4,128)S(1)}, u32[]{:S(2)}, u32[]{:S(2)}) collective-permute-start(f32[4,896]{1,0:T(4,128)S(1)} %get-tuple-element.203), channel_id=1, source_target_pairs={{0,1},{1,0},{2,3},{3,2},{4,5},{5,4},{6,7},{7,6},{8,9},{9,8},{10,11... | collective-permute-start | bytes 43016 | tf_op jit(solution)/shard_map/ppermute | solution.py:53
  121.6 6.0 %collective-permute-start.43 = (f32[4,896]{1,0:T(4,128)S(1)}, f32[4,896]{1,0:T(4,128)S(1)}, u32[]{:S(2)}, u32[]{:S(2)}) collective-permute-start(f32[4,896]{1,0:T(4,128)S(1)} %get-tuple-element.204), channel_id=1, source_target_pairs={{0,2},{1,3},{2,0},{3,1},{4,6},{5,7},{6,4},{7,5},{8,10},{9,11},{10,... | collective-permute-start | bytes 43016 | tf_op jit(solution)/shard_map/ppermute | solution.py:53
  123.5 5.5 %collective-permute-start.44 = (f32[4,896]{1,0:T(4,128)S(1)}, f32[4,896]{1,0:T(4,128)S(1)}, u32[]{:S(2)}, u32[]{:S(2)}) collective-permute-start(f32[4,896]{1,0:T(4,128)S(1)} %get-tuple-element.205), channel_id=1, source_target_pairs={{0,3},{1,2},{2,1},{3,0},{4,7},{5,6},{6,5},{7,4},{8,11},{9,10},{10,... | collective-permute-start | bytes 43016 | tf_op jit(solution)/shard_map/ppermute | solution.py:53

commit v7 on v6

--- a/solution.py
+++ b/solution.py
@@ -771,7 +771,7 @@
         [((total, hidden_units), bf16), ((total, 2 * hidden_units), f32)],
         weight_1st, (2,), groups, parts,
     )
-    out_blocks = lax.optimization_barrier((*out_blocks, *base_2_all))[:groups]
+    out_blocks = lax.optimization_barrier((*out_blocks, *base_2_all[1:-1]))[:groups]
     out_got = return_dp(out_blocks)
 
     hidden, _ = lax.optimization_barrier((source, rows_1))
@@ -824,11 +824,6 @@
         select=same_16, gain=norm_gain, after=(fixed_own,),
     )
     second = pair_seq(mixed_own, mixed_send)
-    prev_w_own, prev_w_send = project(
-        "prev_down", prev_all, weight_1st, (2,), parts, after=(mixed_send,)
-    )
-    prev_pair = pair_seq(prev_w_own, prev_w_send)
-
     def gates_back(gate, up, d_act):
         sig = jax.nn.sigmoid(gate)
         d_gate = d_act * up * sig * (1.0 + gate * (1.0 - sig))
@@ -851,7 +846,7 @@
         "back_rows_2", backward_2,
         second + fixed_pair + (same,),
         [units, units, units, ((total, 1), f32), ((total, 1), f32)],
-        weight_2nd, (0, 1), groups, parts, after=(prev_w_own,),
+        weight_2nd, (0, 1), groups, parts,
     )
     d_rows_got = return_dp(d_rows_blocks)
     dense, dense_terms = dense_rows(
@@ -870,7 +865,7 @@
 
     u, d_mixed_2, *d_rows_back = call(
         "first_grad", first_grad, [packed, part_rows] + [((slots, width), bf16)] * seqs,
-        (), cot_1, same_own, norm_gain, *d_rows_got, after=(dense_terms, prev_pair[1]),
+        (), cot_1, same_own, norm_gain, *d_rows_got, after=(dense_terms,),
     )
     u_all = gather_dp(u)
     dense, _ = lax.optimization_barrier((dense, u))
@@ -890,7 +885,7 @@
     )
 
     back_1_own, back_1_send = project(
-        "back_1", u_all, weight_1st, (2,), parts, mates=prev_all, after=(tick_2,)
+        "back_1", u_all, weight_1st, (2,), parts, others=(prev_all, (2,)), mates=prev_all, after=(tick_2,)
     )
     back_1 = pair_seq(back_1_own, back_1_send)
 
@@ -914,18 +909,19 @@
     grad_2 = ring(grad_2, "section", -1)
     terms_got = trade_seq(terms_parts)
 
-    def backward_1(own, other, prev_own, prev_other, both, scale, weight_1):
-        inner = own[:, hidden_units : hidden_units + 1] + decoded(other[:, hidden_units:])
-        d_act = own[:, :hidden_units] + other[:, :hidden_units].astype(f32)
+    def backward_1(own, other, both, scale, weight_1):
+        many = 2 * hidden_units
+        inner = own[:, many : many + 1] + decoded(other[:, many:])
+        sums = own[:, :many] + other[:, :many].astype(f32)
         through = scale * scale * inner / features
-        d_act = d_act - through * (prev_own + prev_other.astype(f32))
+        d_act = sums[:, :hidden_units] - through * sums[:, hidden_units:]
         d_act = d_act * (weight_1 * scale)
         d_gate, d_up = gates_back(both[:, :hidden_units], both[:, hidden_units:], d_act)
         return d_gate, d_up, through
 
     (d_gate_1, d_up_1, through_1), d_rows_blocks = expand(
         "back_rows_1", backward_1,
-        back_1 + prev_pair + (both_1, scale_2, weight_1),
+        back_1 + (both_1, scale_2, weight_1),
         [units, units, ((total, 1), f32)],
         weight_1st, (0, 1), groups, parts, after=(terms_parts[0],),
     )

time: 130 us -> 128 us (0.985)
    ppermute x15, waiting for transfers between devices: 12 us -> 8.92 us  [gather_dp(): lax.ppermute(block, 'dp', [(partner(z, i, count), z) for z in range(count)])]
    ppermute x14 -> x13, waiting for transfers between devices: 4.18 us -> 6.79 us  [ring(): lax.ppermute(value, axis, [(i, (i + steps) % count) for i in range(count)])]
    ppermute x14 -> x13, starting transfers between devices: 13.3 us -> 11.4 us  [ring(): lax.ppermute(value, axis, [(i, (i + steps) % count) for i in range(count)])]
    pallas_call x5 -> x4, Pallas kernels: 6.64 us -> 6.54 us  [project(): pl.pallas_call(body, name=name, in_specs=specs + [anywhere] * len(after),...]
  transfers between devices with their start and end apart: 45 -> 44, of which waited for: 14 -> 16; matrix products, arithmetic and copies ran while one was open for 0% -> 0% of each run, Pallas kernels for 36% -> 36%
where the time goes in v7:
time: 128 us
  starting transfers between devices  56.4 us (44%)
  Pallas kernels  50.4 us (39%)
  waiting for transfers between devices  19.9 us (16%)
    ppermute x15, starting transfers between devices, gather_dp(): lax.ppermute(block, 'dp', [(partner(z, i, count), z) for z in range(count)])  25.6 us
    ppermute x12, starting transfers between devices, return_dp(): lax.ppermute(blocks[i], 'dp', [(z, partner(z, i, count)) for z in range(c...  17.7 us
    pallas_call x14, Pallas kernels, call(): pl.pallas_call(body, name=name, out_shape=shapes, in_specs=[smem] * n_sma...  17.1 us
    ppermute x13, starting transfers between devices, ring(): lax.ppermute(value, axis, [(i, (i + steps) % count) for i in range(count)])  11.4 us
    pallas_call x2, Pallas kernels, dense_rows(): pl.pallas_call(body, name=name, in_specs=[smem] * 2 + [vmem] * (5 + len(e...  11.3 us
    pallas_call x2, Pallas kernels, outer(): pl.pallas_call(body, name=name, in_specs=[vmem] * (count + 3) + [anywhere...  9.4 us
    ppermute x15, waiting for transfers between devices, gather_dp(): lax.ppermute(block, 'dp', [(partner(z, i, count), z) for z in range(count)])  8.92 us
    ppermute x13, waiting for transfers between devices, ring(): lax.ppermute(value, axis, [(i, (i + steps) % count) for i in range(count)])  6.79 us
  transfers between devices with their start and end apart: 44, of which 16 were waited for; matrix products, arithmetic and copies ran while one was open for 0% of the time, Pallas kernels for 36%

profile of v7, /device:TPU:0, one launch (start us, length us, event | category | flops | bytes accessed | tf_op | source)
XLA Modules:
  0.0 127.7 jit_solution(107224817723269910)
XLA Ops:
  0.6 2.4 %collective-permute-start = (s32[1,1,2,6]{3,2,1,0:T(2,128)}, s32[1,1,2,6]{3,2,1,0:T(2,128)S(1)}, u32[]{:S(2)}, u32[]{:S(2)}) collective-permute-start(s32[1,1,2,6]{3,2,1,0:T(2,128)} %refs_0_.11), channel_id=1, source_target_pairs={{0,24},{8,0},{16,8},{24,16},{1,25},{9,1},{17,9},{25,17},{2,26},{10... | collective-permute-start | bytes 152 | tf_op jit(solution)/shard_map/ppermute | solution.py:19
  3.1 4.3 %own_rows.1 = (bf16[22,3712]{1,0:T(8,128)(2,1)S(1)}, bf16[22,3712]{1,0:T(8,128)(2,1)S(1)}, bf16[48,1024]{1,0:T(8,128)(2,1)S(1)}, bf16[3584,512]{1,0:T(8,128)(2,1)S(1)}) custom-call(s32[1,1,2,6]{3,2,1,0:T(2,128)} %refs_0_.11, s32[2]{0:T(128)} %bitcast.15, f32[1,1,2,6]{3,2,1,0:T(2,128)} %refs_2_.3, bf16[128,7168]{1,0:T(8,128)(2,1)} %bitcast.5, ...), custom_call_target="tpu_custom_call" | custom-call | bytes 7764992 | tf_op jit(solution)/shard_map/own_rows/pallas_call | solution.py:263
  7.4 1.6 %collective-permute-start.3 = (bf16[22,3712]{1,0:T(8,128)(2,1)S(1)}, bf16[22,3712]{1,0:T(8,128)(2,1)S(1)}, u32[]{:S(2)}, u32[]{:S(2)}) collective-permute-start(bf16[22,3712]{1,0:T(8,128)(2,1)S(1)} %get-tuple-element.108), channel_id=1, source_target_pairs={{0,4},{4,0},{1,5},{5,1},{2,6},{6,2},{3,7},{7,3},{8,12},{12,8},{9,1... | collective-permute-start | bytes 489992 | tf_op jit(solution)/shard_map/ppermute | solution.py:19
  9.0 1.3 source_rows.1
  10.3 1.6 %collective-permute-start.4 = (bf16[48,1024]{1,0:T(8,128)(2,1)S(1)}, bf16[48,1024]{1,0:T(8,128)(2,1)S(1)}, u32[]{:S(2)}, u32[]{:S(2)}) collective-permute-start(bf16[48,1024]{1,0:T(8,128)(2,1)S(1)} %get-tuple-element.111.refs_0_), channel_id=1, source_target_pairs={{1,0},{0,1},{3,2},{2,3},{5,4},{4,5},{7,6},{6,7},{9,8},{8,9},{11,10... | collective-permute-start | bytes 294920 | tf_op jit(solution)/shard_map/ppermute | solution.py:45
  11.9 2.6 %collective-permute-start.5 = (bf16[48,1024]{1,0:T(8,128)(2,1)S(1)}, bf16[48,1024]{1,0:T(8,128)(2,1)S(1)}, u32[]{:S(2)}, u32[]{:S(2)}) collective-permute-start(bf16[48,1024]{1,0:T(8,128)(2,1)S(1)} %get-tuple-element.111.refs_0_), channel_id=1, source_target_pairs={{2,0},{3,1},{0,2},{1,3},{6,4},{7,5},{4,6},{5,7},{10,8},{11,9},{8,1... | collective-permute-start | bytes 294920 | tf_op jit(solution)/shard_map/ppermute | solution.py:45
  15.1 1.6 %second_base.1 = (bf16[24,896]{1,0:T(8,128)(2,1)S(1)}, bf16[24,896]{1,0:T(8,128)(2,1)S(1)}, bf16[16,7168]{1,0:T(8,128)(2,1)S(1)}, bf16[6,7168]{1,0:T(8,128)(2,1)S(1)}, bf16[6,7168]{1,0:T(8,128)(2,1)S(1)}) custom-call(s32[1,1,2,6]{3,2,1,0:T(2,128)} %refs_0_.11, s32[2]{0:T(128)} %bitcast.16, bf16[6,10880]{1,0:T(8,128)(2,1)S(1)} %collective-permute-done.1.refs_2_.refs_1_, ...), custom_call_target="tpu_custom_call" | custom-call | bytes 2731008 | tf_op jit(solution)/shard_map/second_base/pallas_call | solution.py:263
  16.8 2.3 %collective-permute-done.2.refs_2_ = bf16[6,3712]{1,0:T(8,128)(2,1)S(1)} collective-permute-done((bf16[6,3712]{1,0:T(8,128)(2,1)S(1)}, bf16[6,3712]{1,0:T(8,128)(2,1)S(1)}, u32[]{:S(2)}, u32[]{:S(2)}) %collective-permute-start.2) | collective-permute-done | bytes 44576 | tf_op jit(solution)/shard_map/ppermute | solution.py:29
  19.1 0.9 collective-permute-done.5.refs_7_.refs_2_
  20.7 2.6 %collective-permute-start.10 = (bf16[48,1024]{1,0:T(8,128)(2,1)S(1)}, bf16[48,1024]{1,0:T(8,128)(2,1)S(1)}, u32[]{:S(2)}, u32[]{:S(2)}) collective-permute-start(bf16[48,1024]{1,0:T(8,128)(2,1)S(1)} %get-tuple-element.111.refs_0_), channel_id=1, source_target_pairs={{3,0},{2,1},{1,2},{0,3},{7,4},{6,5},{5,6},{4,7},{11,8},{10,9},{9,1... | collective-permute-start | bytes 294920 | tf_op jit(solution)/shard_map/ppermute | solution.py:45
  23.3 1.9 %collective-permute-start.8 = (bf16[48,896]{1,0:T(8,128)(2,1)S(1)}, bf16[48,896]{1,0:T(8,128)(2,1)S(1)}, u32[]{:S(2)}, u32[]{:S(2)}) collective-permute-start(bf16[48,896]{1,0:T(8,128)(2,1)S(1)} %get-tuple-element.112.refs_4_.refs_2_.refs_0_.refs_1_.refs_3_), channel_id=1, source_target_pairs={{2,0},{3,1},{0,2},{1,3},{6,4},{7,5},{4,6},{5,7},{10,8},{11,9},{8,1... | collective-permute-start | bytes 258056 | tf_op jit(solution)/shard_map/ppermute | solution.py:45
  25.1 2.5 %collective-permute-start.9 = (bf16[48,896]{1,0:T(8,128)(2,1)S(1)}, bf16[48,896]{1,0:T(8,128)(2,1)S(1)}, u32[]{:S(2)}, u32[]{:S(2)}) collective-permute-start(bf16[48,896]{1,0:T(8,128)(2,1)S(1)} %get-tuple-element.112.refs_4_.refs_2_.refs_0_.refs_1_.refs_3_), channel_id=1, source_target_pairs={{3,0},{2,1},{1,2},{0,3},{7,4},{6,5},{5,6},{4,7},{11,8},{10,9},{9,1... | collective-permute-start | bytes 258056 | tf_op jit(solution)/shard_map/ppermute | solution.py:45
  28.6 3.2 %held_1.1 = (bf16[3584,512]{1,0:T(8,128)(2,1)S(1)}, bf16[3584,512]{1,0:T(8,128)(2,1)S(1)}) custom-call(bf16[2,3,3584,512]{3,2,1,0:T(8,128)(2,1)} %refs_2_.4, bf16[2,3,3584,512]{3,2,1,0:T(8,128)(2,1)} %refs_2_.4, bf16[96,1024]{1,0:T(8,128)(2,1)S(1)} %get-tuple-element.138.refs_2_.refs_0_), custom_call_target="tpu_custom_call" | custom-call | bytes 7340032 | tf_op jit(solution)/shard_map/held_1/pallas_call | solution.py:263
  32.2 1.3 %collective-permute-done.9.refs_3_.refs_6_ = bf16[48,896]{1,0:T(8,128)(2,1)S(1)} collective-permute-done((bf16[48,896]{1,0:T(8,128)(2,1)S(1)}, bf16[48,896]{1,0:T(8,128)(2,1)S(1)}, u32[]{:S(2)}, u32[]{:S(2)}) %collective-permute-start.9) | collective-permute-done | bytes 86048 | tf_op jit(solution)/shard_map/ppermute | solution.py:45
  33.5 1.4 %gate_up_1.1 = (f32[48,1024]{1,0:T(8,128)S(1)}, bf16[48,1024]{1,0:T(8,128)(2,1)S(1)}) custom-call(bf16[48,896]{1,0:T(8,128)(2,1)S(1)} %get-tuple-element.112.refs_4_.refs_2_.refs_0_.refs_1_.refs_3_, bf16[48,896]{1,0:T(8,128)(2,1)S(1)} %collective-permute-done.7.refs_1_.refs_4_, bf16[48,896]{1,0:T(8,128)(2,1)S(1)} %collective-permute-done.8.refs_2_.refs_5_, ...), custom_call_target="tpu_custom_call" | custom-call | flops 352321536 | bytes 7340032 | tf_op jit(solution)/shard_map/gate_up_1/pallas_call | solution.py:338
  34.9 0.9 collective-permute-start.12
  35.8 2.4 %collective-permute-start.13 = (bf16[48,896]{1,0:T(8,128)(2,1)S(1)}, bf16[48,896]{1,0:T(8,128)(2,1)S(1)}, u32[]{:S(2)}, u32[]{:S(2)}) collective-permute-start(bf16[48,896]{1,0:T(8,128)(2,1)S(1)} %base_order.1.refs_6_.refs_0_.refs_2_), channel_id=1, source_target_pairs={{1,0},{0,1},{3,2},{2,3},{5,4},{4,5},{7,6},{6,7},{9,8},{8,9},{11,10... | collective-permute-start | bytes 258056 | tf_op jit(solution)/shard_map/ppermute | solution.py:45
  38.3 0.9 collective-permute-start.14
  39.2 0.7 collective-permute-done.12.refs_1_
  39.8 1.2 down_1.1
  41.0 4.0 %collective-permute-done.14.refs_2_.refs_4_ = bf16[48,896]{1,0:T(8,128)(2,1)S(1)} collective-permute-done((bf16[48,896]{1,0:T(8,128)(2,1)S(1)}, bf16[48,896]{1,0:T(8,128)(2,1)S(1)}, u32[]{:S(2)}, u32[]{:S(2)}) %collective-permute-start.14) | collective-permute-done | bytes 86048 | tf_op jit(solution)/shard_map/ppermute | solution.py:45
  45.1 1.4 %collective-permute-start.21 = (bf16[96,1024]{1,0:T(8,128)(2,1)S(1)}, bf16[96,1024]{1,0:T(8,128)(2,1)S(1)}, u32[]{:S(2)}, u32[]{:S(2)}) collective-permute-start(bf16[96,1024]{1,0:T(8,128)(2,1)S(1)} %get-tuple-element.139), channel_id=1, source_target_pairs={{0,4},{4,0},{1,5},{5,1},{2,6},{6,2},{3,7},{7,3},{8,12},{12,8},{9,1... | collective-permute-start | bytes 589832 | tf_op jit(solution)/shard_map/ppermute | solution.py:19
  46.8 2.4 %collective-permute-start.16 = (bf16[48,896]{1,0:T(8,128)(2,1)S(1)}, bf16[48,896]{1,0:T(8,128)(2,1)S(1)}, u32[]{:S(2)}, u32[]{:S(2)}) collective-permute-start(bf16[48,896]{1,0:T(8,128)(2,1)S(1)} %get-tuple-element.132), channel_id=1, source_target_pairs={{0,2},{1,3},{2,0},{3,1},{4,6},{5,7},{6,4},{7,5},{8,10},{9,11},{10,... | collective-permute-start | bytes 258056 | tf_op jit(solution)/shard_map/ppermute | solution.py:53
  49.3 1.6 %collective-permute-start.17 = (bf16[48,896]{1,0:T(8,128)(2,1)S(1)}, bf16[48,896]{1,0:T(8,128)(2,1)S(1)}, u32[]{:S(2)}, u32[]{:S(2)}) collective-permute-start(bf16[48,896]{1,0:T(8,128)(2,1)S(1)} %get-tuple-element.133), channel_id=1, source_target_pairs={{0,3},{1,2},{2,1},{3,0},{4,7},{5,6},{6,5},{7,4},{8,11},{9,10},{10,... | collective-permute-start | bytes 258056 | tf_op jit(solution)/shard_map/ppermute | solution.py:53
  50.9 2.2 %collective-permute-start.22 = (bf16[48,896]{1,0:T(8,128)(2,1)S(1)}, bf16[48,896]{1,0:T(8,128)(2,1)S(1)}, u32[]{:S(2)}, u32[]{:S(2)}) collective-permute-start(bf16[48,896]{1,0:T(8,128)(2,1)S(1)} %base_order.1.refs_6_.refs_0_.refs_2_), channel_id=1, source_target_pairs={{3,0},{2,1},{1,2},{0,3},{7,4},{6,5},{5,6},{4,7},{11,8},{10,9},{9,1... | collective-permute-start | bytes 258056 | tf_op jit(solution)/shard_map/ppermute | solution.py:45
  53.1 5.6 %dense_a.1 = (bf16[128,7168]{1,0:T(8,128)(2,1)S(1)}, f32[4,7168]{1,0:T(4,128)S(1)}, bf16[3584,512]{1,0:T(8,128)(2,1)S(1)}, bf16[3584,512]{1,0:T(8,128)(2,1)S(1)}, bf16[3584,512]{1,0:T(8,128)(2,1)S(1)}) custom-call(s32[1,1,2,6]{3,2,1,0:T(2,128)} %refs_0_.11, s32[2]{0:T(128)} %bitcast.17, bf16[128,7168]{1,0:T(8,128)(2,1)S(1)} %collective-permute-done.6.hidden_ref, ...), custom_call_target="tpu_custom_call" | custom-call | flops 27525120 | bytes 4587520 | tf_op jit(solution)/shard_map/dense_a/pallas_call | solution.py:567
  58.9 0.9 collective-permute-start.18
  59.8 1.3 %collective-permute-start.19 = (bf16[48,896]{1,0:T(8,128)(2,1)S(1)}, bf16[48,896]{1,0:T(8,128)(2,1)S(1)}, u32[]{:S(2)}, u32[]{:S(2)}) collective-permute-start(bf16[48,896]{1,0:T(8,128)(2,1)S(1)} %get-tuple-element.134.refs_2_.refs_0_.refs_6_.refs_10_.refs_11_), channel_id=1, source_target_pairs={{2,0},{3,1},{0,2},{1,3},{6,4},{7,5},{4,6},{5,7},{10,8},{11,9},{8,1... | collective-permute-start | bytes 258056 | tf_op jit(solution)/shard_map/ppermute | solution.py:45
  61.1 2.2 %collective-permute-start.20 = (bf16[48,896]{1,0:T(8,128)(2,1)S(1)}, bf16[48,896]{1,0:T(8,128)(2,1)S(1)}, u32[]{:S(2)}, u32[]{:S(2)}) collective-permute-start(bf16[48,896]{1,0:T(8,128)(2,1)S(1)} %get-tuple-element.134.refs_2_.refs_0_.refs_6_.refs_10_.refs_11_), channel_id=1, source_target_pairs={{3,0},{2,1},{1,2},{0,3},{7,4},{6,5},{5,6},{4,7},{11,8},{10,9},{9,1... | collective-permute-start | bytes 258056 | tf_op jit(solution)/shard_map/ppermute | solution.py:45
  63.7 2.0 %fixed_2.1 = (f32[48,1536]{1,0:T(8,128)S(1)}, bf16[48,1536]{1,0:T(8,128)(2,1)S(1)}) custom-call(bf16[48,896]{1,0:T(8,128)(2,1)S(1)} %base_order.1.refs_6_.refs_0_.refs_2_, bf16[48,896]{1,0:T(8,128)(2,1)S(1)} %collective-permute-done.13.refs_1_.refs_3_, bf16[48,896]{1,0:T(8,128)(2,1)S(1)} %collective-permute-done.14.refs_2_.refs_4_, ...), custom_call_target="tpu_custom_call" | custom-call | flops 528482304 | bytes 11010048 | tf_op jit(solution)/shard_map/fixed_2/pallas_call | solution.py:338
  65.7 0.6 collective-permute-start.24
  66.3 1.2 collective-permute-done.20.refs_3_.refs_9_.refs_13_.refs_14_
  67.5 1.7 %gate_up_2.1 = (f32[48,1152]{1,0:T(8,128)S(1)}, bf16[48,1152]{1,0:T(8,128)(2,1)S(1)}, bf16[48,3584]{1,0:T(8,128)(2,1)S(1)}) custom-call(bf16[48,896]{1,0:T(8,128)(2,1)S(1)} %get-tuple-element.134.refs_2_.refs_0_.refs_6_.refs_10_.refs_11_, bf16[48,896]{1,0:T(8,128)(2,1)S(1)} %collective-permute-done.18.refs_1_.refs_7_.refs_11_.refs_12_, ...), custom_call_target="tpu_custom_call" | custom-call | flops 352321536 | bytes 7340032 | tf_op jit(solution)/shard_map/gate_up_2/pallas_call | solution.py:338
  69.2 0.7 collective-permute-start.23
  69.9 1.0 collective-permute-done.24.refs_3_
  70.9 3.1 %collective-permute-done.23.refs_1_ = bf16[48,1152]{1,0:T(8,128)(2,1)S(1)} collective-permute-done((bf16[48,1152]{1,0:T(8,128)(2,1)S(1)}, bf16[48,1152]{1,0:T(8,128)(2,1)S(1)}, u32[]{:S(2)}, u32[]{:S(2)}) %collective-permute-start.23) | collective-permute-done | bytes 110624 | tf_op jit(solution)/shard_map/ppermute | solution.py:19
  74.0 2.5 %back_rows_2.1 = (bf16[48,512]{1,0:T(8,128)(2,1)S(1)}, bf16[48,512]{1,0:T(8,128)(2,1)S(1)}, bf16[48,512]{1,0:T(8,128)(2,1)S(1)}, f32[48,1]{1,0:T(8,128)S(1)}, f3...) custom-call(f32[48,1152]{1,0:T(8,128)S(1)} %get-tuple-element.148.re, ...), custom_call_target="tpu_custom_call" | custom-call | flops 352321536 | bytes 7340032 | tf_op jit(solution)/shard_map/back_rows_2/pallas_call | solution.py:377
  76.5 1.1 collective-permute-start.25
  77.6 1.8 %collective-permute-start.26 = (bf16[48,896]{1,0:T(8,128)(2,1)S(1)}, bf16[48,896]{1,0:T(8,128)(2,1)S(1)}, u32[]{:S(2)}, u32[]{:S(2)}) collective-permute-start(bf16[48,896]{1,0:T(8,128)(2,1)S(1)} %get-tuple-element.156), channel_id=1, source_target_pairs={{0,2},{1,3},{2,0},{3,1},{4,6},{5,7},{6,4},{7,5},{8,10},{9,11},{10,... | collective-permute-start | bytes 258056 | tf_op jit(solution)/shard_map/ppermute | solution.py:53
  79.4 1.6 %collective-permute-start.27 = (bf16[48,896]{1,0:T(8,128)(2,1)S(1)}, bf16[48,896]{1,0:T(8,128)(2,1)S(1)}, u32[]{:S(2)}, u32[]{:S(2)}) collective-permute-start(bf16[48,896]{1,0:T(8,128)(2,1)S(1)} %get-tuple-element.157), channel_id=1, source_target_pairs={{0,3},{1,2},{2,1},{3,0},{4,7},{5,6},{6,5},{7,4},{8,11},{9,10},{10,... | collective-permute-start | bytes 258056 | tf_op jit(solution)/shard_map/ppermute | solution.py:53
  81.0 5.6 %dense_b.1 = (bf16[128,7168]{1,0:T(8,128)(2,1)S(1)}, f32[4,7168]{1,0:T(4,128)S(1)}) custom-call(s32[1,1,2,6]{3,2,1,0:T(2,128)} %refs_0_.11, s32[2]{0:T(128)} %bitcast.18, bf16[128,7168]{1,0:T(8,128)(2,1)S(1)} %collective-permute-done.6.hidden_ref, bf16[128,7168]{1,0:T(8,128)(2,1)S(1)} %bitcast.8, ...), custom_call_target="tpu_custom_call", output_to_operand_aliasing={{0}: (7, {})} | custom-call | flops 27525120 | bytes 4587520 | tf_op jit(solution)/shard_map/dense_b/pallas_call | solution.py:567
  87.4 0.7 collective-permute-start.29
  88.2 2.6 %collective-permute-start.31 = (bf16[48,896]{1,0:T(8,128)(2,1)S(1)}, bf16[48,896]{1,0:T(8,128)(2,1)S(1)}, u32[]{:S(2)}, u32[]{:S(2)}) collective-permute-start(bf16[48,896]{1,0:T(8,128)(2,1)S(1)} %get-tuple-element.159.refs_13_.refs_0_.refs_7_), channel_id=1, source_target_pairs={{2,0},{3,1},{0,2},{1,3},{6,4},{7,5},{4,6},{5,7},{10,8},{11,9},{8,1... | collective-permute-start | bytes 258056 | tf_op jit(solution)/shard_map/ppermute | solution.py:45
  90.8 1.7 %collective-permute-start.32 = (bf16[48,896]{1,0:T(8,128)(2,1)S(1)}, bf16[48,896]{1,0:T(8,128)(2,1)S(1)}, u32[]{:S(2)}, u32[]{:S(2)}) collective-permute-start(bf16[48,896]{1,0:T(8,128)(2,1)S(1)} %get-tuple-element.159.refs_13_.refs_0_.refs_7_), channel_id=1, source_target_pairs={{3,0},{2,1},{1,2},{0,3},{7,4},{6,5},{5,6},{4,7},{11,8},{10,9},{9,1... | collective-permute-start | bytes 258056 | tf_op jit(solution)/shard_map/ppermute | solution.py:45
  92.5 4.7 %weight_grad_2.1 = (bf16[1,2,3,3584,512]{4,3,2,1,0:T(8,128)(2,1)}, f32[8,128]{1,0:T(8,128)S(1)}) custom-call(bf16[48,3584]{1,0:T(8,128)(2,1)S(1)} %get-tuple-element.165.refs_0_, f32[48,1]{1,0:T(8,128)S(1)} %get-tuple-element.166.refs_1_, bf16[48,896]{1,0:T(8,128)(2,1)S(1)} %base_order.1.refs_6_.refs_0_.refs_2_, ...), custom_call_target="tpu_custom_call" | custom-call | flops 528482304 | bytes 11010048 | tf_op jit(solution)/shard_map/weight_grad_2/pallas_call | solution.py:424
  97.3 0.9 collective-permute-done.31.refs_2_.refs_9_
  98.2 1.4 %back_1.1 = (f32[48,1152]{1,0:T(8,128)S(1)}, bf16[48,1152]{1,0:T(8,128)(2,1)S(1)}) custom-call(bf16[48,896]{1,0:T(8,128)(2,1)S(1)} %get-tuple-element.159.refs_13_.refs_0_.refs_7_, bf16[48,896]{1,0:T(8,128)(2,1)S(1)} %collective-permute-done.30.refs_1_.refs_8_, bf16[48,896]{1,0:T(8,128)(2,1)S(1)} %collective-permute-done.31.refs_2_.refs_9_, ...), custom_call_target="tpu_custom_call" | custom-call | flops 352321536 | bytes 7340032 | tf_op jit(solution)/shard_map/back_1/pallas_call | solution.py:338
  99.6 1.3 %collective-permute-start.34 = (bf16[48,1152]{1,0:T(8,128)(2,1)S(1)}, bf16[48,1152]{1,0:T(8,128)(2,1)S(1)}, u32[]{:S(2)}, u32[]{:S(2)}) collective-permute-start(bf16[48,1152]{1,0:T(8,128)(2,1)S(1)} %get-tuple-element.171.refs_10_), channel_id=1, source_target_pairs={{0,4},{4,0},{1,5},{5,1},{2,6},{6,2},{3,7},{7,3},{8,12},{12,8},{9,1... | collective-permute-start | bytes 331784 | tf_op jit(solution)/shard_map/ppermute | solution.py:19
  100.9 1.6 %second_grad.1 = (bf16[6,7296]{1,0:T(8,128)(2,1)S(1)}, f32[4,3584]{1,0:T(4,128)S(1)}, f32[4,3584]{1,0:T(4,128)S(1)}) custom-call(s32[1,1,2,6]{3,2,1,0:T(2,128)} %refs_0_.11, s32[2]{0:T(128)} %bitcast.19, bf16[6,10880]{1,0:T(8,128)(2,1)S(1)} %collective-permute-done.1.refs_2_.refs_1_, bf16[6,7168]{1,0:T(8,128)(2,1)S(1)} %get-tuple-element.109.refs_5_.refs_3_, ...), custom_call_target="tpu_custom_call" | custom-call | bytes 2655232 | tf_op jit(solution)/shard_map/second_grad/pallas_call | solution.py:263
  102.6 0.8 collective-permute-start.38
  103.4 1.7 %collective-permute-done.34.refs_1_ = bf16[48,1152]{1,0:T(8,128)(2,1)S(1)} collective-permute-done((bf16[48,1152]{1,0:T(8,128)(2,1)S(1)}, bf16[48,1152]{1,0:T(8,128)(2,1)S(1)}, u32[]{:S(2)}, u32[]{:S(2)}) %collective-permute-start.34) | collective-permute-done | bytes 110624 | tf_op jit(solution)/shard_map/ppermute | solution.py:19
  105.0 2.4 %back_rows_1.1 = (bf16[48,512]{1,0:T(8,128)(2,1)S(1)}, bf16[48,512]{1,0:T(8,128)(2,1)S(1)}, f32[48,1]{1,0:T(8,128)S(1)}, bf16[48,896]{1,0:T(8,128)(2,1)S(1)}, bf...) custom-call(f32[48,1152]{1,0:T(8,128)S(1)} %get-tuple-element.176.refs_0_, ...), custom_call_target="tpu_custom_call" | custom-call | flops 352321536 | bytes 7340032 | tf_op jit(solution)/shard_map/back_rows_1/pallas_call | solution.py:377
  107.4 1.0 collective-permute-start.35
  108.5 1.9 %collective-permute-start.36 = (bf16[48,896]{1,0:T(8,128)(2,1)S(1)}, bf16[48,896]{1,0:T(8,128)(2,1)S(1)}, u32[]{:S(2)}, u32[]{:S(2)}) collective-permute-start(bf16[48,896]{1,0:T(8,128)(2,1)S(1)} %get-tuple-element.186), channel_id=1, source_target_pairs={{0,2},{1,3},{2,0},{3,1},{4,6},{5,7},{6,4},{7,5},{8,10},{9,11},{10,... | collective-permute-start | bytes 258056 | tf_op jit(solution)/shard_map/ppermute | solution.py:53
  110.4 1.5 %collective-permute-start.37 = (bf16[48,896]{1,0:T(8,128)(2,1)S(1)}, bf16[48,896]{1,0:T(8,128)(2,1)S(1)}, u32[]{:S(2)}, u32[]{:S(2)}) collective-permute-start(bf16[48,896]{1,0:T(8,128)(2,1)S(1)} %get-tuple-element.187), channel_id=1, source_target_pairs={{0,3},{1,2},{2,1},{3,0},{4,7},{5,6},{6,5},{7,4},{8,11},{9,10},{10,... | collective-permute-start | bytes 258056 | tf_op jit(solution)/shard_map/ppermute | solution.py:53
  111.9 4.7 %weight_grad_1.1 = (bf16[1,2,3,3584,512]{4,3,2,1,0:T(8,128)(2,1)}, f32[8,128]{1,0:T(8,128)S(1)}) custom-call(f32[48,1]{1,0:T(8,128)S(1)} %get-tuple-element.180.refs_0_.refs_3_, f32[48,1]{1,0:T(8,128)S(1)} %get-tuple-element.175.refs_3_.refs_1_.refs_2_, f32[48,1]{1,0:T(8,128)S(1)} %get-tuple-element.178.refs_4_.refs_2_, ...), custom_call_target="tpu_custom_call", output_to_operand_aliasing={{0}: (18, {})} | custom-call | flops 528482304 | bytes 11010048 | tf_op jit(solution)/shard_map/weight_grad_1/pallas_call | solution.py:424
  117.3 0.9 collective-permute-start.39
  118.2 0.7 collective-permute-start.40
  118.9 1.5 %collective-permute-start.41 = (f32[4,896]{1,0:T(4,128)S(1)}, f32[4,896]{1,0:T(4,128)S(1)}, u32[]{:S(2)}, u32[]{:S(2)}) collective-permute-start(f32[4,896]{1,0:T(4,128)S(1)} %get-tuple-element.199), channel_id=1, source_target_pairs={{0,1},{1,0},{2,3},{3,2},{4,5},{5,4},{6,7},{7,6},{8,9},{9,8},{10,11... | collective-permute-start | bytes 43016 | tf_op jit(solution)/shard_map/ppermute | solution.py:53
  120.4 1.2 collective-permute-start.42
  121.6 1.7 %collective-permute-start.43 = (f32[4,896]{1,0:T(4,128)S(1)}, f32[4,896]{1,0:T(4,128)S(1)}, u32[]{:S(2)}, u32[]{:S(2)}) collective-permute-start(f32[4,896]{1,0:T(4,128)S(1)} %get-tuple-element.201), channel_id=1, source_target_pairs={{0,3},{1,2},{2,1},{3,0},{4,7},{5,6},{6,5},{7,4},{8,11},{9,10},{10,... | collective-permute-start | bytes 43016 | tf_op jit(solution)/shard_map/ppermute | solution.py:53
  123.3 2.5 %finish.1 = (bf16[128,7168]{1,0:T(8,128)(2,1)}, f32[8,128]{1,0:T(8,128)S(1)}) custom-call(s32[1,1,2,6]{3,2,1,0:T(2,128)} %copy-done.4, bf16[128,7168]{1,0:T(8,128)(2,1)S(1)} %collective-permute-done.28.refs_1_, bf16[6,7168]{1,0:T(8,128)(2,1)S(1)} %get-tuple-element.161.refs_2_, bf16[6,7296]{1,0:T(8,128)(2,1)S(1)} %collective-permute-done.33.refs_3_, ...), custom_call_target="tpu_custom_call" | custom-call | bytes 3933696 | tf_op jit(solution)/shard_map/finish/pallas_call | solution.py:263
  125.8 1.3 collective-permute-done.43.refs_3_
  127.1 0.6 gain_sum.1
  (59 shorter events, 5.1 us)
Async XLA Ops:
  0.6 6.7 %collective-permute-start = (s32[1,1,2,6]{3,2,1,0:T(2,128)}, s32[1,1,2,6]{3,2,1,0:T(2,128)S(1)}, u32[]{:S(2)}, u32[]{:S(2)}) collective-permute-start(s32[1,1,2,6]{3,2,1,0:T(2,128)} %refs_0_.11), channel_id=1, source_target_pairs={{0,24},{8,0},{16,8},{24,16},{1,25},{9,1},{17,9},{25,17},{2,26},{10... | collective-permute-start | bytes 152 | tf_op jit(solution)/shard_map/ppermute | solution.py:19
  3.1 5.9 %copy-start.3 = (bf16[1,1,128,7168]{3,2,1,0:T(8,128)(2,1)S(1)}, bf16[1,1,128,7168]{3,2,1,0:T(8,128)(2,1)}, u32[]{:S(2)}) copy-start(bf16[1,1,128,7168]{3,2,1,0:T(8,128)(2,1)} %param.8) | copy-start | bytes 5505028
  3.1 12.1 %copy-start = (bf16[1,1,128,7168]{3,2,1,0:T(8,128)(2,1)S(1)}, bf16[1,1,128,7168]{3,2,1,0:T(8,128)(2,1)}, u32[]{:S(2)}) copy-start(bf16[1,1,128,7168]{3,2,1,0:T(8,128)(2,1)} %param.9) | copy-start | bytes 5505028
  3.1 12.1 %copy-start.2 = (f32[2,2,7168]{2,1,0:T(2,128)S(1)}, f32[2,2,7168]{2,1,0:T(2,128)}, u32[]{:S(2)}) copy-start(f32[2,2,7168]{2,1,0:T(2,128)} %refs_8_.1) | copy-start | bytes 344068
  7.4 1.6 %copy-start.4 = (s32[1,1,2,6]{3,2,1,0:T(2,128)}, s32[1,1,2,6]{3,2,1,0:T(2,128)S(1)}, u32[]{:S(2)}) copy-start(s32[1,1,2,6]{3,2,1,0:T(2,128)S(1)} %collective-permute-done.refs_0_) | copy-start | bytes 148
  7.4 7.7 %collective-permute-start.3 = (bf16[22,3712]{1,0:T(8,128)(2,1)S(1)}, bf16[22,3712]{1,0:T(8,128)(2,1)S(1)}, u32[]{:S(2)}, u32[]{:S(2)}) collective-permute-start(bf16[22,3712]{1,0:T(8,128)(2,1)S(1)} %get-tuple-element.108), channel_id=1, source_target_pairs={{0,4},{4,0},{1,5},{5,1},{2,6},{6,2},{3,7},{7,3},{8,12},{12,8},{9,1... | collective-permute-start | bytes 489992 | tf_op jit(solution)/shard_map/ppermute | solution.py:19
  10.3 4.9 %collective-permute-start.1 = (bf16[6,10880]{1,0:T(8,128)(2,1)S(1)}, bf16[6,10880]{1,0:T(8,128)(2,1)S(1)}, u32[]{:S(2)}, u32[]{:S(2)}) collective-permute-start(bf16[6,10880]{1,0:T(8,128)(2,1)S(1)} %get-tuple-element.106), channel_id=1, source_target_pairs={{0,8},{4,12},{8,16},{12,20},{16,24},{20,28},{24,0},{28,4},{1,9},{5... | collective-permute-start | bytes 391688 | tf_op jit(solution)/shard_map/ppermute | solution.py:29
  10.3 8.8 %collective-permute-start.4 = (bf16[48,1024]{1,0:T(8,128)(2,1)S(1)}, bf16[48,1024]{1,0:T(8,128)(2,1)S(1)}, u32[]{:S(2)}, u32[]{:S(2)}) collective-permute-start(bf16[48,1024]{1,0:T(8,128)(2,1)S(1)} %get-tuple-element.111.refs_0_), channel_id=1, source_target_pairs={{1,0},{0,1},{3,2},{2,3},{5,4},{4,5},{7,6},{6,7},{9,8},{8,9},{11,10... | collective-permute-start | bytes 294920 | tf_op jit(solution)/shard_map/ppermute | solution.py:45
  11.9 8.0 %collective-permute-start.5 = (bf16[48,1024]{1,0:T(8,128)(2,1)S(1)}, bf16[48,1024]{1,0:T(8,128)(2,1)S(1)}, u32[]{:S(2)}, u32[]{:S(2)}) collective-permute-start(bf16[48,1024]{1,0:T(8,128)(2,1)S(1)} %get-tuple-element.111.refs_0_), channel_id=1, source_target_pairs={{2,0},{3,1},{0,2},{1,3},{6,4},{7,5},{4,6},{5,7},{10,8},{11,9},{8,1... | collective-permute-start | bytes 294920 | tf_op jit(solution)/shard_map/ppermute | solution.py:45
  14.5 4.5 %collective-permute-start.2 = (bf16[6,3712]{1,0:T(8,128)(2,1)S(1)}, bf16[6,3712]{1,0:T(8,128)(2,1)S(1)}, u32[]{:S(2)}, u32[]{:S(2)}) collective-permute-start(bf16[6,3712]{1,0:T(8,128)(2,1)S(1)} %get-tuple-element.107), channel_id=1, source_target_pairs={{0,12},{4,8},{8,20},{12,16},{16,28},{20,24},{24,4},{28,0},{1,13},{... | collective-permute-start | bytes 133640 | tf_op jit(solution)/shard_map/ppermute | solution.py:29
  20.4 30.5 %collective-permute-start.6 = (bf16[128,7168]{1,0:T(8,128)(2,1)S(1)}, bf16[128,7168]{1,0:T(8,128)(2,1)S(1)}, u32[]{:S(2)}, u32[]{:S(2)}) collective-permute-start(bf16[128,7168]{1,0:T(8,128)(2,1)S(1)} %bitcast.14), channel_id=1, source_target_pairs={{0,8},{8,16},{16,24},{24,0},{1,9},{9,17},{17,25},{25,1},{2,10},{10... | collective-permute-start | bytes 5505032 | tf_op jit(solution)/shard_map/ppermute | solution.py:19
  20.7 7.4 %collective-permute-start.10 = (bf16[48,1024]{1,0:T(8,128)(2,1)S(1)}, bf16[48,1024]{1,0:T(8,128)(2,1)S(1)}, u32[]{:S(2)}, u32[]{:S(2)}) collective-permute-start(bf16[48,1024]{1,0:T(8,128)(2,1)S(1)} %get-tuple-element.111.refs_0_), channel_id=1, source_target_pairs={{3,0},{2,1},{1,2},{0,3},{7,4},{6,5},{5,6},{4,7},{11,8},{10,9},{9,1... | collective-permute-start | bytes 294920 | tf_op jit(solution)/shard_map/ppermute | solution.py:45
  23.3 9.0 %collective-permute-start.7 = (bf16[48,896]{1,0:T(8,128)(2,1)S(1)}, bf16[48,896]{1,0:T(8,128)(2,1)S(1)}, u32[]{:S(2)}, u32[]{:S(2)}) collective-permute-start(bf16[48,896]{1,0:T(8,128)(2,1)S(1)} %get-tuple-element.112.refs_4_.refs_2_.refs_0_.refs_1_.refs_3_), channel_id=1, source_target_pairs={{1,0},{0,1},{3,2},{2,3},{5,4},{4,5},{7,6},{6,7},{9,8},{8,9},{11,10... | collective-permute-start | bytes 258056 | tf_op jit(solution)/shard_map/ppermute | solution.py:45
  23.3 9.0 %collective-permute-start.8 = (bf16[48,896]{1,0:T(8,128)(2,1)S(1)}, bf16[48,896]{1,0:T(8,128)(2,1)S(1)}, u32[]{:S(2)}, u32[]{:S(2)}) collective-permute-start(bf16[48,896]{1,0:T(8,128)(2,1)S(1)} %get-tuple-element.112.refs_4_.refs_2_.refs_0_.refs_1_.refs_3_), channel_id=1, source_target_pairs={{2,0},{3,1},{0,2},{1,3},{6,4},{7,5},{4,6},{5,7},{10,8},{11,9},{8,1... | collective-permute-start | bytes 258056 | tf_op jit(solution)/shard_map/ppermute | solution.py:45
  25.1 8.4 %collective-permute-start.9 = (bf16[48,896]{1,0:T(8,128)(2,1)S(1)}, bf16[48,896]{1,0:T(8,128)(2,1)S(1)}, u32[]{:S(2)}, u32[]{:S(2)}) collective-permute-start(bf16[48,896]{1,0:T(8,128)(2,1)S(1)} %get-tuple-element.112.refs_4_.refs_2_.refs_0_.refs_1_.refs_3_), channel_id=1, source_target_pairs={{3,0},{2,1},{1,2},{0,3},{7,4},{6,5},{5,6},{4,7},{11,8},{10,9},{9,1... | collective-permute-start | bytes 258056 | tf_op jit(solution)/shard_map/ppermute | solution.py:45
  28.1 4.0 %collective-permute-start.11 = (bf16[24,896]{1,0:T(8,128)(2,1)S(1)}, bf16[24,896]{1,0:T(8,128)(2,1)S(1)}, u32[]{:S(2)}, u32[]{:S(2)}) collective-permute-start(bf16[24,896]{1,0:T(8,128)(2,1)S(1)} %get-tuple-element.119), channel_id=1, source_target_pairs={{0,4},{4,0},{1,5},{5,1},{2,6},{6,2},{3,7},{7,3},{8,12},{12,8},{9,1... | collective-permute-start | bytes 129032 | tf_op jit(solution)/shard_map/ppermute | solution.py:19
  34.9 18.2 %copy-start.1 = (bf16[1,1,128,7168]{3,2,1,0:T(8,128)(2,1)S(1)}, bf16[1,1,128,7168]{3,2,1,0:T(8,128)(2,1)}, u32[]{:S(2)}) copy-start(bf16[1,1,128,7168]{3,2,1,0:T(8,128)(2,1)} %param.10) | copy-start | bytes 5505028
  34.9 4.9 %collective-permute-start.12 = (bf16[48,1024]{1,0:T(8,128)(2,1)S(1)}, bf16[48,1024]{1,0:T(8,128)(2,1)S(1)}, u32[]{:S(2)}, u32[]{:S(2)}) collective-permute-start(bf16[48,1024]{1,0:T(8,128)(2,1)S(1)} %get-tuple-element.121), channel_id=1, source_target_pairs={{0,4},{4,0},{1,5},{5,1},{2,6},{6,2},{3,7},{7,3},{8,12},{12,8},{9,1... | collective-permute-start | bytes 294920 | tf_op jit(solution)/shard_map/ppermute | solution.py:19
  35.8 5.2 %collective-permute-start.13 = (bf16[48,896]{1,0:T(8,128)(2,1)S(1)}, bf16[48,896]{1,0:T(8,128)(2,1)S(1)}, u32[]{:S(2)}, u32[]{:S(2)}) collective-permute-start(bf16[48,896]{1,0:T(8,128)(2,1)S(1)} %base_order.1.refs_6_.refs_0_.refs_2_), channel_id=1, source_target_pairs={{1,0},{0,1},{3,2},{2,3},{5,4},{4,5},{7,6},{6,7},{9,8},{8,9},{11,10... | collective-permute-start | bytes 258056 | tf_op jit(solution)/shard_map/ppermute | solution.py:45
  38.3 6.8 %collective-permute-start.14 = (bf16[48,896]{1,0:T(8,128)(2,1)S(1)}, bf16[48,896]{1,0:T(8,128)(2,1)S(1)}, u32[]{:S(2)}, u32[]{:S(2)}) collective-permute-start(bf16[48,896]{1,0:T(8,128)(2,1)S(1)} %base_order.1.refs_6_.refs_0_.refs_2_), channel_id=1, source_target_pairs={{2,0},{3,1},{0,2},{1,3},{6,4},{7,5},{4,6},{5,7},{10,8},{11,9},{8,1... | collective-permute-start | bytes 258056 | tf_op jit(solution)/shard_map/ppermute | solution.py:45
  45.1 18.3 %collective-permute-start.21 = (bf16[96,1024]{1,0:T(8,128)(2,1)S(1)}, bf16[96,1024]{1,0:T(8,128)(2,1)S(1)}, u32[]{:S(2)}, u32[]{:S(2)}) collective-permute-start(bf16[96,1024]{1,0:T(8,128)(2,1)S(1)} %get-tuple-element.139), channel_id=1, source_target_pairs={{0,4},{4,0},{1,5},{5,1},{2,6},{6,2},{3,7},{7,3},{8,12},{12,8},{9,1... | collective-permute-start | bytes 589832 | tf_op jit(solution)/shard_map/ppermute | solution.py:19
  46.5 12.2 %collective-permute-start.15 = (bf16[48,896]{1,0:T(8,128)(2,1)S(1)}, bf16[48,896]{1,0:T(8,128)(2,1)S(1)}, u32[]{:S(2)}, u32[]{:S(2)}) collective-permute-start(bf16[48,896]{1,0:T(8,128)(2,1)S(1)} %get-tuple-element.131), channel_id=1, source_target_pairs={{0,1},{1,0},{2,3},{3,2},{4,5},{5,4},{6,7},{7,6},{8,9},{9,8},{10,11... | collective-permute-start | bytes 258056 | tf_op jit(solution)/shard_map/ppermute | solution.py:53
  46.8 11.9 %collective-permute-start.16 = (bf16[48,896]{1,0:T(8,128)(2,1)S(1)}, bf16[48,896]{1,0:T(8,128)(2,1)S(1)}, u32[]{:S(2)}, u32[]{:S(2)}) collective-permute-start(bf16[48,896]{1,0:T(8,128)(2,1)S(1)} %get-tuple-element.132), channel_id=1, source_target_pairs={{0,2},{1,3},{2,0},{3,1},{4,6},{5,7},{6,4},{7,5},{8,10},{9,11},{10,... | collective-permute-start | bytes 258056 | tf_op jit(solution)/shard_map/ppermute | solution.py:53
  49.3 9.5 %collective-permute-start.17 = (bf16[48,896]{1,0:T(8,128)(2,1)S(1)}, bf16[48,896]{1,0:T(8,128)(2,1)S(1)}, u32[]{:S(2)}, u32[]{:S(2)}) collective-permute-start(bf16[48,896]{1,0:T(8,128)(2,1)S(1)} %get-tuple-element.133), channel_id=1, source_target_pairs={{0,3},{1,2},{2,1},{3,0},{4,7},{5,6},{6,5},{7,4},{8,11},{9,10},{10,... | collective-permute-start | bytes 258056 | tf_op jit(solution)/shard_map/ppermute | solution.py:53
  50.9 12.8 %collective-permute-start.22 = (bf16[48,896]{1,0:T(8,128)(2,1)S(1)}, bf16[48,896]{1,0:T(8,128)(2,1)S(1)}, u32[]{:S(2)}, u32[]{:S(2)}) collective-permute-start(bf16[48,896]{1,0:T(8,128)(2,1)S(1)} %base_order.1.refs_6_.refs_0_.refs_2_), channel_id=1, source_target_pairs={{3,0},{2,1},{1,2},{0,3},{7,4},{6,5},{5,6},{4,7},{11,8},{10,9},{9,1... | collective-permute-start | bytes 258056 | tf_op jit(solution)/shard_map/ppermute | solution.py:45
  58.9 7.4 %collective-permute-start.18 = (bf16[48,896]{1,0:T(8,128)(2,1)S(1)}, bf16[48,896]{1,0:T(8,128)(2,1)S(1)}, u32[]{:S(2)}, u32[]{:S(2)}) collective-permute-start(bf16[48,896]{1,0:T(8,128)(2,1)S(1)} %get-tuple-element.134.refs_2_.refs_0_.refs_6_.refs_10_.refs_11_), channel_id=1, source_target_pairs={{1,0},{0,1},{3,2},{2,3},{5,4},{4,5},{7,6},{6,7},{9,8},{8,9},{11,10... | collective-permute-start | bytes 258056 | tf_op jit(solution)/shard_map/ppermute | solution.py:45
  59.8 6.5 %collective-permute-start.19 = (bf16[48,896]{1,0:T(8,128)(2,1)S(1)}, bf16[48,896]{1,0:T(8,128)(2,1)S(1)}, u32[]{:S(2)}, u32[]{:S(2)}) collective-permute-start(bf16[48,896]{1,0:T(8,128)(2,1)S(1)} %get-tuple-element.134.refs_2_.refs_0_.refs_6_.refs_10_.refs_11_), channel_id=1, source_target_pairs={{2,0},{3,1},{0,2},{1,3},{6,4},{7,5},{4,6},{5,7},{10,8},{11,9},{8,1... | collective-permute-start | bytes 258056 | tf_op jit(solution)/shard_map/ppermute | solution.py:45
  61.1 6.4 %collective-permute-start.20 = (bf16[48,896]{1,0:T(8,128)(2,1)S(1)}, bf16[48,896]{1,0:T(8,128)(2,1)S(1)}, u32[]{:S(2)}, u32[]{:S(2)}) collective-permute-start(bf16[48,896]{1,0:T(8,128)(2,1)S(1)} %get-tuple-element.134.refs_2_.refs_0_.refs_6_.refs_10_.refs_11_), channel_id=1, source_target_pairs={{3,0},{2,1},{1,2},{0,3},{7,4},{6,5},{5,6},{4,7},{11,8},{10,9},{9,1... | collective-permute-start | bytes 258056 | tf_op jit(solution)/shard_map/ppermute | solution.py:45
  65.7 5.2 %collective-permute-start.24 = (bf16[48,1536]{1,0:T(8,128)(2,1)S(1)}, bf16[48,1536]{1,0:T(8,128)(2,1)S(1)}, u32[]{:S(2)}, u32[]{:S(2)}) collective-permute-start(bf16[48,1536]{1,0:T(8,128)(2,1)S(1)} %get-tuple-element.150), channel_id=1, source_target_pairs={{0,4},{4,0},{1,5},{5,1},{2,6},{6,2},{3,7},{7,3},{8,12},{12,8},{9,1... | collective-permute-start | bytes 442376 | tf_op jit(solution)/shard_map/ppermute | solution.py:19
  69.2 4.8 %collective-permute-start.23 = (bf16[48,1152]{1,0:T(8,128)(2,1)S(1)}, bf16[48,1152]{1,0:T(8,128)(2,1)S(1)}, u32[]{:S(2)}, u32[]{:S(2)}) collective-permute-start(bf16[48,1152]{1,0:T(8,128)(2,1)S(1)} %get-tuple-element.149), channel_id=1, source_target_pairs={{0,4},{4,0},{1,5},{5,1},{2,6},{6,2},{3,7},{7,3},{8,12},{12,8},{9,1... | collective-permute-start | bytes 331784 | tf_op jit(solution)/shard_map/ppermute | solution.py:19
  76.5 10.1 %collective-permute-start.25 = (bf16[48,896]{1,0:T(8,128)(2,1)S(1)}, bf16[48,896]{1,0:T(8,128)(2,1)S(1)}, u32[]{:S(2)}, u32[]{:S(2)}) collective-permute-start(bf16[48,896]{1,0:T(8,128)(2,1)S(1)} %get-tuple-element.155), channel_id=1, source_target_pairs={{0,1},{1,0},{2,3},{3,2},{4,5},{5,4},{6,7},{7,6},{8,9},{9,8},{10,11... | collective-permute-start | bytes 258056 | tf_op jit(solution)/shard_map/ppermute | solution.py:53
  77.6 9.0 %collective-permute-start.26 = (bf16[48,896]{1,0:T(8,128)(2,1)S(1)}, bf16[48,896]{1,0:T(8,128)(2,1)S(1)}, u32[]{:S(2)}, u32[]{:S(2)}) collective-permute-start(bf16[48,896]{1,0:T(8,128)(2,1)S(1)} %get-tuple-element.156), channel_id=1, source_target_pairs={{0,2},{1,3},{2,0},{3,1},{4,6},{5,7},{6,4},{7,5},{8,10},{9,11},{10,... | collective-permute-start | bytes 258056 | tf_op jit(solution)/shard_map/ppermute | solution.py:53
  79.4 7.2 %collective-permute-start.27 = (bf16[48,896]{1,0:T(8,128)(2,1)S(1)}, bf16[48,896]{1,0:T(8,128)(2,1)S(1)}, u32[]{:S(2)}, u32[]{:S(2)}) collective-permute-start(bf16[48,896]{1,0:T(8,128)(2,1)S(1)} %get-tuple-element.157), channel_id=1, source_target_pairs={{0,3},{1,2},{2,1},{3,0},{4,7},{5,6},{6,5},{7,4},{8,11},{9,10},{10,... | collective-permute-start | bytes 258056 | tf_op jit(solution)/shard_map/ppermute | solution.py:53
  87.1 36.1 %collective-permute-start.28 = (bf16[128,7168]{1,0:T(8,128)(2,1)S(1)}, bf16[128,7168]{1,0:T(8,128)(2,1)S(1)}, u32[]{:S(2)}, u32[]{:S(2)}) collective-permute-start(bf16[128,7168]{1,0:T(8,128)(2,1)S(1)} %get-tuple-element.160), channel_id=1, source_target_pairs={{0,24},{8,0},{16,8},{24,16},{1,25},{9,1},{17,9},{25,17},{2,26},{10... | collective-permute-start | bytes 5505032 | tf_op jit(solution)/shard_map/ppermute | solution.py:19
  87.4 5.1 %collective-permute-start.29 = (bf16[6,3584]{1,0:T(8,128)(2,1)S(1)}, bf16[6,3584]{1,0:T(8,128)(2,1)S(1)}, u32[]{:S(2)}, u32[]{:S(2)}) collective-permute-start(bf16[6,3584]{1,0:T(8,128)(2,1)S(1)} %get-tuple-element.164), channel_id=1, source_target_pairs={{0,4},{4,0},{1,5},{5,1},{2,6},{6,2},{3,7},{7,3},{8,12},{12,8},{9,1... | collective-permute-start | bytes 129032 | tf_op jit(solution)/shard_map/ppermute | solution.py:19
  88.1 9.1 %collective-permute-start.30 = (bf16[48,896]{1,0:T(8,128)(2,1)S(1)}, bf16[48,896]{1,0:T(8,128)(2,1)S(1)}, u32[]{:S(2)}, u32[]{:S(2)}) collective-permute-start(bf16[48,896]{1,0:T(8,128)(2,1)S(1)} %get-tuple-element.159.refs_13_.refs_0_.refs_7_), channel_id=1, source_target_pairs={{1,0},{0,1},{3,2},{2,3},{5,4},{4,5},{7,6},{6,7},{9,8},{8,9},{11,10... | collective-permute-start | bytes 258056 | tf_op jit(solution)/shard_map/ppermute | solution.py:45
  88.2 10.0 %collective-permute-start.31 = (bf16[48,896]{1,0:T(8,128)(2,1)S(1)}, bf16[48,896]{1,0:T(8,128)(2,1)S(1)}, u32[]{:S(2)}, u32[]{:S(2)}) collective-permute-start(bf16[48,896]{1,0:T(8,128)(2,1)S(1)} %get-tuple-element.159.refs_13_.refs_0_.refs_7_), channel_id=1, source_target_pairs={{2,0},{3,1},{0,2},{1,3},{6,4},{7,5},{4,6},{5,7},{10,8},{11,9},{8,1... | collective-permute-start | bytes 258056 | tf_op jit(solution)/shard_map/ppermute | solution.py:45
  90.8 7.4 %collective-permute-start.32 = (bf16[48,896]{1,0:T(8,128)(2,1)S(1)}, bf16[48,896]{1,0:T(8,128)(2,1)S(1)}, u32[]{:S(2)}, u32[]{:S(2)}) collective-permute-start(bf16[48,896]{1,0:T(8,128)(2,1)S(1)} %get-tuple-element.159.refs_13_.refs_0_.refs_7_), channel_id=1, source_target_pairs={{3,0},{2,1},{1,2},{0,3},{7,4},{6,5},{5,6},{4,7},{11,8},{10,9},{9,1... | collective-permute-start | bytes 258056 | tf_op jit(solution)/shard_map/ppermute | solution.py:45
  99.6 5.4 %collective-permute-start.34 = (bf16[48,1152]{1,0:T(8,128)(2,1)S(1)}, bf16[48,1152]{1,0:T(8,128)(2,1)S(1)}, u32[]{:S(2)}, u32[]{:S(2)}) collective-permute-start(bf16[48,1152]{1,0:T(8,128)(2,1)S(1)} %get-tuple-element.171.refs_10_), channel_id=1, source_target_pairs={{0,4},{4,0},{1,5},{5,1},{2,6},{6,2},{3,7},{7,3},{8,12},{12,8},{9,1... | collective-permute-start | bytes 331784 | tf_op jit(solution)/shard_map/ppermute | solution.py:19
  102.6 9.3 %collective-permute-start.38 = (f32[4,3584]{1,0:T(4,128)S(1)}, f32[4,3584]{1,0:T(4,128)S(1)}, u32[]{:S(2)}, u32[]{:S(2)}) collective-permute-start(f32[4,3584]{1,0:T(4,128)S(1)} %get-tuple-element.188), channel_id=1, source_target_pairs={{0,4},{4,0},{1,5},{5,1},{2,6},{6,2},{3,7},{7,3},{8,12},{12,8},{9,1... | collective-permute-start | bytes 172040 | tf_op jit(solution)/shard_map/ppermute | solution.py:19
  107.4 9.1 %collective-permute-start.35 = (bf16[48,896]{1,0:T(8,128)(2,1)S(1)}, bf16[48,896]{1,0:T(8,128)(2,1)S(1)}, u32[]{:S(2)}, u32[]{:S(2)}) collective-permute-start(bf16[48,896]{1,0:T(8,128)(2,1)S(1)} %get-tuple-element.185), channel_id=1, source_target_pairs={{0,1},{1,0},{2,3},{3,2},{4,5},{5,4},{6,7},{7,6},{8,9},{9,8},{10,11... | collective-permute-start | bytes 258056 | tf_op jit(solution)/shard_map/ppermute | solution.py:53
  108.5 8.1 %collective-permute-start.36 = (bf16[48,896]{1,0:T(8,128)(2,1)S(1)}, bf16[48,896]{1,0:T(8,128)(2,1)S(1)}, u32[]{:S(2)}, u32[]{:S(2)}) collective-permute-start(bf16[48,896]{1,0:T(8,128)(2,1)S(1)} %get-tuple-element.186), channel_id=1, source_target_pairs={{0,2},{1,3},{2,0},{3,1},{4,6},{5,7},{6,4},{7,5},{8,10},{9,11},{10,... | collective-permute-start | bytes 258056 | tf_op jit(solution)/shard_map/ppermute | solution.py:53
  110.4 6.4 %collective-permute-start.37 = (bf16[48,896]{1,0:T(8,128)(2,1)S(1)}, bf16[48,896]{1,0:T(8,128)(2,1)S(1)}, u32[]{:S(2)}, u32[]{:S(2)}) collective-permute-start(bf16[48,896]{1,0:T(8,128)(2,1)S(1)} %get-tuple-element.187), channel_id=1, source_target_pairs={{0,3},{1,2},{2,1},{3,0},{4,7},{5,6},{6,5},{7,4},{8,11},{9,10},{10,... | collective-permute-start | bytes 258056 | tf_op jit(solution)/shard_map/ppermute | solution.py:53
  111.9 8.5 %collective-permute-start.33 = (bf16[6,7296]{1,0:T(8,128)(2,1)S(1)}, bf16[6,7296]{1,0:T(8,128)(2,1)S(1)}, u32[]{:S(2)}, u32[]{:S(2)}) collective-permute-start(bf16[6,7296]{1,0:T(8,128)(2,1)S(1)} %get-tuple-element.172), channel_id=1, source_target_pairs={{0,24},{8,0},{16,8},{24,16},{1,25},{9,1},{17,9},{25,17},{2,26},{10... | collective-permute-start | bytes 262664 | tf_op jit(solution)/shard_map/ppermute | solution.py:19
  117.3 4.3 %collective-permute-start.39 = (bf16[6,3584]{1,0:T(8,128)(2,1)S(1)}, bf16[6,3584]{1,0:T(8,128)(2,1)S(1)}, u32[]{:S(2)}, u32[]{:S(2)}) collective-permute-start(bf16[6,3584]{1,0:T(8,128)(2,1)S(1)} %get-tuple-element.194), channel_id=1, source_target_pairs={{0,24},{4,28},{8,0},{12,4},{16,8},{20,12},{24,16},{28,20},{1,25},{... | collective-permute-start | bytes 129032 | tf_op jit(solution)/shard_map/ppermute | solution.py:29
  118.2 5.1 %collective-permute-start.40 = (bf16[6,3584]{1,0:T(8,128)(2,1)S(1)}, bf16[6,3584]{1,0:T(8,128)(2,1)S(1)}, u32[]{:S(2)}, u32[]{:S(2)}) collective-permute-start(bf16[6,3584]{1,0:T(8,128)(2,1)S(1)} %get-tuple-element.195), channel_id=1, source_target_pairs={{0,28},{4,24},{8,4},{12,0},{16,12},{20,8},{24,20},{28,16},{1,29},{... | collective-permute-start | bytes 129032 | tf_op jit(solution)/shard_map/ppermute | solution.py:29
  118.9 6.9 %collective-permute-start.41 = (f32[4,896]{1,0:T(4,128)S(1)}, f32[4,896]{1,0:T(4,128)S(1)}, u32[]{:S(2)}, u32[]{:S(2)}) collective-permute-start(f32[4,896]{1,0:T(4,128)S(1)} %get-tuple-element.199), channel_id=1, source_target_pairs={{0,1},{1,0},{2,3},{3,2},{4,5},{5,4},{6,7},{7,6},{8,9},{9,8},{10,11... | collective-permute-start | bytes 43016 | tf_op jit(solution)/shard_map/ppermute | solution.py:53
  120.4 5.5 %collective-permute-start.42 = (f32[4,896]{1,0:T(4,128)S(1)}, f32[4,896]{1,0:T(4,128)S(1)}, u32[]{:S(2)}, u32[]{:S(2)}) collective-permute-start(f32[4,896]{1,0:T(4,128)S(1)} %get-tuple-element.200), channel_id=1, source_target_pairs={{0,2},{1,3},{2,0},{3,1},{4,6},{5,7},{6,4},{7,5},{8,10},{9,11},{10,... | collective-permute-start | bytes 43016 | tf_op jit(solution)/shard_map/ppermute | solution.py:53
  121.6 5.5 %collective-permute-start.43 = (f32[4,896]{1,0:T(4,128)S(1)}, f32[4,896]{1,0:T(4,128)S(1)}, u32[]{:S(2)}, u32[]{:S(2)}) collective-permute-start(f32[4,896]{1,0:T(4,128)S(1)} %get-tuple-element.201), channel_id=1, source_target_pairs={{0,3},{1,2},{2,1},{3,0},{4,7},{5,6},{6,5},{7,4},{8,11},{9,10},{10,... | collective-permute-start | bytes 43016 | tf_op jit(solution)/shard_map/ppermute | solution.py:53
